TPU v7x, 32 devices: a whole 2x2x4 slice. The times are simulated.
32 devices in a mesh: dom: 8 (over z, x), sub: 4 (over y, core).
Axes of the slice: x: 2, y: 2, z: 4, core: 2. Of those that a mesh axis runs over, the one named last changes fastest.
Arguments:
- feats: bfloat16 [12032, 1024], P(('dom', 'sub')), may hold values from -8 to 8
- w_proj: bfloat16 [1024, 1024], replicated, may hold values from -0.375 to 0.375
- w_skip: bfloat16 [1024, 1024], replicated, may hold values from -0.1875 to 0.1875
- attn_src: float32 [4, 256], replicated, may hold values from -0.25 to 0.25
- attn_dst: float32 [4, 256], replicated, may hold values from -0.25 to 0.25
- bias: float32 [1024], replicated, may hold values from -3 to 3
- gain: float32 [1024], replicated, may hold values from 0.5 to 1.5
- shift: float32 [1024], replicated, may hold values from -3 to 3
- cotangent: bfloat16 [12032, 1024], P(('dom', 'sub')), may hold values from -6 to 6
- neighbours: int32 [12032, 16], P(('dom', 'sub')), may hold values from 0 to 469, as said below
- edge_mask: int32 [12032, 16], P(('dom', 'sub')), may hold values from 0 to 1, as said below
- node_mask: int32 [12032], P(('dom', 'sub')), may hold values from 0 to 1, as said below
- send_index: int32 [32, 2, 47], P(('dom', 'sub')), may hold values from 0 to 375, as said below
Outputs:
- output: bfloat16 [12032, 1024], P(('dom', 'sub'))
- grad_feats: bfloat16 [12032, 1024], P(('dom', 'sub'))
- grad_proj: float32 [1024, 1024], replicated
- grad_skip: float32 [1024, 1024], replicated
- grad_attn_src: float32 [4, 256], replicated
- grad_attn_dst: float32 [4, 256], replicated
- grad_bias: float32 [1024], replicated
- grad_gain: float32 [1024], replicated
- grad_shift: float32 [1024], replicated
Inputs may be any that keep to these rules, and one draw needn't show every extreme that they name: `neighbours`: values below 376 are rows of the node's own partition; 376 + j names row send_index[p - 1, 1, j] of the partition below and 423 + j row send_index[p + 1, 0, j] of the partition above. A live slot never names a padded row and never names a partition outside 0 to 31. `edge_mask`: 0 on every slot of a padded node. `node_mask`: on each partition the real nodes come first and fill at least three quarters of its rows. `send_index`: each entry is a real node of the sending partition.
All inputs are finite; a program needn't handle non-finite values.
Results may differ from a plain program's by a relative error of at most 0.015.
Values may be sent and summed in bfloat16 or wider, within the bound.
No kernel may reach another device: no remote copies, remote signals or barrier semaphores. Data moves between devices by JAX's collectives and lax.ppermute only.
A program may use at most 128 MiB of HBM per device.

v0:
```python
import jax
import jax.numpy as jnp
from jax import lax
from jax.sharding import PartitionSpec as P


def passed_along(value, axis, steps):
    count = lax.axis_size(axis)
    initial, last = (max(0, -steps), min(count, count - steps))
    return lax.ppermute(value, axis, [(source, source + steps) for source in range(initial, last)])


def leaky_soft(values):
    return 0.2 * values + 0.8 * jax.nn.softplus(values)


def leaky_slope(values):
    return 0.2 + 0.8 * jax.nn.sigmoid(values)


def softmax_weights(edge_in, self_in, mask_block):
    scores = leaky_soft(edge_in)
    self_score = leaky_soft(self_in)
    live = mask_block[:, :, None] > 0
    masked = jnp.where(live, scores, -1e30)
    highest_score = jnp.maximum(self_score, jnp.max(masked, axis=1))
    weights = jnp.where(live, jnp.exp(masked - highest_score[:, None, :]), 0.0)
    self_weight = jnp.exp(self_score - highest_score)
    denominator = self_weight + jnp.sum(weights, axis=1)
    return (weights / denominator[:, None, :], self_weight / denominator)


def contract_rows(left_side, right_side):
    return lax.dot_general(
        left_side, right_side, (((0,), (0,)), ((), ())), preferred_element_type=jnp.float32
    )


def contract_cols(left_side, right_side):
    return lax.dot_general(
        left_side, right_side, (((1,), (1,)), ((), ())), preferred_element_type=jnp.float32
    )


def per_device(
    feats,
    w_proj,
    w_skip,
    attn_src,
    attn_dst,
    bias,
    gain,
    shift,
    cotangent,
    neighbours,
    edge_mask,
    node_mask,
    send_index,
):
    node_rows = feats.shape[0]
    heads_count, head_width = attn_src.shape
    concat_width = heads_count * head_width
    halo_rows = send_index.shape[2]
    block_rows = min(node_rows, 752)
    block_count = node_rows // block_rows
    ext_rows = node_rows + 2 * halo_rows
    projected = jnp.dot(feats, w_proj, preferred_element_type=jnp.float32)
    rounded = projected.astype(jnp.bfloat16)
    down_rows = send_index[0, 0]
    up_rows = send_index[0, 1]
    from_below = passed_along(rounded[up_rows], ("dom", "sub"), 1)
    from_above = passed_along(rounded[down_rows], ("dom", "sub"), -1)
    extended = jnp.concatenate([rounded, from_below, from_above], axis=0)
    ext_heads = extended.reshape(ext_rows, heads_count, head_width)
    el_source = jnp.einsum("rhc,hc->rh", ext_heads, attn_src, preferred_element_type=jnp.float32)
    el_target = jnp.einsum(
        "rhc,hc->rh", ext_heads[:node_rows], attn_dst, preferred_element_type=jnp.float32
    )

    def block_inputs(index):
        start = index * block_rows
        source_block = lax.dynamic_slice_in_dim(el_source, start, block_rows, 0)
        self_block = lax.dynamic_slice_in_dim(ext_heads, start, block_rows, 0)
        edge_in = el_source[neighbours] + el_target[:, None, :]
        self_in = source_block + el_target
        edge_weights, self_weight = softmax_weights(edge_in, self_in, edge_mask)
        return (neighbours, self_block, edge_in, self_in, edge_weights, self_weight)

    def forward_block(index):
        neighbour_block, self_block, edge_in, self_in, edge_weights, self_weight = block_inputs(
            index
        )
        gathered = ext_heads[neighbour_block]
        summed = jnp.einsum(
            "bkh,bkhc->bhc", edge_weights, gathered, preferred_element_type=jnp.float32
        )
        return self_weight[:, :, None] * self_block.astype(jnp.float32) + summed

    aggregated = lax.map(forward_block, jnp.arange(block_count)).reshape(node_rows, concat_width)
    skip_part = jnp.dot(feats, w_skip, preferred_element_type=jnp.float32)
    pre_act = aggregated + skip_part + bias
    activated = jax.nn.elu(pre_act)
    real = node_mask.astype(jnp.float32)[:, None]
    local_count = jnp.sum(real)
    local_mass = jnp.sum(real * activated, axis=0)
    node_total, mass_total = lax.psum((local_count, local_mass), ("dom", "sub"))
    mean_value = mass_total / node_total
    spread_total = lax.psum(jnp.sum(real * (activated - mean_value) ** 2, axis=0), ("dom", "sub"))
    variance = spread_total / node_total
    inv_std = lax.rsqrt(variance + 1e-05)
    normed = (activated - mean_value) * inv_std
    output = (real * (gain * normed + shift)).astype(jnp.bfloat16)
    grad_out = real * cotangent.astype(jnp.float32)
    sum_grad, sum_grad_norm = lax.psum(
        (jnp.sum(grad_out, axis=0), jnp.sum(grad_out * normed, axis=0)), ("dom", "sub")
    )
    grad_act = (
        real
        * inv_std
        * gain
        * (grad_out - sum_grad / node_total - normed * sum_grad_norm / node_total)
    )
    grad_pre = grad_act * jnp.where(pre_act > 0, 1.0, jnp.exp(jnp.minimum(pre_act, 0.0)))
    skip_rounded = grad_pre.astype(jnp.bfloat16)
    local_bias_grad = jnp.sum(grad_pre, axis=0)
    grad_heads = grad_pre.reshape(node_rows, heads_count, head_width)

    def backward_block(carry, index):
        ext_grad, source_grad = carry
        neighbour_block, self_block, edge_in, self_in, edge_weights, self_weight = block_inputs(
            index
        )
        gathered = ext_heads[neighbour_block]
        weight_grad = jnp.einsum(
            "bhc,bkhc->bkh", grad_heads, gathered, preferred_element_type=jnp.float32
        )
        self_weight_grad = jnp.sum(grad_heads * self_block.astype(jnp.float32), axis=-1)
        weighted = self_weight * self_weight_grad + jnp.sum(edge_weights * weight_grad, axis=1)
        score_grad = edge_weights * (weight_grad - weighted[:, None, :]) * leaky_slope(edge_in)
        self_score_grad = self_weight * (self_weight_grad - weighted) * leaky_slope(self_in)
        flat_rows = neighbour_block.reshape(-1)
        edge_rows = (edge_weights[:, :, :, None] * grad_heads[:, None]).reshape(-1, concat_width)
        ext_grad = ext_grad.at[flat_rows].add(edge_rows)
        source_grad = source_grad.at[flat_rows].add(score_grad.reshape(-1, heads_count))
        self_rows = (self_weight[:, :, None] * grad_heads).reshape(block_rows, concat_width)
        target_grad = self_score_grad + jnp.sum(score_grad, axis=1)
        return ((ext_grad, source_grad), (self_rows, self_score_grad, target_grad))

    start_carry = (
        jnp.zeros((ext_rows, concat_width), jnp.float32),
        jnp.zeros((ext_rows, heads_count), jnp.float32),
    )
    (ext_grad, source_grad), (self_rows, self_score_grad, target_grad) = lax.scan(
        backward_block, start_carry, jnp.arange(block_count)
    )
    self_rows = self_rows.reshape(node_rows, concat_width)
    self_score_grad = self_score_grad.reshape(node_rows, heads_count)
    target_grad = target_grad.reshape(node_rows, heads_count)
    source_grad = source_grad.at[:node_rows].add(self_score_grad)
    local_src_grad = jnp.einsum(
        "rh,rhc->hc", source_grad, ext_heads, preferred_element_type=jnp.float32
    )
    local_dst_grad = jnp.einsum(
        "rh,rhc->hc", target_grad, ext_heads[:node_rows], preferred_element_type=jnp.float32
    )
    ext_grad = ext_grad + (source_grad[:, :, None] * attn_src).reshape(ext_rows, concat_width)
    own_grad = (
        ext_grad[:node_rows]
        + self_rows
        + (target_grad[:, :, None] * attn_dst).reshape(node_rows, concat_width)
    )
    back_below = passed_along(
        ext_grad[node_rows : node_rows + halo_rows].astype(jnp.bfloat16), ("dom", "sub"), -1
    ).astype(jnp.float32)
    back_above = passed_along(
        ext_grad[node_rows + halo_rows :].astype(jnp.bfloat16), ("dom", "sub"), 1
    ).astype(jnp.float32)
    own_grad = own_grad.at[up_rows].add(back_below).at[down_rows].add(back_above)
    grad_rounded = own_grad.astype(jnp.bfloat16)
    local_proj_grad = contract_rows(feats, grad_rounded)
    grad_feats = (contract_cols(grad_rounded, w_proj) + contract_cols(skip_rounded, w_skip)).astype(
        jnp.bfloat16
    )
    local_skip_grad = contract_rows(feats, skip_rounded)
    proj_grad, skip_weight_grad, src_grad, dst_grad, bias_grad = lax.psum(
        (local_proj_grad, local_skip_grad, local_src_grad, local_dst_grad, local_bias_grad),
        ("dom", "sub"),
    )
    return (
        output,
        grad_feats,
        proj_grad,
        skip_weight_grad,
        src_grad,
        dst_grad,
        bias_grad,
        sum_grad_norm,
        sum_grad,
    )


def solution(mesh):
    in_specs = (
        P(("dom", "sub"), None),
        P(),
        P(),
        P(),
        P(),
        P(),
        P(),
        P(),
        P(("dom", "sub"), None),
        P(("dom", "sub"), None),
        P(("dom", "sub"), None),
        P(("dom", "sub")),
        P(("dom", "sub"), None, None),
    )
    out_specs = (
        P(("dom", "sub"), None),
        P(("dom", "sub"), None),
        P(),
        P(),
        P(),
        P(),
        P(),
        P(),
        P(),
    )
    return jax.shard_map(
        per_device, mesh=mesh, in_specs=in_specs, out_specs=out_specs, check_vma=False
    )
```

profile of v0, /device:TPU:0, one launch (start us, length us, event | category | flops | bytes accessed | tf_op | source)
XLA Modules:
  0.0 594.4 jit_solution(7123466741107131260)
XLA Ops:
  8.6 2.8 convolution_convert_fusion
  12.1 3.0 collective-permute-start
  26.3 20.6 %gather_fusion.3 = bf16[6016,4,256]{2,1,0:T(4,128)(2,1)} fusion(bf16[470,4,256]{2,1,0:T(4,128)(2,1)S(1)} %reshape.213, s32[6144]{0:T(1024)S(1)} %pad_clamp_fusion), kind=kCustom, calls=%fused_computation.3 | custom fusion | bytes 24665600 | tf_op jit(solution)/shard_map/while/body/eval_jaxpr/gather | solution.py:93
  46.9 12.1 %gather_fusion.2 = f32[6016,4]{1,0:T(8,128)} fusion(f32[470,4]{1,0:T(8,128)S(1)} %copy.56, s32[6144]{0:T(1024)S(1)} %pad_clamp_fusion), kind=kCustom, calls=%fused_computation.2 | custom fusion | bytes 216576 | tf_op jit(solution)/shard_map/while/body/eval_jaxpr/gather | solution.py:84
  59.0 4.4 copy.57
  67.0 6.6 %fusion.2 = f32[376,4,1,256]{3,2,1,0:T(1,128)S(1)} fusion(bf16[376,16,4,256]{3,2,1,0:T(4,128)(2,1)} %bitcast.113, f32[376,16,4,1]{1,0,2,3:T(8,128)} %fusion.69), kind=kOutput, calls=%fused_computation.11 | convolution fusion | flops 12320768 | bytes 13957120 | tf_op jit(solution)/shard_map/while/body/eval_jaxpr/bkh,bkhc->bhc/dot_general | solution.py:94
  75.4 2.7 multiply_reduce_fusion.2
  78.1 44.6 %all-reduce.2 = (f32[1024]{0:T(1024)S(1)}, f32[]{:T(128)}) all-reduce(f32[1024]{0:T(1024)S(1)} %get-tuple-element.152, f32[]{:T(128)} %convert_reduce_fusion), channel_id=1, replica_groups=mesh['dom'=8,'sub'=4] {'dom','sub'}, use_global_device_ids=true, to_apply=%region_3.4 | all-reduce | flops 1025 | bytes 8200 | tf_op jit(solution)/shard_map/psum | solution.py:106
  125.6 40.3 %psum.72 = f32[1024]{0:T(1024)S(1)} all-reduce(f32[1024]{0:T(1024)S(1)} %multiply_reduce_fusion.1), channel_id=1, replica_groups=mesh['dom'=8,'sub'=4] {'dom','sub'}, use_global_device_ids=true, to_apply=%region_7.8 | all-reduce | flops 1024 | bytes 8192 | tf_op jit(solution)/shard_map/psum | solution.py:108
  169.1 40.1 %all-reduce.1 = (f32[1024]{0:T(1024)S(1)}, f32[1024]{0:T(1024)S(1)}) all-reduce(f32[1024]{0:T(1024)S(1)} %get-tuple-element.127, f32[1024]{0:T(1024)S(1)} %get-tuple-element.126), channel_id=1, replica_groups=mesh['dom'=8,'sub'=4] {'dom','sub'}, use_global_device_ids=true, to_apply=%region_11.12 | all-reduce | flops 2048 | bytes 16384 | tf_op jit(solution)/shard_map/psum | solution.py:114
  209.9 5.9 fusion.53
  215.8 5.3 reshape.299
  221.1 2.8 reshape.216
  225.6 6.3 %fusion = f32[376,4,1,16]{3,2,1,0:T(1,128)S(1)} fusion(bf16[376,4,256,1]{2,3,1,0:T(2,128)(2,1)S(1)} %copy-done.16, bf16[376,16,4,256]{3,2,1,0:T(4,128)(2,1)} %bitcast.114), kind=kOutput, calls=%fused_computation.9 | convolution fusion | flops 12320768 | bytes 13187072 | tf_op jit(solution)/shard_map/while/body/eval_jaxpr/bhc,bkhc->bkh/dot_general | solution.py:134
  234.8 3.7 fusion.56
  238.6 4.5 copy.84
  243.1 33.9 %scatter_custom_fusion = f32[470,4]{1,0:T(8,128)S(1)} fusion(s32[6016]{0:T(1024)S(1)} %fusion.40, f32[6016,4]{1,0:T(8,128)} %bitcast.123, f32[]{:T(128)} %constant.121.clone.1), kind=kCustom, calls=%fused_computation.71 | custom fusion | flops 24064 | bytes 8032 | tf_op jit(solution)/shard_map/while/body/eval_jaxpr/scatter-add | solution.py:144
  277.3 3.7 copy.65
  281.0 8.7 %broadcast_multiply_fusion = f32[376,16,4,256]{3,2,1,0:T(4,128)S(1)} fusion(f32[376,4,256]{2,1,0:T(4,128)} %reshape.216, f32[376,16,4]{2,1,0:T(8,128)} %copy.65), kind=kLoop, calls=%fused_computation.8 | loop fusion | flops 6160384 | bytes 26277888 | tf_op jit(solution)/shard_map/while/body/eval_jaxpr/mul | solution.py:142
  289.7 13.8 %copy.90 = f32[752,8,4,256]{3,1,2,0:T(8,128)} copy(f32[752,8,4,256]{3,2,1,0:T(4,128)S(1)} %bitcast.109) | data formatting | bytes 49283072
  312.3 56.5 %scatter_fusion = f32[470,1024]{1,0:T(8,128)} fusion(f32[470,1024]{1,0:T(8,128)} %broadcast_multiply_fusion.1, s32[6016]{0:T(1024)S(1)} %fusion.40, f32[6016,1024]{1,0:T(8,128)} %bitcast.108), kind=kCustom, calls=%fused_computation.5 | custom fusion | flops 6160384 | bytes 73948672 | tf_op jit(solution)/shard_map/while/body/eval_jaxpr/scatter-add | solution.py:143
  371.9 3.2 collective-permute-start.3
  375.2 4.4 fusion.8
  379.6 3.3 convolution_bitcast_fusion
  382.9 3.7 scatter_custom_fusion.2
  386.6 3.7 scatter_custom_fusion.3
  390.3 4.7 convolution_bitcast_fusion.1
  396.9 42.7 %all-reduce = (f32[4,256]{1,0:T(4,128)}, f32[4,256]{1,0:T(4,128)}, f32[1024]{0:T(1024)}) all-reduce(f32[4,256]{1,0:T(4,128)S(1)} %get-tuple-element.155, f32[4,256]{1,0:T(4,128)S(1)} %get-tuple-element.154, f32[1024]{0:T(1024)S(1)} %copy-done.20), channel_id=1, replica_groups=mesh['dom'=8,'sub'=4] {'dom','sub'}, use_global_device_ids=true, to_apply=%region_21.22 | all-reduce | flops 3072 | bytes 24576 | tf_op jit(solution)/shard_map/psum | solution.py:185
  439.6 2.6 fusion.30
  444.1 132.5 %all-reduce.6.cloned.1.call-done = (f32[1024,1024]{0,1:T(8,128)}, f32[1024,1024]{0,1:T(8,128)}) async-done(((f32[1024,1024]{0,1:T(8,128)}, f32[1024,1024]{0,1:T(8,128)}), (f32[1024,1024]{0,1:T(8,128)}, f32[1024,1024]{0,1:T(8,128)})) %all-reduce.6.cloned.1.call-update) | async-done | bytes 8388624 | tf_op jit(solution)/shard_map/psum | solution.py:185
  576.7 5.3 copy.67
  582.0 5.3 copy.68
  (136 shorter events, 45.7 us)
Async XLA Ops:
  7.2 67.5 %copy-start = (bf16[1024,1024]{1,0:T(8,128)(2,1)S(1)}, bf16[1024,1024]{1,0:T(8,128)(2,1)}, u32[]{:S(2)}) copy-start(bf16[1024,1024]{1,0:T(8,128)(2,1)} %param.17) | copy-start | bytes 6291460
  7.2 569.5 %all-reduce.6.cloned.1.call-start = ((), (), s32[]{:S(2)}) async-start(), calls=%async_computation | async-start | bytes 16777216 | tf_op jit(solution)/shard_map/psum | solution.py:185
  8.1 7.0 %copy-start.28 = (s32[47]{0:T(128)}, s32[47]{0:T(128)S(1)}, u32[]{:S(2)}) copy-start(s32[47]{0:T(128)S(1)} %get-tuple-element.151) | copy-start | bytes 568
  11.4 10.3 %copy-start.6 = (bf16[376,1024]{1,0:T(8,128)(2,1)}, bf16[376,1024]{1,0:T(8,128)(2,1)S(1)}, u32[]{:S(2)}) copy-start(bf16[376,1024]{1,0:T(8,128)(2,1)S(1)} %convolution_convert_fusion) | copy-start | bytes 2310148
  11.4 7.9 %copy-start.17 = (s32[376,16]{0,1:T(8,128)S(1)}, s32[376,16]{0,1:T(8,128)}, u32[]{:S(2)}) copy-start(s32[376,16]{0,1:T(8,128)} %param.24) | copy-start | bytes 72196
  12.1 9.6 %collective-permute-start = (bf16[47,1024]{1,0:T(8,128)(2,1)S(1)}, bf16[47,1024]{1,0:T(8,128)(2,1)}, u32[]{:S(2)}, u32[]{:S(2)}) collective-permute-start(bf16[47,1024]{1,0:T(8,128)(2,1)S(1)} %gather_fusion), channel_id=1, source_target_pairs={{0,1},{1,2},{2,3},{3,4},{4,5},{5,6},{6,7},{7,8},{8,9},{9,10},{10,1... | collective-permute-start | bytes 288776 | tf_op jit(solution)/shard_map/ppermute | solution.py:10
  15.1 4.6 copy-start.22
  16.4 3.6 copy-start.18
  16.4 3.8 copy-start.21
  16.4 4.0 copy-start.23
  16.4 5.2 collective-permute-start.1
  25.8 21.2 %copy-start.2 = (bf16[470,4,256]{2,1,0:T(4,128)(2,1)}, bf16[470,4,256]{2,1,0:T(4,128)(2,1)S(1)}, u32[]{:S(2)}) copy-start(bf16[470,4,256]{2,1,0:T(4,128)(2,1)S(1)} %reshape.213) | copy-start | bytes 2887684
  67.0 6.6 %copy-start.9 = (bf16[376,4,256]{2,1,0:T(4,128)(2,1)S(1)}, bf16[376,4,256]{2,1,0:T(4,128)(2,1)}, u32[]{:S(2)}) copy-start(bf16[376,4,256]{2,1,0:T(4,128)(2,1)} %slice.49) | copy-start | bytes 2310148
  125.5 84.3 %copy-start.25 = (f32[1024]{0:T(1024)S(1)}, f32[1024]{0:T(1024)}, u32[]{:S(2)}) copy-start(f32[1024]{0:T(1024)} %param.21) | copy-start | bytes 12292
  125.5 84.3 %copy-start.26 = (f32[1024]{0:T(1024)S(1)}, f32[1024]{0:T(1024)}, u32[]{:S(2)}) copy-start(f32[1024]{0:T(1024)} %param.22) | copy-start | bytes 12292
  209.2 6.6 %copy-start.24 = (f32[1024]{0:T(1024)}, f32[1024]{0:T(1024)S(1)}, u32[]{:S(2)}) copy-start(f32[1024]{0:T(1024)S(1)} %get-tuple-element.132) | copy-start | bytes 12292
  209.2 6.6 %copy-start.27 = (f32[1024]{0:T(1024)}, f32[1024]{0:T(1024)S(1)}, u32[]{:S(2)}) copy-start(f32[1024]{0:T(1024)S(1)} %get-tuple-element.131) | copy-start | bytes 12292
  223.9 1.7 copy-start.16
  225.6 8.4 %copy-start.10 = (bf16[376,4,256]{2,1,0:T(4,128)(2,1)S(1)}, bf16[376,4,256]{2,1,0:T(4,128)(2,1)}, u32[]{:S(2)}) copy-start(bf16[376,4,256]{2,1,0:T(4,128)(2,1)} %slice.49) | copy-start | bytes 2310148
  232.8 1.4 copy-start.7
  243.1 34.2 %copy-start.14 = (f32[376,16,4]{1,0,2:T(8,128)S(1)}, f32[376,16,4]{1,0,2:T(8,128)}, u32[]{:S(2)}) copy-start(f32[376,16,4]{1,0,2:T(8,128)} %fusion.27) | copy-start | bytes 288772
  308.6 2.1 copy-start.8
  368.7 6.4 %copy-start.1 = (f32[470,1024]{1,0:T(8,128)S(1)}, f32[470,1024]{1,0:T(8,128)}, u32[]{:S(2)}) copy-start(f32[470,1024]{1,0:T(8,128)} %scatter_fusion) | copy-start | bytes 5775364
  368.7 6.4 %copy-start.19 = (f32[1,2,4,128]{3,1,2,0:T(2,128)S(1)}, f32[1,2,4,128]{3,1,2,0:T(2,128)}, u32[]{:S(2)}) copy-start(f32[1,2,4,128]{3,1,2,0:T(2,128)} %copy.93) | copy-start | bytes 12292
  370.6 12.4 %collective-permute-start.2 = (bf16[47,1024]{1,0:T(8,128)(2,1)S(1)}, bf16[47,1024]{1,0:T(8,128)(2,1)S(1)}, u32[]{:S(2)}, u32[]{:S(2)}) collective-permute-start(bf16[47,1024]{1,0:T(8,128)(2,1)S(1)} %get-tuple-element.145), channel_id=1, source_target_pairs={{1,0},{2,1},{3,2},{4,3},{5,4},{6,5},{7,6},{8,7},{9,8},{10,9},{11,1... | collective-permute-start | bytes 288776 | tf_op jit(solution)/shard_map/ppermute | solution.py:10
  371.9 14.7 %collective-permute-start.3 = (bf16[47,1024]{1,0:T(8,128)(2,1)S(1)}, bf16[47,1024]{1,0:T(8,128)(2,1)S(1)}, u32[]{:S(2)}, u32[]{:S(2)}) collective-permute-start(bf16[47,1024]{1,0:T(8,128)(2,1)S(1)} %get-tuple-element.144), channel_id=1, source_target_pairs={{0,1},{1,2},{2,3},{3,4},{4,5},{5,6},{6,7},{7,8},{8,9},{9,10},{10,1... | collective-permute-start | bytes 288776 | tf_op jit(solution)/shard_map/ppermute | solution.py:10
  375.1 4.4 copy-start.4
  375.2 4.4 copy-start.12
  395.0 1.7 copy-start.3
  395.0 1.9 copy-start.20
  439.6 2.6 copy-start.5
  439.6 2.6 copy-start.15
  (4 other events, 3.6 us)
Sparse Core Ops, SparseCore 0:
  395.2 181.4 all-reduce.5
where the time goes:
time: 605 us; the launch traced here: 594 us
  blocking collectives  168 us (28%)
  other arithmetic  142 us (23%)
  waiting for transfers between devices  133 us (22%)
  local copies, waits for them, and re-layouts  95.5 us (16%)
  matrix products  33.3 us (6%)
  between operations  14.8 us (2%)
  starting transfers between devices  8.98 us (1%)
    psum x1, waiting for transfers between devices, per_device(): lax.psum((local_proj_grad, local_skip_grad, local_src_grad, local_dst_gra...  133 us
    scatter-add x1, other arithmetic, backward_block(): ext_grad = ext_grad.at[flat_rows].add(edge_rows)  56.5 us
    psum x1, blocking collectives, per_device(): node_total, mass_total = lax.psum((local_count, local_mass), ('dom', 'sub'))  44.6 us
    psum x1, blocking collectives, per_device(): lax.psum((local_proj_grad, local_skip_grad, local_src_grad, local_dst_gra...  42.7 us
    psum x1, blocking collectives, per_device(): lax.psum(jnp.sum(real * (activated - mean_value) ** 2, axis=0), ('dom', '...  40.3 us
    psum x1, blocking collectives, per_device(): lax.psum((jnp.sum(grad_out, axis=0), jnp.sum(grad_out * normed, axis=0)),...  40.1 us
    scatter-add x1, other arithmetic, backward_block(): source_grad.at[flat_rows].add(score_grad.reshape(-1, heads_count))  33.9 us
    unnamed x74, local copies, waits for them, and re-layouts  33.6 us
  transfers between devices with their start and end apart: 5, of which 1 were waited for; matrix products, arithmetic and copies ran while one was open for 4% of the time, Pallas kernels for 0%

commit v1 on v0

v1 whole, which is shorter than its diff:
```python
import functools

import jax
import jax.numpy as jnp
from jax import lax
from jax.experimental import pallas as pl
from jax.experimental.pallas import tpu as pltpu
from jax.sharding import PartitionSpec as P

AXES = ("dom", "sub")
F32 = jnp.float32
BF16 = jnp.bfloat16
NEG = -1e30
STEP = 64
SHARDS = 16
CHUNK = 32
LANES = 128
VMEM = 56 * 1024 * 1024


def params(**more):
    return pltpu.CompilerParams(vmem_limit_bytes=VMEM, **more)


def mm(a, b, contract):
    return lax.dot_general(a, b, ((contract[:1], contract[1:]), ((), ())), preferred_element_type=F32)


def pad_rows(value, rows):
    extra = rows - value.shape[0]
    if extra == 0:
        return value
    return jnp.concatenate([value, jnp.zeros((extra,) + value.shape[1:], value.dtype)], axis=0)


def three_parts(value):
    high = value.astype(BF16)
    rest = value - high.astype(F32)
    middle = rest.astype(BF16)
    low = (rest - middle.astype(F32)).astype(BF16)
    return high, middle, low


def one_hot(rows, index_ref, side, scratch, width):
    halo = index_ref.shape[2]
    scratch[...] = jnp.full(scratch.shape, -1, jnp.int32)
    scratch[0:1, 0:halo] = index_ref[0, side : side + 1, :]
    wanted = scratch[0:1, 0:width]
    return (lax.broadcasted_iota(jnp.int32, (rows, width), 0) == wanted).astype(BF16)


def halo_rows_kernel(feats_ref, index_ref, down_ref, up_ref, scratch):
    rows = feats_ref.shape[0]
    for side, out in ((0, down_ref), (1, up_ref)):
        picked = one_hot(rows, index_ref, side, scratch, out.shape[0])
        out[...] = mm(picked, feats_ref[...], (0, 0)).astype(BF16)


def project_kernel(feats_ref, proj_ref, skip_w_ref, neighbours_ref, mask_ref, zq_ref, skip_ref, count_ref, padded_ref):
    node_rows = feats_ref.shape[0]
    rows, columns = count_ref.shape
    halo = (columns - rows) // 2

    @pl.when(pl.program_id(0) == 0)
    def _():
        padded_ref[...] = pad_rows(feats_ref[...].astype(F32), rows).astype(BF16)
        base = lax.broadcasted_iota(jnp.int32, (8, columns), 1)
        for start in range(0, rows, 8):
            own = lax.broadcasted_iota(jnp.int32, (8, columns), 0) + start
            total = (base == own).astype(F32)
            if start < node_rows:
                names = neighbours_ref[start : start + 8, :]
                live = mask_ref[start : start + 8, :] > 0
                names = jnp.where(live, names, -1)
                for slot in range(names.shape[1]):
                    total += (base == names[:, slot : slot + 1]).astype(F32)
            count_ref[start : start + 8, :] = total

    feats = padded_ref[...]
    zq_ref[...] = mm(feats, proj_ref[...], (1, 0)).astype(BF16)
    skip_ref[...] = mm(feats, skip_w_ref[...], (1, 0))


def attend_kernel(
    zq_ref, below_ref, above_ref, proj_ref, skip_ref, count_ref, src_ref, dst_ref, bias_ref, cot_ref, real_ref,
    ext_ref, weight_ref, slope_ref, pre_ref, stats_ref, halo_ref, target_scr,
):
    rows, columns = count_ref.shape
    half = (columns - rows) // 2

    @pl.when(pl.program_id(0) == 0)
    def _():
        halo_ref[...] = jnp.zeros_like(halo_ref)
        halo_ref[0 : below_ref.shape[0], :] = below_ref[...]
        halo_ref[half : half + above_ref.shape[0], :] = above_ref[...]

    ext_ref[0:rows, :] = zq_ref[...]
    ext_ref[rows:columns, :] = mm(halo_ref[...], proj_ref[...], (1, 0)).astype(BF16)
    ext = ext_ref[...]
    own = zq_ref[...]
    width = ext.shape[1]
    source = jnp.zeros((8, columns), F32)
    target = jnp.zeros((rows, LANES), F32)
    for part in three_parts(src_ref[0]):
        source += mm(jnp.broadcast_to(part, (8, width)), ext, (1, 1))
    for part in three_parts(dst_ref[0]):
        target += mm(own, jnp.broadcast_to(part, (LANES, width)), (1, 1))
    target_scr[...] = target
    source = source[0:1, :]

    def chunk(index, carry):
        where = pl.ds(pl.multiple_of(index * CHUNK, CHUNK), CHUNK)
        column = target_scr[where, :]
        value = jnp.concatenate([column] * (columns // LANES), axis=1) + source
        count = count_ref[where, :]
        small = jnp.exp(-jnp.abs(value))
        score = 0.2 * value + 0.8 * (jnp.maximum(value, 0.0) + jnp.log(1.0 + small))
        masked = jnp.where(count > 0, score, NEG)
        highest = jnp.max(masked, axis=1, keepdims=True)
        weight = jnp.exp(masked - highest) * count
        sigmoid = jnp.where(value >= 0, 1.0, small) / (1.0 + small)
        weight_ref[0, where, :] = weight.astype(BF16)
        slope_ref[0, where, :] = (weight * (0.2 + 0.8 * sigmoid)).astype(BF16)
        return carry

    lax.fori_loop(0, rows // CHUNK, chunk, 0)
    weights = weight_ref[0]
    total = mm(weights, jnp.ones((columns, LANES), BF16), (1, 0))
    scale = 1.0 / total
    scale = jnp.concatenate([scale] * (width // LANES), axis=1)
    pre = mm(weights, ext, (1, 0)) * scale + skip_ref[...] + bias_ref[...]
    pre_ref[...] = pre
    act = jnp.where(pre > 0, pre, jnp.exp(jnp.minimum(pre, 0.0)) - 1.0)
    real = real_ref[...]
    cot = pad_rows(cot_ref[...].astype(F32), rows) * real
    nodes = jnp.sum(jnp.broadcast_to(real, act.shape), axis=0, keepdims=True)
    mean = jnp.sum(act * real, axis=0, keepdims=True) / nodes
    centred = act - mean
    stats_ref[...] = jnp.zeros_like(stats_ref)
    stats_ref[0:1, :] = nodes
    stats_ref[1:2, :] = mean
    stats_ref[2:3, :] = jnp.sum(real * centred * centred, axis=0, keepdims=True)
    stats_ref[3:4, :] = jnp.sum(cot, axis=0, keepdims=True)
    stats_ref[4:5, :] = jnp.sum(cot * centred, axis=0, keepdims=True)


def merge(first, second):
    nodes = first[0:1] + second[0:1]
    gap = second[1:2] - first[1:2]
    part = second[0:1] / nodes
    mean = first[1:2] + gap * part
    spread = first[2:3] + second[2:3] + gap * gap * first[0:1] * part
    shift = first[3:4] + second[3:4]
    gain = first[4:5] + second[4:5] - (mean - first[1:2]) * first[3:4] - (mean - second[1:2]) * second[3:4]
    return jnp.concatenate([nodes, mean, spread, shift, gain, first[5:]], axis=0)


def place_blocks(out_ref, slot, value, me):
    size = value.shape[0] // SHARDS
    for block in range(SHARDS):
        at = pl.multiple_of((block ^ me) * size, size)
        out_ref[slot, pl.ds(at, size), :] = value[block * size : (block + 1) * size, :]


def norm_kernel(
    where_ref, pre_ref, stats_ref, cot_ref, real_ref, gain_ref, shift_ref, feats_ref,
    out_ref, dskip_ref, send_ref, keep_ref, bias_ref,
):
    rows = pre_ref.shape[0]
    node_rows = out_ref.shape[0]
    step = pl.program_id(0)
    pre = pre_ref[...]
    act = jnp.where(pre > 0, pre, jnp.exp(jnp.minimum(pre, 0.0)) - 1.0)
    steep = jnp.where(pre > 0, 1.0, jnp.exp(jnp.minimum(pre, 0.0)))
    real = real_ref[...]
    grad = pad_rows(cot_ref[...].astype(F32), rows) * real
    nodes = stats_ref[0:1, :]
    inverse = lax.rsqrt(stats_ref[2:3, :] / nodes + 1e-05)
    normed = (act - stats_ref[1:2, :]) * inverse
    gain = gain_ref[...]
    out_ref[...] = (real * (gain * normed + shift_ref[...]))[:node_rows].astype(BF16)
    grad_shift = stats_ref[3:4, :] / nodes
    grad_gain = stats_ref[4:5, :] * inverse / nodes
    grad_pre = real * (inverse * gain) * (grad - grad_shift - normed * grad_gain) * steep
    bias_ref[0] = jnp.broadcast_to(jnp.sum(grad_pre, axis=0, keepdims=True), bias_ref.shape[1:])
    dskip = grad_pre.astype(BF16)
    dskip_ref[...] = dskip
    grads = mm(feats_ref[...], dskip, (0, 0)).astype(BF16)

    @pl.when(step < 2)
    def _():
        place_blocks(send_ref, 0, grads, where_ref[4 + step % 2])

    @pl.when(step >= 2)
    def _():
        place_blocks(keep_ref, 0, grads, where_ref[4 + step % 2])


def back_kernel(
    where_ref, weight_ref, slope_ref, ext_ref, dskip_ref, src_ref, dst_ref, feats_ref, halo_ref,
    grad_ref, own_ref, below_ref, above_ref, small_ref, dal_scr, tgt_scr, inv_scr,
):
    rows, columns = weight_ref.shape[1:]
    half = (columns - rows) // 2
    width = ext_ref.shape[1]
    weights = weight_ref[0]
    ext = ext_ref[...]
    dskip = dskip_ref[...]
    dal_scr[...] = mm(dskip, ext, (1, 1))
    inverse = 1.0 / mm(weights, jnp.ones((columns, LANES), BF16), (1, 0))
    inv_scr[...] = inverse
    dst = dst_ref[0]

    def chunk(index, carry):
        by_source, by_target = carry
        where = pl.ds(pl.multiple_of(index * CHUNK, CHUNK), CHUNK)
        scale = jnp.concatenate([inv_scr[where, :]] * (columns // LANES), axis=1)
        dalpha = dal_scr[where, :]
        mean = jnp.sum(weight_ref[0, where, :].astype(F32) * scale * dalpha, axis=1, keepdims=True)
        du = slope_ref[0, where, :].astype(F32) * scale * (dalpha - mean)
        target = jnp.sum(du, axis=1, keepdims=True)
        tgt_scr[where, :] = target * dst
        by_target += (target * ext_ref[where, :].astype(F32)).reshape(CHUNK // 8, 8, width).sum(axis=0)
        by_source += du.reshape(CHUNK // 8, 8, columns).sum(axis=0)
        return by_source, by_target

    start = (jnp.zeros((8, columns), F32), jnp.zeros((8, width), F32))
    by_source, by_target = lax.fori_loop(0, rows // CHUNK, chunk, start)
    spread = jnp.concatenate([inverse] * (width // LANES), axis=1)
    scaled = (dskip.astype(F32) * spread).astype(BF16)
    dz = mm(weights, scaled, (0, 0))
    source = jnp.broadcast_to(jnp.sum(by_source, axis=0, keepdims=True), by_source.shape)
    dz += mm(source.astype(BF16), jnp.broadcast_to(src_ref[0] * 0.125, (8, width)).astype(BF16), (0, 0))
    dz_own = dz[:rows] + tgt_scr[...]
    own_ref[...] = dz_own
    dz_halo = dz[rows:].astype(BF16)
    below_ref[...] = dz_halo[: below_ref.shape[0]]
    above_ref[...] = dz_halo[half : half + above_ref.shape[0]]
    small_ref[0] = jnp.zeros(small_ref.shape[1:], F32)
    high, middle, low = three_parts(source)
    small_ref[0, 0:1, :] = (mm(high, ext, (1, 0)) + mm(middle, ext, (1, 0)) + mm(low, ext, (1, 0)))[0:1]
    small_ref[0, 1:2, :] = jnp.sum(by_target, axis=0, keepdims=True)
    grads = mm(feats_ref[...], dz_own.astype(BF16), (0, 0)) + mm(halo_ref[...], dz_halo, (0, 0))
    place_blocks(grad_ref, 0, grads.astype(BF16), where_ref[4 + pl.program_id(0)])


def feats_kernel(where_ref, send_ref, keep_ref, low_ref, high_ref, index_ref, dskip_ref, proj_ref, skip_ref, out_ref, total, picks, scratch):
    step = pl.program_id(0)
    rows = send_ref.shape[0]
    count = low_ref.shape[0]

    @pl.when(step == 0)
    def _():
        total[...] = jnp.zeros_like(total)
        picks[0] = one_hot(rows, index_ref, 1, scratch, count)
        picks[1] = one_hot(rows, index_ref, 0, scratch, count)

    own = jnp.where(step < 2, send_ref[...], keep_ref[...])
    own += mm(picks[0], high_ref[...], (1, 0)) + mm(picks[1], low_ref[...], (1, 0))
    total[...] += mm(own.astype(BF16), proj_ref[...], (1, 1)) + mm(dskip_ref[...], skip_ref[...], (1, 1))

    @pl.when(step == pl.num_programs(0) - 1)
    def _():
        out_ref[...] = total[: out_ref.shape[0]].astype(BF16)


def assemble_kernel(where_ref, send_ref, keep_ref, out_ref):
    step = pl.program_id(0)
    me = where_ref[4 + step % 2]
    size = out_ref.shape[0] // SHARDS
    for block in range(SHARDS):
        at = pl.multiple_of((block ^ me) * size, size)
        rows = slice(block * size, (block + 1) * size)
        out_ref[pl.ds(at, size), :] = jnp.where(step < 2, send_ref[0, rows, :], keep_ref[0, rows, :]).astype(F32)


def per_device(
    feats, w_proj, w_skip, attn_src, attn_dst, bias, gain, shift, cotangent, neighbours, edge_mask, node_mask, send_index,
):
    node_rows, depth = feats.shape
    heads, width = attn_src.shape
    concat = heads * width
    halo = send_index.shape[2]
    devices = lax.axis_size(AXES)
    bits = devices.bit_length() - 1
    rows = -(-node_rows // LANES) * LANES
    columns = rows + 2 * STEP
    halo_pad = -(-halo // 16) * 16
    me = lax.axis_index(AXES)
    pair_count = heads // 2

    def passed(value, steps):
        initial, last = (max(0, -steps), min(devices, devices - steps))
        return lax.ppermute(value, AXES, [(source, source + steps) for source in range(initial, last)])

    def swapped(value, bit):
        return lax.ppermute(value, AXES, [(source, source ^ (1 << bit)) for source in range(devices)])

    def bit(which):
        return (me >> which) & 1

    order_a, order_b = (2, 1, 3, 4), (1, 2, 3, 4)
    place_a = sum(bit(b) << (3 - i) for i, b in enumerate(order_a))
    place_b = sum(bit(b) << (3 - i) for i, b in enumerate(order_b))
    core = bit(0)
    where = jnp.stack([2 * (1 - core), 2 * (1 - core) + 1, 2 * core, 2 * core + 1, place_a, place_b]).astype(jnp.int32)
    where_send = where
    where_keep = jnp.concatenate([where[2:4], where[:2], where[4:]])

    real = jnp.pad(node_mask.astype(F32), (0, rows - node_rows))[:, None]
    names = neighbours + jnp.where(neighbours >= node_rows, rows - node_rows, 0)
    names = names + jnp.where(neighbours >= node_rows + halo, STEP - halo, 0)
    src3, dst3 = attn_src[:, None, :], attn_dst[:, None, :]
    bias2, gain2, shift2 = bias[None], gain[None], shift[None]

    down, up = pl.pallas_call(
        halo_rows_kernel,
        out_shape=[jax.ShapeDtypeStruct((halo_pad, depth), BF16)] * 2,
        scratch_shapes=[pltpu.VMEM((8, LANES), jnp.int32)],
        compiler_params=params(),
        name="halo_rows",
    )(feats, send_index)
    from_below = passed(up, 1)
    from_above = passed(down, -1)

    by_head = lambda n: pl.BlockSpec((n, width), lambda h: (0, h))
    whole = lambda *shape: pl.BlockSpec(shape, lambda *_: (0,) * len(shape))
    vector = pl.BlockSpec((1, 1, width), lambda h: (h, 0, 0))
    zq, skip, count, padded = pl.pallas_call(
        project_kernel,
        grid=(heads,),
        in_specs=[
            whole(node_rows, depth), by_head(depth), by_head(depth), whole(*neighbours.shape), whole(*edge_mask.shape),
        ],
        out_specs=[by_head(rows), by_head(rows), whole(rows, columns), whole(rows, depth)],
        out_shape=[
            jax.ShapeDtypeStruct((rows, concat), BF16),
            jax.ShapeDtypeStruct((rows, concat), F32),
            jax.ShapeDtypeStruct((rows, columns), F32),
            jax.ShapeDtypeStruct((rows, depth), BF16),
        ],
        compiler_params=params(),
        cost_estimate=pl.CostEstimate(flops=4 * rows * depth * concat, bytes_accessed=8_000_000, transcendentals=0),
        name="project",
    )(feats, w_proj, w_skip, names, edge_mask)

    by_edges = pl.BlockSpec((1, rows, columns), lambda h: (h, 0, 0))
    ext, weight, slope, pre, stats, halo_feats = pl.pallas_call(
        attend_kernel,
        grid=(heads,),
        in_specs=[
            by_head(rows), whole(halo_pad, depth), whole(halo_pad, depth), by_head(depth), by_head(rows),
            whole(rows, columns), vector, vector, by_head(1), by_head(node_rows), whole(rows, 1),
        ],
        out_specs=[
            by_head(columns), by_edges, by_edges, by_head(rows), by_head(8), whole(columns - rows, depth),
        ],
        out_shape=[
            jax.ShapeDtypeStruct((columns, concat), BF16),
            jax.ShapeDtypeStruct((heads, rows, columns), BF16),
            jax.ShapeDtypeStruct((heads, rows, columns), BF16),
            jax.ShapeDtypeStruct((rows, concat), F32),
            jax.ShapeDtypeStruct((8, concat), F32),
            jax.ShapeDtypeStruct((columns - rows, depth), BF16),
        ],
        scratch_shapes=[pltpu.VMEM((rows, LANES), F32)],
        compiler_params=params(),
        cost_estimate=pl.CostEstimate(flops=10**9, bytes_accessed=8_000_000, transcendentals=10**6),
        name="attend",
    )(zq, from_below, from_above, w_proj, skip, count, src3, dst3, bias2, cotangent, real)

    for which in range(bits):
        other = swapped(stats, which)
        mine_first = bit(which) == 0
        stats = merge(jnp.where(mine_first, stats, other), jnp.where(mine_first, other, stats))

    head_of = lambda n: pl.BlockSpec((n, width), lambda t, w: (0, w[t]))
    vector_of = pl.BlockSpec((1, 1, width), lambda t, w: (w[t], 0, 0))
    early = pl.BlockSpec((1, depth, width), lambda t, w: (jnp.minimum(t, 1), 0, 0))
    late = pl.BlockSpec((1, depth, width), lambda t, w: (jnp.maximum(t - 2, 0), 0, 0))
    half_grad = jax.ShapeDtypeStruct((2, depth, width), BF16)
    output, dskip, skip_send, skip_keep, bias_part = pl.pallas_call(
        norm_kernel,
        grid_spec=pltpu.PrefetchScalarGridSpec(
            num_scalar_prefetch=1,
            grid=(heads,),
            in_specs=[
                head_of(rows), head_of(8), head_of(node_rows), whole(rows, 1), head_of(1), head_of(1), whole(rows, depth),
            ],
            out_specs=[
                head_of(node_rows), head_of(rows), early, late, pl.BlockSpec((1, 8, width), lambda t, w: (w[t], 0, 0)),
            ],
        ),
        out_shape=[
            jax.ShapeDtypeStruct((node_rows, concat), BF16),
            jax.ShapeDtypeStruct((rows, concat), BF16),
            half_grad,
            half_grad,
            jax.ShapeDtypeStruct((heads, 8, width), F32),
        ],
        compiler_params=params(),
        cost_estimate=pl.CostEstimate(flops=2 * rows * depth * concat, bytes_accessed=8_000_000, transcendentals=0),
        name="norm",
    )(where, pre, stats, cotangent, real, gain2, shift2, padded)

    def backward(order):
        spec = lambda n: pl.BlockSpec((n, width), lambda t, w: (0, t))
        edges = pl.BlockSpec((1, rows, columns), lambda t, w: (w[t], 0, 0))
        return pl.pallas_call(
            back_kernel,
            grid_spec=pltpu.PrefetchScalarGridSpec(
                num_scalar_prefetch=1,
                grid=(2,),
                in_specs=[
                    edges, edges, head_of(columns), head_of(rows), vector_of, vector_of,
                    whole(rows, depth), whole(columns - rows, depth),
                ],
                out_specs=[
                    pl.BlockSpec((1, depth, width), lambda t, w: (t, 0, 0)), spec(rows), spec(halo_pad), spec(halo_pad),
                    pl.BlockSpec((1, 8, width), lambda t, w: (t, 0, 0)),
                ],
                scratch_shapes=[
                    pltpu.VMEM((rows, columns), F32), pltpu.VMEM((rows, width), F32), pltpu.VMEM((rows, LANES), F32),
                ],
            ),
            out_shape=[
                half_grad,
                jax.ShapeDtypeStruct((rows, 2 * width), F32),
                jax.ShapeDtypeStruct((halo_pad, 2 * width), BF16),
                jax.ShapeDtypeStruct((halo_pad, 2 * width), BF16),
                jax.ShapeDtypeStruct((2, 8, width), F32),
            ],
            compiler_params=params(),
            cost_estimate=pl.CostEstimate(flops=10**9, bytes_accessed=8_000_000, transcendentals=0),
            name="back",
        )(order, weight, slope, ext, dskip, src3, dst3, padded, halo_feats)

    proj_send, own_send, below_send, above_send, small_send = backward(where_send)
    proj_keep, own_keep, below_keep, above_keep, small_keep = backward(where_keep)

    def scatter(send, keep):
        both = keep + swapped(send, 0)
        one, two = both[0], both[1]
        for which in range(2):
            cut = one.shape[0] // 2
            one, two = (
                one[:cut] + swapped(one[cut:], order_a[which]),
                two[:cut] + swapped(two[cut:], order_b[which]),
            )
        both = jnp.stack([one, two])
        for which in order_a[2:]:
            cut = both.shape[1] // 2
            both = both[:, :cut] + swapped(both[:, cut:], which)
        for which in range(5, bits):
            both = both + swapped(both, which)
        return both

    def gather(both):
        for which in order_a[:1:-1]:
            both = jnp.concatenate([both, swapped(both, which)], axis=1)
        one, two = both[0], both[1]
        for which in (1, 0):
            one, two = (
                jnp.concatenate([one, swapped(one, order_a[which])], axis=0),
                jnp.concatenate([two, swapped(two, order_b[which])], axis=0),
            )
        both = jnp.stack([one, two])
        return pl.pallas_call(
            assemble_kernel,
            grid_spec=pltpu.PrefetchScalarGridSpec(
                num_scalar_prefetch=1, grid=(heads,), in_specs=[early, late], out_specs=head_of(depth)
            ),
            out_shape=jax.ShapeDtypeStruct((depth, concat), F32),
            compiler_params=params(),
            name="assemble",
        )(where, swapped(both, 0), both)

    grad_skip = gather(scatter(skip_send, skip_keep))
    back_below = passed(jnp.concatenate([below_send, below_keep], axis=1), -1)
    back_above = passed(jnp.concatenate([above_send, above_keep], axis=1), 1)
    grad_proj = gather(scatter(proj_send, proj_keep))

    pair = lambda first: pl.BlockSpec((rows, width), lambda t, w: (0, jnp.clip(t - first, 0, 1)))
    returned = pl.BlockSpec((halo_pad, width), lambda t, w: (0, (t + 2) % 4))
    grad_feats = pl.pallas_call(
        feats_kernel,
        grid_spec=pltpu.PrefetchScalarGridSpec(
            num_scalar_prefetch=1,
            grid=(heads,),
            in_specs=[
                pair(0), pair(2), returned, returned, whole(*send_index.shape), head_of(rows), head_of(depth), head_of(depth),
            ],
            out_specs=whole(node_rows, depth),
            scratch_shapes=[
                pltpu.VMEM((rows, depth), F32), pltpu.VMEM((2, rows, halo_pad), BF16), pltpu.VMEM((8, LANES), jnp.int32),
            ],
        ),
        out_shape=jax.ShapeDtypeStruct((node_rows, depth), BF16),
        compiler_params=params(),
        cost_estimate=pl.CostEstimate(flops=4 * rows * depth * concat, bytes_accessed=8_000_000, transcendentals=0),
        name="features",
    )(where, own_send, own_keep, back_above, back_below, send_index, dskip, w_proj, w_skip)

    small = jnp.where(
        core == 0,
        jnp.concatenate([small_keep, small_send], axis=0),
        jnp.concatenate([small_send, small_keep], axis=0),
    )[:, :2]
    small = jnp.concatenate([small, bias_part[:, :1]], axis=1)
    for which in range(bits):
        small = small + swapped(small, which)
    inverse = lax.rsqrt(stats[2] / stats[0] + 1e-05)
    return (
        output,
        grad_feats,
        grad_proj,
        grad_skip,
        small[:, 0],
        small[:, 1],
        small[:, 2].reshape(concat),
        stats[4] * inverse,
        stats[3],
    )


def solution(mesh):
    rows = P(AXES, None)
    in_specs = (rows,) + (P(),) * 7 + (rows, rows, rows, P(AXES), P(AXES, None, None))
    out_specs = (rows, rows) + (P(),) * 7
    return jax.shard_map(per_device, mesh=mesh, in_specs=in_specs, out_specs=out_specs, check_vma=False)
```

time: 605 us -> 197 us (0.33); the launches traced: 594 us -> 194 us
  blocking collectives: 168 us -> 0 us
  other arithmetic: 142 us -> 5.19 us
  waiting for transfers between devices: 133 us -> 43.1 us
  local copies, waits for them, and re-layouts: 95.5 us -> 12.8 us
  Pallas kernels: 0 us -> 71.4 us
  starting transfers between devices: 8.98 us -> 60.4 us
  matrix products: 33.3 us -> 0 us
  between operations: 14.8 us -> 1.32 us
    psum x4 -> x0, blocking collectives: 168 us -> none  [the longest x1 44.6 us: per_device(): node_total, mass_total = lax.psum((local_count, local_mass), ('dom', 'sub'))]
    psum x1 -> x0, waiting for transfers between devices: 133 us -> none  [per_device(): lax.psum((local_proj_grad, local_skip_grad, local_src_grad, local_dst_gra...]
    scatter-add x4 -> x0, other arithmetic: 97.7 us -> none  [the longest x1 56.5 us: backward_block(): ext_grad = ext_grad.at[flat_rows].add(edge_rows)]
    pallas_call x0 -> x9, Pallas kernels: none -> 71.4 us  [the longest x2 22.3 us: backward(): pl.pallas_call(back_kernel, grid_spec=pltpu.PrefetchScalarGridSpec(num_sc...]
    ppermute x4 -> x42, starting transfers between devices: 8.94 us -> 60.4 us  [the longest x38 53.7 us: swapped(): lax.ppermute(value, AXES, [(source, source ^ 1 << bit) for source in rang...]
    ppermute x4 -> x42, waiting for transfers between devices: 0.01 us -> 43.1 us  [the longest x38 43.1 us: swapped(): lax.ppermute(value, AXES, [(source, source ^ 1 << bit) for source in rang...]
    gather x5 -> x0, local copies, waits for them, and re-layouts: 39.1 us -> none  [the longest x1 20.6 us: forward_block(): gathered = ext_heads[neighbour_block]]
    dot_general x12 -> x0, matrix products: 33.3 us -> none  [the longest x2 8.05 us: contract_rows(): lax.dot_general(left_side, right_side, (((0,), (0,)), ((), ())), preferre...]
  transfers between devices with their start and end apart: 5 -> 42, of which waited for: 1 -> 23; matrix products, arithmetic and copies ran while one was open for 4% -> 6% of each run, Pallas kernels for 0% -> 22%
where the time goes in v1:
time: 197 us; the launch traced here: 194 us
  Pallas kernels  71.4 us (36%)
  starting transfers between devices  60.4 us (31%)
  waiting for transfers between devices  43.1 us (22%)
  local copies, waits for them, and re-layouts  12.8 us (6%)
  other arithmetic  5.19 us (3%)
    ppermute x38, starting transfers between devices, swapped(): lax.ppermute(value, AXES, [(source, source ^ 1 << bit) for source in rang...  53.7 us
    ppermute x38, waiting for transfers between devices, swapped(): lax.ppermute(value, AXES, [(source, source ^ 1 << bit) for source in rang...  43.1 us
    pallas_call x2, Pallas kernels, backward(): pl.pallas_call(back_kernel, grid_spec=pltpu.PrefetchScalarGridSpec(num_sc...  22.3 us
    pallas_call x1, Pallas kernels, per_device(): pl.pallas_call(attend_kernel, grid=(heads,), in_specs=[by_head(rows), who...  14.7 us
    pallas_call x2, Pallas kernels, gather(): pl.pallas_call(assemble_kernel, grid_spec=pltpu.PrefetchScalarGridSpec(nu...  10.3 us
    pallas_call x1, Pallas kernels, per_device(): pl.pallas_call(project_kernel, grid=(heads,), in_specs=[whole(node_rows,...  7.6 us
    pallas_call x1, Pallas kernels, per_device(): pl.pallas_call(norm_kernel, grid_spec=pltpu.PrefetchScalarGridSpec(num_sc...  7.32 us
    pallas_call x1, Pallas kernels, per_device(): pl.pallas_call(feats_kernel, grid_spec=pltpu.PrefetchScalarGridSpec(num_s...  7.04 us
  transfers between devices with their start and end apart: 42, of which 23 were waited for; matrix products, arithmetic and copies ran while one was open for 6% of the time, Pallas kernels for 22%

profile of v1, /device:TPU:0, one launch (start us, length us, event | category | flops | bytes accessed | tf_op | source)
XLA Modules:
  0.0 194.3 jit_solution(3241854276220005110)
XLA Ops:
  0.6 2.2 %halo_rows.1 = (bf16[48,1024]{1,0:T(8,128)(2,1)}, bf16[48,1024]{1,0:T(8,128)(2,1)}) custom-call(bf16[376,1024]{1,0:T(8,128)(2,1)} %feats_ref.3, s32[1,2,47]{2,1,0:T(2,128)} %index_ref.3), custom_call_target="tpu_custom_call" | custom-call | tf_op jit(solution)/shard_map/halo_rows/pallas_call | solution.py:316
  2.8 2.3 %collective-permute-start = (bf16[48,1024]{1,0:T(8,128)(2,1)}, bf16[48,1024]{1,0:T(8,128)(2,1)S(1)}, u32[]{:S(2)}, u32[]{:S(2)}) collective-permute-start(bf16[48,1024]{1,0:T(8,128)(2,1)} %get-tuple-element.37), channel_id=1, source_target_pairs={{0,1},{1,2},{2,3},{3,4},{4,5},{5,6},{6,7},{7,8},{8,9},{9,10},{10,1... | collective-permute-start | bytes 294920 | tf_op jit(solution)/shard_map/ppermute | solution.py:294
  13.8 7.6 %project.1 = (bf16[384,1024]{1,0:T(8,128)(2,1)}, f32[384,1024]{1,0:T(8,128)}, f32[384,512]{1,0:T(8,128)}, bf16[384,1024]{1,0:T(8,128)(2,1)}) custom-call(bf16[376,1024]{1,0:T(8,128)(2,1)} %feats_ref.3, bf16[1024,1024]{1,0:T(8,128)(2,1)} %proj_ref.5, bf16[1024,1024]{1,0:T(8,128)(2,1)} %skip_ref.1, s32[376,16]{1,0:T(8,128)} %add.199.neighbours_ref, ...), custom_call_target="tpu_custom_call" | custom-call | flops 1610612736 | bytes 8000000 | tf_op jit(solution)/shard_map/project/pallas_call | solution.py:329
  22.1 14.7 %attend.1 = (bf16[512,1024]{1,0:T(8,128)(2,1)}, bf16[4,384,512]{2,1,0:T(8,128)(2,1)}, bf16[4,384,512]{2,1,0:T(8,128)(2,1)}, f32[384,1024]{1,0:T(8,128)}, f32[8,1024]{1,0:T(8,128)}, /*index=5*/bf16[128,1024]{1,0:T(8,128)(2,1)}) custom-call(bf16[384,1024]{1,0:T(8,128)(2,1)} %get-tuple-element.36.zq_ref, bf16[48,1024]{1,0:T(8,128)(2,1)} %copy-done.8, ...), custom_call_target="tpu_custom_call" | custom-call | flops 1000000000 | bytes 8000000 | tf_op jit(solution)/shard_map/attend/pallas_call | solution.py:348
  36.8 3.3 %collective-permute-start.2 = (f32[8,1024]{1,0:T(8,128)}, f32[8,1024]{1,0:T(8,128)S(1)}, u32[]{:S(2)}, u32[]{:S(2)}) collective-permute-start(f32[8,1024]{1,0:T(8,128)} %get-tuple-element.42), channel_id=1, source_target_pairs={{0,1},{1,0},{2,3},{3,2},{4,5},{5,4},{6,7},{7,6},{8,9},{9,8},{10,11... | collective-permute-start | bytes 98312 | tf_op jit(solution)/shard_map/ppermute | solution.py:297
  42.1 2.0 %collective-permute-start.3 = (f32[8,1024]{1,0:T(8,128)S(1)}, f32[8,1024]{1,0:T(8,128)S(1)}, u32[]{:S(2)}, u32[]{:S(2)}) collective-permute-start(f32[8,1024]{1,0:T(8,128)S(1)} %concatenate.79), channel_id=1, source_target_pairs={{0,2},{1,3},{2,0},{3,1},{4,6},{5,7},{6,4},{7,5},{8,10},{9,11},{10,... | collective-permute-start | bytes 98312 | tf_op jit(solution)/shard_map/ppermute | solution.py:297
  44.1 2.0 %collective-permute-done.3 = f32[8,1024]{1,0:T(8,128)S(1)} collective-permute-done((f32[8,1024]{1,0:T(8,128)S(1)}, f32[8,1024]{1,0:T(8,128)S(1)}, u32[]{:S(2)}, u32[]{:S(2)}) %collective-permute-start.3) | collective-permute-done | bytes 32800 | tf_op jit(solution)/shard_map/ppermute | solution.py:297
  46.2 2.9 %collective-permute-start.4 = (f32[8,1024]{1,0:T(8,128)S(1)}, f32[8,1024]{1,0:T(8,128)S(1)}, u32[]{:S(2)}, u32[]{:S(2)}) collective-permute-start(f32[8,1024]{1,0:T(8,128)S(1)} %concatenate.80), channel_id=1, source_target_pairs={{0,4},{1,5},{2,6},{3,7},{4,0},{5,1},{6,2},{7,3},{8,12},{9,13},{10,... | collective-permute-start | bytes 98312 | tf_op jit(solution)/shard_map/ppermute | solution.py:297
  49.1 1.9 collective-permute-done.4
  51.2 3.1 %collective-permute-start.5 = (f32[8,1024]{1,0:T(8,128)S(1)}, f32[8,1024]{1,0:T(8,128)S(1)}, u32[]{:S(2)}, u32[]{:S(2)}) collective-permute-start(f32[8,1024]{1,0:T(8,128)S(1)} %concatenate.81), channel_id=1, source_target_pairs={{0,8},{1,9},{2,10},{3,11},{4,12},{5,13},{6,14},{7,15},{8,0},{9,1},... | collective-permute-start | bytes 98312 | tf_op jit(solution)/shard_map/ppermute | solution.py:297
  56.3 3.2 %collective-permute-start.6 = (f32[8,1024]{1,0:T(8,128)S(1)}, f32[8,1024]{1,0:T(8,128)S(1)}, u32[]{:S(2)}, u32[]{:S(2)}) collective-permute-start(f32[8,1024]{1,0:T(8,128)S(1)} %concatenate.82), channel_id=1, source_target_pairs={{0,16},{1,17},{2,18},{3,19},{4,20},{5,21},{6,22},{7,23},{8,24},{9,... | collective-permute-start | bytes 98312 | tf_op jit(solution)/shard_map/ppermute | solution.py:297
  62.8 7.3 %norm.1 = (bf16[376,1024]{1,0:T(8,128)(2,1)}, bf16[384,1024]{1,0:T(8,128)(2,1)}, bf16[2,1024,256]{2,1,0:T(8,128)(2,1)}, bf16[2,1024,256]{2,1,0:T(8,128)(2,1)}, f32[4,8,256]{2,1,0:T(8,128)}) custom-call(s32[6]{0:T(128)} %stack.63.where_ref, f32[384,1024]{1,0:T(8,128)} %get-tuple-element.41.pre_ref, f32[8,1024]{1,0:T(8,128)} %concatenate.83.stats_ref, ...), custom_call_target="tpu_custom_call" | custom-call | flops 805306368 | bytes 8000000 | tf_op jit(solution)/shard_map/norm/pallas_call | solution.py:382
  70.2 11.1 %back.2 = (bf16[2,1024,256]{2,1,0:T(8,128)(2,1)}, f32[384,512]{1,0:T(8,128)}, bf16[48,512]{1,0:T(8,128)(2,1)}, bf16[48,512]{1,0:T(8,128)(2,1)}, f32[2,8,256]{2,1,0:T(8,128)}) custom-call(s32[6]{0:T(128)} %stack.63.where_ref, bf16[4,384,512]{2,1,0:T(8,128)(2,1)} %get-tuple-element.45.weight_ref, bf16[4,384,512]{2,1,0:T(8,128)(2,1)} %get-tuple-element.46.slope_ref, ...), custom_call_target="tpu_custom_call" | custom-call | flops 1000000000 | bytes 8000000 | tf_op jit(solution)/shard_map/back/pallas_call | solution.py:409
  82.5 11.2 %back.3 = (bf16[2,1024,256]{2,1,0:T(8,128)(2,1)}, f32[384,512]{1,0:T(8,128)}, bf16[48,512]{1,0:T(8,128)(2,1)}, bf16[48,512]{1,0:T(8,128)(2,1)}, f32[2,8,256]{2,1,0:T(8,128)}) custom-call(s32[6]{0:T(128)} %concatenate.84.where_ref, bf16[4,384,512]{2,1,0:T(8,128)(2,1)} %get-tuple-element.45.weight_ref, bf16[4,384,512]{2,1,0:T(8,128)(2,1)} %get-tuple-element.46.slope_ref, ...), custom_call_target="tpu_custom_call" | custom-call | flops 1000000000 | bytes 8000000 | tf_op jit(solution)/shard_map/back/pallas_call | solution.py:409
  99.3 4.0 %collective-permute-done.24 = bf16[512,256]{1,0:T(8,128)(2,1)S(1)} collective-permute-done((bf16[512,256]{1,0:T(8,128)(2,1)S(1)}, bf16[512,256]{1,0:T(8,128)(2,1)S(1)}, u32[]{:S(2)}, u32[]{:S(2)}) %collective-permute-start.24) | collective-permute-done | bytes 262176 | tf_op jit(solution)/shard_map/ppermute | solution.py:297
  105.7 3.2 %collective-permute-done.10 = bf16[512,256]{1,0:T(8,128)(2,1)S(1)} collective-permute-done((bf16[512,256]{1,0:T(8,128)(2,1)S(1)}, bf16[512,256]{1,0:T(8,128)(2,1)S(1)}, u32[]{:S(2)}, u32[]{:S(2)}) %collective-permute-start.10) | collective-permute-done | bytes 262176 | tf_op jit(solution)/shard_map/ppermute | solution.py:297
  111.5 2.0 %collective-permute-start.28 = (bf16[2,128,256]{2,1,0:T(8,128)(2,1)S(1)}, bf16[2,128,256]{2,1,0:T(8,128)(2,1)S(1)}, u32[]{:S(2)}, u32[]{:S(2)}) collective-permute-start(bf16[2,128,256]{2,1,0:T(8,128)(2,1)S(1)} %pad_maximum_fusion.8), channel_id=1, source_target_pairs={{0,8},{1,9},{2,10},{3,11},{4,12},{5,13},{6,14},{7,15},{8,0},{9,1},... | collective-permute-start | bytes 393224 | tf_op jit(solution)/shard_map/ppermute | solution.py:297
  118.0 3.1 %collective-permute-start.29 = (bf16[2,64,256]{2,1,0:T(8,128)(2,1)S(1)}, bf16[2,64,256]{2,1,0:T(8,128)(2,1)S(1)}, u32[]{:S(2)}, u32[]{:S(2)}) collective-permute-start(bf16[2,64,256]{2,1,0:T(8,128)(2,1)S(1)} %slice.517), channel_id=1, source_target_pairs={{0,16},{1,17},{2,18},{3,19},{4,20},{5,21},{6,22},{7,23},{8,24},{9,... | collective-permute-start | bytes 196616 | tf_op jit(solution)/shard_map/ppermute | solution.py:297
  121.2 3.8 %collective-permute-start.15 = (bf16[2,64,256]{2,1,0:T(8,128)(2,1)S(1)}, bf16[2,64,256]{2,1,0:T(8,128)(2,1)S(1)}, u32[]{:S(2)}, u32[]{:S(2)}) collective-permute-start(bf16[2,64,256]{2,1,0:T(8,128)(2,1)S(1)} %slice.503), channel_id=1, source_target_pairs={{0,16},{1,17},{2,18},{3,19},{4,20},{5,21},{6,22},{7,23},{8,24},{9,... | collective-permute-start | bytes 196616 | tf_op jit(solution)/shard_map/ppermute | solution.py:297
  134.8 2.6 %collective-permute-done.31 = bf16[2,128,256]{2,1,0:T(8,128)(2,1)S(1)} collective-permute-done((bf16[2,128,256]{2,1,0:T(8,128)(2,1)S(1)}, bf16[2,128,256]{2,1,0:T(8,128)(2,1)S(1)}, u32[]{:S(2)}, u32[]{:S(2)}) %collective-permute-start.31) | collective-permute-done | bytes 131104 | tf_op jit(solution)/shard_map/ppermute | solution.py:297
  137.6 2.2 %collective-permute-start.34 = (bf16[256,256]{1,0:T(8,128)(2,1)S(1)}, bf16[256,256]{1,0:T(8,128)(2,1)S(1)}, u32[]{:S(2)}, u32[]{:S(2)}) collective-permute-start(bf16[256,256]{1,0:T(8,128)(2,1)S(1)} %get-tuple-element.94), channel_id=1, source_target_pairs={{0,4},{1,5},{2,6},{3,7},{4,0},{5,1},{6,2},{7,3},{8,12},{9,13},{10,... | collective-permute-start | bytes 393224 | tf_op jit(solution)/shard_map/ppermute | solution.py:297
  139.9 2.0 %collective-permute-start.18 = (bf16[256,256]{1,0:T(8,128)(2,1)S(1)}, bf16[256,256]{1,0:T(8,128)(2,1)S(1)}, u32[]{:S(2)}, u32[]{:S(2)}) collective-permute-start(bf16[256,256]{1,0:T(8,128)(2,1)S(1)} %get-tuple-element.95), channel_id=1, source_target_pairs={{0,2},{1,3},{2,0},{3,1},{4,6},{5,7},{6,4},{7,5},{8,10},{9,11},{10,... | collective-permute-start | bytes 393224 | tf_op jit(solution)/shard_map/ppermute | solution.py:297
  143.4 2.8 %collective-permute-start.33 = (bf16[512,256]{1,0:T(8,128)(2,1)S(1)}, bf16[512,256]{1,0:T(8,128)(2,1)S(1)}, u32[]{:S(2)}, u32[]{:S(2)}) collective-permute-start(bf16[512,256]{1,0:T(8,128)(2,1)S(1)} %pad_maximum_fusion.6), channel_id=1, source_target_pairs={{0,4},{1,5},{2,6},{3,7},{4,0},{5,1},{6,2},{7,3},{8,12},{9,13},{10,... | collective-permute-start | bytes 786440 | tf_op jit(solution)/shard_map/ppermute | solution.py:297
  146.3 2.7 %collective-permute-start.19 = (bf16[512,256]{1,0:T(8,128)(2,1)S(1)}, bf16[512,256]{1,0:T(8,128)(2,1)S(1)}, u32[]{:S(2)}, u32[]{:S(2)}) collective-permute-start(bf16[512,256]{1,0:T(8,128)(2,1)S(1)} %pad_maximum_fusion.3), channel_id=1, source_target_pairs={{0,4},{1,5},{2,6},{3,7},{4,0},{5,1},{6,2},{7,3},{8,12},{9,13},{10,... | collective-permute-start | bytes 786440 | tf_op jit(solution)/shard_map/ppermute | solution.py:297
  149.1 4.8 %collective-permute-done.33 = bf16[512,256]{1,0:T(8,128)(2,1)S(1)} collective-permute-done((bf16[512,256]{1,0:T(8,128)(2,1)S(1)}, bf16[512,256]{1,0:T(8,128)(2,1)S(1)}, u32[]{:S(2)}, u32[]{:S(2)}) %collective-permute-start.33) | collective-permute-done | bytes 262176 | tf_op jit(solution)/shard_map/ppermute | solution.py:297
  154.3 2.5 %collective-permute-done.19 = bf16[512,256]{1,0:T(8,128)(2,1)S(1)} collective-permute-done((bf16[512,256]{1,0:T(8,128)(2,1)S(1)}, bf16[512,256]{1,0:T(8,128)(2,1)S(1)}, u32[]{:S(2)}, u32[]{:S(2)}) %collective-permute-start.19) | collective-permute-done | bytes 262176 | tf_op jit(solution)/shard_map/ppermute | solution.py:297
  158.3 2.7 %collective-permute-done.38 = f32[4,3,256]{2,1,0:T(4,128)S(1)} collective-permute-done((f32[4,3,256]{2,1,0:T(4,128)S(1)}, f32[4,3,256]{2,1,0:T(4,128)S(1)}, u32[]{:S(2)}, u32[]{:S(2)}) %collective-permute-start.38) | collective-permute-done | bytes 12320 | tf_op jit(solution)/shard_map/ppermute | solution.py:297
  162.1 2.6 %collective-permute-done.39 = f32[4,3,256]{2,1,0:T(4,128)S(1)} collective-permute-done((f32[4,3,256]{2,1,0:T(4,128)S(1)}, f32[4,3,256]{2,1,0:T(4,128)S(1)}, u32[]{:S(2)}, u32[]{:S(2)}) %collective-permute-start.39) | collective-permute-done | bytes 12320 | tf_op jit(solution)/shard_map/ppermute | solution.py:297
  168.4 2.0 %collective-permute-start.41 = (f32[4,3,256]{2,1,0:T(4,128)S(1)}, f32[4,3,256]{2,1,0:T(4,128)S(1)}, u32[]{:S(2)}, u32[]{:S(2)}) collective-permute-start(f32[4,3,256]{2,1,0:T(4,128)S(1)} %add.247), channel_id=1, source_target_pairs={{0,16},{1,17},{2,18},{3,19},{4,20},{5,21},{6,22},{7,23},{8,24},{9,... | collective-permute-start | bytes 36872 | tf_op jit(solution)/shard_map/ppermute | solution.py:297
  175.0 7.0 %features.1 = bf16[376,1024]{1,0:T(8,128)(2,1)} custom-call(s32[6]{0:T(128)} %stack.63.where_ref, f32[384,512]{1,0:T(8,128)} %get-tuple-element.50.send_ref, f32[384,512]{1,0:T(8,128)} %get-tuple-element.51.keep_ref, bf16[48,1024]{1,0:T(8,128)(2,1)} %copy-done.7, bf16[48,1024]{1,0:T(8,128)(2,1)} %copy-done.6, s32[1,2,47]{2,1,0:T(2,128)} %index_ref.3, ...), custom_call_target="tpu_custom_call" | custom-call | flops 1610612736 | bytes 8000000 | tf_op jit(solution)/shard_map/features/pallas_call | solution.py:485
  183.0 5.2 %assemble.2 = f32[1024,1024]{1,0:T(8,128)} custom-call(s32[6]{0:T(128)} %stack.63.where_ref, bf16[2,1024,256]{2,1,0:T(8,128)(2,1)} %copy-done.3, bf16[2,1024,256]{2,1,0:T(8,128)(2,1)} %copy-done.1), custom_call_target="tpu_custom_call" | custom-call | tf_op jit(solution)/shard_map/assemble/pallas_call | solution.py:468
  189.1 5.2 %assemble.3 = f32[1024,1024]{1,0:T(8,128)} custom-call(s32[6]{0:T(128)} %stack.63.where_ref, bf16[2,1024,256]{2,1,0:T(8,128)(2,1)} %copy-done.2, bf16[2,1024,256]{2,1,0:T(8,128)(2,1)} %copy-done), custom_call_target="tpu_custom_call" | custom-call | tf_op jit(solution)/shard_map/assemble/pallas_call | solution.py:468
  (182 shorter events, 57.8 us)
Async XLA Ops:
  2.8 18.6 %collective-permute-start = (bf16[48,1024]{1,0:T(8,128)(2,1)}, bf16[48,1024]{1,0:T(8,128)(2,1)S(1)}, u32[]{:S(2)}, u32[]{:S(2)}) collective-permute-start(bf16[48,1024]{1,0:T(8,128)(2,1)} %get-tuple-element.37), channel_id=1, source_target_pairs={{0,1},{1,2},{2,3},{3,4},{4,5},{5,6},{6,7},{7,8},{8,9},{9,10},{10,1... | collective-permute-start | bytes 294920 | tf_op jit(solution)/shard_map/ppermute | solution.py:294
  5.2 16.2 %collective-permute-start.1 = (bf16[48,1024]{1,0:T(8,128)(2,1)}, bf16[48,1024]{1,0:T(8,128)(2,1)S(1)}, u32[]{:S(2)}, u32[]{:S(2)}) collective-permute-start(bf16[48,1024]{1,0:T(8,128)(2,1)} %get-tuple-element.38), channel_id=1, source_target_pairs={{1,0},{2,1},{3,2},{4,3},{5,4},{6,5},{7,6},{8,7},{9,8},{10,9},{11,1... | collective-permute-start | bytes 294920 | tf_op jit(solution)/shard_map/ppermute | solution.py:294
  56.3 5.1 %collective-permute-start.6 = (f32[8,1024]{1,0:T(8,128)S(1)}, f32[8,1024]{1,0:T(8,128)S(1)}, u32[]{:S(2)}, u32[]{:S(2)}) collective-permute-start(f32[8,1024]{1,0:T(8,128)S(1)} %concatenate.82), channel_id=1, source_target_pairs={{0,16},{1,17},{2,18},{3,19},{4,20},{5,21},{6,22},{7,23},{8,24},{9,... | collective-permute-start | bytes 98312 | tf_op jit(solution)/shard_map/ppermute | solution.py:297
  70.1 23.6 %collective-permute-start.23 = (bf16[2,1024,256]{2,1,0:T(8,128)(2,1)}, bf16[2,1024,256]{2,1,0:T(8,128)(2,1)S(1)}, u32[]{:S(2)}, u32[]{:S(2)}) collective-permute-start(bf16[2,1024,256]{2,1,0:T(8,128)(2,1)} %get-tuple-element.59), channel_id=1, source_target_pairs={{0,1},{1,0},{2,3},{3,2},{4,5},{5,4},{6,7},{7,6},{8,9},{9,8},{10,11... | collective-permute-start | bytes 3145736 | tf_op jit(solution)/shard_map/ppermute | solution.py:297
  81.3 14.2 %collective-permute-start.9 = (bf16[2,1024,256]{2,1,0:T(8,128)(2,1)}, bf16[2,1024,256]{2,1,0:T(8,128)(2,1)S(1)}, u32[]{:S(2)}, u32[]{:S(2)}) collective-permute-start(bf16[2,1024,256]{2,1,0:T(8,128)(2,1)} %get-tuple-element.57), channel_id=1, source_target_pairs={{0,1},{1,0},{2,3},{3,2},{4,5},{5,4},{6,7},{7,6},{8,9},{9,8},{10,11... | collective-permute-start | bytes 3145736 | tf_op jit(solution)/shard_map/ppermute | solution.py:297
  94.0 9.2 %collective-permute-start.24 = (bf16[512,256]{1,0:T(8,128)(2,1)S(1)}, bf16[512,256]{1,0:T(8,128)(2,1)S(1)}, u32[]{:S(2)}, u32[]{:S(2)}) collective-permute-start(bf16[512,256]{1,0:T(8,128)(2,1)S(1)} %get-tuple-element.87), channel_id=1, source_target_pairs={{0,4},{1,5},{2,6},{3,7},{4,0},{5,1},{6,2},{7,3},{8,12},{9,13},{10,... | collective-permute-start | bytes 786440 | tf_op jit(solution)/shard_map/ppermute | solution.py:297
  94.9 9.2 %collective-permute-start.26 = (bf16[512,256]{1,0:T(8,128)(2,1)S(1)}, bf16[512,256]{1,0:T(8,128)(2,1)S(1)}, u32[]{:S(2)}, u32[]{:S(2)}) collective-permute-start(bf16[512,256]{1,0:T(8,128)(2,1)S(1)} %get-tuple-element.88), channel_id=1, source_target_pairs={{0,2},{1,3},{2,0},{3,1},{4,6},{5,7},{6,4},{7,5},{8,10},{9,11},{10,... | collective-permute-start | bytes 786440 | tf_op jit(solution)/shard_map/ppermute | solution.py:297
  95.8 13.0 %collective-permute-start.10 = (bf16[512,256]{1,0:T(8,128)(2,1)S(1)}, bf16[512,256]{1,0:T(8,128)(2,1)S(1)}, u32[]{:S(2)}, u32[]{:S(2)}) collective-permute-start(bf16[512,256]{1,0:T(8,128)(2,1)S(1)} %get-tuple-element.91), channel_id=1, source_target_pairs={{0,4},{1,5},{2,6},{3,7},{4,0},{5,1},{6,2},{7,3},{8,12},{9,13},{10,... | collective-permute-start | bytes 786440 | tf_op jit(solution)/shard_map/ppermute | solution.py:297
  96.7 13.0 %collective-permute-start.12 = (bf16[512,256]{1,0:T(8,128)(2,1)S(1)}, bf16[512,256]{1,0:T(8,128)(2,1)S(1)}, u32[]{:S(2)}, u32[]{:S(2)}) collective-permute-start(bf16[512,256]{1,0:T(8,128)(2,1)S(1)} %get-tuple-element.92), channel_id=1, source_target_pairs={{0,2},{1,3},{2,0},{3,1},{4,6},{5,7},{6,4},{7,5},{8,10},{9,11},{10,... | collective-permute-start | bytes 786440 | tf_op jit(solution)/shard_map/ppermute | solution.py:297
  104.2 7.1 %collective-permute-start.27 = (bf16[256,256]{1,0:T(8,128)(2,1)S(1)}, bf16[256,256]{1,0:T(8,128)(2,1)S(1)}, u32[]{:S(2)}, u32[]{:S(2)}) collective-permute-start(bf16[256,256]{1,0:T(8,128)(2,1)S(1)} %slice.513), channel_id=1, source_target_pairs={{0,4},{1,5},{2,6},{3,7},{4,0},{5,1},{6,2},{7,3},{8,12},{9,13},{10,... | collective-permute-start | bytes 393224 | tf_op jit(solution)/shard_map/ppermute | solution.py:297
  105.5 5.9 %collective-permute-start.25 = (bf16[256,256]{1,0:T(8,128)(2,1)S(1)}, bf16[256,256]{1,0:T(8,128)(2,1)S(1)}, u32[]{:S(2)}, u32[]{:S(2)}) collective-permute-start(bf16[256,256]{1,0:T(8,128)(2,1)S(1)} %slice.509), channel_id=1, source_target_pairs={{0,2},{1,3},{2,0},{3,1},{4,6},{5,7},{6,4},{7,5},{8,10},{9,11},{10,... | collective-permute-start | bytes 393224 | tf_op jit(solution)/shard_map/ppermute | solution.py:297
  109.8 5.0 %collective-permute-start.13 = (bf16[256,256]{1,0:T(8,128)(2,1)S(1)}, bf16[256,256]{1,0:T(8,128)(2,1)S(1)}, u32[]{:S(2)}, u32[]{:S(2)}) collective-permute-start(bf16[256,256]{1,0:T(8,128)(2,1)S(1)} %slice.499), channel_id=1, source_target_pairs={{0,4},{1,5},{2,6},{3,7},{4,0},{5,1},{6,2},{7,3},{8,12},{9,13},{10,... | collective-permute-start | bytes 393224 | tf_op jit(solution)/shard_map/ppermute | solution.py:297
  111.5 6.5 %collective-permute-start.28 = (bf16[2,128,256]{2,1,0:T(8,128)(2,1)S(1)}, bf16[2,128,256]{2,1,0:T(8,128)(2,1)S(1)}, u32[]{:S(2)}, u32[]{:S(2)}) collective-permute-start(bf16[2,128,256]{2,1,0:T(8,128)(2,1)S(1)} %pad_maximum_fusion.8), channel_id=1, source_target_pairs={{0,8},{1,9},{2,10},{3,11},{4,12},{5,13},{6,14},{7,15},{8,0},{9,1},... | collective-permute-start | bytes 393224 | tf_op jit(solution)/shard_map/ppermute | solution.py:297
  116.1 5.0 %collective-permute-start.14 = (bf16[2,128,256]{2,1,0:T(8,128)(2,1)S(1)}, bf16[2,128,256]{2,1,0:T(8,128)(2,1)S(1)}, u32[]{:S(2)}, u32[]{:S(2)}) collective-permute-start(bf16[2,128,256]{2,1,0:T(8,128)(2,1)S(1)} %pad_maximum_fusion.9), channel_id=1, source_target_pairs={{0,8},{1,9},{2,10},{3,11},{4,12},{5,13},{6,14},{7,15},{8,0},{9,1},... | collective-permute-start | bytes 393224 | tf_op jit(solution)/shard_map/ppermute | solution.py:297
  118.0 7.0 %collective-permute-start.29 = (bf16[2,64,256]{2,1,0:T(8,128)(2,1)S(1)}, bf16[2,64,256]{2,1,0:T(8,128)(2,1)S(1)}, u32[]{:S(2)}, u32[]{:S(2)}) collective-permute-start(bf16[2,64,256]{2,1,0:T(8,128)(2,1)S(1)} %slice.517), channel_id=1, source_target_pairs={{0,16},{1,17},{2,18},{3,19},{4,20},{5,21},{6,22},{7,23},{8,24},{9,... | collective-permute-start | bytes 196616 | tf_op jit(solution)/shard_map/ppermute | solution.py:297
  121.2 7.1 %collective-permute-start.15 = (bf16[2,64,256]{2,1,0:T(8,128)(2,1)S(1)}, bf16[2,64,256]{2,1,0:T(8,128)(2,1)S(1)}, u32[]{:S(2)}, u32[]{:S(2)}) collective-permute-start(bf16[2,64,256]{2,1,0:T(8,128)(2,1)S(1)} %slice.503), channel_id=1, source_target_pairs={{0,16},{1,17},{2,18},{3,19},{4,20},{5,21},{6,22},{7,23},{8,24},{9,... | collective-permute-start | bytes 196616 | tf_op jit(solution)/shard_map/ppermute | solution.py:297
  125.0 6.5 %collective-permute-start.30 = (bf16[2,64,256]{2,1,0:T(8,128)(2,1)S(1)}, bf16[2,64,256]{2,1,0:T(8,128)(2,1)S(1)}, u32[]{:S(2)}, u32[]{:S(2)}) collective-permute-start(bf16[2,64,256]{2,1,0:T(8,128)(2,1)S(1)} %slice_add_fusion.4), channel_id=1, source_target_pairs={{0,16},{1,17},{2,18},{3,19},{4,20},{5,21},{6,22},{7,23},{8,24},{9,... | collective-permute-start | bytes 196616 | tf_op jit(solution)/shard_map/ppermute | solution.py:297
  128.3 5.9 %collective-permute-start.16 = (bf16[2,64,256]{2,1,0:T(8,128)(2,1)S(1)}, bf16[2,64,256]{2,1,0:T(8,128)(2,1)S(1)}, u32[]{:S(2)}, u32[]{:S(2)}) collective-permute-start(bf16[2,64,256]{2,1,0:T(8,128)(2,1)S(1)} %slice_add_fusion.5), channel_id=1, source_target_pairs={{0,16},{1,17},{2,18},{3,19},{4,20},{5,21},{6,22},{7,23},{8,24},{9,... | collective-permute-start | bytes 196616 | tf_op jit(solution)/shard_map/ppermute | solution.py:297
  131.5 6.0 %collective-permute-start.31 = (bf16[2,128,256]{2,1,0:T(8,128)(2,1)S(1)}, bf16[2,128,256]{2,1,0:T(8,128)(2,1)S(1)}, u32[]{:S(2)}, u32[]{:S(2)}) collective-permute-start(bf16[2,128,256]{2,1,0:T(8,128)(2,1)S(1)} %pad_maximum_fusion.11), channel_id=1, source_target_pairs={{0,8},{1,9},{2,10},{3,11},{4,12},{5,13},{6,14},{7,15},{8,0},{9,1},... | collective-permute-start | bytes 393224 | tf_op jit(solution)/shard_map/ppermute | solution.py:297
  132.4 24.7 %collective-permute-start.37 = (f32[4,3,256]{2,1,0:T(4,128)S(1)}, f32[4,3,256]{2,1,0:T(4,128)S(1)}, u32[]{:S(2)}, u32[]{:S(2)}) collective-permute-start(f32[4,3,256]{2,1,0:T(4,128)S(1)} %pad_maximum_fusion.14), channel_id=1, source_target_pairs={{0,1},{1,0},{2,3},{3,2},{4,5},{5,4},{6,7},{7,6},{8,9},{9,8},{10,11... | collective-permute-start | bytes 36872 | tf_op jit(solution)/shard_map/ppermute | solution.py:297
  134.3 5.5 %collective-permute-start.17 = (bf16[2,128,256]{2,1,0:T(8,128)(2,1)S(1)}, bf16[2,128,256]{2,1,0:T(8,128)(2,1)S(1)}, u32[]{:S(2)}, u32[]{:S(2)}) collective-permute-start(bf16[2,128,256]{2,1,0:T(8,128)(2,1)S(1)} %pad_maximum_fusion.10), channel_id=1, source_target_pairs={{0,8},{1,9},{2,10},{3,11},{4,12},{5,13},{6,14},{7,15},{8,0},{9,1},... | collective-permute-start | bytes 393224 | tf_op jit(solution)/shard_map/ppermute | solution.py:297
  137.5 5.9 %collective-permute-start.32 = (bf16[256,256]{1,0:T(8,128)(2,1)S(1)}, bf16[256,256]{1,0:T(8,128)(2,1)S(1)}, u32[]{:S(2)}, u32[]{:S(2)}) collective-permute-start(bf16[256,256]{1,0:T(8,128)(2,1)S(1)} %get-tuple-element.93), channel_id=1, source_target_pairs={{0,2},{1,3},{2,0},{3,1},{4,6},{5,7},{6,4},{7,5},{8,10},{9,11},{10,... | collective-permute-start | bytes 393224 | tf_op jit(solution)/shard_map/ppermute | solution.py:297
  137.6 8.5 %collective-permute-start.34 = (bf16[256,256]{1,0:T(8,128)(2,1)S(1)}, bf16[256,256]{1,0:T(8,128)(2,1)S(1)}, u32[]{:S(2)}, u32[]{:S(2)}) collective-permute-start(bf16[256,256]{1,0:T(8,128)(2,1)S(1)} %get-tuple-element.94), channel_id=1, source_target_pairs={{0,4},{1,5},{2,6},{3,7},{4,0},{5,1},{6,2},{7,3},{8,12},{9,13},{10,... | collective-permute-start | bytes 393224 | tf_op jit(solution)/shard_map/ppermute | solution.py:297
  139.9 6.4 %collective-permute-start.18 = (bf16[256,256]{1,0:T(8,128)(2,1)S(1)}, bf16[256,256]{1,0:T(8,128)(2,1)S(1)}, u32[]{:S(2)}, u32[]{:S(2)}) collective-permute-start(bf16[256,256]{1,0:T(8,128)(2,1)S(1)} %get-tuple-element.95), channel_id=1, source_target_pairs={{0,2},{1,3},{2,0},{3,1},{4,6},{5,7},{6,4},{7,5},{8,10},{9,11},{10,... | collective-permute-start | bytes 393224 | tf_op jit(solution)/shard_map/ppermute | solution.py:297
  141.9 7.1 %collective-permute-start.20 = (bf16[256,256]{1,0:T(8,128)(2,1)S(1)}, bf16[256,256]{1,0:T(8,128)(2,1)S(1)}, u32[]{:S(2)}, u32[]{:S(2)}) collective-permute-start(bf16[256,256]{1,0:T(8,128)(2,1)S(1)} %get-tuple-element.96), channel_id=1, source_target_pairs={{0,4},{1,5},{2,6},{3,7},{4,0},{5,1},{6,2},{7,3},{8,12},{9,13},{10,... | collective-permute-start | bytes 393224 | tf_op jit(solution)/shard_map/ppermute | solution.py:297
  143.4 10.5 %collective-permute-start.33 = (bf16[512,256]{1,0:T(8,128)(2,1)S(1)}, bf16[512,256]{1,0:T(8,128)(2,1)S(1)}, u32[]{:S(2)}, u32[]{:S(2)}) collective-permute-start(bf16[512,256]{1,0:T(8,128)(2,1)S(1)} %pad_maximum_fusion.6), channel_id=1, source_target_pairs={{0,4},{1,5},{2,6},{3,7},{4,0},{5,1},{6,2},{7,3},{8,12},{9,13},{10,... | collective-permute-start | bytes 786440 | tf_op jit(solution)/shard_map/ppermute | solution.py:297
  146.2 7.8 %collective-permute-start.35 = (bf16[512,256]{1,0:T(8,128)(2,1)S(1)}, bf16[512,256]{1,0:T(8,128)(2,1)S(1)}, u32[]{:S(2)}, u32[]{:S(2)}) collective-permute-start(bf16[512,256]{1,0:T(8,128)(2,1)S(1)} %pad_maximum_fusion.7), channel_id=1, source_target_pairs={{0,2},{1,3},{2,0},{3,1},{4,6},{5,7},{6,4},{7,5},{8,10},{9,11},{10,... | collective-permute-start | bytes 786440 | tf_op jit(solution)/shard_map/ppermute | solution.py:297
  146.3 10.5 %collective-permute-start.19 = (bf16[512,256]{1,0:T(8,128)(2,1)S(1)}, bf16[512,256]{1,0:T(8,128)(2,1)S(1)}, u32[]{:S(2)}, u32[]{:S(2)}) collective-permute-start(bf16[512,256]{1,0:T(8,128)(2,1)S(1)} %pad_maximum_fusion.3), channel_id=1, source_target_pairs={{0,4},{1,5},{2,6},{3,7},{4,0},{5,1},{6,2},{7,3},{8,12},{9,13},{10,... | collective-permute-start | bytes 786440 | tf_op jit(solution)/shard_map/ppermute | solution.py:297
  149.0 7.8 %collective-permute-start.21 = (bf16[512,256]{1,0:T(8,128)(2,1)S(1)}, bf16[512,256]{1,0:T(8,128)(2,1)S(1)}, u32[]{:S(2)}, u32[]{:S(2)}) collective-permute-start(bf16[512,256]{1,0:T(8,128)(2,1)S(1)} %pad_maximum_fusion.4), channel_id=1, source_target_pairs={{0,2},{1,3},{2,0},{3,1},{4,6},{5,7},{6,4},{7,5},{8,10},{9,11},{10,... | collective-permute-start | bytes 786440 | tf_op jit(solution)/shard_map/ppermute | solution.py:297
  154.2 34.0 %collective-permute-start.36 = (bf16[2,1024,256]{2,1,0:T(8,128)(2,1)S(1)}, bf16[2,1024,256]{2,1,0:T(8,128)(2,1)S(1)}, u32[]{:S(2)}, u32[]{:S(2)}) collective-permute-start(bf16[2,1024,256]{2,1,0:T(8,128)(2,1)S(1)} %pad_maximum_fusion.1.keep_ref), channel_id=1, source_target_pairs={{0,1},{1,0},{2,3},{3,2},{4,5},{5,4},{6,7},{7,6},{8,9},{9,8},{10,11... | collective-permute-start | bytes 3145736 | tf_op jit(solution)/shard_map/ppermute | solution.py:297
  157.0 25.0 %collective-permute-start.22 = (bf16[2,1024,256]{2,1,0:T(8,128)(2,1)S(1)}, bf16[2,1024,256]{2,1,0:T(8,128)(2,1)S(1)}, u32[]{:S(2)}, u32[]{:S(2)}) collective-permute-start(bf16[2,1024,256]{2,1,0:T(8,128)(2,1)S(1)} %pad_maximum_fusion.keep_ref), channel_id=1, source_target_pairs={{0,1},{1,0},{2,3},{3,2},{4,5},{5,4},{6,7},{7,6},{8,9},{9,8},{10,11... | collective-permute-start | bytes 3145736 | tf_op jit(solution)/shard_map/ppermute | solution.py:297
  166.1 8.2 %collective-permute-start.8 = (bf16[48,1024]{1,0:T(8,128)(2,1)S(1)}, bf16[48,1024]{1,0:T(8,128)(2,1)S(1)}, u32[]{:S(2)}, u32[]{:S(2)}) collective-permute-start(bf16[48,1024]{1,0:T(8,128)(2,1)S(1)} %pad_maximum_fusion.13), channel_id=1, source_target_pairs={{1,0},{2,1},{3,2},{4,3},{5,4},{6,5},{7,6},{8,7},{9,8},{10,9},{11,1... | collective-permute-start | bytes 294920 | tf_op jit(solution)/shard_map/ppermute | solution.py:294
  (27 other events, 170.7 us)

commit v2 on v1

v2 whole, which is shorter than its diff:
```python
import functools

import jax
import jax.numpy as jnp
from jax import lax
from jax.experimental import pallas as pl
from jax.experimental.pallas import tpu as pltpu
from jax.sharding import PartitionSpec as P

AXES = ("dom", "sub")
F32 = jnp.float32
BF16 = jnp.bfloat16
NEG = -1e30
LN2 = 0.6931471805599453
STEP = 64
SHARDS = 16
CHUNK = 32
LANES = 128
MIB = 1024 * 1024


def params(mib=24):
    return pltpu.CompilerParams(vmem_limit_bytes=mib * MIB)


def cost(us):
    return pl.CostEstimate(flops=int(us * 1.1e9), bytes_accessed=1_000_000, transcendentals=0)


def mm(a, b, contract):
    return lax.dot_general(a, b, ((contract[:1], contract[1:]), ((), ())), preferred_element_type=F32)


def pad_rows(value, rows):
    extra = rows - value.shape[0]
    if extra == 0:
        return value
    return jnp.concatenate([value, jnp.zeros((extra,) + value.shape[1:], value.dtype)], axis=0)


def three_parts(value):
    high = value.astype(BF16)
    rest = value - high.astype(F32)
    middle = rest.astype(BF16)
    low = (rest - middle.astype(F32)).astype(BF16)
    return high, middle, low


def repeat_lanes(value, columns):
    return jnp.concatenate([value] * (columns // value.shape[1]), axis=1)


def fold_rows(value):
    return value.reshape(value.shape[0] // 8, 8, value.shape[1])


def real_rows(mask_ref, rows, columns):
    count = jnp.sum(mask_ref[...].astype(F32), axis=1, keepdims=True)
    real = lax.broadcasted_iota(jnp.int32, (rows, columns), 0).astype(F32) < count
    return count, real


def one_hot(rows, index_ref, scratch):
    halo = index_ref.shape[2]
    scratch[...] = jnp.full(scratch.shape, -1, jnp.int32)
    scratch[0:1, 0:halo] = index_ref[0, 0:1, :]
    scratch[0:1, LANES : LANES + halo] = index_ref[0, 1:2, :]
    wanted = scratch[0:1, :]
    return (lax.broadcasted_iota(jnp.int32, (rows, 2 * LANES), 0) == wanted).astype(BF16)


def halo_rows_kernel(feats_ref, index_ref, down_ref, up_ref, scratch):
    picked = one_hot(feats_ref.shape[0], index_ref, scratch)
    rows = mm(picked, feats_ref[...], (0, 0)).astype(BF16)
    down_ref[...] = rows[: down_ref.shape[0]]
    up_ref[...] = rows[LANES : LANES + up_ref.shape[0]]


def project_kernel(
    where_ref, feats_ref, proj_ref, skip_w_ref, neighbours_ref, mask_ref, zq_ref, skip_ref, count_ref, flipped_ref, padded,
    *, halo,
):
    node_rows = feats_ref.shape[0]
    columns, rows = count_ref.shape

    @pl.when(pl.program_id(0) == 0)
    def _():
        feats = pad_rows(feats_ref[...].astype(F32), rows).astype(BF16)
        padded[...] = feats
        flipped_ref[...] = feats.T

    zq_ref[...] = mm(padded[...], proj_ref[...], (1, 0)).astype(BF16)
    skip_ref[...] = mm(padded[...], skip_w_ref[...], (1, 0))

    names = neighbours_ref[...]
    names = names + jnp.where(names >= node_rows, rows - node_rows, 0)
    names = names + jnp.where(names >= rows + halo, STEP - halo, 0)
    names = jnp.where(mask_ref[...] > 0, names, -1)
    names = jnp.concatenate([names, jnp.full((names.shape[0], rows - node_rows), -1, jnp.int32)], axis=1)
    own = lax.broadcasted_iota(jnp.int32, (8, rows), 1)
    share = columns // 4

    def chunk(index, carry):
        start = pl.multiple_of(pl.program_id(0) * share + index * 8, 8)
        source = lax.broadcasted_iota(jnp.int32, (8, rows), 0) + start
        total = (source == own).astype(F32)
        for slot in range(names.shape[0]):
            total += jnp.where(source == names[slot : slot + 1, :], 1.0, 0.0)
        count_ref[pl.ds(start, 8), :] = jnp.where(total > 0, jnp.log(jnp.maximum(total, 1.0)) * (1.0 / LN2), NEG)
        return carry

    lax.fori_loop(0, share // 8, chunk, 0)


def attend_kernel(
    zq_ref, below_ref, above_ref, proj_ref, skip_ref, count_ref, src_ref, dst_ref, bias_ref, cot_ref, mask_ref,
    ext_ref, weight_ref, source_ref, target_ref, scale_ref, pre_ref, stats_ref, flipped_ref, halo_scr, score_scr,
):
    columns, rows = count_ref.shape
    half = (columns - rows) // 2
    head = pl.program_id(0)

    @pl.when(head == 0)
    def _():
        halo_scr[...] = jnp.zeros_like(halo_scr)
        halo_scr[0 : below_ref.shape[0], :] = below_ref[...]
        halo_scr[half : half + above_ref.shape[0], :] = above_ref[...]
        flipped_ref[...] = halo_scr[...].T

    ext_ref[0:rows, :] = zq_ref[...]
    ext_ref[rows:columns, :] = mm(halo_scr[...], proj_ref[...], (1, 0)).astype(BF16)
    ext = ext_ref[...]
    width = ext.shape[1]
    parts = three_parts(src_ref[pl.ds(head, 1), :] * (1.0 / LN2))
    vectors = jnp.concatenate([jnp.broadcast_to(part, (LANES, width)) for part in parts], axis=0)
    source = mm(ext, vectors, (1, 1))
    source_ref[0] = source[:, :LANES] + source[:, LANES : 2 * LANES] + source[:, 2 * LANES :]
    parts = three_parts(dst_ref[pl.ds(head, 1), :] * (1.0 / LN2))
    vectors = jnp.concatenate([jnp.broadcast_to(part, (16, width)) for part in parts], axis=0)
    target = mm(vectors, zq_ref[...], (1, 1))
    target = target[0:8] + target[16:24] + target[32:40]
    target_ref[0] = target
    target = target[0:1]

    def score(index, highest):
        where = pl.ds(pl.multiple_of(index * CHUNK, CHUNK), CHUNK)
        value = repeat_lanes(source_ref[0, where, :], rows) + target
        small = jnp.exp2(-jnp.abs(value))
        result = jnp.maximum(value, 0.2 * value) + (0.8 / LN2) * jnp.log(1.0 + small) + count_ref[where, :]
        score_scr[where, :] = result
        return jnp.maximum(highest, jnp.max(fold_rows(result), axis=0))

    highest = lax.fori_loop(0, columns // CHUNK, score, jnp.full((8, rows), NEG, F32))
    highest = jnp.max(highest, axis=0, keepdims=True)

    def weigh(index, carry):
        where = pl.ds(pl.multiple_of(index * CHUNK, CHUNK), CHUNK)
        weight_ref[0, where, :] = jnp.exp2(score_scr[where, :] - highest).astype(BF16)
        return carry

    lax.fori_loop(0, columns // CHUNK, weigh, 0)
    weights = weight_ref[0]
    wide = jnp.concatenate([ext, jnp.ones((columns, LANES), BF16)], axis=1)
    summed = mm(weights, wide, (0, 0))
    scale = 1.0 / summed[:, width:]
    scale_ref[0] = scale
    pre = summed[:, :width] * repeat_lanes(scale, width) + skip_ref[...] + bias_ref[...]
    pre_ref[...] = pre
    act = jnp.where(pre > 0, pre, jnp.exp(jnp.minimum(pre, 0.0)) - 1.0)
    nodes, real = real_rows(mask_ref, rows, width)
    cot = jnp.where(real, pad_rows(cot_ref[...].astype(F32), rows), 0.0)
    mean = jnp.sum(jnp.where(real, act, 0.0), axis=0, keepdims=True) / nodes
    centred = jnp.where(real, act - mean, 0.0)
    stats_ref[...] = jnp.zeros_like(stats_ref)
    stats_ref[0:1, :] = jnp.broadcast_to(nodes, mean.shape)
    stats_ref[1:2, :] = mean
    stats_ref[2:3, :] = jnp.sum(centred * centred, axis=0, keepdims=True)
    stats_ref[3:4, :] = jnp.sum(cot, axis=0, keepdims=True)
    stats_ref[4:5, :] = jnp.sum(cot * centred, axis=0, keepdims=True)


def merged(first, second):
    nodes = first[0:1] + second[0:1]
    gap = second[1:2] - first[1:2]
    part = second[0:1] / nodes
    mean = first[1:2] + gap * part
    spread = first[2:3] + second[2:3] + gap * gap * first[0:1] * part
    shift = first[3:4] + second[3:4]
    gain = first[4:5] + second[4:5] - (mean - first[1:2]) * first[3:4] - (mean - second[1:2]) * second[3:4]
    return nodes, mean, spread, shift, gain


def in_order(mine, other, bit):
    mine_first = bit == 0
    return jnp.where(mine_first, mine, other), jnp.where(mine_first, other, mine)


def merge_kernel(where_ref, mine_ref, other_ref, out_ref, *, which):
    bit = (where_ref[6] >> which) & 1
    lines = merged(*in_order(mine_ref[...], other_ref[...], bit))
    out_ref[...] = jnp.zeros_like(out_ref)
    for line, value in enumerate(lines):
        out_ref[line : line + 1, :] = value


def place_blocks(out_ref, value, me):
    size = value.shape[0] // SHARDS
    for block in range(SHARDS):
        at = pl.multiple_of((block ^ me) * size, size)
        out_ref[pl.ds(at, size), :] = value[block * size : (block + 1) * size, :]


def core_sum_kernel(mine, other, out_refs):
    for out_index, out_ref in enumerate(out_refs):
        size = out_ref.shape[1]
        rows = slice(out_index * size, (out_index + 1) * size)
        for head in range(2):
            out_ref[head] = (mine(head, rows).astype(F32) + other(head, rows).astype(F32)).astype(BF16)


def share_sum_kernel(*refs, deps):
    ins, outs = refs[:4], refs[4 + deps :]
    size = outs[0].shape[1]
    for piece, out_ref in enumerate(outs):
        rows = slice(piece * size, (piece + 1) * size)
        total = ins[0][:, rows, :].astype(F32) + ins[1][:, rows, :].astype(F32)
        out_ref[...] = (total + ins[2][:, rows, :].astype(F32) + ins[3][:, rows, :].astype(F32)).astype(BF16)


def join_kernel(*refs):
    out_ref = refs[-1]
    size = refs[0].shape[1]
    for piece in range(4):
        out_ref[:, piece * size : (piece + 1) * size, :] = refs[piece][...]


def norm_kernel(
    where_ref, pre_ref, stats_ref, other_ref, cot_ref, mask_ref, gain_ref, shift_ref, flipped_ref,
    out_ref, dskip_ref, send_ref, keep_ref, small_ref, norm_grad_ref, *, last_bit,
):
    rows = pre_ref.shape[0]
    node_rows = out_ref.shape[0]
    step = pl.program_id(0)
    pre = pre_ref[...]
    steep = jnp.exp(jnp.minimum(pre, 0.0))
    act = jnp.where(pre > 0, pre, steep - 1.0)
    real = real_rows(mask_ref, rows, pre.shape[1])[1]
    first, second = in_order(stats_ref[...], other_ref[...], (where_ref[6] >> last_bit) & 1)
    nodes, mean, spread, total, cross = merged(first, second)
    inverse = lax.rsqrt(spread / nodes + 1e-05)
    normed = (act - mean) * inverse
    gain = gain_ref[...]
    out_ref[...] = jnp.where(real, gain * normed + shift_ref[...], 0.0)[:node_rows].astype(BF16)
    norm_grad_ref[...] = jnp.zeros_like(norm_grad_ref)
    norm_grad_ref[0:1, :] = cross * inverse
    norm_grad_ref[1:2, :] = total
    grad = pad_rows(cot_ref[...].astype(F32), rows) - total / nodes - normed * (cross * inverse / nodes)
    grad_pre = jnp.where(real, grad * (inverse * gain) * steep, 0.0)
    small_ref[0] = jnp.zeros(small_ref.shape[1:], F32)
    small_ref[0, 2:3, :] = jnp.sum(grad_pre, axis=0, keepdims=True)
    dskip = grad_pre.astype(BF16)
    dskip_ref[...] = dskip
    grads = mm(flipped_ref[...], dskip, (1, 0)).astype(BF16)

    @pl.when(step < 2)
    def _():
        place_blocks(send_ref.at[0], grads, where_ref[4])

    @pl.when(step >= 2)
    def _():
        place_blocks(keep_ref.at[0], grads, where_ref[4])


def back_kernel(
    where_ref, weight_ref, source_ref, target_ref, scale_ref, ext_ref, dskip_ref, src_ref, dst_ref, flipped_ref, halo_ref,
    small_in, *rest, part,
):
    send_ref, keep_ref, small_ref, own_ref, below_ref, above_ref, dal_scr, sum_scr = rest[-8:]
    columns, rows = weight_ref.shape[1:]
    half = (columns - rows) // 2
    width = ext_ref.shape[1]
    step = pl.program_id(0)
    head = where_ref[2 * step + part]
    ext = ext_ref[...]
    dskip = dskip_ref[...]
    dal_scr[...] = mm(ext, dskip, (1, 1))
    target = target_ref[0, 0:1, :]

    def average(index, carry):
        total, mean = carry
        where = pl.ds(pl.multiple_of(index * CHUNK, CHUNK), CHUNK)
        weight = weight_ref[0, where, :].astype(F32)
        return total + jnp.sum(fold_rows(weight), axis=0), mean + jnp.sum(fold_rows(weight * dal_scr[where, :]), axis=0)

    nothing = jnp.zeros((8, rows), F32)
    total, mean = lax.fori_loop(0, columns // CHUNK, average, (nothing, nothing))
    scale = 1.0 / jnp.sum(total, axis=0, keepdims=True)
    mean = jnp.sum(mean, axis=0, keepdims=True) * scale

    def slopes(index, by_target):
        where = pl.ds(pl.multiple_of(index * CHUNK, CHUNK), CHUNK)
        value = repeat_lanes(source_ref[0, where, :], rows) + target
        slope = (0.6 + 0.4 * jnp.tanh(value * (0.5 * LN2))) * scale
        du = weight_ref[0, where, :].astype(F32) * slope * (dal_scr[where, :] - mean)
        sum_scr[where, :] = sum(du[:, at : at + LANES] for at in range(0, rows, LANES))
        return by_target + jnp.sum(fold_rows(du), axis=0)

    by_target = lax.fori_loop(0, columns // CHUNK, slopes, nothing)
    by_target = jnp.sum(by_target, axis=0, keepdims=True)
    by_source = jnp.sum(sum_scr[...], axis=1, keepdims=True)
    scaled = (dskip.astype(F32) * repeat_lanes(scale_ref[0], width)).astype(BF16)
    dz = mm(weight_ref[0], scaled, (1, 0)) + by_source * src_ref[pl.ds(head, 1), :]
    high, middle, low = three_parts(by_target)
    row = lax.broadcasted_iota(jnp.int32, (16, rows), 0)
    lines = jnp.where(row == 1, middle.astype(F32), jnp.where(row == 3, low.astype(F32), high.astype(F32)))
    lines = jnp.where(row < 4, lines, 0.0).astype(BF16)
    dst_high, dst_middle, _ = three_parts(dst_ref[pl.ds(head, 1), :])
    row = lax.broadcasted_iota(jnp.int32, (16, width), 0)
    vectors = jnp.where(row == 2, dst_middle.astype(F32), dst_high.astype(F32)).astype(BF16)
    dz_own = dz[:rows] + mm(lines, vectors, (0, 0))
    own_ref[...] = dz_own
    dz_halo = dz[rows:].astype(BF16)
    below_ref[...] = dz_halo[: below_ref.shape[0]]
    above_ref[...] = dz_halo[half : half + above_ref.shape[0]]
    sums = mm(lines, ext[:rows], (1, 0))
    small_ref[0] = small_in[0]
    small_ref[0, 0:1, :] = jnp.sum(by_source * ext.astype(F32), axis=0, keepdims=True)
    small_ref[0, 1:2, :] = sums[0:1] + sums[1:2] + sums[3:4]
    grads = mm(flipped_ref[...], dz_own.astype(BF16), (1, 0)) + mm(halo_ref[...], dz_halo, (1, 0))
    grads = grads.astype(BF16)

    @pl.when(step == 0)
    def _():
        place_blocks(send_ref, grads, where_ref[4])

    @pl.when(step == 1)
    def _():
        place_blocks(keep_ref, grads, where_ref[4])


def feats_kernel(own_ref, low_ref, high_ref, index_ref, dskip_ref, proj_ref, skip_ref, out_ref, total, picks, scratch):
    step = pl.program_id(0)
    rows = own_ref.shape[0]
    count = low_ref.shape[0]

    @pl.when(step == 0)
    def _():
        total[...] = jnp.zeros_like(total)
        picks[...] = one_hot(rows, index_ref, scratch)

    own = own_ref[...] + mm(picks[:, :count], low_ref[...], (1, 0))
    own += mm(picks[:, LANES : LANES + count], high_ref[...], (1, 0))
    total[...] += mm(own.astype(BF16), proj_ref[...], (1, 1)) + mm(dskip_ref[...], skip_ref[...], (1, 1))

    @pl.when(step == pl.num_programs(0) - 1)
    def _():
        out_ref[...] = total[: out_ref.shape[0]].astype(BF16)


def assemble_kernel(where_ref, *refs):
    out_ref = refs[-1]
    me = where_ref[4]
    size = out_ref.shape[0] // SHARDS
    for block in range(SHARDS):
        at = pl.multiple_of((block ^ me) * size, size)
        rows = slice(block % 4 * size, (block % 4 + 1) * size)
        out_ref[pl.ds(at, size), :] = refs[block // 4][0, rows, :].astype(F32)


def per_device(
    feats, w_proj, w_skip, attn_src, attn_dst, bias, gain, shift, cotangent, neighbours, edge_mask, node_mask, send_index,
):
    node_rows, depth = feats.shape
    heads, width = attn_src.shape
    concat = heads * width
    slots = neighbours.shape[1]
    halo = send_index.shape[2]
    devices = lax.axis_size(AXES)
    bits = devices.bit_length() - 1
    rows = -(-node_rows // LANES) * LANES
    columns = rows + 2 * STEP
    halo_pad = -(-halo // 16) * 16
    me = lax.axis_index(AXES)

    def passed(value, steps):
        initial, last = (max(0, -steps), min(devices, devices - steps))
        return lax.ppermute(value, AXES, [(source, source + steps) for source in range(initial, last)])

    def swapped(value, distance):
        return lax.ppermute(value, AXES, [(source, source ^ distance) for source in range(devices)])

    def bit(which):
        return (me >> which) & 1

    place = ((me >> 1) & 3) * 4 + ((me >> 3) & 3)
    core = bit(0)
    send, keep = 2 * (1 - core), 2 * core
    where = jnp.stack([send, send + 1, keep, keep + 1, place, place, me]).astype(jnp.int32)

    mask = node_mask.reshape(1, node_rows)
    bias2, gain2, shift2 = bias[None], gain[None], shift[None]

    down, up = pl.pallas_call(
        halo_rows_kernel,
        out_shape=[jax.ShapeDtypeStruct((halo_pad, depth), BF16)] * 2,
        scratch_shapes=[pltpu.VMEM((8, 2 * LANES), jnp.int32)],
        compiler_params=params(8),
        name="halo_rows",
    )(feats, send_index)
    from_below = passed(up, 1)
    from_above = passed(down, -1)

    def spec(shape, index):
        return pl.BlockSpec(shape, index)

    def whole(*shape):
        return pl.BlockSpec(shape, lambda *_: (0,) * len(shape))

    by_head = lambda n: pl.BlockSpec((n, width), lambda h, *_: (0, h))
    stacked = lambda *shape: pl.BlockSpec((1, *shape), lambda h, *_: (h, 0, 0))
    shape_of = jax.ShapeDtypeStruct
    in_hbm = lambda value: pltpu.with_memory_space_constraint(value, pltpu.HBM)
    zq, skip, count, flipped = pl.pallas_call(
        lambda *refs: project_kernel(*refs, halo=halo),
        grid_spec=pltpu.PrefetchScalarGridSpec(
            num_scalar_prefetch=1,
            grid=(heads,),
            in_specs=[
                whole(node_rows, depth), by_head(depth), by_head(depth), whole(slots, node_rows), whole(slots, node_rows),
            ],
            out_specs=[by_head(rows), by_head(rows), whole(columns, rows), whole(depth, rows)],
            scratch_shapes=[pltpu.VMEM((rows, depth), BF16)],
        ),
        out_shape=[
            shape_of((rows, concat), BF16),
            shape_of((rows, concat), F32),
            shape_of((columns, rows), F32),
            shape_of((depth, rows), BF16),
        ],
        compiler_params=params(),
        cost_estimate=cost(5),
        name="project",
    )(where, in_hbm(feats), in_hbm(w_proj), in_hbm(w_skip), neighbours.T, edge_mask.T)

    ext, weight, source, target, scale, pre, stats, halo_flipped = pl.pallas_call(
        attend_kernel,
        grid=(heads,),
        in_specs=[
            by_head(rows), whole(halo_pad, depth), whole(halo_pad, depth), by_head(depth), by_head(rows),
            whole(columns, rows), whole(heads, width), whole(heads, width), by_head(1), by_head(node_rows),
            whole(1, node_rows),
        ],
        out_specs=[
            by_head(columns), stacked(columns, rows), stacked(columns, LANES), stacked(8, rows), stacked(rows, LANES),
            by_head(rows), by_head(8), whole(depth, columns - rows),
        ],
        out_shape=[
            shape_of((columns, concat), BF16),
            shape_of((heads, columns, rows), BF16),
            shape_of((heads, columns, LANES), F32),
            shape_of((heads, 8, rows), F32),
            shape_of((heads, rows, LANES), F32),
            shape_of((rows, concat), F32),
            shape_of((8, concat), F32),
            shape_of((depth, columns - rows), BF16),
        ],
        scratch_shapes=[pltpu.VMEM((columns - rows, depth), BF16), pltpu.VMEM((columns, rows), F32)],
        compiler_params=params(),
        cost_estimate=cost(8),
        name="attend",
    )(zq, from_below, from_above, in_hbm(w_proj), skip, count, attn_src, attn_dst, bias2, in_hbm(cotangent), mask)

    for which in range(bits - 1):
        stats = pl.pallas_call(
            functools.partial(merge_kernel, which=which),
            in_specs=[pl.BlockSpec(memory_space=pltpu.SMEM)] + [pl.BlockSpec(memory_space=pltpu.VMEM)] * 2,
            out_shape=shape_of(stats.shape, F32),
            compiler_params=params(1),
            name="merge",
        )(where, stats, swapped(stats, 1 << which))
    other = swapped(stats, 1 << (bits - 1))

    head_of = lambda n: pl.BlockSpec((n, width), lambda t, w: (0, w[t]))
    early = pl.BlockSpec((1, depth, width), lambda t, w: (jnp.minimum(t, 1), 0, 0))
    late = pl.BlockSpec((1, depth, width), lambda t, w: (jnp.maximum(t - 2, 0), 0, 0))
    half_grad = shape_of((2, depth, width), BF16)
    output, dskip, skip_send, skip_keep, small, norm_grad = pl.pallas_call(
        functools.partial(norm_kernel, last_bit=bits - 1),
        grid_spec=pltpu.PrefetchScalarGridSpec(
            num_scalar_prefetch=1,
            grid=(heads,),
            in_specs=[
                head_of(rows), head_of(8), head_of(8), head_of(node_rows), whole(1, node_rows), head_of(1), head_of(1),
                whole(depth, rows),
            ],
            out_specs=[
                head_of(node_rows), head_of(rows), early, late, pl.BlockSpec((1, 8, width), lambda t, w: (w[t], 0, 0)),
                head_of(8),
            ],
        ),
        out_shape=[
            shape_of((node_rows, concat), BF16),
            shape_of((rows, concat), BF16),
            half_grad,
            half_grad,
            shape_of((heads, 8, width), F32),
            shape_of((8, concat), F32),
        ],
        compiler_params=params(),
        cost_estimate=cost(4),
        name="norm",
    )(where, pre, stats, other, cotangent, mask, gain2, shift2, flipped)

    def backward(part, small, *rest):
        shared, deps = rest[:3], rest[3:]
        head_at = lambda n: pl.BlockSpec((n, width), lambda t, w: (0, w[2 * t + part]))
        stack_at = lambda *shape: pl.BlockSpec((1, *shape), lambda t, w: (w[2 * t + part], 0, 0))
        return pl.pallas_call(
            lambda *refs: back_kernel(*refs, part=part),
            grid_spec=pltpu.PrefetchScalarGridSpec(
                num_scalar_prefetch=1,
                grid=(2,),
                in_specs=[
                    stack_at(columns, rows), stack_at(columns, LANES), stack_at(8, rows), stack_at(rows, LANES),
                    head_at(columns), head_at(rows), whole(heads, width), whole(heads, width),
                    whole(depth, rows), whole(depth, columns - rows), stack_at(8, width),
                ] + [pl.BlockSpec(memory_space=pl.ANY)] * len(rest),
                out_specs=[
                    whole(depth, width), whole(depth, width), stack_at(8, width),
                    head_at(rows), head_at(halo_pad), head_at(halo_pad),
                ],
                scratch_shapes=[pltpu.VMEM((columns, rows), F32), pltpu.VMEM((columns, LANES), F32)],
            ),
            out_shape=[
                shape_of((depth, width), BF16),
                shape_of((depth, width), BF16),
                shape_of((heads, 8, width), F32),
                shape_of((rows, concat), F32),
                shape_of((halo_pad, concat), BF16),
                shape_of((halo_pad, concat), BF16),
            ],
            input_output_aliases={11 + i: 2 + i for i in range(1 + len(shared))},
            compiler_params=params(),
            cost_estimate=cost(6),
            name="back",
        )(where, weight, source, target, scale, ext, dskip, attn_src, attn_dst, flipped, halo_flipped, small, *rest)

    half = (2, depth, width)
    quarter = (2, depth // 4, width)
    piece = (2, depth // SHARDS, width)
    anywhere = pl.BlockSpec(memory_space=pl.ANY)
    vmem = pl.BlockSpec(memory_space=pltpu.VMEM)

    def step_call(kernel, name, shapes, arrays, deps=()):
        return pl.pallas_call(
            kernel,
            in_specs=[vmem] * len(arrays) + [anywhere] * len(deps),
            out_shape=[shape_of(shape, BF16) for shape in shapes],
            compiler_params=params(1),
            cost_estimate=cost(0.7),
            name=name,
        )(*arrays, *deps)

    def over_plane(shares):
        return [swapped(share, distance << 1) for distance, share in zip((1, 2, 3), shares)]

    def over_line(shares):
        return [swapped(share, distance << 3) for distance, share in zip((1, 2, 3), shares)]

    def skip_core_sum(keep_ref, other_ref, *refs):
        core_sum_kernel(lambda h, rows: keep_ref[h, rows, :], lambda h, rows: other_ref[h, rows, :], refs[-4:])

    def proj_core_sum(one_ref, two_ref, other_one, other_two, *refs):
        mine, other = (one_ref, two_ref), (other_one, other_two)
        core_sum_kernel(lambda h, rows: mine[h][rows, :], lambda h, rows: other[h][rows, :], refs[-4:])

    def share_sum(name, arrays, count, deps):
        shapes = [(2, arrays[0].shape[1] // count, width)] * count
        return step_call(functools.partial(share_sum_kernel, deps=len(deps)), name, shapes, arrays, deps)

    def join(name, arrays, deps):
        return step_call(join_kernel, name, [(2, 4 * arrays[0].shape[1], width)], arrays, deps)[0]

    def assemble(pieces, first, *out):
        def block(share):
            at = share if pieces[share].shape[1] == depth else 0
            return pl.BlockSpec((1, depth // 4, width), lambda t, w: (t, at, 0))

        return pl.pallas_call(
            assemble_kernel,
            grid_spec=pltpu.PrefetchScalarGridSpec(
                num_scalar_prefetch=1,
                grid=(2,),
                in_specs=[block(share) for share in range(4)] + [anywhere] * len(out),
                out_specs=pl.BlockSpec((depth, width), lambda t, w: (0, w[t + first])),
            ),
            out_shape=jax.ShapeDtypeStruct((depth, concat), F32),
            input_output_aliases={5: 0} if out else {},
            compiler_params=params(8),
            cost_estimate=cost(2),
            name="assemble",
        )(where, *pieces, *out)

    def beyond(value):
        for which in range(5, bits):
            value = value + swapped(value, 1 << which)
        return value

    skip_other = swapped(skip_send, 1)
    send_a, keep_a, small, own, below, above = backward(0, small)
    other_a = swapped(send_a, 1)
    s_mine, *s_rest = step_call(skip_core_sum, "s_core", [quarter] * 4, [skip_keep, skip_other], [keep_a])
    s_got = over_plane(s_rest)
    send_b, keep_b, small, own, below, above = backward(1, small, own, below, above, s_mine)
    other_b = swapped(send_b, 1)
    back_below = passed(below, -1)
    back_above = passed(above, 1)
    p_mine, *p_rest = step_call(proj_core_sum, "p_core", [quarter] * 4, [keep_a, keep_b, other_a, other_b])
    p_got = over_plane(p_rest)
    s_mine, *s_rest = share_sum("s_plane", [s_mine, *s_got], 4, [p_mine])
    s_got = over_line(s_rest)
    grad_feats = pl.pallas_call(
        feats_kernel,
        grid=(heads,),
        in_specs=[
            by_head(rows), by_head(halo_pad), by_head(halo_pad), whole(*send_index.shape), by_head(rows),
            by_head(depth), by_head(depth),
        ],
        out_specs=whole(node_rows, depth),
        scratch_shapes=[
            pltpu.VMEM((rows, depth), F32), pltpu.VMEM((rows, 2 * LANES), BF16), pltpu.VMEM((8, 2 * LANES), jnp.int32),
        ],
        out_shape=shape_of((node_rows, depth), BF16),
        compiler_params=params(),
        cost_estimate=cost(6),
        name="features",
    )(own, back_above, back_below, send_index, dskip, w_proj, w_skip)

    s_piece = beyond(share_sum("s_line", [s_mine, *s_got], 1, [grad_feats])[0])
    s_got = over_line([s_piece] * 3)
    p_mine, *p_rest = share_sum("p_plane", [p_mine, *p_got], 4, [s_piece])
    p_got = over_line(p_rest)
    s_share = join("s_join", [s_piece, *s_got], [p_mine])
    s_got = over_plane([s_share] * 3)
    p_piece = beyond(share_sum("p_line", [p_mine, *p_got], 1, [s_share])[0])
    p_got = over_line([p_piece] * 3)
    p_share = join("p_join", [p_piece, *p_got], [])
    p_got = [p_share, *over_plane([p_share] * 3)]
    s_half = join("s_half", [s_share, *s_got], [p_share])
    s_other = swapped(s_half, 1)
    grad_skip = assemble([s_other] * 4, 0, assemble([s_half] * 4, 2))
    grad_proj = assemble([swapped(share, 1) for share in p_got], 0, assemble(p_got, 2))

    for which in range(bits):
        small = small + swapped(small, 1 << which)
    return (
        output,
        grad_feats,
        grad_proj,
        grad_skip,
        small[:, 0],
        small[:, 1],
        small[:, 2].reshape(concat),
        norm_grad[0],
        norm_grad[1],
    )


def solution(mesh):
    rows = P(AXES, None)
    in_specs = (rows,) + (P(),) * 7 + (rows, rows, rows, P(AXES), P(AXES, None, None))
    out_specs = (rows, rows) + (P(),) * 7
    return jax.shard_map(per_device, mesh=mesh, in_specs=in_specs, out_specs=out_specs, check_vma=False)
```

time: 197 us -> 151 us (0.77); the launches traced: 194 us -> 151 us
  Pallas kernels: 71.4 us -> 48.9 us
  waiting for transfers between devices: 43.1 us -> 32.7 us
  local copies, waits for them, and re-layouts: 12.8 us -> 6.35 us
  other arithmetic: 5.19 us -> 0.03 us
    pallas_call x7 -> x22, Pallas kernels: 54.6 us -> 38.8 us  [the longest x2 10.3 us: backward(): pl.pallas_call(lambda *refs: back_kernel(*refs, part=part), grid_spec=plt...]
    ppermute x38 -> x42, waiting for transfers between devices: 43.1 us -> 32.7 us  [swapped(): lax.ppermute(value, AXES, [(source, source ^ distance) for source in rang...]
    pallas_call x1, Pallas kernels: 14.7 us -> 9.65 us  [per_device(): pl.pallas_call(attend_kernel, grid=(heads,), in_specs=[by_head(rows), who...]
    broadcast_in_dim x3 -> x0, local copies, waits for them, and re-layouts: 3.36 us -> none  [the longest x2 2.56 us: per_device(): src3, dst3 = (attn_src[:, None, :], attn_dst[:, None, :])]
    ppermute x38 -> x42, starting transfers between devices: 53.7 us -> 55.3 us  [swapped(): lax.ppermute(value, AXES, [(source, source ^ distance) for source in rang...]
    unnamed x36 -> x31, local copies, waits for them, and re-layouts: 5.43 us -> 5.05 us
  transfers between devices with their start and end apart: 42 -> 46, of which waited for: 23 -> 17; matrix products, arithmetic and copies ran while one was open for 6% -> 1% of each run, Pallas kernels for 22% -> 20%
where the time goes in v2:
time: 151 us
  starting transfers between devices  61.8 us (41%)
  Pallas kernels  48.9 us (32%)
  waiting for transfers between devices  32.7 us (22%)
  local copies, waits for them, and re-layouts  6.35 us (4%)
    ppermute x42, starting transfers between devices, swapped(): lax.ppermute(value, AXES, [(source, source ^ distance) for source in rang...  55.3 us
    ppermute x42, waiting for transfers between devices, swapped(): lax.ppermute(value, AXES, [(source, source ^ distance) for source in rang...  32.7 us
    pallas_call x2, Pallas kernels, backward(): pl.pallas_call(lambda *refs: back_kernel(*refs, part=part), grid_spec=plt...  10.3 us
    pallas_call x1, Pallas kernels, per_device(): pl.pallas_call(attend_kernel, grid=(heads,), in_specs=[by_head(rows), who...  9.65 us
    pallas_call x4, Pallas kernels, assemble(): pl.pallas_call(assemble_kernel, grid_spec=pltpu.PrefetchScalarGridSpec(nu...  7.87 us
    pallas_call x1, Pallas kernels, per_device(): pl.pallas_call(lambda *refs: project_kernel(*refs, halo=halo), grid_spec=...  7.76 us
    ppermute x4, starting transfers between devices, passed(): lax.ppermute(value, AXES, [(source, source + steps) for source in range(i...  6.42 us
    unnamed x31, local copies, waits for them, and re-layouts  5.05 us
  transfers between devices with their start and end apart: 46, of which 17 were waited for; matrix products, arithmetic and copies ran while one was open for 1% of the time, Pallas kernels for 20%

profile of v2, /device:TPU:0, one launch (start us, length us, event | category | flops | bytes accessed | tf_op | source)
XLA Modules:
  0.0 150.7 jit_solution(14397666172553275991)
XLA Ops:
  2.9 2.4 %collective-permute-start = (bf16[48,1024]{1,0:T(8,128)(2,1)S(1)}, bf16[48,1024]{1,0:T(8,128)(2,1)S(1)}, u32[]{:S(2)}, u32[]{:S(2)}) collective-permute-start(bf16[48,1024]{1,0:T(8,128)(2,1)S(1)} %get-tuple-element.58), channel_id=1, source_target_pairs={{0,1},{1,2},{2,3},{3,4},{4,5},{5,6},{6,7},{7,8},{8,9},{9,10},{10,1... | collective-permute-start | bytes 294920 | tf_op jit(solution)/shard_map/ppermute | solution.py:387
  8.2 7.8 %project.1 = (bf16[384,1024]{1,0:T(8,128)(2,1)S(1)}, f32[384,1024]{1,0:T(8,128)S(1)}, f32[512,384]{1,0:T(8,128)S(1)}, bf16[1024,384]{1,0:T(8,128)(2,1)S(1)}) custom-call(s32[7]{0:T(128)S(1)} %stack.28.refs_0_.where_ref, bf16[376,1024]{1,0:T(8,128)(2,1)} %feats_ref.1, bf16[1024,1024]{1,0:T(8,128)(2,1)} %proj_ref.3, bf16[1024,1024]{1,0:T(8,128)(2,1)} %skip_ref.1, ...), custom_call_target="tpu_custom_call" | custom-call | flops 5500000256 | bytes 1000000 | tf_op jit(solution)/shard_map/project/pallas_call | solution.py:423
  16.0 9.6 %attend.1 = (bf16[512,1024]{1,0:T(8,128)(2,1)S(1)}, bf16[4,512,384]{2,1,0:T(8,128)(2,1)S(1)}, f32[4,512,128]{2,1,0:T(8,128)S(1)}, f32[4,8,384]{2,1,0:T(8,128)S(1...) custom-call(bf16[384,1024]{1,0:T(8,128)(2,1)S(1)} %get-tuple-element, ...), custom_call_target="tpu_custom_call" | custom-call | flops 8800000000 | bytes 1000000 | tf_op jit(solution)/shard_map/attend/pallas_call | solution.py:445
  25.7 3.3 %collective-permute-start.2 = (f32[8,1024]{1,0:T(8,128)S(1)}, f32[8,1024]{1,0:T(8,128)S(1)}, u32[]{:S(2)}, u32[]{:S(2)}) collective-permute-start(f32[8,1024]{1,0:T(8,128)S(1)} %get-tuple-element.63.mine_ref), channel_id=1, source_target_pairs={{0,1},{1,0},{2,3},{3,2},{4,5},{5,4},{6,7},{7,6},{8,9},{9,8},{10,11... | collective-permute-start | bytes 98312 | tf_op jit(solution)/shard_map/ppermute | solution.py:390
  30.5 2.0 %collective-permute-start.3 = (f32[8,1024]{1,0:T(8,128)S(1)}, f32[8,1024]{1,0:T(8,128)S(1)}, u32[]{:S(2)}, u32[]{:S(2)}) collective-permute-start(f32[8,1024]{1,0:T(8,128)S(1)} %merge.4.mine_ref), channel_id=1, source_target_pairs={{0,2},{1,3},{2,0},{3,1},{4,6},{5,7},{6,4},{7,5},{8,10},{9,11},{10,... | collective-permute-start | bytes 98312 | tf_op jit(solution)/shard_map/ppermute | solution.py:390
  32.5 2.0 %collective-permute-done.3.other_ref = f32[8,1024]{1,0:T(8,128)S(1)} collective-permute-done((f32[8,1024]{1,0:T(8,128)S(1)}, f32[8,1024]{1,0:T(8,128)S(1)}, u32[]{:S(2)}, u32[]{:S(2)}) %collective-permute-start.3) | collective-permute-done | bytes 32800 | tf_op jit(solution)/shard_map/ppermute | solution.py:390
  35.1 2.9 %collective-permute-start.4 = (f32[8,1024]{1,0:T(8,128)S(1)}, f32[8,1024]{1,0:T(8,128)S(1)}, u32[]{:S(2)}, u32[]{:S(2)}) collective-permute-start(f32[8,1024]{1,0:T(8,128)S(1)} %merge.5.mine_ref), channel_id=1, source_target_pairs={{0,4},{1,5},{2,6},{3,7},{4,0},{5,1},{6,2},{7,3},{8,12},{9,13},{10,... | collective-permute-start | bytes 98312 | tf_op jit(solution)/shard_map/ppermute | solution.py:390
  38.0 1.9 %collective-permute-done.4.other_ref = f32[8,1024]{1,0:T(8,128)S(1)} collective-permute-done((f32[8,1024]{1,0:T(8,128)S(1)}, f32[8,1024]{1,0:T(8,128)S(1)}, u32[]{:S(2)}, u32[]{:S(2)}) %collective-permute-start.4) | collective-permute-done | bytes 32800 | tf_op jit(solution)/shard_map/ppermute | solution.py:390
  40.4 3.1 %collective-permute-start.5 = (f32[8,1024]{1,0:T(8,128)S(1)}, f32[8,1024]{1,0:T(8,128)S(1)}, u32[]{:S(2)}, u32[]{:S(2)}) collective-permute-start(f32[8,1024]{1,0:T(8,128)S(1)} %merge.6.mine_ref), channel_id=1, source_target_pairs={{0,8},{1,9},{2,10},{3,11},{4,12},{5,13},{6,14},{7,15},{8,0},{9,1},... | collective-permute-start | bytes 98312 | tf_op jit(solution)/shard_map/ppermute | solution.py:390
  46.0 3.2 %collective-permute-start.6 = (f32[8,1024]{1,0:T(8,128)S(1)}, f32[8,1024]{1,0:T(8,128)S(1)}, u32[]{:S(2)}, u32[]{:S(2)}) collective-permute-start(f32[8,1024]{1,0:T(8,128)S(1)} %merge.7.stats_ref), channel_id=1, source_target_pairs={{0,16},{1,17},{2,18},{3,19},{4,20},{5,21},{6,22},{7,23},{8,24},{9,... | collective-permute-start | bytes 98312 | tf_op jit(solution)/shard_map/ppermute | solution.py:390
  51.2 4.9 %norm.1 = (bf16[376,1024]{1,0:T(8,128)(2,1)}, bf16[384,1024]{1,0:T(8,128)(2,1)S(1)}, bf16[2,1024,256]{2,1,0:T(8,128)(2,1)S(1)}, bf16[2,1024,256]{2,1,0:T(8,128)(...) custom-call(s32[7]{0:T(128)S(1)} %stack.28.refs_0_.where_ref, f32[384,1024]{1,0:T(8,128)S(1)} %get-tuple-element.62.pre_ref, ...), custom_call_target="tpu_custom_call" | custom-call | flops 4400000000 | bytes 1000000 | tf_op jit(solution)/shard_map/norm/pallas_call | solution.py:487
  56.1 5.1 %back.2 = (bf16[1024,256]{1,0:T(8,128)(2,1)S(1)}, bf16[1024,256]{1,0:T(8,128)(2,1)S(1)}, f32[4,8,256]{2,1,0:T(8,128)S(1)}, f32[384,1024]{1,0:T(8,128)S(1)}, bf16...) custom-call(s32[7]{0:T(128)S(1)} %stack.28.refs_0_.where_ref, ...), custom_call_target="tpu_custom_call", output_to_operand_aliasing={{2}: (11, {})} | custom-call | flops 6600000000 | bytes 1000000 | tf_op jit(solution)/shard_map/back/pallas_call | solution.py:518
  62.0 5.1 %back.3 = (bf16[1024,256]{1,0:T(8,128)(2,1)S(1)}, bf16[1024,256]{1,0:T(8,128)(2,1)S(1)}, f32[4,8,256]{2,1,0:T(8,128)S(1)}, f32[384,1024]{1,0:T(8,128)S(1)}, bf16...) custom-call(s32[7]{0:T(128)S(1)} %stack.28.refs_0_.where_ref, ...), custom_call_target="tpu_custom_call", output_to_operand_aliasing={{2}: (11, {}), {3}: (12, {}), {4}: (13, {}), {5}: (14, {})} | custom-call | flops 6600000000 | bytes 1000000 | tf_op jit(solution)/shard_map/back/pallas_call | solution.py:518
  69.2 2.0 %collective-permute-start.17 = (bf16[2,256,256]{2,1,0:T(8,128)(2,1)S(1)}, bf16[2,256,256]{2,1,0:T(8,128)(2,1)S(1)}, u32[]{:S(2)}, u32[]{:S(2)}) collective-permute-start(bf16[2,256,256]{2,1,0:T(8,128)(2,1)S(1)} %get-tuple-element.94), channel_id=1, source_target_pairs={{0,6},{1,7},{2,4},{3,5},{4,2},{5,3},{6,0},{7,1},{8,14},{9,15},{10,... | collective-permute-start | bytes 786440 | tf_op jit(solution)/shard_map/ppermute | solution.py:390
  77.6 5.4 %collective-permute-done.17.refs_3_ = bf16[2,256,256]{2,1,0:T(8,128)(2,1)S(1)} collective-permute-done((bf16[2,256,256]{2,1,0:T(8,128)(2,1)S(1)}, bf16[2,256,256]{2,1,0:T(8,128)(2,1)S(1)}, u32[]{:S(2)}, u32[]{:S(2)}) %collective-permute-start.17) | collective-permute-done | bytes 262176 | tf_op jit(solution)/shard_map/ppermute | solution.py:390
  83.1 2.8 %collective-permute-start.18 = (bf16[2,64,256]{2,1,0:T(8,128)(2,1)S(1)}, bf16[2,64,256]{2,1,0:T(8,128)(2,1)S(1)}, u32[]{:S(2)}, u32[]{:S(2)}) collective-permute-start(bf16[2,64,256]{2,1,0:T(8,128)(2,1)S(1)} %get-tuple-element.96), channel_id=1, source_target_pairs={{0,8},{1,9},{2,10},{3,11},{4,12},{5,13},{6,14},{7,15},{8,0},{9,1},... | collective-permute-start | bytes 196616 | tf_op jit(solution)/shard_map/ppermute | solution.py:390
  86.6 2.9 %collective-permute-start.19 = (bf16[2,64,256]{2,1,0:T(8,128)(2,1)S(1)}, bf16[2,64,256]{2,1,0:T(8,128)(2,1)S(1)}, u32[]{:S(2)}, u32[]{:S(2)}) collective-permute-start(bf16[2,64,256]{2,1,0:T(8,128)(2,1)S(1)} %get-tuple-element.97), channel_id=1, source_target_pairs={{0,16},{1,17},{2,18},{3,19},{4,20},{5,21},{6,22},{7,23},{8,24},{9,... | collective-permute-start | bytes 196616 | tf_op jit(solution)/shard_map/ppermute | solution.py:390
  89.9 3.6 %collective-permute-start.20 = (bf16[2,64,256]{2,1,0:T(8,128)(2,1)S(1)}, bf16[2,64,256]{2,1,0:T(8,128)(2,1)S(1)}, u32[]{:S(2)}, u32[]{:S(2)}) collective-permute-start(bf16[2,64,256]{2,1,0:T(8,128)(2,1)S(1)} %get-tuple-element.98), channel_id=1, source_target_pairs={{0,24},{1,25},{2,26},{3,27},{4,28},{5,29},{6,30},{7,31},{8,16},{9,... | collective-permute-start | bytes 196616 | tf_op jit(solution)/shard_map/ppermute | solution.py:390
  94.4 2.6 %collective-permute-start.14 = (bf16[2,256,256]{2,1,0:T(8,128)(2,1)S(1)}, bf16[2,256,256]{2,1,0:T(8,128)(2,1)S(1)}, u32[]{:S(2)}, u32[]{:S(2)}) collective-permute-start(bf16[2,256,256]{2,1,0:T(8,128)(2,1)S(1)} %get-tuple-element.91), channel_id=1, source_target_pairs={{0,6},{1,7},{2,4},{3,5},{4,2},{5,3},{6,0},{7,1},{8,14},{9,15},{10,... | collective-permute-start | bytes 786440 | tf_op jit(solution)/shard_map/ppermute | solution.py:390
  97.0 4.7 %features.1.refs_4_ = bf16[376,1024]{1,0:T(8,128)(2,1)} custom-call(f32[384,1024]{1,0:T(8,128)S(1)} %get-tuple-element.82.own_ref, bf16[48,1024]{1,0:T(8,128)(2,1)S(1)} %collective-permute-done.8.low_ref, bf16[48,1024]{1,0:T(8,128)(2,1)S(1)} %collective-permute-done.9.high_ref, s32[1,2,47]{2,1,0:T(2,128)S(1)} %copy-done.2, ...), custom_call_target="tpu_custom_call" | custom-call | flops 6600000000 | bytes 1000000 | tf_op jit(solution)/shard_map/features/pallas_call | solution.py:622
  103.8 2.7 %collective-permute-start.25 = (bf16[2,64,256]{2,1,0:T(8,128)(2,1)S(1)}, bf16[2,64,256]{2,1,0:T(8,128)(2,1)S(1)}, u32[]{:S(2)}, u32[]{:S(2)}) collective-permute-start(bf16[2,64,256]{2,1,0:T(8,128)(2,1)S(1)} %s_line.1.refs_4_.refs_0_), channel_id=1, source_target_pairs={{0,16},{1,17},{2,18},{3,19},{4,20},{5,21},{6,22},{7,23},{8,24},{9,... | collective-permute-start | bytes 196616 | tf_op jit(solution)/shard_map/ppermute | solution.py:390
  109.5 2.0 %collective-permute-start.22 = (bf16[2,64,256]{2,1,0:T(8,128)(2,1)S(1)}, bf16[2,64,256]{2,1,0:T(8,128)(2,1)S(1)}, u32[]{:S(2)}, u32[]{:S(2)}) collective-permute-start(bf16[2,64,256]{2,1,0:T(8,128)(2,1)S(1)} %get-tuple-element.101), channel_id=1, source_target_pairs={{0,16},{1,17},{2,18},{3,19},{4,20},{5,21},{6,22},{7,23},{8,24},{9,... | collective-permute-start | bytes 196616 | tf_op jit(solution)/shard_map/ppermute | solution.py:390
  111.6 2.1 %collective-permute-done.25.refs_2_ = bf16[2,64,256]{2,1,0:T(8,128)(2,1)S(1)} collective-permute-done((bf16[2,64,256]{2,1,0:T(8,128)(2,1)S(1)}, bf16[2,64,256]{2,1,0:T(8,128)(2,1)S(1)}, u32[]{:S(2)}, u32[]{:S(2)}) %collective-permute-start.25) | collective-permute-done | bytes 65568 | tf_op jit(solution)/shard_map/ppermute | solution.py:390
  115.2 4.5 %collective-permute-done.23.refs_3_ = bf16[2,64,256]{2,1,0:T(8,128)(2,1)S(1)} collective-permute-done((bf16[2,64,256]{2,1,0:T(8,128)(2,1)S(1)}, bf16[2,64,256]{2,1,0:T(8,128)(2,1)S(1)}, u32[]{:S(2)}, u32[]{:S(2)}) %collective-permute-start.23) | collective-permute-done | bytes 65568 | tf_op jit(solution)/shard_map/ppermute | solution.py:390
  122.4 2.5 %collective-permute-start.37 = (bf16[2,256,256]{2,1,0:T(8,128)(2,1)S(1)}, bf16[2,256,256]{2,1,0:T(8,128)(2,1)S(1)}, u32[]{:S(2)}, u32[]{:S(2)}) collective-permute-start(bf16[2,256,256]{2,1,0:T(8,128)(2,1)S(1)} %s_join.1.refs_4_.refs_0_), channel_id=1, source_target_pairs={{0,2},{1,3},{2,0},{3,1},{4,6},{5,7},{6,4},{7,5},{8,10},{9,11},{10,... | collective-permute-start | bytes 786440 | tf_op jit(solution)/shard_map/ppermute | solution.py:390
  129.7 2.8 %collective-permute-done.28.refs_2_ = bf16[2,64,256]{2,1,0:T(8,128)(2,1)S(1)} collective-permute-done((bf16[2,64,256]{2,1,0:T(8,128)(2,1)S(1)}, bf16[2,64,256]{2,1,0:T(8,128)(2,1)S(1)}, u32[]{:S(2)}, u32[]{:S(2)}) %collective-permute-start.28) | collective-permute-done | bytes 65568 | tf_op jit(solution)/shard_map/ppermute | solution.py:390
  133.7 2.3 %collective-permute-start.31 = (bf16[2,256,256]{2,1,0:T(8,128)(2,1)S(1)}, bf16[2,256,256]{2,1,0:T(8,128)(2,1)S(1)}, u32[]{:S(2)}, u32[]{:S(2)}) collective-permute-start(bf16[2,256,256]{2,1,0:T(8,128)(2,1)S(1)} %p_join.1.refs_0_.refs_4_), channel_id=1, source_target_pairs={{0,2},{1,3},{2,0},{3,1},{4,6},{5,7},{6,4},{7,5},{8,10},{9,11},{10,... | collective-permute-start | bytes 786440 | tf_op jit(solution)/shard_map/ppermute | solution.py:390
  140.9 2.0 %collective-permute-done.31.refs_1_ = bf16[2,256,256]{2,1,0:T(8,128)(2,1)S(1)} collective-permute-done((bf16[2,256,256]{2,1,0:T(8,128)(2,1)S(1)}, bf16[2,256,256]{2,1,0:T(8,128)(2,1)S(1)}, u32[]{:S(2)}, u32[]{:S(2)}) %collective-permute-start.31) | collective-permute-done | bytes 262176 | tf_op jit(solution)/shard_map/ppermute | solution.py:390
  142.8 2.0 %assemble.6.refs_4_ = f32[1024,1024]{1,0:T(8,128)} custom-call(s32[7]{0:T(128)S(1)} %stack.28.refs_0_.where_ref, bf16[2,1024,256]{2,1,0:T(8,128)(2,1)S(1)} %s_half.1.refs_0_.refs_1_.refs_2_.refs_3_, bf16[2,1024,256]{2,1,0:T(8,128)(2,1)S(1)} %s_half.1.refs_0_.refs_1_.refs_2_.refs_3_, bf16[2,1024,256]{2,1,0:T(8,128)(2,1)S(1)} %s_half.1.refs_0_.refs_1_.refs_2_.refs_3_, ...), custom_call_target="tpu_custom_call" | custom-call | flops 2200000000 | bytes 1000000 | tf_op jit(solution)/shard_map/assemble/pallas_call | solution.py:589
  144.8 2.0 %assemble.4.refs_4_ = f32[1024,1024]{1,0:T(8,128)} custom-call(s32[7]{0:T(128)S(1)} %stack.28.refs_0_.where_ref, bf16[2,256,256]{2,1,0:T(8,128)(2,1)S(1)} %p_join.1.refs_0_.refs_4_, bf16[2,256,256]{2,1,0:T(8,128)(2,1)S(1)} %collective-permute-done.31.refs_1_, bf16[2,256,256]{2,1,0:T(8,128)(2,1)S(1)} %collective-permute-done.33.refs_2_, ...), custom_call_target="tpu_custom_call" | custom-call | flops 2200000000 | bytes 1000000 | tf_op jit(solution)/shard_map/assemble/pallas_call | solution.py:589
  146.8 2.0 %assemble.5 = f32[1024,1024]{1,0:T(8,128)} custom-call(s32[7]{0:T(128)S(1)} %stack.28.refs_0_.where_ref, bf16[2,256,256]{2,1,0:T(8,128)(2,1)S(1)} %collective-permute-done.30.refs_0_, bf16[2,256,256]{2,1,0:T(8,128)(2,1)S(1)} %collective-permute-done.32.refs_1_, ...), custom_call_target="tpu_custom_call", output_to_operand_aliasing={{}: (5, {})} | custom-call | flops 2200000000 | bytes 1000000 | tf_op jit(solution)/shard_map/assemble/pallas_call | solution.py:589
  148.8 2.0 %assemble.7 = f32[1024,1024]{1,0:T(8,128)} custom-call(s32[7]{0:T(128)S(1)} %stack.28.refs_0_.where_ref, bf16[2,1024,256]{2,1,0:T(8,128)(2,1)S(1)} %collective-permute-done.40.refs_0_.refs_1_.refs_2_.refs_3_, bf16[2,1024,256]{2,1,0:T(8,128)(2,1)S(1)} %collective-permute-done.40.refs_0_.refs_1_.refs_2_.refs_3_, ...), custom_call_target="tpu_custom_call", output_to_operand_aliasing={{}: (5, {})} | custom-call | flops 2200000000 | bytes 1000000 | tf_op jit(solution)/shard_map/assemble/pallas_call | solution.py:589
  (124 shorter events, 43.4 us)
Async XLA Ops:
  2.9 13.0 %collective-permute-start = (bf16[48,1024]{1,0:T(8,128)(2,1)S(1)}, bf16[48,1024]{1,0:T(8,128)(2,1)S(1)}, u32[]{:S(2)}, u32[]{:S(2)}) collective-permute-start(bf16[48,1024]{1,0:T(8,128)(2,1)S(1)} %get-tuple-element.58), channel_id=1, source_target_pairs={{0,1},{1,2},{2,3},{3,4},{4,5},{5,6},{6,7},{7,8},{8,9},{9,10},{10,1... | collective-permute-start | bytes 294920 | tf_op jit(solution)/shard_map/ppermute | solution.py:387
  5.3 10.7 %collective-permute-start.1 = (bf16[48,1024]{1,0:T(8,128)(2,1)S(1)}, bf16[48,1024]{1,0:T(8,128)(2,1)S(1)}, u32[]{:S(2)}, u32[]{:S(2)}) collective-permute-start(bf16[48,1024]{1,0:T(8,128)(2,1)S(1)} %get-tuple-element.59), channel_id=1, source_target_pairs={{1,0},{2,1},{3,2},{4,3},{5,4},{6,5},{7,6},{8,7},{9,8},{10,9},{11,1... | collective-permute-start | bytes 294920 | tf_op jit(solution)/shard_map/ppermute | solution.py:387
  61.2 10.0 %collective-permute-start.10 = (bf16[1024,256]{1,0:T(8,128)(2,1)S(1)}, bf16[1024,256]{1,0:T(8,128)(2,1)S(1)}, u32[]{:S(2)}, u32[]{:S(2)}) collective-permute-start(bf16[1024,256]{1,0:T(8,128)(2,1)S(1)} %get-tuple-element.86), channel_id=1, source_target_pairs={{0,1},{1,0},{2,3},{3,2},{4,5},{5,4},{6,7},{7,6},{8,9},{9,8},{10,11... | collective-permute-start | bytes 1572872 | tf_op jit(solution)/shard_map/ppermute | solution.py:390
  67.7 8.3 %collective-permute-start.15 = (bf16[2,256,256]{2,1,0:T(8,128)(2,1)S(1)}, bf16[2,256,256]{2,1,0:T(8,128)(2,1)S(1)}, u32[]{:S(2)}, u32[]{:S(2)}) collective-permute-start(bf16[2,256,256]{2,1,0:T(8,128)(2,1)S(1)} %get-tuple-element.92), channel_id=1, source_target_pairs={{0,2},{1,3},{2,0},{3,1},{4,6},{5,7},{6,4},{7,5},{8,10},{9,11},{10,... | collective-permute-start | bytes 786440 | tf_op jit(solution)/shard_map/ppermute | solution.py:390
  67.7 9.8 %collective-permute-start.16 = (bf16[2,256,256]{2,1,0:T(8,128)(2,1)S(1)}, bf16[2,256,256]{2,1,0:T(8,128)(2,1)S(1)}, u32[]{:S(2)}, u32[]{:S(2)}) collective-permute-start(bf16[2,256,256]{2,1,0:T(8,128)(2,1)S(1)} %get-tuple-element.93), channel_id=1, source_target_pairs={{0,4},{1,5},{2,6},{3,7},{4,0},{5,1},{6,2},{7,3},{8,12},{9,13},{10,... | collective-permute-start | bytes 786440 | tf_op jit(solution)/shard_map/ppermute | solution.py:390
  69.2 13.7 %collective-permute-start.17 = (bf16[2,256,256]{2,1,0:T(8,128)(2,1)S(1)}, bf16[2,256,256]{2,1,0:T(8,128)(2,1)S(1)}, u32[]{:S(2)}, u32[]{:S(2)}) collective-permute-start(bf16[2,256,256]{2,1,0:T(8,128)(2,1)S(1)} %get-tuple-element.94), channel_id=1, source_target_pairs={{0,6},{1,7},{2,4},{3,5},{4,2},{5,3},{6,0},{7,1},{8,14},{9,15},{10,... | collective-permute-start | bytes 786440 | tf_op jit(solution)/shard_map/ppermute | solution.py:390
  71.2 22.3 %collective-permute-start.8 = (bf16[48,1024]{1,0:T(8,128)(2,1)S(1)}, bf16[48,1024]{1,0:T(8,128)(2,1)S(1)}, u32[]{:S(2)}, u32[]{:S(2)}) collective-permute-start(bf16[48,1024]{1,0:T(8,128)(2,1)S(1)} %get-tuple-element.83), channel_id=1, source_target_pairs={{0,1},{1,2},{2,3},{3,4},{4,5},{5,6},{6,7},{7,8},{8,9},{9,10},{10,1... | collective-permute-start | bytes 294920 | tf_op jit(solution)/shard_map/ppermute | solution.py:387
  72.5 21.0 %collective-permute-start.9 = (bf16[48,1024]{1,0:T(8,128)(2,1)S(1)}, bf16[48,1024]{1,0:T(8,128)(2,1)S(1)}, u32[]{:S(2)}, u32[]{:S(2)}) collective-permute-start(bf16[48,1024]{1,0:T(8,128)(2,1)S(1)} %get-tuple-element.84), channel_id=1, source_target_pairs={{1,0},{2,1},{3,2},{4,3},{5,4},{6,5},{7,6},{8,7},{9,8},{10,9},{11,1... | collective-permute-start | bytes 294920 | tf_op jit(solution)/shard_map/ppermute | solution.py:387
  76.0 9.9 %collective-permute-start.42 = (f32[4,8,256]{2,1,0:T(8,128)S(1)}, f32[4,8,256]{2,1,0:T(8,128)S(1)}, u32[]{:S(2)}, u32[]{:S(2)}) collective-permute-start(f32[4,8,256]{2,1,0:T(8,128)S(1)} %add.31), channel_id=1, source_target_pairs={{0,2},{1,3},{2,0},{3,1},{4,6},{5,7},{6,4},{7,5},{8,10},{9,11},{10,... | collective-permute-start | bytes 98312 | tf_op jit(solution)/shard_map/ppermute | solution.py:390
  83.1 11.3 %collective-permute-start.18 = (bf16[2,64,256]{2,1,0:T(8,128)(2,1)S(1)}, bf16[2,64,256]{2,1,0:T(8,128)(2,1)S(1)}, u32[]{:S(2)}, u32[]{:S(2)}) collective-permute-start(bf16[2,64,256]{2,1,0:T(8,128)(2,1)S(1)} %get-tuple-element.96), channel_id=1, source_target_pairs={{0,8},{1,9},{2,10},{3,11},{4,12},{5,13},{6,14},{7,15},{8,0},{9,1},... | collective-permute-start | bytes 196616 | tf_op jit(solution)/shard_map/ppermute | solution.py:390
  86.6 15.1 %collective-permute-start.19 = (bf16[2,64,256]{2,1,0:T(8,128)(2,1)S(1)}, bf16[2,64,256]{2,1,0:T(8,128)(2,1)S(1)}, u32[]{:S(2)}, u32[]{:S(2)}) collective-permute-start(bf16[2,64,256]{2,1,0:T(8,128)(2,1)S(1)} %get-tuple-element.97), channel_id=1, source_target_pairs={{0,16},{1,17},{2,18},{3,19},{4,20},{5,21},{6,22},{7,23},{8,24},{9,... | collective-permute-start | bytes 196616 | tf_op jit(solution)/shard_map/ppermute | solution.py:390
  89.9 11.9 %collective-permute-start.20 = (bf16[2,64,256]{2,1,0:T(8,128)(2,1)S(1)}, bf16[2,64,256]{2,1,0:T(8,128)(2,1)S(1)}, u32[]{:S(2)}, u32[]{:S(2)}) collective-permute-start(bf16[2,64,256]{2,1,0:T(8,128)(2,1)S(1)} %get-tuple-element.98), channel_id=1, source_target_pairs={{0,24},{1,25},{2,26},{3,27},{4,28},{5,29},{6,30},{7,31},{8,16},{9,... | collective-permute-start | bytes 196616 | tf_op jit(solution)/shard_map/ppermute | solution.py:390
  93.5 10.3 %collective-permute-start.12 = (bf16[2,256,256]{2,1,0:T(8,128)(2,1)S(1)}, bf16[2,256,256]{2,1,0:T(8,128)(2,1)S(1)}, u32[]{:S(2)}, u32[]{:S(2)}) collective-permute-start(bf16[2,256,256]{2,1,0:T(8,128)(2,1)S(1)} %get-tuple-element.89), channel_id=1, source_target_pairs={{0,2},{1,3},{2,0},{3,1},{4,6},{5,7},{6,4},{7,5},{8,10},{9,11},{10,... | collective-permute-start | bytes 786440 | tf_op jit(solution)/shard_map/ppermute | solution.py:390
  93.5 13.0 %collective-permute-start.13 = (bf16[2,256,256]{2,1,0:T(8,128)(2,1)S(1)}, bf16[2,256,256]{2,1,0:T(8,128)(2,1)S(1)}, u32[]{:S(2)}, u32[]{:S(2)}) collective-permute-start(bf16[2,256,256]{2,1,0:T(8,128)(2,1)S(1)} %get-tuple-element.90), channel_id=1, source_target_pairs={{0,4},{1,5},{2,6},{3,7},{4,0},{5,1},{6,2},{7,3},{8,12},{9,13},{10,... | collective-permute-start | bytes 786440 | tf_op jit(solution)/shard_map/ppermute | solution.py:390
  94.4 13.1 %collective-permute-start.14 = (bf16[2,256,256]{2,1,0:T(8,128)(2,1)S(1)}, bf16[2,256,256]{2,1,0:T(8,128)(2,1)S(1)}, u32[]{:S(2)}, u32[]{:S(2)}) collective-permute-start(bf16[2,256,256]{2,1,0:T(8,128)(2,1)S(1)} %get-tuple-element.91), channel_id=1, source_target_pairs={{0,6},{1,7},{2,4},{3,5},{4,2},{5,3},{6,0},{7,1},{8,14},{9,15},{10,... | collective-permute-start | bytes 786440 | tf_op jit(solution)/shard_map/ppermute | solution.py:390
  101.7 19.6 %collective-permute-start.44 = (f32[4,8,256]{2,1,0:T(8,128)S(1)}, f32[4,8,256]{2,1,0:T(8,128)S(1)}, u32[]{:S(2)}, u32[]{:S(2)}) collective-permute-start(f32[4,8,256]{2,1,0:T(8,128)S(1)} %add.33), channel_id=1, source_target_pairs={{0,8},{1,9},{2,10},{3,11},{4,12},{5,13},{6,14},{7,15},{8,0},{9,1},... | collective-permute-start | bytes 98312 | tf_op jit(solution)/shard_map/ppermute | solution.py:390
  103.0 6.5 %collective-permute-start.26 = (bf16[2,64,256]{2,1,0:T(8,128)(2,1)S(1)}, bf16[2,64,256]{2,1,0:T(8,128)(2,1)S(1)}, u32[]{:S(2)}, u32[]{:S(2)}) collective-permute-start(bf16[2,64,256]{2,1,0:T(8,128)(2,1)S(1)} %s_line.1.refs_4_.refs_0_), channel_id=1, source_target_pairs={{0,24},{1,25},{2,26},{3,27},{4,28},{5,29},{6,30},{7,31},{8,16},{9,... | collective-permute-start | bytes 196616 | tf_op jit(solution)/shard_map/ppermute | solution.py:390
  103.8 9.8 %collective-permute-start.25 = (bf16[2,64,256]{2,1,0:T(8,128)(2,1)S(1)}, bf16[2,64,256]{2,1,0:T(8,128)(2,1)S(1)}, u32[]{:S(2)}, u32[]{:S(2)}) collective-permute-start(bf16[2,64,256]{2,1,0:T(8,128)(2,1)S(1)} %s_line.1.refs_4_.refs_0_), channel_id=1, source_target_pairs={{0,16},{1,17},{2,18},{3,19},{4,20},{5,21},{6,22},{7,23},{8,24},{9,... | collective-permute-start | bytes 196616 | tf_op jit(solution)/shard_map/ppermute | solution.py:390
  106.5 8.6 %collective-permute-start.24 = (bf16[2,64,256]{2,1,0:T(8,128)(2,1)S(1)}, bf16[2,64,256]{2,1,0:T(8,128)(2,1)S(1)}, u32[]{:S(2)}, u32[]{:S(2)}) collective-permute-start(bf16[2,64,256]{2,1,0:T(8,128)(2,1)S(1)} %s_line.1.refs_4_.refs_0_), channel_id=1, source_target_pairs={{0,8},{1,9},{2,10},{3,11},{4,12},{5,13},{6,14},{7,15},{8,0},{9,1},... | collective-permute-start | bytes 196616 | tf_op jit(solution)/shard_map/ppermute | solution.py:390
  107.6 7.6 %collective-permute-start.21 = (bf16[2,64,256]{2,1,0:T(8,128)(2,1)S(1)}, bf16[2,64,256]{2,1,0:T(8,128)(2,1)S(1)}, u32[]{:S(2)}, u32[]{:S(2)}) collective-permute-start(bf16[2,64,256]{2,1,0:T(8,128)(2,1)S(1)} %get-tuple-element.100), channel_id=1, source_target_pairs={{0,8},{1,9},{2,10},{3,11},{4,12},{5,13},{6,14},{7,15},{8,0},{9,1},... | collective-permute-start | bytes 196616 | tf_op jit(solution)/shard_map/ppermute | solution.py:390
  113.6 6.1 %collective-permute-start.23 = (bf16[2,64,256]{2,1,0:T(8,128)(2,1)S(1)}, bf16[2,64,256]{2,1,0:T(8,128)(2,1)S(1)}, u32[]{:S(2)}, u32[]{:S(2)}) collective-permute-start(bf16[2,64,256]{2,1,0:T(8,128)(2,1)S(1)} %get-tuple-element.102), channel_id=1, source_target_pairs={{0,24},{1,25},{2,26},{3,27},{4,28},{5,29},{6,30},{7,31},{8,16},{9,... | collective-permute-start | bytes 196616 | tf_op jit(solution)/shard_map/ppermute | solution.py:390
  119.7 8.1 %collective-permute-start.29 = (bf16[2,64,256]{2,1,0:T(8,128)(2,1)S(1)}, bf16[2,64,256]{2,1,0:T(8,128)(2,1)S(1)}, u32[]{:S(2)}, u32[]{:S(2)}) collective-permute-start(bf16[2,64,256]{2,1,0:T(8,128)(2,1)S(1)} %p_line.1.refs_0_), channel_id=1, source_target_pairs={{0,24},{1,25},{2,26},{3,27},{4,28},{5,29},{6,30},{7,31},{8,16},{9,... | collective-permute-start | bytes 196616 | tf_op jit(solution)/shard_map/ppermute | solution.py:390
  121.4 12.3 %collective-permute-start.39 = (bf16[2,256,256]{2,1,0:T(8,128)(2,1)S(1)}, bf16[2,256,256]{2,1,0:T(8,128)(2,1)S(1)}, u32[]{:S(2)}, u32[]{:S(2)}) collective-permute-start(bf16[2,256,256]{2,1,0:T(8,128)(2,1)S(1)} %s_join.1.refs_4_.refs_0_), channel_id=1, source_target_pairs={{0,6},{1,7},{2,4},{3,5},{4,2},{5,3},{6,0},{7,1},{8,14},{9,15},{10,... | collective-permute-start | bytes 786440 | tf_op jit(solution)/shard_map/ppermute | solution.py:390
  121.5 14.6 %collective-permute-start.38 = (bf16[2,256,256]{2,1,0:T(8,128)(2,1)S(1)}, bf16[2,256,256]{2,1,0:T(8,128)(2,1)S(1)}, u32[]{:S(2)}, u32[]{:S(2)}) collective-permute-start(bf16[2,256,256]{2,1,0:T(8,128)(2,1)S(1)} %s_join.1.refs_4_.refs_0_), channel_id=1, source_target_pairs={{0,4},{1,5},{2,6},{3,7},{4,0},{5,1},{6,2},{7,3},{8,12},{9,13},{10,... | collective-permute-start | bytes 786440 | tf_op jit(solution)/shard_map/ppermute | solution.py:390
  122.4 14.6 %collective-permute-start.37 = (bf16[2,256,256]{2,1,0:T(8,128)(2,1)S(1)}, bf16[2,256,256]{2,1,0:T(8,128)(2,1)S(1)}, u32[]{:S(2)}, u32[]{:S(2)}) collective-permute-start(bf16[2,256,256]{2,1,0:T(8,128)(2,1)S(1)} %s_join.1.refs_4_.refs_0_), channel_id=1, source_target_pairs={{0,2},{1,3},{2,0},{3,1},{4,6},{5,7},{6,4},{7,5},{8,10},{9,11},{10,... | collective-permute-start | bytes 786440 | tf_op jit(solution)/shard_map/ppermute | solution.py:390
  132.5 7.6 %collective-permute-start.35 = (bf16[2,256,256]{2,1,0:T(8,128)(2,1)S(1)}, bf16[2,256,256]{2,1,0:T(8,128)(2,1)S(1)}, u32[]{:S(2)}, u32[]{:S(2)}) collective-permute-start(bf16[2,256,256]{2,1,0:T(8,128)(2,1)S(1)} %p_join.1.refs_0_.refs_4_), channel_id=1, source_target_pairs={{0,6},{1,7},{2,4},{3,5},{4,2},{5,3},{6,0},{7,1},{8,14},{9,15},{10,... | collective-permute-start | bytes 786440 | tf_op jit(solution)/shard_map/ppermute | solution.py:390
  132.6 8.3 %collective-permute-start.33 = (bf16[2,256,256]{2,1,0:T(8,128)(2,1)S(1)}, bf16[2,256,256]{2,1,0:T(8,128)(2,1)S(1)}, u32[]{:S(2)}, u32[]{:S(2)}) collective-permute-start(bf16[2,256,256]{2,1,0:T(8,128)(2,1)S(1)} %p_join.1.refs_0_.refs_4_), channel_id=1, source_target_pairs={{0,4},{1,5},{2,6},{3,7},{4,0},{5,1},{6,2},{7,3},{8,12},{9,13},{10,... | collective-permute-start | bytes 786440 | tf_op jit(solution)/shard_map/ppermute | solution.py:390
  133.7 9.1 %collective-permute-start.31 = (bf16[2,256,256]{2,1,0:T(8,128)(2,1)S(1)}, bf16[2,256,256]{2,1,0:T(8,128)(2,1)S(1)}, u32[]{:S(2)}, u32[]{:S(2)}) collective-permute-start(bf16[2,256,256]{2,1,0:T(8,128)(2,1)S(1)} %p_join.1.refs_0_.refs_4_), channel_id=1, source_target_pairs={{0,2},{1,3},{2,0},{3,1},{4,6},{5,7},{6,4},{7,5},{8,10},{9,11},{10,... | collective-permute-start | bytes 786440 | tf_op jit(solution)/shard_map/ppermute | solution.py:390
  137.1 11.6 %collective-permute-start.40 = (bf16[2,1024,256]{2,1,0:T(8,128)(2,1)S(1)}, bf16[2,1024,256]{2,1,0:T(8,128)(2,1)S(1)}, u32[]{:S(2)}, u32[]{:S(2)}) collective-permute-start(bf16[2,1024,256]{2,1,0:T(8,128)(2,1)S(1)} %s_half.1.refs_0_.refs_1_.refs_2_.refs_3_), channel_id=1, source_target_pairs={{0,1},{1,0},{2,3},{3,2},{4,5},{5,4},{6,7},{7,6},{8,9},{9,8},{10,11... | collective-permute-start | bytes 3145736 | tf_op jit(solution)/shard_map/ppermute | solution.py:390
  138.4 8.3 %collective-permute-start.30 = (bf16[2,256,256]{2,1,0:T(8,128)(2,1)S(1)}, bf16[2,256,256]{2,1,0:T(8,128)(2,1)S(1)}, u32[]{:S(2)}, u32[]{:S(2)}) collective-permute-start(bf16[2,256,256]{2,1,0:T(8,128)(2,1)S(1)} %p_join.1.refs_0_.refs_4_), channel_id=1, source_target_pairs={{0,1},{1,0},{2,3},{3,2},{4,5},{5,4},{6,7},{7,6},{8,9},{9,8},{10,11... | collective-permute-start | bytes 786440 | tf_op jit(solution)/shard_map/ppermute | solution.py:390
  140.1 6.6 %collective-permute-start.36 = (bf16[2,256,256]{2,1,0:T(8,128)(2,1)S(1)}, bf16[2,256,256]{2,1,0:T(8,128)(2,1)S(1)}, u32[]{:S(2)}, u32[]{:S(2)}) collective-permute-start(bf16[2,256,256]{2,1,0:T(8,128)(2,1)S(1)} %collective-permute-done.35.refs_3_), channel_id=1, source_target_pairs={{0,1},{1,0},{2,3},{3,2},{4,5},{5,4},{6,7},{7,6},{8,9},{9,8},{10,11... | collective-permute-start | bytes 786440 | tf_op jit(solution)/shard_map/ppermute | solution.py:390
  140.9 5.9 %collective-permute-start.34 = (bf16[2,256,256]{2,1,0:T(8,128)(2,1)S(1)}, bf16[2,256,256]{2,1,0:T(8,128)(2,1)S(1)}, u32[]{:S(2)}, u32[]{:S(2)}) collective-permute-start(bf16[2,256,256]{2,1,0:T(8,128)(2,1)S(1)} %collective-permute-done.33.refs_2_), channel_id=1, source_target_pairs={{0,1},{1,0},{2,3},{3,2},{4,5},{5,4},{6,7},{7,6},{8,9},{9,8},{10,11... | collective-permute-start | bytes 786440 | tf_op jit(solution)/shard_map/ppermute | solution.py:390
  (29 other events, 275.0 us)

commit v3 on v2

v3 whole, which is shorter than its diff:
```python
import functools

import jax
import jax.numpy as jnp
from jax import lax
from jax.experimental import pallas as pl
from jax.experimental.pallas import tpu as pltpu
from jax.sharding import PartitionSpec as P

AXES = ("dom", "sub")
F32 = jnp.float32
BF16 = jnp.bfloat16
NEG = -1e30
LN2 = 0.6931471805599453
STEP = 64
SHARDS = 16
CHUNK = 32
LANES = 128
MIB = 1024 * 1024


def params(mib=24):
    return pltpu.CompilerParams(vmem_limit_bytes=mib * MIB)


def cost(us):
    return pl.CostEstimate(flops=int(us * 1.1e9), bytes_accessed=int(us * 1e6), transcendentals=0)


def mm(a, b, contract):
    return lax.dot_general(a, b, ((contract[:1], contract[1:]), ((), ())), preferred_element_type=F32)


def pad_rows(value, rows):
    extra = rows - value.shape[0]
    if extra == 0:
        return value
    return jnp.concatenate([value, jnp.zeros((extra,) + value.shape[1:], value.dtype)], axis=0)


def three_parts(value):
    high = value.astype(BF16)
    rest = value - high.astype(F32)
    middle = rest.astype(BF16)
    low = (rest - middle.astype(F32)).astype(BF16)
    return high, middle, low


def two_parts(value):
    high = value.astype(BF16).astype(F32)
    return jnp.concatenate([high, value - high], axis=0).astype(BF16)


def whole_of(parts):
    parts = parts.astype(F32)
    return parts[:8] + parts[8:]


def repeat_lanes(value, columns):
    return jnp.concatenate([value] * (columns // value.shape[1]), axis=1)


def fold_rows(value):
    return value.reshape(value.shape[0] // 8, 8, value.shape[1])


def real_rows(mask_ref, rows, columns):
    count = jnp.sum(mask_ref[...].astype(F32), axis=1, keepdims=True)
    real = lax.broadcasted_iota(jnp.int32, (rows, columns), 0).astype(F32) < count
    return count, real


def one_hot(rows, index_ref, scratch, odd):
    halo = index_ref.shape[2]
    down, up = index_ref[0, 0:1, :], index_ref[0, 1:2, :]
    scratch[...] = jnp.full(scratch.shape, -1, jnp.int32)
    scratch[0:1, 0:halo] = jnp.where(odd, down, up)
    scratch[0:1, LANES : LANES + halo] = jnp.where(odd, up, down)
    wanted = scratch[0:1, :]
    return (lax.broadcasted_iota(jnp.int32, (rows, 2 * LANES), 0) == wanted).astype(BF16)


def own_index():
    return lax.axis_index(AXES[0]) * lax.axis_size(AXES[1]) + lax.axis_index(AXES[1])


def is_odd():
    return lax.axis_index(AXES[1]) % 2 == 1


def own_place():
    me = own_index()
    return (me // 2 % 4) * 4 + me // 8 % 4


def head_at(step):
    core = lax.axis_index(AXES[1]) % 2
    return (2 - 2 * core if step < 2 else 2 * core) + step % 2


def halo_rows_kernel(feats_ref, index_ref, near_ref, far_ref, scratch):
    picked = one_hot(feats_ref.shape[0], index_ref, scratch, is_odd())
    rows = mm(picked, feats_ref[...], (0, 0)).astype(BF16)
    near_ref[...] = rows[: near_ref.shape[0]]
    far_ref[...] = rows[LANES : LANES + far_ref.shape[0]]


def project_kernel(
    feats_ref, proj_ref, skip_w_ref, neighbours_ref, mask_ref, zq_ref, skip_ref, count_ref, flipped_ref, padded,
    *, halo,
):
    node_rows = feats_ref.shape[0]
    columns, rows = count_ref.shape

    @pl.when(pl.program_id(0) == 0)
    def _():
        feats = pad_rows(feats_ref[...].astype(F32), rows).astype(BF16)
        padded[...] = feats
        flipped_ref[...] = feats.T

    zq_ref[...] = mm(padded[...], proj_ref[...], (1, 0)).astype(BF16)
    skip_ref[...] = mm(padded[...], skip_w_ref[...], (1, 0))

    names = neighbours_ref[...]
    names = names + jnp.where(names >= node_rows, rows - node_rows, 0)
    names = names + jnp.where(names >= rows + halo, STEP - halo, 0)
    names = jnp.where(mask_ref[...] > 0, names, -1)
    names = jnp.concatenate([names, jnp.full((names.shape[0], rows - node_rows), -1, jnp.int32)], axis=1)
    own = lax.broadcasted_iota(jnp.int32, (8, rows), 1)
    share = columns // 4

    def chunk(index, carry):
        start = pl.multiple_of(pl.program_id(0) * share + index * 8, 8)
        source = lax.broadcasted_iota(jnp.int32, (8, rows), 0) + start
        total = (source == own).astype(F32)
        for slot in range(names.shape[0]):
            total += jnp.where(source == names[slot : slot + 1, :], 1.0, 0.0)
        count_ref[pl.ds(start, 8), :] = jnp.where(total > 0, jnp.log(jnp.maximum(total, 1.0)) * (1.0 / LN2), NEG)
        return carry

    lax.fori_loop(0, share // 8, chunk, 0, unroll=2)


def attend_kernel(
    zq_ref, near_ref, far_ref, proj_ref, skip_ref, count_ref, src_ref, dst_ref, bias_ref, cot_ref, mask_ref,
    ext_ref, weight_ref, source_ref, target_ref, scale_ref, pre_ref, stats_ref, flipped_ref, halo_scr, score_scr,
):
    columns, rows = count_ref.shape
    half = (columns - rows) // 2
    head = pl.program_id(0)

    @pl.when(head == 0)
    def _():
        halo_scr[...] = jnp.zeros_like(halo_scr)
        near_at = jnp.where(is_odd(), 0, half)
        halo_scr[pl.ds(pl.multiple_of(near_at, 16), near_ref.shape[0]), :] = near_ref[...]
        halo_scr[pl.ds(pl.multiple_of(half - near_at, 16), far_ref.shape[0]), :] = far_ref[...]
        flipped_ref[...] = halo_scr[...].T

    ext_ref[0:rows, :] = zq_ref[...]
    ext_ref[rows:columns, :] = mm(halo_scr[...], proj_ref[...], (1, 0)).astype(BF16)
    ext = ext_ref[...]
    width = ext.shape[1]
    parts = three_parts(src_ref[pl.ds(head, 1), :] * (1.0 / LN2))
    vectors = jnp.concatenate([jnp.broadcast_to(part, (LANES, width)) for part in parts], axis=0)
    source = mm(ext, vectors, (1, 1))
    source_ref[0] = source[:, :LANES] + source[:, LANES : 2 * LANES] + source[:, 2 * LANES :]
    parts = three_parts(dst_ref[pl.ds(head, 1), :] * (1.0 / LN2))
    vectors = jnp.concatenate([jnp.broadcast_to(part, (16, width)) for part in parts], axis=0)
    target = mm(vectors, zq_ref[...], (1, 1))
    target = target[0:8] + target[16:24] + target[32:40]
    target_ref[0] = target
    target = target[0:1]

    def score(index, highest):
        where = pl.ds(pl.multiple_of(index * CHUNK, CHUNK), CHUNK)
        value = repeat_lanes(source_ref[0, where, :], rows) + target
        small = jnp.exp2(-jnp.abs(value))
        result = jnp.maximum(value, 0.2 * value) + (0.8 / LN2) * jnp.log(1.0 + small) + count_ref[where, :]
        score_scr[where, :] = result
        return jnp.maximum(highest, jnp.max(fold_rows(result), axis=0))

    highest = lax.fori_loop(0, columns // CHUNK, score, jnp.full((8, rows), NEG, F32), unroll=2)
    highest = jnp.max(highest, axis=0, keepdims=True)

    def weigh(index, carry):
        where = pl.ds(pl.multiple_of(index * CHUNK, CHUNK), CHUNK)
        weight_ref[0, where, :] = jnp.exp2(score_scr[where, :] - highest).astype(BF16)
        return carry

    lax.fori_loop(0, columns // CHUNK, weigh, 0, unroll=2)
    weights = weight_ref[0]
    wide = jnp.concatenate([ext, jnp.ones((columns, LANES), BF16)], axis=1)
    summed = mm(weights, wide, (0, 0))
    scale = 1.0 / summed[:, width:]
    scale_ref[0] = scale
    pre = summed[:, :width] * repeat_lanes(scale, width) + skip_ref[...] + bias_ref[...]
    pre_ref[...] = pre
    act = jnp.where(pre > 0, pre, jnp.exp(jnp.minimum(pre, 0.0)) - 1.0)
    nodes, real = real_rows(mask_ref, rows, width)
    cot = jnp.where(real, pad_rows(cot_ref[...].astype(F32), rows), 0.0)
    mean = jnp.sum(jnp.where(real, act, 0.0), axis=0, keepdims=True) / nodes
    centred = jnp.where(real, act - mean, 0.0)
    stats_ref[...] = jnp.zeros_like(stats_ref)
    stats_ref[0:1, :] = jnp.broadcast_to(nodes, mean.shape)
    stats_ref[1:2, :] = mean
    stats_ref[2:3, :] = jnp.sum(centred * centred, axis=0, keepdims=True)
    stats_ref[3:4, :] = jnp.sum(cot, axis=0, keepdims=True)
    stats_ref[4:5, :] = jnp.sum(cot * centred, axis=0, keepdims=True)


def merged(first, second):
    nodes = first[0:1] + second[0:1]
    gap = second[1:2] - first[1:2]
    part = second[0:1] / nodes
    mean = first[1:2] + gap * part
    spread = first[2:3] + second[2:3] + gap * gap * first[0:1] * part
    shift = first[3:4] + second[3:4]
    gain = first[4:5] + second[4:5] - (mean - first[1:2]) * first[3:4] - (mean - second[1:2]) * second[3:4]
    return nodes, mean, spread, shift, gain


def in_order(mine, other, bit):
    mine_first = bit == 0
    return jnp.where(mine_first, mine, other), jnp.where(mine_first, other, mine)


def merge_kernel(mine_ref, other_ref, out_ref, *, which):
    bit = own_index() // 2**which % 2
    lines = merged(*in_order(mine_ref[...], other_ref[...], bit))
    out_ref[...] = jnp.zeros_like(out_ref)
    for line, value in enumerate(lines):
        out_ref[line : line + 1, :] = value


def place_blocks(out_ref, value, me):
    size = value.shape[0] // SHARDS
    for block in range(SHARDS):
        at = pl.multiple_of((block ^ me) * size, size)
        out_ref[pl.ds(at, size), :] = value[block * size : (block + 1) * size, :]


def core_shares_kernel(keep_ref, other_ref, *outs):
    size = keep_ref.shape[1] // 4 - 4
    for head in range(2):
        vectors = two_parts(whole_of(keep_ref[head, 4 * size :, :]) + whole_of(other_ref[head, 4 * size :, :]))
        for index, out_ref in enumerate(outs):
            rows = slice(index * size, (index + 1) * size)
            out_ref[head, :size, :] = (keep_ref[head, rows, :].astype(F32) + other_ref[head, rows, :].astype(F32)).astype(BF16)
            out_ref[head, size:, :] = vectors


def sum_of_four(refs, head, rows):
    first, second, third, fourth = (ref[head, rows, :].astype(F32) for ref in refs)
    return (first + second + third + fourth).astype(BF16)


def ordered_sum(refs, start, me, scratch):
    for index, ref in enumerate(refs):
        for head in range(2):
            scratch[index ^ me, head] = whole_of(ref[head, start:, :])
    return [scratch[0, head] + scratch[1, head] + scratch[2, head] + scratch[3, head] for head in range(2)]


def plane_sum_kernel(*refs, deps):
    ins, outs, scratch = refs[:4], refs[4 + deps : -1], refs[-1]
    size = outs[0].shape[1] - 16
    vectors = ordered_sum(ins, 4 * size, own_place() // 4, scratch)
    for head in range(2):
        for index, out_ref in enumerate(outs):
            out_ref[head, :size, :] = sum_of_four(ins, head, slice(index * size, (index + 1) * size))
            out_ref[head, size:, :] = two_parts(vectors[head])


def line_sum_kernel(*refs, deps):
    ins, (out_ref, small_ref, scratch) = refs[:4], refs[4 + deps :]
    size = out_ref.shape[1]
    vectors = ordered_sum(ins, size, own_place() % 4, scratch)
    for head in range(2):
        out_ref[head] = sum_of_four(ins, head, slice(0, size))
        small_ref[head] = vectors[head]


def vectors_kernel(mine_ref, other_ref, src_ref, dst_ref, bias_ref):
    odd = is_odd()
    width = src_ref.shape[1]
    for head in range(4):
        mine, other = mine_ref[head % 2], other_ref[head % 2]
        value = jnp.where(odd == (head >= 2), mine, other)
        src_ref[head : head + 1, :] = value[0:1]
        dst_ref[head : head + 1, :] = value[1:2]
        bias_ref[:, head * width : (head + 1) * width] = value[2:3]


def share_sum_kernel(*refs, deps):
    ins, outs = refs[:4], refs[4 + deps :]
    size = outs[0].shape[1]
    for head in range(2):
        for index, out_ref in enumerate(outs):
            out_ref[head] = sum_of_four(ins, head, slice(index * size, (index + 1) * size))


def join_kernel(*refs):
    out_ref = refs[-1]
    size = refs[0].shape[1]
    for piece in range(4):
        out_ref[:, piece * size : (piece + 1) * size, :] = refs[piece][...]


def two_sum_kernel(mine_ref, other_ref, *outs, deps=0):
    outs = outs[deps:]
    size = outs[0].shape[1]
    for piece, out_ref in enumerate(outs):
        rows = slice(piece * size, (piece + 1) * size)
        out_ref[...] = (mine_ref[:, rows, :].astype(F32) + other_ref[:, rows, :].astype(F32)).astype(BF16)


def norm_kernel(
    pre_ref, stats_ref, other_ref, cot_ref, mask_ref, gain_ref, shift_ref, flipped_ref,
    out_ref, dskip_ref, send_ref, keep_ref, small_ref, gain_grad_ref, shift_grad_ref, out_scr, done, *, last_bit,
):
    rows = pre_ref.shape[0]
    node_rows, width = out_scr.shape[1:]
    real = real_rows(mask_ref, rows, width)[1]
    copies = []
    for step in range(4):
        head = head_at(step)
        lanes = pl.ds(pl.multiple_of(head * width, width), width)
        pre = pre_ref[:, lanes]
        steep = jnp.exp(jnp.minimum(pre, 0.0))
        act = jnp.where(pre > 0, pre, steep - 1.0)
        first, second = in_order(stats_ref[:, lanes], other_ref[:, lanes], own_index() // 2**last_bit % 2)
        nodes, mean, spread, total, cross = merged(first, second)
        inverse = lax.rsqrt(spread / nodes + 1e-05)
        normed = (act - mean) * inverse
        gain = gain_ref[:, lanes]
        out_scr[step] = jnp.where(real, gain * normed + shift_ref[:, lanes], 0.0)[:node_rows].astype(BF16)
        copies.append(pltpu.make_async_copy(out_scr.at[step], out_ref.at[:, lanes], done.at[step]))
        copies[-1].start()
        gain_grad_ref[:, lanes] = cross * inverse
        shift_grad_ref[:, lanes] = total
        grad = pad_rows(cot_ref[:, lanes].astype(F32), rows) - total / nodes - normed * (cross * inverse / nodes)
        grad_pre = jnp.where(real, grad * (inverse * gain) * steep, 0.0)
        small_ref[head] = jnp.broadcast_to(jnp.sum(grad_pre, axis=0, keepdims=True), small_ref.shape[1:])
        dskip = grad_pre.astype(BF16)
        dskip_ref[:, lanes] = dskip
        grads = mm(flipped_ref[...], dskip, (1, 0)).astype(BF16)
        place_blocks((send_ref if step < 2 else keep_ref).at[step % 2], grads, own_place())
    for copy in copies:
        copy.wait()


def back_kernel(
    weight_ref, source_ref, target_ref, scale_ref, ext_ref, dskip_ref, src_ref, dst_ref, flipped_ref, halo_ref,
    small_in, *rest, part,
):
    grad_ref, own_ref, near_ref, far_ref, dal_scr, sum_scr = rest[-6:]
    columns, rows = weight_ref.shape[1:]
    half = (columns - rows) // 2
    width = src_ref.shape[1]
    depth = flipped_ref.shape[0]
    count = near_ref.shape[0]
    if part:
        near_ref[:, : 2 * width] = rest[0][...]
        far_ref[:, : 2 * width] = rest[1][...]
    for step in range(2):
        head = head_at(part + step)
        lanes = pl.ds(pl.multiple_of(head * width, width), width)
        target = target_ref[head, 0:1, :]
        dskip = dskip_ref[:, lanes]
        dal_scr[...] = mm(ext_ref[:, lanes], dskip, (1, 1))

        def average(index, carry):
            total, mean = carry
            where = pl.ds(pl.multiple_of(index * CHUNK, CHUNK), CHUNK)
            weight = weight_ref[head, where, :].astype(F32)
            return total + jnp.sum(fold_rows(weight), axis=0), mean + jnp.sum(fold_rows(weight * dal_scr[where, :]), axis=0)

        nothing = jnp.zeros((8, rows), F32)
        total, mean = lax.fori_loop(0, columns // CHUNK, average, (nothing, nothing), unroll=2)
        scale = 1.0 / jnp.sum(total, axis=0, keepdims=True)
        mean = jnp.sum(mean, axis=0, keepdims=True) * scale

        def slopes(index, by_target):
            where = pl.ds(pl.multiple_of(index * CHUNK, CHUNK), CHUNK)
            value = repeat_lanes(source_ref[head, where, :], rows) + target
            slope = (0.6 + 0.4 * jnp.tanh(value * (0.5 * LN2))) * scale
            du = weight_ref[head, where, :].astype(F32) * slope * (dal_scr[where, :] - mean)
            sum_scr[where, :] = sum(du[:, at : at + LANES] for at in range(0, rows, LANES))
            return by_target + jnp.sum(fold_rows(du), axis=0)

        by_target = lax.fori_loop(0, columns // CHUNK, slopes, nothing, unroll=2)
        by_target = jnp.sum(by_target, axis=0, keepdims=True)
        by_source = jnp.sum(sum_scr[...], axis=1, keepdims=True)
        ext = ext_ref[:, lanes]
        scaled = (dskip.astype(F32) * repeat_lanes(scale_ref[head], width)).astype(BF16)
        dz = mm(weight_ref[head], scaled, (1, 0)) + by_source * src_ref[pl.ds(head, 1), :]
        high, middle, low = three_parts(by_target)
        row = lax.broadcasted_iota(jnp.int32, (16, rows), 0)
        lines = jnp.where(row == 1, middle.astype(F32), jnp.where(row == 3, low.astype(F32), high.astype(F32)))
        lines = jnp.where(row < 4, lines, 0.0).astype(BF16)
        dst_high, dst_middle, _ = three_parts(dst_ref[pl.ds(head, 1), :])
        row = lax.broadcasted_iota(jnp.int32, (16, width), 0)
        vectors = jnp.where(row == 2, dst_middle.astype(F32), dst_high.astype(F32)).astype(BF16)
        dz_own = dz[:rows] + mm(lines, vectors, (0, 0))
        mine = slice(step * width, (step + 1) * width)
        dz_own = dz_own.astype(BF16)
        own_ref[:, mine] = dz_own
        dz_halo = dz[rows:].astype(BF16)
        below, above = dz[rows : rows + count], dz[rows + half : rows + half + count]
        odd = is_odd()
        at = part * width + step * width
        near_ref[:, at : at + width] = jnp.where(odd, below, above).astype(BF16)
        far_ref[:, at : at + width] = jnp.where(odd, above, below).astype(BF16)
        sums = mm(lines, ext[:rows], (1, 0))
        source_sum = jnp.sum(by_source * ext.astype(F32), axis=0, keepdims=True)
        row = lax.broadcasted_iota(jnp.int32, (8, width), 0)
        lines = jnp.where(row == 0, source_sum, jnp.where(row == 1, sums[0:1] + sums[1:2] + sums[3:4], small_in[head]))
        grad_ref[step, depth:, :] = two_parts(jnp.where(row < 3, lines, 0.0))
        grads = mm(flipped_ref[...], dz_own, (1, 0)) + mm(halo_ref[...], dz_halo, (1, 0))
        place_blocks(grad_ref.at[step], grads.astype(BF16), own_place())


def feats_kernel(own_one, own_two, dskip_ref, proj_ref, skip_ref, total_ref):
    width = own_one.shape[1] // 2
    total = mm(dskip_ref[...], skip_ref[...], (1, 1))
    for step in range(4):
        lanes = pl.ds(pl.multiple_of(head_at(step) * width, width), width)
        own = (own_one if step < 2 else own_two)[:, step % 2 * width : (step % 2 + 1) * width]
        total += mm(own, proj_ref[:, lanes], (1, 1))
    total_ref[...] = total


def feats_halo_kernel(total_ref, near_ref, far_ref, index_ref, proj_ref, out_ref, scratch):
    rows = total_ref.shape[0]
    count = near_ref.shape[0]
    width = near_ref.shape[1] // 4
    picks = one_hot(rows, index_ref, scratch, is_odd())
    picks = jnp.concatenate([picks[:, :count], picks[:, LANES : LANES + count]], axis=1)
    sent = jnp.concatenate([near_ref[...], far_ref[...]], axis=0)
    product = jnp.zeros((2 * count, proj_ref.shape[0]), F32)
    for step in range(4):
        lanes = pl.ds(pl.multiple_of(head_at(step) * width, width), width)
        other = (step + 2) % 4 * width
        product += mm(sent[:, other : other + width], proj_ref[:, lanes], (1, 1))
    high, middle, _ = three_parts(product)
    total = total_ref[...] + mm(picks, high, (1, 0)) + mm(picks, middle, (1, 0))
    out_ref[...] = total[: out_ref.shape[0]].astype(BF16)


def assemble_kernel(*refs, first, pieces):
    out_ref, scratch, done = refs[-3:]
    size, width = scratch.shape[2:]
    me = own_place()
    each = SHARDS // pieces
    copies = []
    for step in range(2):
        lanes = pl.ds(pl.multiple_of(head_at(first + step) * width, width), width)
        for block in range(SHARDS):
            at = pl.multiple_of((block ^ me) * size, size)
            rows = slice(block % each * size, (block % each + 1) * size)
            scratch[step, block] = refs[block // each][step, rows, :].astype(F32)
            copies.append(pltpu.make_async_copy(scratch.at[step, block], out_ref.at[pl.ds(at, size), lanes], done.at[step, block]))
            copies[-1].start()
    for copy in copies:
        copy.wait()


def per_device(
    feats, w_proj, w_skip, attn_src, attn_dst, bias, gain, shift, cotangent, neighbours, edge_mask, node_mask, send_index,
):
    node_rows, depth = feats.shape
    heads, width = attn_src.shape
    concat = heads * width
    slots = neighbours.shape[1]
    halo = send_index.shape[2]
    devices = lax.axis_size(AXES)
    bits = devices.bit_length() - 1
    rows = -(-node_rows // LANES) * LANES
    columns = rows + 2 * STEP
    halo_pad = -(-halo // 16) * 16

    def far_swapped(value):
        pairs = [(low, low + 1) for low in range(1, devices - 1, 2)]
        return lax.ppermute(value, AXES, pairs + [(high, low) for low, high in pairs])

    def swapped(value, distance):
        return lax.ppermute(value, AXES, [(source, source ^ distance) for source in range(devices)])

    mask = node_mask.reshape(1, node_rows)
    bias2, gain2, shift2 = bias[None], gain[None], shift[None]

    in_hbm = lambda value: pltpu.with_memory_space_constraint(value, pltpu.HBM)
    near, far = pl.pallas_call(
        halo_rows_kernel,
        out_shape=[jax.ShapeDtypeStruct((halo_pad, depth), BF16)] * 2,
        scratch_shapes=[pltpu.VMEM((8, 2 * LANES), jnp.int32)],
        compiler_params=params(8),
        name="halo_rows",
    )(in_hbm(feats), in_hbm(send_index))
    near, far = swapped(near, 1), far_swapped(far)

    def spec(shape, index):
        return pl.BlockSpec(shape, index)

    def whole(*shape):
        return pl.BlockSpec(shape, lambda *_: (0,) * len(shape))

    by_head = lambda n: pl.BlockSpec((n, width), lambda h, *_: (0, h))
    stacked = lambda *shape: pl.BlockSpec((1, *shape), lambda h, *_: (h, 0, 0))
    shape_of = jax.ShapeDtypeStruct
    zq, skip, count, flipped = pl.pallas_call(
        functools.partial(project_kernel, halo=halo),
        grid=(heads,),
        in_specs=[
            whole(node_rows, depth), by_head(depth), by_head(depth), whole(slots, node_rows), whole(slots, node_rows),
        ],
        out_specs=[by_head(rows), by_head(rows), whole(columns, rows), whole(depth, rows)],
        scratch_shapes=[pltpu.VMEM((rows, depth), BF16)],
        out_shape=[
            shape_of((rows, concat), BF16),
            shape_of((rows, concat), F32),
            shape_of((columns, rows), F32),
            shape_of((depth, rows), BF16),
        ],
        compiler_params=params(),
        cost_estimate=cost(5),
        name="project",
    )(in_hbm(feats), in_hbm(w_proj), in_hbm(w_skip), in_hbm(neighbours.T), in_hbm(edge_mask.T))

    ext, weight, source, target, scale, pre, stats, halo_flipped = pl.pallas_call(
        attend_kernel,
        grid=(heads,),
        in_specs=[
            by_head(rows), whole(halo_pad, depth), whole(halo_pad, depth), by_head(depth), by_head(rows),
            whole(columns, rows), whole(heads, width), whole(heads, width), by_head(1), by_head(node_rows),
            whole(1, node_rows),
        ],
        out_specs=[
            by_head(columns), stacked(columns, rows), stacked(columns, LANES), stacked(8, rows), stacked(rows, LANES),
            by_head(rows), by_head(8), whole(depth, columns - rows),
        ],
        out_shape=[
            shape_of((columns, concat), BF16),
            shape_of((heads, columns, rows), BF16),
            shape_of((heads, columns, LANES), F32),
            shape_of((heads, 8, rows), F32),
            shape_of((heads, rows, LANES), F32),
            shape_of((rows, concat), F32),
            shape_of((8, concat), F32),
            shape_of((depth, columns - rows), BF16),
        ],
        scratch_shapes=[pltpu.VMEM((columns - rows, depth), BF16), pltpu.VMEM((columns, rows), F32)],
        compiler_params=params(),
        cost_estimate=cost(8),
        name="attend",
    )(zq, near, far, in_hbm(w_proj), skip, count, attn_src, attn_dst, bias2, in_hbm(cotangent), mask)

    for which in range(bits - 1):
        stats = pl.pallas_call(
            functools.partial(merge_kernel, which=which),
            in_specs=[pl.BlockSpec(memory_space=pltpu.VMEM)] * 2,
            out_shape=shape_of(stats.shape, F32),
            compiler_params=params(1),
            name="merge",
        )(stats, swapped(stats, 1 << which))
    other = swapped(stats, 1 << (bits - 1))

    vmem = pl.BlockSpec(memory_space=pltpu.VMEM)
    anywhere = pl.BlockSpec(memory_space=pl.ANY)
    half_grad = shape_of((2, depth, width), BF16)
    output, dskip, skip_send, skip_keep, small, gain_grad, shift_grad = pl.pallas_call(
        functools.partial(norm_kernel, last_bit=bits - 1),
        in_specs=[vmem] * 8,
        out_specs=[anywhere] + [vmem] * 6,
        out_shape=[
            pltpu.HBM((node_rows, concat), BF16),
            shape_of((rows, concat), BF16),
            half_grad,
            half_grad,
            shape_of((heads, 8, width), F32),
            jax.ShapeDtypeStruct((1, concat), F32),
            jax.ShapeDtypeStruct((1, concat), F32),
        ],
        scratch_shapes=[pltpu.VMEM((heads, node_rows, width), BF16), pltpu.SemaphoreType.DMA((heads,))],
        compiler_params=params(16),
        cost_estimate=cost(0.1),
        name="norm",
    )(pre, stats, other, cotangent, mask, gain2, shift2, flipped)

    def backward(part, arrays=(), deps=()):
        return pl.pallas_call(
            functools.partial(back_kernel, part=part),
            in_specs=[vmem] * (11 + len(arrays)) + [anywhere] * len(deps),
            out_shape=[
                shape_of((2, depth + 16, width), BF16),
                shape_of((rows, 2 * width), BF16),
                shape_of((halo_pad, (2 + part) * width), BF16),
                shape_of((halo_pad, (2 + part) * width), BF16),
            ],
            scratch_shapes=[pltpu.VMEM((columns, rows), F32), pltpu.VMEM((columns, LANES), F32)],
            compiler_params=params(8),
            cost_estimate=cost(0.1),
            name="back",
        )(weight, source, target, scale, ext, dskip, attn_src, attn_dst, flipped, halo_flipped, small, *arrays, *deps)

    quarter = (2, depth // 4, width)
    piece = (2, depth // SHARDS, width)
    def step_call(kernel, name, shapes, arrays, deps=()):
        return pl.pallas_call(
            kernel,
            in_specs=[vmem] * len(arrays) + [anywhere] * len(deps),
            out_shape=[shape_of(shape, BF16) for shape in shapes],
            compiler_params=params(1),
            cost_estimate=cost(0.1),
            name=name,
        )(*arrays, *deps)

    def over_plane(shares):
        return [swapped(share, distance << 1) for distance, share in zip((1, 2, 3), shares)]

    def over_line(shares):
        return [swapped(share, distance << 3) for distance, share in zip((1, 2, 3), shares)]

    def ordered_call(kernel, name, shapes, arrays, deps):
        return pl.pallas_call(
            functools.partial(kernel, deps=len(deps)),
            in_specs=[vmem] * len(arrays) + [anywhere] * len(deps),
            out_shape=shapes,
            scratch_shapes=[pltpu.VMEM((4, 2, 8, width), F32)],
            compiler_params=params(1),
            cost_estimate=cost(0.1),
            name=name,
        )(*arrays, *deps)

    def plane_sum(arrays, deps):
        shapes = [shape_of((2, depth // SHARDS + 16, width), BF16)] * 4
        return ordered_call(plane_sum_kernel, "p_plane", shapes, arrays, deps)

    def line_sum(arrays, deps):
        shapes = [shape_of(piece, BF16), shape_of((2, 8, width), F32)]
        return ordered_call(line_sum_kernel, "p_line", shapes, arrays, deps)

    def share_sum(name, arrays, count, deps):
        shapes = [(2, arrays[0].shape[1] // count, width)] * count
        return step_call(functools.partial(share_sum_kernel, deps=len(deps)), name, shapes, arrays, deps)

    def join(name, arrays, deps):
        return step_call(join_kernel, name, [(2, 4 * arrays[0].shape[1], width)], arrays, deps)[0]

    def assemble(pieces, first, *out):
        return pl.pallas_call(
            functools.partial(assemble_kernel, first=first, pieces=len(pieces)),
            in_specs=[vmem] * len(pieces) + [anywhere] * len(out),
            out_specs=anywhere,
            out_shape=pltpu.HBM((depth, concat), F32),
            scratch_shapes=[pltpu.VMEM((2, SHARDS, depth // SHARDS, width), F32), pltpu.SemaphoreType.DMA((2, SHARDS))],
            input_output_aliases={len(pieces): 0} if out else {},
            compiler_params=params(8),
            cost_estimate=cost(0.1),
            name="assemble",
        )(*pieces, *out)

    def beyond(value):
        for which in range(5, bits):
            value = value + swapped(value, 1 << which)
        return value

    def after(value, *others):
        return lax.optimization_barrier((value, *others))[0]

    skip_other = swapped(skip_send, 1)
    proj_send, own_send, near_send, far_send = backward(0)
    proj_other = swapped(proj_send, 1)
    s_mine, *s_rest = step_call(
        functools.partial(two_sum_kernel, deps=1), "s_core", [quarter] * 4, [skip_keep, skip_other], [proj_send]
    )
    s_got = over_plane(s_rest)
    proj_keep, own_keep, back_near, back_far = backward(2, [near_send, far_send], [s_mine])
    p_mine, *p_rest = step_call(core_shares_kernel, "p_core", [(2, depth // 4 + 16, width)] * 4, [proj_keep, proj_other])
    p_got = over_plane(p_rest)
    s_mine, *s_rest = share_sum("s_plane", [s_mine, *s_got], 4, [p_mine])
    s_got = over_line(s_rest)
    s_piece = beyond(share_sum("s_line", [s_mine, *s_got], 1, [])[0])
    s_got = over_line([s_piece] * 3)
    p_mine, *p_rest = plane_sum([p_mine, *p_got], [])
    p_got = over_line(p_rest)
    s_share = join("s_join", [s_piece, *s_got], [p_mine])
    s_got = [s_share, *over_plane([s_share] * 3)]
    p_piece, small = line_sum([p_mine, *p_got], [s_share])
    p_piece, small = beyond(p_piece), beyond(small)
    p_got = over_line([p_piece] * 3)
    small_other = swapped(small, 1)
    p_share = join("p_join", [p_piece, *p_got], [])
    p_got = over_plane([p_share] * 3)
    s_half = join("s_half", s_got, [p_share])
    grad_skip = assemble([swapped(s_half, 1)], 0, assemble([s_half], 2))
    back_near, back_far = swapped(after(back_near, p_share), 1), far_swapped(after(back_far, p_share))
    feats_total = pl.pallas_call(
        feats_kernel,
        in_specs=[vmem] * 5,
        out_specs=vmem,
        out_shape=shape_of((rows, depth), F32),
        compiler_params=params(8),
        cost_estimate=cost(0.1),
        name="features",
    )(own_send, own_keep, dskip, w_proj, w_skip)
    grad_src, grad_dst, grad_bias = pl.pallas_call(
        vectors_kernel,
        out_shape=[
            jax.ShapeDtypeStruct((heads, width), F32),
            jax.ShapeDtypeStruct((heads, width), F32),
            jax.ShapeDtypeStruct((1, concat), F32),
        ],
        compiler_params=params(1),
        cost_estimate=cost(0.1),
        name="vectors",
    )(small, small_other)
    p_got = [p_share, *(after(share, grad_skip, grad_src, back_near, back_far, feats_total) for share in p_got)]
    p_other = [swapped(share, 1) for share in p_got]
    grad_proj = assemble(p_other, 0, assemble(p_got, 2))

    grad_feats = pl.pallas_call(
        feats_halo_kernel,
        in_specs=[vmem] * 5,
        out_specs=vmem,
        scratch_shapes=[pltpu.VMEM((8, 2 * LANES), jnp.int32)],
        out_shape=jax.ShapeDtypeStruct((node_rows, depth), BF16),
        compiler_params=params(8),
        cost_estimate=cost(0.1),
        name="features_halo",
    )(feats_total, back_near, back_far, send_index, w_proj)

    return (
        output,
        grad_feats,
        grad_proj,
        grad_skip,
        grad_src,
        grad_dst,
        grad_bias.reshape(concat),
        gain_grad.reshape(concat),
        shift_grad.reshape(concat),
    )


def solution(mesh):
    rows = P(AXES, None)
    in_specs = (rows,) + (P(),) * 7 + (rows, rows, rows, P(AXES), P(AXES, None, None))
    out_specs = (rows, rows) + (P(),) * 7
    return jax.shard_map(per_device, mesh=mesh, in_specs=in_specs, out_specs=out_specs, check_vma=False)
```

time: 151 us -> 132 us (0.87)
  Pallas kernels: 48.9 us -> 40.5 us
  starting transfers between devices: 61.8 us -> 53.6 us
  local copies, waits for them, and re-layouts: 6.35 us -> 0.06 us
  waiting for transfers between devices: 32.7 us -> 36.7 us
    pallas_call x9 -> x13, Pallas kernels: 35.5 us -> 29.3 us  [the longest x2 8.09 us: backward(): pl.pallas_call(functools.partial(back_kernel, part=part), in_specs=[vmem]...]
    ppermute x4 -> x2, starting transfers between devices: 6.42 us -> 1.31 us  [far_swapped(): lax.ppermute(value, AXES, pairs + [(high, low) for low, high in pairs])]
    unnamed x31 -> x20, local copies, waits for them, and re-layouts: 5.05 us -> 0.06 us
    ppermute x42 -> x39, waiting for transfers between devices: 32.7 us -> 36.7 us  [swapped(): lax.ppermute(value, AXES, [(source, source ^ distance) for source in rang...]
    ppermute x42 -> x39, starting transfers between devices: 55.3 us -> 52.3 us  [swapped(): lax.ppermute(value, AXES, [(source, source ^ distance) for source in rang...]
    pallas_call x4, Pallas kernels: 2.34 us -> 0.18 us  [per_device(): pl.pallas_call(functools.partial(merge_kernel, which=which), in_specs=[pl...]
  transfers between devices with their start and end apart: 46 -> 41, of which waited for: 17 -> 16; matrix products, arithmetic and copies ran while one was open for 1% -> 0% of each run, Pallas kernels for 20% -> 19%
where the time goes in v3:
time: 132 us
  starting transfers between devices  53.6 us (41%)
  Pallas kernels  40.5 us (31%)
  waiting for transfers between devices  36.7 us (28%)
    ppermute x39, starting transfers between devices, swapped(): lax.ppermute(value, AXES, [(source, source ^ distance) for source in rang...  52.3 us
    ppermute x39, waiting for transfers between devices, swapped(): lax.ppermute(value, AXES, [(source, source ^ distance) for source in rang...  36.7 us
    pallas_call x1, Pallas kernels, per_device(): pl.pallas_call(attend_kernel, grid=(heads,), in_specs=[by_head(rows), who...  8.62 us
    pallas_call x2, Pallas kernels, backward(): pl.pallas_call(functools.partial(back_kernel, part=part), in_specs=[vmem]...  8.09 us
    pallas_call x1, Pallas kernels, per_device(): pl.pallas_call(functools.partial(project_kernel, halo=halo), grid=(heads,...  6.57 us
    pallas_call x4, Pallas kernels, assemble(): pl.pallas_call(functools.partial(assemble_kernel, first=first, pieces=len...  6.43 us
    pallas_call x1, Pallas kernels, per_device(): pl.pallas_call(functools.partial(norm_kernel, last_bit=bits - 1), in_spec...  3.45 us
  transfers between devices with their start and end apart: 41, of which 16 were waited for; matrix products, arithmetic and copies ran while one was open for 0% of the time, Pallas kernels for 19%

profile of v3, /device:TPU:0, one launch (start us, length us, event | category | flops | bytes accessed | tf_op | source)
XLA Modules:
  0.0 132.0 jit_solution(6997604496652546563)
XLA Ops:
  3.5 6.6 %project.1 = (bf16[384,1024]{1,0:T(8,128)(2,1)S(1)}, f32[384,1024]{1,0:T(8,128)S(1)}, f32[512,384]{1,0:T(8,128)S(1)}, bf16[1024,384]{1,0:T(8,128)(2,1)S(1)}) custom-call(bf16[376,1024]{1,0:T(8,128)(2,1)} %feats_ref.3, bf16[1024,1024]{1,0:T(8,128)(2,1)} %proj_ref.7, bf16[1024,1024]{1,0:T(8,128)(2,1)} %skip_ref.1, s32[16,376]{1,0:T(8,128)} %bitcast.11, ...), custom_call_target="tpu_custom_call" | custom-call | flops 5500000256 | bytes 5000000 | tf_op jit(solution)/shard_map/project/pallas_call | solution.py:512
  10.2 8.6 %attend.1 = (bf16[512,1024]{1,0:T(8,128)(2,1)S(1)}, bf16[4,512,384]{2,1,0:T(8,128)(2,1)S(1)}, f32[4,512,128]{2,1,0:T(8,128)S(1)}, f32[4,8,384]{2,1,0:T(8,128)S(1...) custom-call(bf16[384,1024]{1,0:T(8,128)(2,1)S(1)} %get-tuple-element, ...), custom_call_target="tpu_custom_call" | custom-call | flops 8800000000 | bytes 8000000 | tf_op jit(solution)/shard_map/attend/pallas_call | solution.py:531
  18.8 4.0 %collective-permute-start.2 = (f32[8,1024]{1,0:T(8,128)S(1)}, f32[8,1024]{1,0:T(8,128)S(1)}, u32[]{:S(2)}, u32[]{:S(2)}) collective-permute-start(f32[8,1024]{1,0:T(8,128)S(1)} %get-tuple-element.70.mine_ref), channel_id=1, source_target_pairs={{0,1},{1,0},{2,3},{3,2},{4,5},{5,4},{6,7},{7,6},{8,9},{9,8},{10,11... | collective-permute-start | bytes 98312 | tf_op jit(solution)/shard_map/ppermute | solution.py:488
  25.2 2.5 %collective-permute-done.3.other_ref = f32[8,1024]{1,0:T(8,128)S(1)} collective-permute-done((f32[8,1024]{1,0:T(8,128)S(1)}, f32[8,1024]{1,0:T(8,128)S(1)}, u32[]{:S(2)}, u32[]{:S(2)}) %collective-permute-start.3) | collective-permute-done | bytes 32800 | tf_op jit(solution)/shard_map/ppermute | solution.py:488
  27.7 1.9 %collective-permute-start.4 = (f32[8,1024]{1,0:T(8,128)S(1)}, f32[8,1024]{1,0:T(8,128)S(1)}, u32[]{:S(2)}, u32[]{:S(2)}) collective-permute-start(f32[8,1024]{1,0:T(8,128)S(1)} %merge.5.mine_ref), channel_id=1, source_target_pairs={{0,4},{1,5},{2,6},{3,7},{4,0},{5,1},{6,2},{7,3},{8,12},{9,13},{10,... | collective-permute-start | bytes 98312 | tf_op jit(solution)/shard_map/ppermute | solution.py:488
  29.5 2.1 %collective-permute-done.4.other_ref = f32[8,1024]{1,0:T(8,128)S(1)} collective-permute-done((f32[8,1024]{1,0:T(8,128)S(1)}, f32[8,1024]{1,0:T(8,128)S(1)}, u32[]{:S(2)}, u32[]{:S(2)}) %collective-permute-start.4) | collective-permute-done | bytes 32800 | tf_op jit(solution)/shard_map/ppermute | solution.py:488
  31.7 2.8 %collective-permute-start.5 = (f32[8,1024]{1,0:T(8,128)S(1)}, f32[8,1024]{1,0:T(8,128)S(1)}, u32[]{:S(2)}, u32[]{:S(2)}) collective-permute-start(f32[8,1024]{1,0:T(8,128)S(1)} %merge.6.mine_ref), channel_id=1, source_target_pairs={{0,8},{1,9},{2,10},{3,11},{4,12},{5,13},{6,14},{7,15},{8,0},{9,1},... | collective-permute-start | bytes 98312 | tf_op jit(solution)/shard_map/ppermute | solution.py:488
  34.5 1.9 %collective-permute-done.5.other_ref = f32[8,1024]{1,0:T(8,128)S(1)} collective-permute-done((f32[8,1024]{1,0:T(8,128)S(1)}, f32[8,1024]{1,0:T(8,128)S(1)}, u32[]{:S(2)}, u32[]{:S(2)}) %collective-permute-start.5) | collective-permute-done | bytes 32800 | tf_op jit(solution)/shard_map/ppermute | solution.py:488
  36.4 3.1 %collective-permute-start.6 = (f32[8,1024]{1,0:T(8,128)S(1)}, f32[8,1024]{1,0:T(8,128)S(1)}, u32[]{:S(2)}, u32[]{:S(2)}) collective-permute-start(f32[8,1024]{1,0:T(8,128)S(1)} %merge.7.stats_ref), channel_id=1, source_target_pairs={{0,16},{1,17},{2,18},{3,19},{4,20},{5,21},{6,22},{7,23},{8,24},{9,... | collective-permute-start | bytes 98312 | tf_op jit(solution)/shard_map/ppermute | solution.py:488
  39.5 1.9 %collective-permute-done.6.other_ref = f32[8,1024]{1,0:T(8,128)S(1)} collective-permute-done((f32[8,1024]{1,0:T(8,128)S(1)}, f32[8,1024]{1,0:T(8,128)S(1)}, u32[]{:S(2)}, u32[]{:S(2)}) %collective-permute-start.6) | collective-permute-done | bytes 32800 | tf_op jit(solution)/shard_map/ppermute | solution.py:488
  41.4 3.4 %norm.1 = (bf16[376,1024]{1,0:T(8,128)(2,1)}, bf16[384,1024]{1,0:T(8,128)(2,1)S(1)}, bf16[2,1024,256]{2,1,0:T(8,128)(2,1)S(1)}, bf16[2,1024,256]{2,1,0:T(8,128)(...) custom-call(f32[384,1024]{1,0:T(8,128)S(1)} %get-tuple-element.69.pre_ref, ...), custom_call_target="tpu_custom_call" | custom-call | flops 110000000 | bytes 100000 | tf_op jit(solution)/shard_map/norm/pallas_call | solution.py:572
  45.0 3.9 %back.2 = (bf16[2,1040,256]{2,1,0:T(8,128)(2,1)S(1)}, bf16[384,512]{1,0:T(8,128)(2,1)S(1)}, bf16[48,512]{1,0:T(8,128)(2,1)S(1)}, bf16[48,512]{1,0:T(8,128)(2,1)S(1)}) custom-call(bf16[4,512,384]{2,1,0:T(8,128)(2,1)S(1)} %get-tuple-element.73.weight_ref, f32[4,512,128]{2,1,0:T(8,128)S(1)} %get-tuple-element.74.source_ref, ...), custom_call_target="tpu_custom_call" | custom-call | flops 110000000 | bytes 100000 | tf_op jit(solution)/shard_map/back/pallas_call | solution.py:592
  53.3 4.2 %back.3 = (bf16[2,1040,256]{2,1,0:T(8,128)(2,1)S(1)}, bf16[384,512]{1,0:T(8,128)(2,1)S(1)}, bf16[48,1024]{1,0:T(8,128)(2,1)S(1)}, bf16[48,1024]{1,0:T(8,128)(2,1)S(1)}) custom-call(bf16[4,512,384]{2,1,0:T(8,128)(2,1)S(1)} %get-tuple-element.73.weight_ref, f32[4,512,128]{2,1,0:T(8,128)S(1)} %get-tuple-element.74.source_ref, ...), custom_call_target="tpu_custom_call" | custom-call | flops 110000000 | bytes 100000 | tf_op jit(solution)/shard_map/back/pallas_call | solution.py:592
  61.3 4.8 %collective-permute-done.17.refs_3_ = bf16[2,256,256]{2,1,0:T(8,128)(2,1)S(1)} collective-permute-done((bf16[2,256,256]{2,1,0:T(8,128)(2,1)S(1)}, bf16[2,256,256]{2,1,0:T(8,128)(2,1)S(1)}, u32[]{:S(2)}, u32[]{:S(2)}) %collective-permute-start.17) | collective-permute-done | bytes 262176 | tf_op jit(solution)/shard_map/ppermute | solution.py:488
  66.2 2.0 %collective-permute-start.18 = (bf16[2,64,256]{2,1,0:T(8,128)(2,1)S(1)}, bf16[2,64,256]{2,1,0:T(8,128)(2,1)S(1)}, u32[]{:S(2)}, u32[]{:S(2)}) collective-permute-start(bf16[2,64,256]{2,1,0:T(8,128)(2,1)S(1)} %get-tuple-element.103), channel_id=1, source_target_pairs={{0,8},{1,9},{2,10},{3,11},{4,12},{5,13},{6,14},{7,15},{8,0},{9,1},... | collective-permute-start | bytes 196616 | tf_op jit(solution)/shard_map/ppermute | solution.py:488
  68.2 2.8 %collective-permute-start.19 = (bf16[2,64,256]{2,1,0:T(8,128)(2,1)S(1)}, bf16[2,64,256]{2,1,0:T(8,128)(2,1)S(1)}, u32[]{:S(2)}, u32[]{:S(2)}) collective-permute-start(bf16[2,64,256]{2,1,0:T(8,128)(2,1)S(1)} %get-tuple-element.104), channel_id=1, source_target_pairs={{0,16},{1,17},{2,18},{3,19},{4,20},{5,21},{6,22},{7,23},{8,24},{9,... | collective-permute-start | bytes 196616 | tf_op jit(solution)/shard_map/ppermute | solution.py:488
  71.0 3.7 %collective-permute-start.20 = (bf16[2,64,256]{2,1,0:T(8,128)(2,1)S(1)}, bf16[2,64,256]{2,1,0:T(8,128)(2,1)S(1)}, u32[]{:S(2)}, u32[]{:S(2)}) collective-permute-start(bf16[2,64,256]{2,1,0:T(8,128)(2,1)S(1)} %get-tuple-element.105), channel_id=1, source_target_pairs={{0,24},{1,25},{2,26},{3,27},{4,28},{5,29},{6,30},{7,31},{8,16},{9,... | collective-permute-start | bytes 196616 | tf_op jit(solution)/shard_map/ppermute | solution.py:488
  74.7 2.4 %collective-permute-done.20.refs_3_ = bf16[2,64,256]{2,1,0:T(8,128)(2,1)S(1)} collective-permute-done((bf16[2,64,256]{2,1,0:T(8,128)(2,1)S(1)}, bf16[2,64,256]{2,1,0:T(8,128)(2,1)S(1)}, u32[]{:S(2)}, u32[]{:S(2)}) %collective-permute-start.20) | collective-permute-done | bytes 65568 | tf_op jit(solution)/shard_map/ppermute | solution.py:488
  77.1 3.8 %collective-permute-start.23 = (bf16[2,64,256]{2,1,0:T(8,128)(2,1)S(1)}, bf16[2,64,256]{2,1,0:T(8,128)(2,1)S(1)}, u32[]{:S(2)}, u32[]{:S(2)}) collective-permute-start(bf16[2,64,256]{2,1,0:T(8,128)(2,1)S(1)} %s_line.1.refs_0_), channel_id=1, source_target_pairs={{0,24},{1,25},{2,26},{3,27},{4,28},{5,29},{6,30},{7,31},{8,16},{9,... | collective-permute-start | bytes 196616 | tf_op jit(solution)/shard_map/ppermute | solution.py:488
  83.5 2.6 %collective-permute-done.22.refs_2_ = bf16[2,64,256]{2,1,0:T(8,128)(2,1)S(1)} collective-permute-done((bf16[2,64,256]{2,1,0:T(8,128)(2,1)S(1)}, bf16[2,64,256]{2,1,0:T(8,128)(2,1)S(1)}, u32[]{:S(2)}, u32[]{:S(2)}) %collective-permute-start.22) | collective-permute-done | bytes 65568 | tf_op jit(solution)/shard_map/ppermute | solution.py:488
  88.1 1.6 %collective-permute-start.31 = (bf16[2,256,256]{2,1,0:T(8,128)(2,1)S(1)}, bf16[2,256,256]{2,1,0:T(8,128)(2,1)S(1)}, u32[]{:S(2)}, u32[]{:S(2)}) collective-permute-start(bf16[2,256,256]{2,1,0:T(8,128)(2,1)S(1)} %s_join.1.refs_4_.refs_0_), channel_id=1, source_target_pairs={{0,2},{1,3},{2,0},{3,1},{4,6},{5,7},{6,4},{7,5},{8,10},{9,11},{10,... | collective-permute-start | bytes 786440 | tf_op jit(solution)/shard_map/ppermute | solution.py:488
  89.7 2.2 %collective-permute-start.13 = (bf16[2,80,256]{2,1,0:T(8,128)(2,1)S(1)}, bf16[2,80,256]{2,1,0:T(8,128)(2,1)S(1)}, u32[]{:S(2)}, u32[]{:S(2)}) collective-permute-start(bf16[2,80,256]{2,1,0:T(8,128)(2,1)S(1)} %get-tuple-element.97), channel_id=1, source_target_pairs={{0,16},{1,17},{2,18},{3,19},{4,20},{5,21},{6,22},{7,23},{8,24},{9,... | collective-permute-start | bytes 245768 | tf_op jit(solution)/shard_map/ppermute | solution.py:488
  92.5 6.6 %collective-permute-done.13.refs_2_ = bf16[2,80,256]{2,1,0:T(8,128)(2,1)S(1)} collective-permute-done((bf16[2,80,256]{2,1,0:T(8,128)(2,1)S(1)}, bf16[2,80,256]{2,1,0:T(8,128)(2,1)S(1)}, u32[]{:S(2)}, u32[]{:S(2)}) %collective-permute-start.13) | collective-permute-done | bytes 81952 | tf_op jit(solution)/shard_map/ppermute | solution.py:488
  102.2 3.1 %collective-permute-done.26.refs_3_ = bf16[2,64,256]{2,1,0:T(8,128)(2,1)S(1)} collective-permute-done((bf16[2,64,256]{2,1,0:T(8,128)(2,1)S(1)}, bf16[2,64,256]{2,1,0:T(8,128)(2,1)S(1)}, u32[]{:S(2)}, u32[]{:S(2)}) %collective-permute-start.26) | collective-permute-done | bytes 65568 | tf_op jit(solution)/shard_map/ppermute | solution.py:488
  106.7 2.9 %collective-permute-done.24.refs_1_ = bf16[2,64,256]{2,1,0:T(8,128)(2,1)S(1)} collective-permute-done((bf16[2,64,256]{2,1,0:T(8,128)(2,1)S(1)}, bf16[2,64,256]{2,1,0:T(8,128)(2,1)S(1)}, u32[]{:S(2)}, u32[]{:S(2)}) %collective-permute-start.24) | collective-permute-done | bytes 65568 | tf_op jit(solution)/shard_map/ppermute | solution.py:488
  115.3 1.8 %features.1.total_ref = f32[384,1024]{1,0:T(8,128)S(1)} custom-call(bf16[384,512]{1,0:T(8,128)(2,1)S(1)} %get-tuple-element.81.own_one, bf16[384,512]{1,0:T(8,128)(2,1)S(1)} %get-tuple-element.88.own_two, bf16[384,1024]{1,0:T(8,128)(2,1)S(1)} %get-tuple-element.78.dskip_ref, bf16[1024,1024]{1,0:T(8,128)(2,1)S(1)} %copy-done, bf16[1024,1024]{1,0:T(8,128)(2,1)S(1)} %copy-done.1), custom_call_target="tpu_custom_call" | custom-call | flops 110000000 | bytes 100000 | tf_op jit(solution)/shard_map/features/pallas_call | solution.py:699
  117.8 1.6 %assemble.4.refs_1_ = f32[1024,1024]{1,0:T(8,128)} custom-call(bf16[2,1024,256]{2,1,0:T(8,128)(2,1)S(1)} %s_half.1.refs_0_), custom_call_target="tpu_custom_call" | custom-call | flops 110000000 | bytes 100000 | tf_op jit(solution)/shard_map/assemble/pallas_call | solution.py:652
  119.4 1.6 %assemble.5 = f32[1024,1024]{1,0:T(8,128)} custom-call(bf16[2,1024,256]{2,1,0:T(8,128)(2,1)S(1)} %collective-permute-done.34.refs_0_, f32[1024,1024]{1,0:T(8,128)} %assemble.4.refs_1_), custom_call_target="tpu_custom_call", output_to_operand_aliasing={{}: (1, {})} | custom-call | flops 110000000 | bytes 100000 | tf_op jit(solution)/shard_map/assemble/pallas_call | solution.py:652
  121.1 1.9 %collective-permute-start.29 = (bf16[2,256,256]{2,1,0:T(8,128)(2,1)S(1)}, bf16[2,256,256]{2,1,0:T(8,128)(2,1)S(1)}, u32[]{:S(2)}, u32[]{:S(2)}) collective-permute-start(bf16[2,256,256]{2,1,0:T(8,128)(2,1)S(1)} %p_join.1.refs_4_.refs_0_), channel_id=1, source_target_pairs={{0,1},{1,0},{2,3},{3,2},{4,5},{5,4},{6,7},{7,6},{8,9},{9,8},{10,11... | collective-permute-start | bytes 786440 | tf_op jit(solution)/shard_map/ppermute | solution.py:488
  126.5 2.1 %features_halo.1 = bf16[376,1024]{1,0:T(8,128)(2,1)} custom-call(f32[384,1024]{1,0:T(8,128)S(1)} %features.1.total_ref, bf16[48,1024]{1,0:T(8,128)(2,1)S(1)} %collective-permute-done.27.near_ref, bf16[48,1024]{1,0:T(8,128)(2,1)S(1)} %collective-permute-done.28.far_ref, s32[1,2,47]{2,1,0:T(2,128)S(1)} %copy-done.7, bf16[1024,1024]{1,0:T(8,128)(2,1)S(1)} %copy-done), custom_call_target="tpu_custom_call" | custom-call | flops 110000000 | bytes 100000 | tf_op jit(solution)/shard_map/features_halo/pallas_call | solution.py:723
  128.6 1.6 %assemble.6.refs_4_ = f32[1024,1024]{1,0:T(8,128)} custom-call(bf16[2,256,256]{2,1,0:T(8,128)(2,1)S(1)} %p_join.1.refs_4_.refs_0_, bf16[2,256,256]{2,1,0:T(8,128)(2,1)S(1)} %collective-permute-done.30.refs_1_, bf16[2,256,256]{2,1,0:T(8,128)(2,1)S(1)} %collective-permute-done.37.refs_2_, bf16[2,256,256]{2,1,0:T(8,128)(2,1)S(1)} %collective-permute-done.39.refs_3_), custom_call_target="tpu_custom_call" | custom-call | flops 110000000 | bytes 100000 | tf_op jit(solution)/shard_map/assemble/pallas_call | solution.py:652
  130.2 1.6 %assemble.7 = f32[1024,1024]{1,0:T(8,128)} custom-call(bf16[2,256,256]{2,1,0:T(8,128)(2,1)S(1)} %collective-permute-done.29.refs_0_, bf16[2,256,256]{2,1,0:T(8,128)(2,1)S(1)} %collective-permute-done.36.refs_1_, bf16[2,256,256]{2,1,0:T(8,128)(2,1)S(1)} %collective-permute-done.38.refs_2_, ...), custom_call_target="tpu_custom_call", output_to_operand_aliasing={{}: (4, {})} | custom-call | flops 110000000 | bytes 100000 | tf_op jit(solution)/shard_map/assemble/pallas_call | solution.py:652
  (97 shorter events, 33.2 us)
Async XLA Ops:
  2.2 7.8 %collective-permute-start = (bf16[48,1024]{1,0:T(8,128)(2,1)S(1)}, bf16[48,1024]{1,0:T(8,128)(2,1)S(1)}, u32[]{:S(2)}, u32[]{:S(2)}) collective-permute-start(bf16[48,1024]{1,0:T(8,128)(2,1)S(1)} %get-tuple-element.65), channel_id=1, source_target_pairs={{0,1},{1,0},{2,3},{3,2},{4,5},{5,4},{6,7},{7,6},{8,9},{9,8},{10,11... | collective-permute-start | bytes 294920 | tf_op jit(solution)/shard_map/ppermute | solution.py:488
  2.8 7.3 %collective-permute-start.1 = (bf16[48,1024]{1,0:T(8,128)(2,1)S(1)}, bf16[48,1024]{1,0:T(8,128)(2,1)S(1)}, u32[]{:S(2)}, u32[]{:S(2)}) collective-permute-start(bf16[48,1024]{1,0:T(8,128)(2,1)S(1)} %get-tuple-element.66), channel_id=1, source_target_pairs={{1,2},{3,4},{5,6},{7,8},{9,10},{11,12},{13,14},{15,16},{17,18},{19... | collective-permute-start | bytes 294920 | tf_op jit(solution)/shard_map/ppermute | solution.py:485
  18.8 4.8 %collective-permute-start.2 = (f32[8,1024]{1,0:T(8,128)S(1)}, f32[8,1024]{1,0:T(8,128)S(1)}, u32[]{:S(2)}, u32[]{:S(2)}) collective-permute-start(f32[8,1024]{1,0:T(8,128)S(1)} %get-tuple-element.70.mine_ref), channel_id=1, source_target_pairs={{0,1},{1,0},{2,3},{3,2},{4,5},{5,4},{6,7},{7,6},{8,9},{9,8},{10,11... | collective-permute-start | bytes 98312 | tf_op jit(solution)/shard_map/ppermute | solution.py:488
  36.4 5.0 %collective-permute-start.6 = (f32[8,1024]{1,0:T(8,128)S(1)}, f32[8,1024]{1,0:T(8,128)S(1)}, u32[]{:S(2)}, u32[]{:S(2)}) collective-permute-start(f32[8,1024]{1,0:T(8,128)S(1)} %merge.7.stats_ref), channel_id=1, source_target_pairs={{0,16},{1,17},{2,18},{3,19},{4,20},{5,21},{6,22},{7,23},{8,24},{9,... | collective-permute-start | bytes 98312 | tf_op jit(solution)/shard_map/ppermute | solution.py:488
  48.9 8.5 %collective-permute-start.8 = (bf16[2,1040,256]{2,1,0:T(8,128)(2,1)S(1)}, bf16[2,1040,256]{2,1,0:T(8,128)(2,1)S(1)}, u32[]{:S(2)}, u32[]{:S(2)}) collective-permute-start(bf16[2,1040,256]{2,1,0:T(8,128)(2,1)S(1)} %get-tuple-element.86.outs_0_), channel_id=1, source_target_pairs={{0,1},{1,0},{2,3},{3,2},{4,5},{5,4},{6,7},{7,6},{8,9},{9,8},{10,11... | collective-permute-start | bytes 3194888 | tf_op jit(solution)/shard_map/ppermute | solution.py:488
  49.7 10.2 %collective-permute-start.15 = (bf16[2,256,256]{2,1,0:T(8,128)(2,1)S(1)}, bf16[2,256,256]{2,1,0:T(8,128)(2,1)S(1)}, u32[]{:S(2)}, u32[]{:S(2)}) collective-permute-start(bf16[2,256,256]{2,1,0:T(8,128)(2,1)S(1)} %get-tuple-element.99), channel_id=1, source_target_pairs={{0,2},{1,3},{2,0},{3,1},{4,6},{5,7},{6,4},{7,5},{8,10},{9,11},{10,... | collective-permute-start | bytes 786440 | tf_op jit(solution)/shard_map/ppermute | solution.py:488
  50.4 10.9 %collective-permute-start.16 = (bf16[2,256,256]{2,1,0:T(8,128)(2,1)S(1)}, bf16[2,256,256]{2,1,0:T(8,128)(2,1)S(1)}, u32[]{:S(2)}, u32[]{:S(2)}) collective-permute-start(bf16[2,256,256]{2,1,0:T(8,128)(2,1)S(1)} %get-tuple-element.100), channel_id=1, source_target_pairs={{0,4},{1,5},{2,6},{3,7},{4,0},{5,1},{6,2},{7,3},{8,12},{9,13},{10,... | collective-permute-start | bytes 786440 | tf_op jit(solution)/shard_map/ppermute | solution.py:488
  51.9 14.2 %collective-permute-start.17 = (bf16[2,256,256]{2,1,0:T(8,128)(2,1)S(1)}, bf16[2,256,256]{2,1,0:T(8,128)(2,1)S(1)}, u32[]{:S(2)}, u32[]{:S(2)}) collective-permute-start(bf16[2,256,256]{2,1,0:T(8,128)(2,1)S(1)} %get-tuple-element.101), channel_id=1, source_target_pairs={{0,6},{1,7},{2,4},{3,5},{4,2},{5,3},{6,0},{7,1},{8,14},{9,15},{10,... | collective-permute-start | bytes 786440 | tf_op jit(solution)/shard_map/ppermute | solution.py:488
  57.7 23.2 %collective-permute-start.9 = (bf16[2,272,256]{2,1,0:T(8,128)(2,1)S(1)}, bf16[2,272,256]{2,1,0:T(8,128)(2,1)S(1)}, u32[]{:S(2)}, u32[]{:S(2)}) collective-permute-start(bf16[2,272,256]{2,1,0:T(8,128)(2,1)S(1)} %get-tuple-element.92), channel_id=1, source_target_pairs={{0,2},{1,3},{2,0},{3,1},{4,6},{5,7},{6,4},{7,5},{8,10},{9,11},{10,... | collective-permute-start | bytes 835592 | tf_op jit(solution)/shard_map/ppermute | solution.py:488
  58.4 23.2 %collective-permute-start.10 = (bf16[2,272,256]{2,1,0:T(8,128)(2,1)S(1)}, bf16[2,272,256]{2,1,0:T(8,128)(2,1)S(1)}, u32[]{:S(2)}, u32[]{:S(2)}) collective-permute-start(bf16[2,272,256]{2,1,0:T(8,128)(2,1)S(1)} %get-tuple-element.93), channel_id=1, source_target_pairs={{0,4},{1,5},{2,6},{3,7},{4,0},{5,1},{6,2},{7,3},{8,12},{9,13},{10,... | collective-permute-start | bytes 835592 | tf_op jit(solution)/shard_map/ppermute | solution.py:488
  59.9 21.7 %collective-permute-start.11 = (bf16[2,272,256]{2,1,0:T(8,128)(2,1)S(1)}, bf16[2,272,256]{2,1,0:T(8,128)(2,1)S(1)}, u32[]{:S(2)}, u32[]{:S(2)}) collective-permute-start(bf16[2,272,256]{2,1,0:T(8,128)(2,1)S(1)} %get-tuple-element.94), channel_id=1, source_target_pairs={{0,6},{1,7},{2,4},{3,5},{4,2},{5,3},{6,0},{7,1},{8,14},{9,15},{10,... | collective-permute-start | bytes 835592 | tf_op jit(solution)/shard_map/ppermute | solution.py:488
  68.2 6.5 %collective-permute-start.19 = (bf16[2,64,256]{2,1,0:T(8,128)(2,1)S(1)}, bf16[2,64,256]{2,1,0:T(8,128)(2,1)S(1)}, u32[]{:S(2)}, u32[]{:S(2)}) collective-permute-start(bf16[2,64,256]{2,1,0:T(8,128)(2,1)S(1)} %get-tuple-element.104), channel_id=1, source_target_pairs={{0,16},{1,17},{2,18},{3,19},{4,20},{5,21},{6,22},{7,23},{8,24},{9,... | collective-permute-start | bytes 196616 | tf_op jit(solution)/shard_map/ppermute | solution.py:488
  71.0 6.1 %collective-permute-start.20 = (bf16[2,64,256]{2,1,0:T(8,128)(2,1)S(1)}, bf16[2,64,256]{2,1,0:T(8,128)(2,1)S(1)}, u32[]{:S(2)}, u32[]{:S(2)}) collective-permute-start(bf16[2,64,256]{2,1,0:T(8,128)(2,1)S(1)} %get-tuple-element.105), channel_id=1, source_target_pairs={{0,24},{1,25},{2,26},{3,27},{4,28},{5,29},{6,30},{7,31},{8,16},{9,... | collective-permute-start | bytes 196616 | tf_op jit(solution)/shard_map/ppermute | solution.py:488
  77.1 6.3 %collective-permute-start.23 = (bf16[2,64,256]{2,1,0:T(8,128)(2,1)S(1)}, bf16[2,64,256]{2,1,0:T(8,128)(2,1)S(1)}, u32[]{:S(2)}, u32[]{:S(2)}) collective-permute-start(bf16[2,64,256]{2,1,0:T(8,128)(2,1)S(1)} %s_line.1.refs_0_), channel_id=1, source_target_pairs={{0,24},{1,25},{2,26},{3,27},{4,28},{5,29},{6,30},{7,31},{8,16},{9,... | collective-permute-start | bytes 196616 | tf_op jit(solution)/shard_map/ppermute | solution.py:488
  80.9 5.2 %collective-permute-start.22 = (bf16[2,64,256]{2,1,0:T(8,128)(2,1)S(1)}, bf16[2,64,256]{2,1,0:T(8,128)(2,1)S(1)}, u32[]{:S(2)}, u32[]{:S(2)}) collective-permute-start(bf16[2,64,256]{2,1,0:T(8,128)(2,1)S(1)} %s_line.1.refs_0_), channel_id=1, source_target_pairs={{0,16},{1,17},{2,18},{3,19},{4,20},{5,21},{6,22},{7,23},{8,24},{9,... | collective-permute-start | bytes 196616 | tf_op jit(solution)/shard_map/ppermute | solution.py:488
  80.9 5.2 %collective-permute-start.21 = (bf16[2,64,256]{2,1,0:T(8,128)(2,1)S(1)}, bf16[2,64,256]{2,1,0:T(8,128)(2,1)S(1)}, u32[]{:S(2)}, u32[]{:S(2)}) collective-permute-start(bf16[2,64,256]{2,1,0:T(8,128)(2,1)S(1)} %s_line.1.refs_0_), channel_id=1, source_target_pairs={{0,8},{1,9},{2,10},{3,11},{4,12},{5,13},{6,14},{7,15},{8,0},{9,1},... | collective-permute-start | bytes 196616 | tf_op jit(solution)/shard_map/ppermute | solution.py:488
  81.8 10.2 %collective-permute-start.12 = (bf16[2,80,256]{2,1,0:T(8,128)(2,1)S(1)}, bf16[2,80,256]{2,1,0:T(8,128)(2,1)S(1)}, u32[]{:S(2)}, u32[]{:S(2)}) collective-permute-start(bf16[2,80,256]{2,1,0:T(8,128)(2,1)S(1)} %get-tuple-element.96), channel_id=1, source_target_pairs={{0,8},{1,9},{2,10},{3,11},{4,12},{5,13},{6,14},{7,15},{8,0},{9,1},... | collective-permute-start | bytes 245768 | tf_op jit(solution)/shard_map/ppermute | solution.py:488
  86.2 23.4 %collective-permute-start.33 = (bf16[2,256,256]{2,1,0:T(8,128)(2,1)S(1)}, bf16[2,256,256]{2,1,0:T(8,128)(2,1)S(1)}, u32[]{:S(2)}, u32[]{:S(2)}) collective-permute-start(bf16[2,256,256]{2,1,0:T(8,128)(2,1)S(1)} %s_join.1.refs_4_.refs_0_), channel_id=1, source_target_pairs={{0,6},{1,7},{2,4},{3,5},{4,2},{5,3},{6,0},{7,1},{8,14},{9,15},{10,... | collective-permute-start | bytes 786440 | tf_op jit(solution)/shard_map/ppermute | solution.py:488
  86.5 23.0 %collective-permute-start.32 = (bf16[2,256,256]{2,1,0:T(8,128)(2,1)S(1)}, bf16[2,256,256]{2,1,0:T(8,128)(2,1)S(1)}, u32[]{:S(2)}, u32[]{:S(2)}) collective-permute-start(bf16[2,256,256]{2,1,0:T(8,128)(2,1)S(1)} %s_join.1.refs_4_.refs_0_), channel_id=1, source_target_pairs={{0,4},{1,5},{2,6},{3,7},{4,0},{5,1},{6,2},{7,3},{8,12},{9,13},{10,... | collective-permute-start | bytes 786440 | tf_op jit(solution)/shard_map/ppermute | solution.py:488
  88.1 21.5 %collective-permute-start.31 = (bf16[2,256,256]{2,1,0:T(8,128)(2,1)S(1)}, bf16[2,256,256]{2,1,0:T(8,128)(2,1)S(1)}, u32[]{:S(2)}, u32[]{:S(2)}) collective-permute-start(bf16[2,256,256]{2,1,0:T(8,128)(2,1)S(1)} %s_join.1.refs_4_.refs_0_), channel_id=1, source_target_pairs={{0,2},{1,3},{2,0},{3,1},{4,6},{5,7},{6,4},{7,5},{8,10},{9,11},{10,... | collective-permute-start | bytes 786440 | tf_op jit(solution)/shard_map/ppermute | solution.py:488
  89.7 9.3 %collective-permute-start.13 = (bf16[2,80,256]{2,1,0:T(8,128)(2,1)S(1)}, bf16[2,80,256]{2,1,0:T(8,128)(2,1)S(1)}, u32[]{:S(2)}, u32[]{:S(2)}) collective-permute-start(bf16[2,80,256]{2,1,0:T(8,128)(2,1)S(1)} %get-tuple-element.97), channel_id=1, source_target_pairs={{0,16},{1,17},{2,18},{3,19},{4,20},{5,21},{6,22},{7,23},{8,24},{9,... | collective-permute-start | bytes 245768 | tf_op jit(solution)/shard_map/ppermute | solution.py:488
  91.9 7.1 %collective-permute-start.14 = (bf16[2,80,256]{2,1,0:T(8,128)(2,1)S(1)}, bf16[2,80,256]{2,1,0:T(8,128)(2,1)S(1)}, u32[]{:S(2)}, u32[]{:S(2)}) collective-permute-start(bf16[2,80,256]{2,1,0:T(8,128)(2,1)S(1)} %get-tuple-element.98), channel_id=1, source_target_pairs={{0,24},{1,25},{2,26},{3,27},{4,28},{5,29},{6,30},{7,31},{8,16},{9,... | collective-permute-start | bytes 245768 | tf_op jit(solution)/shard_map/ppermute | solution.py:488
  99.1 6.1 %collective-permute-start.26 = (bf16[2,64,256]{2,1,0:T(8,128)(2,1)S(1)}, bf16[2,64,256]{2,1,0:T(8,128)(2,1)S(1)}, u32[]{:S(2)}, u32[]{:S(2)}) collective-permute-start(bf16[2,64,256]{2,1,0:T(8,128)(2,1)S(1)} %get-tuple-element.106.refs_0_), channel_id=1, source_target_pairs={{0,24},{1,25},{2,26},{3,27},{4,28},{5,29},{6,30},{7,31},{8,16},{9,... | collective-permute-start | bytes 196616 | tf_op jit(solution)/shard_map/ppermute | solution.py:488
  100.7 6.0 %collective-permute-start.25 = (bf16[2,64,256]{2,1,0:T(8,128)(2,1)S(1)}, bf16[2,64,256]{2,1,0:T(8,128)(2,1)S(1)}, u32[]{:S(2)}, u32[]{:S(2)}) collective-permute-start(bf16[2,64,256]{2,1,0:T(8,128)(2,1)S(1)} %get-tuple-element.106.refs_0_), channel_id=1, source_target_pairs={{0,16},{1,17},{2,18},{3,19},{4,20},{5,21},{6,22},{7,23},{8,24},{9,... | collective-permute-start | bytes 196616 | tf_op jit(solution)/shard_map/ppermute | solution.py:488
  109.7 5.0 %collective-permute-start.34 = (bf16[2,1024,256]{2,1,0:T(8,128)(2,1)S(1)}, bf16[2,1024,256]{2,1,0:T(8,128)(2,1)S(1)}, u32[]{:S(2)}, u32[]{:S(2)}) collective-permute-start(bf16[2,1024,256]{2,1,0:T(8,128)(2,1)S(1)} %s_half.1.refs_0_), channel_id=1, source_target_pairs={{0,1},{1,0},{2,3},{3,2},{4,5},{5,4},{6,7},{7,6},{8,9},{9,8},{10,11... | collective-permute-start | bytes 3145736 | tf_op jit(solution)/shard_map/ppermute | solution.py:488
  109.7 13.2 %collective-permute-start.39 = (bf16[2,256,256]{2,1,0:T(8,128)(2,1)S(1)}, bf16[2,256,256]{2,1,0:T(8,128)(2,1)S(1)}, u32[]{:S(2)}, u32[]{:S(2)}) collective-permute-start(bf16[2,256,256]{2,1,0:T(8,128)(2,1)S(1)} %p_join.1.refs_4_.refs_0_), channel_id=1, source_target_pairs={{0,6},{1,7},{2,4},{3,5},{4,2},{5,3},{6,0},{7,1},{8,14},{9,15},{10,... | collective-permute-start | bytes 786440 | tf_op jit(solution)/shard_map/ppermute | solution.py:488
  110.2 13.8 %collective-permute-start.37 = (bf16[2,256,256]{2,1,0:T(8,128)(2,1)S(1)}, bf16[2,256,256]{2,1,0:T(8,128)(2,1)S(1)}, u32[]{:S(2)}, u32[]{:S(2)}) collective-permute-start(bf16[2,256,256]{2,1,0:T(8,128)(2,1)S(1)} %p_join.1.refs_4_.refs_0_), channel_id=1, source_target_pairs={{0,4},{1,5},{2,6},{3,7},{4,0},{5,1},{6,2},{7,3},{8,12},{9,13},{10,... | collective-permute-start | bytes 786440 | tf_op jit(solution)/shard_map/ppermute | solution.py:488
  111.7 13.3 %collective-permute-start.30 = (bf16[2,256,256]{2,1,0:T(8,128)(2,1)S(1)}, bf16[2,256,256]{2,1,0:T(8,128)(2,1)S(1)}, u32[]{:S(2)}, u32[]{:S(2)}) collective-permute-start(bf16[2,256,256]{2,1,0:T(8,128)(2,1)S(1)} %p_join.1.refs_4_.refs_0_), channel_id=1, source_target_pairs={{0,2},{1,3},{2,0},{3,1},{4,6},{5,7},{6,4},{7,5},{8,10},{9,11},{10,... | collective-permute-start | bytes 786440 | tf_op jit(solution)/shard_map/ppermute | solution.py:488
  114.5 6.6 %collective-permute-start.27 = (bf16[48,1024]{1,0:T(8,128)(2,1)S(1)}, bf16[48,1024]{1,0:T(8,128)(2,1)S(1)}, u32[]{:S(2)}, u32[]{:S(2)}) collective-permute-start(bf16[48,1024]{1,0:T(8,128)(2,1)S(1)} %get-tuple-element.107), channel_id=1, source_target_pairs={{0,1},{1,0},{2,3},{3,2},{4,5},{5,4},{6,7},{7,6},{8,9},{9,8},{10,11... | collective-permute-start | bytes 294920 | tf_op jit(solution)/shard_map/ppermute | solution.py:488
  114.7 8.3 %collective-permute-start.28 = (bf16[48,1024]{1,0:T(8,128)(2,1)S(1)}, bf16[48,1024]{1,0:T(8,128)(2,1)S(1)}, u32[]{:S(2)}, u32[]{:S(2)}) collective-permute-start(bf16[48,1024]{1,0:T(8,128)(2,1)S(1)} %get-tuple-element.109), channel_id=1, source_target_pairs={{1,2},{3,4},{5,6},{7,8},{9,10},{11,12},{13,14},{15,16},{17,18},{19... | collective-permute-start | bytes 294920 | tf_op jit(solution)/shard_map/ppermute | solution.py:485
  121.1 9.1 %collective-permute-start.29 = (bf16[2,256,256]{2,1,0:T(8,128)(2,1)S(1)}, bf16[2,256,256]{2,1,0:T(8,128)(2,1)S(1)}, u32[]{:S(2)}, u32[]{:S(2)}) collective-permute-start(bf16[2,256,256]{2,1,0:T(8,128)(2,1)S(1)} %p_join.1.refs_4_.refs_0_), channel_id=1, source_target_pairs={{0,1},{1,0},{2,3},{3,2},{4,5},{5,4},{6,7},{7,6},{8,9},{9,8},{10,11... | collective-permute-start | bytes 786440 | tf_op jit(solution)/shard_map/ppermute | solution.py:488
  125.0 5.2 %collective-permute-start.36 = (bf16[2,256,256]{2,1,0:T(8,128)(2,1)S(1)}, bf16[2,256,256]{2,1,0:T(8,128)(2,1)S(1)}, u32[]{:S(2)}, u32[]{:S(2)}) collective-permute-start(bf16[2,256,256]{2,1,0:T(8,128)(2,1)S(1)} %collective-permute-done.30.refs_1_), channel_id=1, source_target_pairs={{0,1},{1,0},{2,3},{3,2},{4,5},{5,4},{6,7},{7,6},{8,9},{9,8},{10,11... | collective-permute-start | bytes 786440 | tf_op jit(solution)/shard_map/ppermute | solution.py:488
  (19 other events, 213.4 us)

commit v4 on v3

--- a/solution.py
+++ b/solution.py
@@ -90,7 +90,7 @@
 
 def own_place():
     me = own_index()
-    return (me // 2 % 4) * 4 + me // 8 % 4
+    return (me // 2 % 4) * 4 + (me // 8 % 2) * 2 + me // 16 % 2
 
 
 def head_at(step):
@@ -300,11 +300,33 @@
             out_ref[head] = sum_of_four(ins, head, slice(index * size, (index + 1) * size))
 
 
-def join_kernel(*refs):
-    out_ref = refs[-1]
-    size = refs[0].shape[1]
-    for piece in range(4):
-        out_ref[:, piece * size : (piece + 1) * size, :] = refs[piece][...]
+def pair_join_kernel(mine_ref, other_ref, *rest):
+    size = mine_ref.shape[1]
+    rest[-1][:, :size, :] = mine_ref[...]
+    rest[-1][:, size:, :] = other_ref[...]
+
+
+def heads_join_kernel(mine_ref, other_ref, *outs):
+    size = mine_ref.shape[1]
+    for head, out_ref in enumerate(outs):
+        out_ref[:size, :] = mine_ref[head]
+        out_ref[size:, :] = other_ref[head]
+
+
+def half_join_kernel(*refs):
+    for share, near, out_ref in zip(refs[:2], refs[2:4], refs[4:]):
+        size = share.shape[0]
+        out_ref[:size, :] = share[...]
+        out_ref[size:, :] = near[...]
+
+
+def plane_join_kernel(half_one, half_two, far_one, far_two, low_ref, high_ref):
+    size = half_one.shape[0] // 2
+    low_ref[0] = half_one[...]
+    high_ref[0] = far_one[...]
+    for part, out_ref in ((slice(0, size), low_ref), (slice(size, 2 * size), high_ref)):
+        out_ref[1, :size, :] = half_two[part, :]
+        out_ref[1, size:, :] = far_two[part, :]
 
 
 def two_sum_kernel(mine_ref, other_ref, *outs, deps=0):
@@ -620,7 +642,7 @@
         return [swapped(share, distance << 1) for distance, share in zip((1, 2, 3), shares)]
 
     def over_line(shares):
-        return [swapped(share, distance << 3) for distance, share in zip((1, 2, 3), shares)]
+        return [swapped(share, distance) for distance, share in zip((16, 8, 24), shares)]
 
     def ordered_call(kernel, name, shapes, arrays, deps):
         return pl.pallas_call(
@@ -641,12 +663,16 @@
         shapes = [shape_of(piece, BF16), shape_of((2, 8, width), F32)]
         return ordered_call(line_sum_kernel, "p_line", shapes, arrays, deps)
 
+    def two_sum(name, arrays, count, deps=()):
+        shapes = [(2, arrays[0].shape[1] // count, width)] * count
+        return step_call(functools.partial(two_sum_kernel, deps=len(deps)), name, shapes, arrays, deps)
+
+    def pair_join(name, mine, other, deps=()):
+        return step_call(pair_join_kernel, name, [(2, 2 * mine.shape[1], width)], [mine, other], deps)[0]
+
     def share_sum(name, arrays, count, deps):
         shapes = [(2, arrays[0].shape[1] // count, width)] * count
         return step_call(functools.partial(share_sum_kernel, deps=len(deps)), name, shapes, arrays, deps)
-
-    def join(name, arrays, deps):
-        return step_call(join_kernel, name, [(2, 4 * arrays[0].shape[1], width)], arrays, deps)[0]
 
     def assemble(pieces, first, *out):
         return pl.pallas_call(
@@ -679,23 +705,23 @@
     proj_keep, own_keep, back_near, back_far = backward(2, [near_send, far_send], [s_mine])
     p_mine, *p_rest = step_call(core_shares_kernel, "p_core", [(2, depth // 4 + 16, width)] * 4, [proj_keep, proj_other])
     p_got = over_plane(p_rest)
-    s_mine, *s_rest = share_sum("s_plane", [s_mine, *s_got], 4, [p_mine])
-    s_got = over_line(s_rest)
-    s_piece = beyond(share_sum("s_line", [s_mine, *s_got], 1, [])[0])
-    s_got = over_line([s_piece] * 3)
+    s_mine, s_rest = share_sum("s_plane", [s_mine, *s_got], 2, [p_mine])
+    s_mine, s_rest = two_sum("s_line", [s_mine, swapped(s_rest, 8)], 2)
     p_mine, *p_rest = plane_sum([p_mine, *p_got], [])
     p_got = over_line(p_rest)
-    s_share = join("s_join", [s_piece, *s_got], [p_mine])
-    s_got = [s_share, *over_plane([s_share] * 3)]
-    p_piece, small = line_sum([p_mine, *p_got], [s_share])
+    s_piece = beyond(two_sum("s_line", [s_mine, swapped(s_rest, 16)], 1, [p_mine])[0])
+    s_piece = pair_join("s_join", s_piece, swapped(s_piece, 16))
+    s_share = step_call(heads_join_kernel, "s_share", [(depth // 4, width)] * 2, [s_piece, swapped(s_piece, 8)])
+    s_near = (swapped(s_share[0], 2), swapped(s_share[1], 4))
+    s_sent = step_call(half_join_kernel, "s_near", [(depth // 2, width)] * 2, [*s_share, *s_near])
+    s_far = (swapped(s_sent[0], 4), swapped(s_sent[1], 2))
+    back_near, back_far = swapped(after(back_near, p_mine), 1), far_swapped(after(back_far, p_mine))
+    p_piece, small = line_sum([p_mine, *p_got], [back_near, back_far])
     p_piece, small = beyond(p_piece), beyond(small)
-    p_got = over_line([p_piece] * 3)
     small_other = swapped(small, 1)
-    p_share = join("p_join", [p_piece, *p_got], [])
+    p_piece = pair_join("p_join", p_piece, swapped(p_piece, 16))
+    p_share = pair_join("p_join", p_piece, swapped(p_piece, 8), [small_other])
     p_got = over_plane([p_share] * 3)
-    s_half = join("s_half", s_got, [p_share])
-    grad_skip = assemble([swapped(s_half, 1)], 0, assemble([s_half], 2))
-    back_near, back_far = swapped(after(back_near, p_share), 1), far_swapped(after(back_far, p_share))
     feats_total = pl.pallas_call(
         feats_kernel,
         in_specs=[vmem] * 5,
@@ -716,8 +742,11 @@
         cost_estimate=cost(0.1),
         name="vectors",
     )(small, small_other)
-    p_got = [p_share, *(after(share, grad_skip, grad_src, back_near, back_far, feats_total) for share in p_got)]
+    p_got = [p_share, *(after(share, grad_src, back_near, back_far, feats_total) for share in p_got)]
     p_other = [swapped(share, 1) for share in p_got]
+    s_halves = step_call(plane_join_kernel, "s_half", [(2, depth // 2, width)] * 2, [*s_sent, *s_far])
+    s_other = [swapped(half, 1) for half in s_halves]
+    grad_skip = assemble(s_other, 0, assemble(s_halves, 2))
     grad_proj = assemble(p_other, 0, assemble(p_got, 2))
 
     grad_feats = pl.pallas_call(

time: 132 us -> 130 us (0.985)
  starting transfers between devices: 53.6 us -> 49.3 us
  waiting for transfers between devices: 36.7 us -> 38.9 us
    ppermute x39 -> x38, starting transfers between devices: 52.3 us -> 47.6 us  [swapped(): lax.ppermute(value, AXES, [(source, source ^ distance) for source in rang...]
    ppermute x39 -> x38, waiting for transfers between devices: 36.7 us -> 38.9 us  [swapped(): lax.ppermute(value, AXES, [(source, source ^ distance) for source in rang...]
  transfers between devices with their start and end apart: 41 -> 40, of which waited for: 16 -> 17; matrix products, arithmetic and copies ran while one was open for 0% -> 0% of each run, Pallas kernels for 19% -> 19%
where the time goes in v4:
time: 130 us
  starting transfers between devices  49.3 us (38%)
  Pallas kernels  40.4 us (31%)
  waiting for transfers between devices  38.9 us (30%)
    ppermute x38, starting transfers between devices, swapped(): lax.ppermute(value, AXES, [(source, source ^ distance) for source in rang...  47.6 us
    ppermute x38, waiting for transfers between devices, swapped(): lax.ppermute(value, AXES, [(source, source ^ distance) for source in rang...  38.9 us
    pallas_call x1, Pallas kernels, per_device(): pl.pallas_call(attend_kernel, grid=(heads,), in_specs=[by_head(rows), who...  8.62 us
    pallas_call x2, Pallas kernels, backward(): pl.pallas_call(functools.partial(back_kernel, part=part), in_specs=[vmem]...  7.91 us
    pallas_call x1, Pallas kernels, per_device(): pl.pallas_call(functools.partial(project_kernel, halo=halo), grid=(heads,...  6.57 us
    pallas_call x4, Pallas kernels, assemble(): pl.pallas_call(functools.partial(assemble_kernel, first=first, pieces=len...  6.46 us
    pallas_call x1, Pallas kernels, per_device(): pl.pallas_call(functools.partial(norm_kernel, last_bit=bits - 1), in_spec...  3.44 us
  transfers between devices with their start and end apart: 40, of which 17 were waited for; matrix products, arithmetic and copies ran while one was open for 0% of the time, Pallas kernels for 19%

profile of v4, /device:TPU:0, one launch (start us, length us, event | category | flops | bytes accessed | tf_op | source)
XLA Modules:
  0.0 129.8 jit_solution(2736608134281908460)
XLA Ops:
  3.5 6.6 %project.1 = (bf16[384,1024]{1,0:T(8,128)(2,1)S(1)}, f32[384,1024]{1,0:T(8,128)S(1)}, f32[512,384]{1,0:T(8,128)S(1)}, bf16[1024,384]{1,0:T(8,128)(2,1)S(1)}) custom-call(bf16[376,1024]{1,0:T(8,128)(2,1)} %feats_ref.3, bf16[1024,1024]{1,0:T(8,128)(2,1)} %proj_ref.7, bf16[1024,1024]{1,0:T(8,128)(2,1)} %skip_ref.1, s32[16,376]{1,0:T(8,128)} %bitcast.11, ...), custom_call_target="tpu_custom_call" | custom-call | flops 5500000256 | bytes 5000000 | tf_op jit(solution)/shard_map/project/pallas_call | solution.py:534
  10.2 8.6 %attend.1 = (bf16[512,1024]{1,0:T(8,128)(2,1)S(1)}, bf16[4,512,384]{2,1,0:T(8,128)(2,1)S(1)}, f32[4,512,128]{2,1,0:T(8,128)S(1)}, f32[4,8,384]{2,1,0:T(8,128)S(1...) custom-call(bf16[384,1024]{1,0:T(8,128)(2,1)S(1)} %get-tuple-element, ...), custom_call_target="tpu_custom_call" | custom-call | flops 8800000000 | bytes 8000000 | tf_op jit(solution)/shard_map/attend/pallas_call | solution.py:553
  18.8 4.0 %collective-permute-start.2 = (f32[8,1024]{1,0:T(8,128)S(1)}, f32[8,1024]{1,0:T(8,128)S(1)}, u32[]{:S(2)}, u32[]{:S(2)}) collective-permute-start(f32[8,1024]{1,0:T(8,128)S(1)} %get-tuple-element.76.mine_ref), channel_id=1, source_target_pairs={{0,1},{1,0},{2,3},{3,2},{4,5},{5,4},{6,7},{7,6},{8,9},{9,8},{10,11... | collective-permute-start | bytes 98312 | tf_op jit(solution)/shard_map/ppermute | solution.py:510
  25.2 2.5 %collective-permute-done.3.other_ref = f32[8,1024]{1,0:T(8,128)S(1)} collective-permute-done((f32[8,1024]{1,0:T(8,128)S(1)}, f32[8,1024]{1,0:T(8,128)S(1)}, u32[]{:S(2)}, u32[]{:S(2)}) %collective-permute-start.3) | collective-permute-done | bytes 32800 | tf_op jit(solution)/shard_map/ppermute | solution.py:510
  27.7 1.9 %collective-permute-start.4 = (f32[8,1024]{1,0:T(8,128)S(1)}, f32[8,1024]{1,0:T(8,128)S(1)}, u32[]{:S(2)}, u32[]{:S(2)}) collective-permute-start(f32[8,1024]{1,0:T(8,128)S(1)} %merge.5.mine_ref), channel_id=1, source_target_pairs={{0,4},{1,5},{2,6},{3,7},{4,0},{5,1},{6,2},{7,3},{8,12},{9,13},{10,... | collective-permute-start | bytes 98312 | tf_op jit(solution)/shard_map/ppermute | solution.py:510
  29.5 2.1 %collective-permute-done.4.other_ref = f32[8,1024]{1,0:T(8,128)S(1)} collective-permute-done((f32[8,1024]{1,0:T(8,128)S(1)}, f32[8,1024]{1,0:T(8,128)S(1)}, u32[]{:S(2)}, u32[]{:S(2)}) %collective-permute-start.4) | collective-permute-done | bytes 32800 | tf_op jit(solution)/shard_map/ppermute | solution.py:510
  31.7 2.8 %collective-permute-start.5 = (f32[8,1024]{1,0:T(8,128)S(1)}, f32[8,1024]{1,0:T(8,128)S(1)}, u32[]{:S(2)}, u32[]{:S(2)}) collective-permute-start(f32[8,1024]{1,0:T(8,128)S(1)} %merge.6.mine_ref), channel_id=1, source_target_pairs={{0,8},{1,9},{2,10},{3,11},{4,12},{5,13},{6,14},{7,15},{8,0},{9,1},... | collective-permute-start | bytes 98312 | tf_op jit(solution)/shard_map/ppermute | solution.py:510
  34.5 1.9 %collective-permute-done.5.other_ref = f32[8,1024]{1,0:T(8,128)S(1)} collective-permute-done((f32[8,1024]{1,0:T(8,128)S(1)}, f32[8,1024]{1,0:T(8,128)S(1)}, u32[]{:S(2)}, u32[]{:S(2)}) %collective-permute-start.5) | collective-permute-done | bytes 32800 | tf_op jit(solution)/shard_map/ppermute | solution.py:510
  36.4 3.1 %collective-permute-start.6 = (f32[8,1024]{1,0:T(8,128)S(1)}, f32[8,1024]{1,0:T(8,128)S(1)}, u32[]{:S(2)}, u32[]{:S(2)}) collective-permute-start(f32[8,1024]{1,0:T(8,128)S(1)} %merge.7.stats_ref), channel_id=1, source_target_pairs={{0,16},{1,17},{2,18},{3,19},{4,20},{5,21},{6,22},{7,23},{8,24},{9,... | collective-permute-start | bytes 98312 | tf_op jit(solution)/shard_map/ppermute | solution.py:510
  39.5 1.9 %collective-permute-done.6.other_ref = f32[8,1024]{1,0:T(8,128)S(1)} collective-permute-done((f32[8,1024]{1,0:T(8,128)S(1)}, f32[8,1024]{1,0:T(8,128)S(1)}, u32[]{:S(2)}, u32[]{:S(2)}) %collective-permute-start.6) | collective-permute-done | bytes 32800 | tf_op jit(solution)/shard_map/ppermute | solution.py:510
  41.4 3.4 %norm.1 = (bf16[376,1024]{1,0:T(8,128)(2,1)}, bf16[384,1024]{1,0:T(8,128)(2,1)S(1)}, bf16[2,1024,256]{2,1,0:T(8,128)(2,1)S(1)}, bf16[2,1024,256]{2,1,0:T(8,128)(...) custom-call(f32[384,1024]{1,0:T(8,128)S(1)} %get-tuple-element.75.pre_ref, ...), custom_call_target="tpu_custom_call" | custom-call | flops 110000000 | bytes 100000 | tf_op jit(solution)/shard_map/norm/pallas_call | solution.py:594
  45.0 3.9 %back.2 = (bf16[2,1040,256]{2,1,0:T(8,128)(2,1)S(1)}, bf16[384,512]{1,0:T(8,128)(2,1)S(1)}, bf16[48,512]{1,0:T(8,128)(2,1)S(1)}, bf16[48,512]{1,0:T(8,128)(2,1)S(1)}) custom-call(bf16[4,512,384]{2,1,0:T(8,128)(2,1)S(1)} %get-tuple-element.79.weight_ref, f32[4,512,128]{2,1,0:T(8,128)S(1)} %get-tuple-element.80.source_ref, ...), custom_call_target="tpu_custom_call" | custom-call | flops 110000000 | bytes 100000 | tf_op jit(solution)/shard_map/back/pallas_call | solution.py:614
  53.3 4.0 %back.3 = (bf16[2,1040,256]{2,1,0:T(8,128)(2,1)S(1)}, bf16[384,512]{1,0:T(8,128)(2,1)S(1)}, bf16[48,1024]{1,0:T(8,128)(2,1)S(1)}, bf16[48,1024]{1,0:T(8,128)(2,1)S(1)}) custom-call(bf16[4,512,384]{2,1,0:T(8,128)(2,1)S(1)} %get-tuple-element.79.weight_ref, f32[4,512,128]{2,1,0:T(8,128)S(1)} %get-tuple-element.80.source_ref, ...), custom_call_target="tpu_custom_call" | custom-call | flops 110000000 | bytes 100000 | tf_op jit(solution)/shard_map/back/pallas_call | solution.py:614
  61.1 5.0 %collective-permute-done.29.refs_3_ = bf16[2,256,256]{2,1,0:T(8,128)(2,1)S(1)} collective-permute-done((bf16[2,256,256]{2,1,0:T(8,128)(2,1)S(1)}, bf16[2,256,256]{2,1,0:T(8,128)(2,1)S(1)}, u32[]{:S(2)}, u32[]{:S(2)}) %collective-permute-start.29) | collective-permute-done | bytes 262176 | tf_op jit(solution)/shard_map/ppermute | solution.py:510
  66.2 2.0 %collective-permute-start.30 = (bf16[2,128,256]{2,1,0:T(8,128)(2,1)S(1)}, bf16[2,128,256]{2,1,0:T(8,128)(2,1)S(1)}, u32[]{:S(2)}, u32[]{:S(2)}) collective-permute-start(bf16[2,128,256]{2,1,0:T(8,128)(2,1)S(1)} %get-tuple-element.118), channel_id=1, source_target_pairs={{0,8},{1,9},{2,10},{3,11},{4,12},{5,13},{6,14},{7,15},{8,0},{9,1},... | collective-permute-start | bytes 393224 | tf_op jit(solution)/shard_map/ppermute | solution.py:510
  68.2 3.1 %collective-permute-done.30.other_ref = bf16[2,128,256]{2,1,0:T(8,128)(2,1)S(1)} collective-permute-done((bf16[2,128,256]{2,1,0:T(8,128)(2,1)S(1)}, bf16[2,128,256]{2,1,0:T(8,128)(2,1)S(1)}, u32[]{:S(2)}, u32[]{:S(2)}) %collective-permute-start.30) | collective-permute-done | bytes 131104 | tf_op jit(solution)/shard_map/ppermute | solution.py:510
  71.3 3.5 %collective-permute-start.31 = (bf16[2,64,256]{2,1,0:T(8,128)(2,1)S(1)}, bf16[2,64,256]{2,1,0:T(8,128)(2,1)S(1)}, u32[]{:S(2)}, u32[]{:S(2)}) collective-permute-start(bf16[2,64,256]{2,1,0:T(8,128)(2,1)S(1)} %get-tuple-element.120), channel_id=1, source_target_pairs={{0,16},{1,17},{2,18},{3,19},{4,20},{5,21},{6,22},{7,23},{8,24},{9,... | collective-permute-start | bytes 196616 | tf_op jit(solution)/shard_map/ppermute | solution.py:510
  74.8 2.0 %collective-permute-done.11.refs_3_ = bf16[2,272,256]{2,1,0:T(8,128)(2,1)S(1)} collective-permute-done((bf16[2,272,256]{2,1,0:T(8,128)(2,1)S(1)}, bf16[2,272,256]{2,1,0:T(8,128)(2,1)S(1)}, u32[]{:S(2)}, u32[]{:S(2)}) %collective-permute-start.11) | collective-permute-done | bytes 278560 | tf_op jit(solution)/shard_map/ppermute | solution.py:510
  76.9 3.0 %collective-permute-start.14 = (bf16[2,80,256]{2,1,0:T(8,128)(2,1)S(1)}, bf16[2,80,256]{2,1,0:T(8,128)(2,1)S(1)}, u32[]{:S(2)}, u32[]{:S(2)}) collective-permute-start(bf16[2,80,256]{2,1,0:T(8,128)(2,1)S(1)} %get-tuple-element.105), channel_id=1, source_target_pairs={{0,16},{1,17},{2,18},{3,19},{4,20},{5,21},{6,22},{7,23},{8,24},{9,... | collective-permute-start | bytes 245768 | tf_op jit(solution)/shard_map/ppermute | solution.py:510
  81.1 4.3 %collective-permute-start.15 = (bf16[2,80,256]{2,1,0:T(8,128)(2,1)S(1)}, bf16[2,80,256]{2,1,0:T(8,128)(2,1)S(1)}, u32[]{:S(2)}, u32[]{:S(2)}) collective-permute-start(bf16[2,80,256]{2,1,0:T(8,128)(2,1)S(1)} %get-tuple-element.106), channel_id=1, source_target_pairs={{0,8},{1,9},{2,10},{3,11},{4,12},{5,13},{6,14},{7,15},{8,0},{9,1},... | collective-permute-start | bytes 245768 | tf_op jit(solution)/shard_map/ppermute | solution.py:510
  85.6 3.9 %collective-permute-start.16 = (bf16[2,80,256]{2,1,0:T(8,128)(2,1)S(1)}, bf16[2,80,256]{2,1,0:T(8,128)(2,1)S(1)}, u32[]{:S(2)}, u32[]{:S(2)}) collective-permute-start(bf16[2,80,256]{2,1,0:T(8,128)(2,1)S(1)} %get-tuple-element.107), channel_id=1, source_target_pairs={{0,24},{1,25},{2,26},{3,27},{4,28},{5,29},{6,30},{7,31},{8,16},{9,... | collective-permute-start | bytes 245768 | tf_op jit(solution)/shard_map/ppermute | solution.py:510
  89.6 3.8 %collective-permute-done.16.refs_3_ = bf16[2,80,256]{2,1,0:T(8,128)(2,1)S(1)} collective-permute-done((bf16[2,80,256]{2,1,0:T(8,128)(2,1)S(1)}, bf16[2,80,256]{2,1,0:T(8,128)(2,1)S(1)}, u32[]{:S(2)}, u32[]{:S(2)}) %collective-permute-start.16) | collective-permute-done | bytes 81952 | tf_op jit(solution)/shard_map/ppermute | solution.py:510
  93.6 2.0 %collective-permute-done.33.other_ref = bf16[2,128,256]{2,1,0:T(8,128)(2,1)S(1)} collective-permute-done((bf16[2,128,256]{2,1,0:T(8,128)(2,1)S(1)}, bf16[2,128,256]{2,1,0:T(8,128)(2,1)S(1)}, u32[]{:S(2)}, u32[]{:S(2)}) %collective-permute-start.33) | collective-permute-done | bytes 131104 | tf_op jit(solution)/shard_map/ppermute | solution.py:510
  95.9 1.7 %collective-permute-start.35 = (bf16[256,256]{1,0:T(8,128)(2,1)S(1)}, bf16[256,256]{1,0:T(8,128)(2,1)S(1)}, u32[]{:S(2)}, u32[]{:S(2)}) collective-permute-start(bf16[256,256]{1,0:T(8,128)(2,1)S(1)} %get-tuple-element.122.refs_1_), channel_id=1, source_target_pairs={{0,4},{1,5},{2,6},{3,7},{4,0},{5,1},{6,2},{7,3},{8,12},{9,13},{10,... | collective-permute-start | bytes 393224 | tf_op jit(solution)/shard_map/ppermute | solution.py:510
  97.6 1.9 %collective-permute-done.17.other_ref = bf16[2,64,256]{2,1,0:T(8,128)(2,1)S(1)} collective-permute-done((bf16[2,64,256]{2,1,0:T(8,128)(2,1)S(1)}, bf16[2,64,256]{2,1,0:T(8,128)(2,1)S(1)}, u32[]{:S(2)}, u32[]{:S(2)}) %collective-permute-start.17) | collective-permute-done | bytes 65568 | tf_op jit(solution)/shard_map/ppermute | solution.py:510
  100.9 1.8 %collective-permute-start.36 = (bf16[512,256]{1,0:T(8,128)(2,1)S(1)}, bf16[512,256]{1,0:T(8,128)(2,1)S(1)}, u32[]{:S(2)}, u32[]{:S(2)}) collective-permute-start(bf16[512,256]{1,0:T(8,128)(2,1)S(1)} %get-tuple-element.123.half_one), channel_id=1, source_target_pairs={{0,4},{1,5},{2,6},{3,7},{4,0},{5,1},{6,2},{7,3},{8,12},{9,13},{10,... | collective-permute-start | bytes 786440 | tf_op jit(solution)/shard_map/ppermute | solution.py:510
  106.2 1.8 %collective-permute-start.21 = (bf16[2,256,256]{2,1,0:T(8,128)(2,1)S(1)}, bf16[2,256,256]{2,1,0:T(8,128)(2,1)S(1)}, u32[]{:S(2)}, u32[]{:S(2)}) collective-permute-start(bf16[2,256,256]{2,1,0:T(8,128)(2,1)S(1)} %p_join.3.refs_0_), channel_id=1, source_target_pairs={{0,2},{1,3},{2,0},{3,1},{4,6},{5,7},{6,4},{7,5},{8,10},{9,11},{10,... | collective-permute-start | bytes 786440 | tf_op jit(solution)/shard_map/ppermute | solution.py:510
  108.0 2.1 %collective-permute-done.36.far_one = bf16[512,256]{1,0:T(8,128)(2,1)S(1)} collective-permute-done((bf16[512,256]{1,0:T(8,128)(2,1)S(1)}, bf16[512,256]{1,0:T(8,128)(2,1)S(1)}, u32[]{:S(2)}, u32[]{:S(2)}) %collective-permute-start.36) | collective-permute-done | bytes 262176 | tf_op jit(solution)/shard_map/ppermute | solution.py:510
  110.2 7.1 %collective-permute-done.37.far_two = bf16[512,256]{1,0:T(8,128)(2,1)S(1)} collective-permute-done((bf16[512,256]{1,0:T(8,128)(2,1)S(1)}, bf16[512,256]{1,0:T(8,128)(2,1)S(1)}, u32[]{:S(2)}, u32[]{:S(2)}) %collective-permute-start.37) | collective-permute-done | bytes 262176 | tf_op jit(solution)/shard_map/ppermute | solution.py:510
  117.9 1.8 %features.1.total_ref = f32[384,1024]{1,0:T(8,128)S(1)} custom-call(bf16[384,512]{1,0:T(8,128)(2,1)S(1)} %get-tuple-element.87.own_one, bf16[384,512]{1,0:T(8,128)(2,1)S(1)} %get-tuple-element.94.own_two, bf16[384,1024]{1,0:T(8,128)(2,1)S(1)} %get-tuple-element.84.dskip_ref, bf16[1024,1024]{1,0:T(8,128)(2,1)S(1)} %copy-done, bf16[1024,1024]{1,0:T(8,128)(2,1)S(1)} %copy-done.1), custom_call_target="tpu_custom_call" | custom-call | flops 110000000 | bytes 100000 | tf_op jit(solution)/shard_map/features/pallas_call | solution.py:725
  121.0 2.1 %features_halo.1 = bf16[376,1024]{1,0:T(8,128)(2,1)} custom-call(f32[384,1024]{1,0:T(8,128)S(1)} %features.1.total_ref, bf16[48,1024]{1,0:T(8,128)(2,1)S(1)} %collective-permute-done.12.near_ref.refs_4_, bf16[48,1024]{1,0:T(8,128)(2,1)S(1)} %collective-permute-done.13.far_ref.refs_5_, s32[1,2,47]{2,1,0:T(2,128)S(1)} %copy-done.7, bf16[1024,1024]{1,0:T(8,128)(2,1)S(1)} %copy-done), custom_call_target="tpu_custom_call" | custom-call | flops 110000000 | bytes 100000 | tf_op jit(solution)/shard_map/features_halo/pallas_call | solution.py:752
  126.4 1.6 %assemble.5 = f32[1024,1024]{1,0:T(8,128)} custom-call(bf16[2,256,256]{2,1,0:T(8,128)(2,1)S(1)} %collective-permute-done.20.refs_0_, bf16[2,256,256]{2,1,0:T(8,128)(2,1)S(1)} %collective-permute-done.22.refs_1_, bf16[2,256,256]{2,1,0:T(8,128)(2,1)S(1)} %collective-permute-done.24.refs_2_, ...), custom_call_target="tpu_custom_call", output_to_operand_aliasing={{}: (4, {})} | custom-call | flops 110000000 | bytes 100000 | tf_op jit(solution)/shard_map/assemble/pallas_call | solution.py:678
  (99 shorter events, 27.5 us)
Async XLA Ops:
  2.2 7.8 %collective-permute-start = (bf16[48,1024]{1,0:T(8,128)(2,1)S(1)}, bf16[48,1024]{1,0:T(8,128)(2,1)S(1)}, u32[]{:S(2)}, u32[]{:S(2)}) collective-permute-start(bf16[48,1024]{1,0:T(8,128)(2,1)S(1)} %get-tuple-element.71), channel_id=1, source_target_pairs={{0,1},{1,0},{2,3},{3,2},{4,5},{5,4},{6,7},{7,6},{8,9},{9,8},{10,11... | collective-permute-start | bytes 294920 | tf_op jit(solution)/shard_map/ppermute | solution.py:510
  2.8 7.3 %collective-permute-start.1 = (bf16[48,1024]{1,0:T(8,128)(2,1)S(1)}, bf16[48,1024]{1,0:T(8,128)(2,1)S(1)}, u32[]{:S(2)}, u32[]{:S(2)}) collective-permute-start(bf16[48,1024]{1,0:T(8,128)(2,1)S(1)} %get-tuple-element.72), channel_id=1, source_target_pairs={{1,2},{3,4},{5,6},{7,8},{9,10},{11,12},{13,14},{15,16},{17,18},{19... | collective-permute-start | bytes 294920 | tf_op jit(solution)/shard_map/ppermute | solution.py:507
  48.9 8.3 %collective-permute-start.8 = (bf16[2,1040,256]{2,1,0:T(8,128)(2,1)S(1)}, bf16[2,1040,256]{2,1,0:T(8,128)(2,1)S(1)}, u32[]{:S(2)}, u32[]{:S(2)}) collective-permute-start(bf16[2,1040,256]{2,1,0:T(8,128)(2,1)S(1)} %get-tuple-element.92.outs_0_), channel_id=1, source_target_pairs={{0,1},{1,0},{2,3},{3,2},{4,5},{5,4},{6,7},{7,6},{8,9},{9,8},{10,11... | collective-permute-start | bytes 3194888 | tf_op jit(solution)/shard_map/ppermute | solution.py:510
  49.7 10.0 %collective-permute-start.27 = (bf16[2,256,256]{2,1,0:T(8,128)(2,1)S(1)}, bf16[2,256,256]{2,1,0:T(8,128)(2,1)S(1)}, u32[]{:S(2)}, u32[]{:S(2)}) collective-permute-start(bf16[2,256,256]{2,1,0:T(8,128)(2,1)S(1)} %get-tuple-element.114), channel_id=1, source_target_pairs={{0,2},{1,3},{2,0},{3,1},{4,6},{5,7},{6,4},{7,5},{8,10},{9,11},{10,... | collective-permute-start | bytes 786440 | tf_op jit(solution)/shard_map/ppermute | solution.py:510
  50.4 10.7 %collective-permute-start.28 = (bf16[2,256,256]{2,1,0:T(8,128)(2,1)S(1)}, bf16[2,256,256]{2,1,0:T(8,128)(2,1)S(1)}, u32[]{:S(2)}, u32[]{:S(2)}) collective-permute-start(bf16[2,256,256]{2,1,0:T(8,128)(2,1)S(1)} %get-tuple-element.115), channel_id=1, source_target_pairs={{0,4},{1,5},{2,6},{3,7},{4,0},{5,1},{6,2},{7,3},{8,12},{9,13},{10,... | collective-permute-start | bytes 786440 | tf_op jit(solution)/shard_map/ppermute | solution.py:510
  51.9 14.2 %collective-permute-start.29 = (bf16[2,256,256]{2,1,0:T(8,128)(2,1)S(1)}, bf16[2,256,256]{2,1,0:T(8,128)(2,1)S(1)}, u32[]{:S(2)}, u32[]{:S(2)}) collective-permute-start(bf16[2,256,256]{2,1,0:T(8,128)(2,1)S(1)} %get-tuple-element.116), channel_id=1, source_target_pairs={{0,6},{1,7},{2,4},{3,5},{4,2},{5,3},{6,0},{7,1},{8,14},{9,15},{10,... | collective-permute-start | bytes 786440 | tf_op jit(solution)/shard_map/ppermute | solution.py:510
  57.5 17.3 %collective-permute-start.9 = (bf16[2,272,256]{2,1,0:T(8,128)(2,1)S(1)}, bf16[2,272,256]{2,1,0:T(8,128)(2,1)S(1)}, u32[]{:S(2)}, u32[]{:S(2)}) collective-permute-start(bf16[2,272,256]{2,1,0:T(8,128)(2,1)S(1)} %get-tuple-element.98), channel_id=1, source_target_pairs={{0,2},{1,3},{2,0},{3,1},{4,6},{5,7},{6,4},{7,5},{8,10},{9,11},{10,... | collective-permute-start | bytes 835592 | tf_op jit(solution)/shard_map/ppermute | solution.py:510
  58.2 16.6 %collective-permute-start.10 = (bf16[2,272,256]{2,1,0:T(8,128)(2,1)S(1)}, bf16[2,272,256]{2,1,0:T(8,128)(2,1)S(1)}, u32[]{:S(2)}, u32[]{:S(2)}) collective-permute-start(bf16[2,272,256]{2,1,0:T(8,128)(2,1)S(1)} %get-tuple-element.99), channel_id=1, source_target_pairs={{0,4},{1,5},{2,6},{3,7},{4,0},{5,1},{6,2},{7,3},{8,12},{9,13},{10,... | collective-permute-start | bytes 835592 | tf_op jit(solution)/shard_map/ppermute | solution.py:510
  59.7 17.0 %collective-permute-start.11 = (bf16[2,272,256]{2,1,0:T(8,128)(2,1)S(1)}, bf16[2,272,256]{2,1,0:T(8,128)(2,1)S(1)}, u32[]{:S(2)}, u32[]{:S(2)}) collective-permute-start(bf16[2,272,256]{2,1,0:T(8,128)(2,1)S(1)} %get-tuple-element.100), channel_id=1, source_target_pairs={{0,6},{1,7},{2,4},{3,5},{4,2},{5,3},{6,0},{7,1},{8,14},{9,15},{10,... | collective-permute-start | bytes 835592 | tf_op jit(solution)/shard_map/ppermute | solution.py:510
  66.2 5.0 %collective-permute-start.30 = (bf16[2,128,256]{2,1,0:T(8,128)(2,1)S(1)}, bf16[2,128,256]{2,1,0:T(8,128)(2,1)S(1)}, u32[]{:S(2)}, u32[]{:S(2)}) collective-permute-start(bf16[2,128,256]{2,1,0:T(8,128)(2,1)S(1)} %get-tuple-element.118), channel_id=1, source_target_pairs={{0,8},{1,9},{2,10},{3,11},{4,12},{5,13},{6,14},{7,15},{8,0},{9,1},... | collective-permute-start | bytes 393224 | tf_op jit(solution)/shard_map/ppermute | solution.py:510
  71.3 8.7 %collective-permute-start.31 = (bf16[2,64,256]{2,1,0:T(8,128)(2,1)S(1)}, bf16[2,64,256]{2,1,0:T(8,128)(2,1)S(1)}, u32[]{:S(2)}, u32[]{:S(2)}) collective-permute-start(bf16[2,64,256]{2,1,0:T(8,128)(2,1)S(1)} %get-tuple-element.120), channel_id=1, source_target_pairs={{0,16},{1,17},{2,18},{3,19},{4,20},{5,21},{6,22},{7,23},{8,24},{9,... | collective-permute-start | bytes 196616 | tf_op jit(solution)/shard_map/ppermute | solution.py:510
  76.9 12.6 %collective-permute-start.14 = (bf16[2,80,256]{2,1,0:T(8,128)(2,1)S(1)}, bf16[2,80,256]{2,1,0:T(8,128)(2,1)S(1)}, u32[]{:S(2)}, u32[]{:S(2)}) collective-permute-start(bf16[2,80,256]{2,1,0:T(8,128)(2,1)S(1)} %get-tuple-element.105), channel_id=1, source_target_pairs={{0,16},{1,17},{2,18},{3,19},{4,20},{5,21},{6,22},{7,23},{8,24},{9,... | collective-permute-start | bytes 245768 | tf_op jit(solution)/shard_map/ppermute | solution.py:510
  80.0 5.7 %collective-permute-start.32 = (bf16[2,64,256]{2,1,0:T(8,128)(2,1)S(1)}, bf16[2,64,256]{2,1,0:T(8,128)(2,1)S(1)}, u32[]{:S(2)}, u32[]{:S(2)}) collective-permute-start(bf16[2,64,256]{2,1,0:T(8,128)(2,1)S(1)} %s_line.3.mine_ref), channel_id=1, source_target_pairs={{0,16},{1,17},{2,18},{3,19},{4,20},{5,21},{6,22},{7,23},{8,24},{9,... | collective-permute-start | bytes 196616 | tf_op jit(solution)/shard_map/ppermute | solution.py:510
  80.2 13.2 %collective-permute-start.12 = (bf16[48,1024]{1,0:T(8,128)(2,1)S(1)}, bf16[48,1024]{1,0:T(8,128)(2,1)S(1)}, u32[]{:S(2)}, u32[]{:S(2)}) collective-permute-start(bf16[48,1024]{1,0:T(8,128)(2,1)S(1)} %get-tuple-element.102), channel_id=1, source_target_pairs={{0,1},{1,0},{2,3},{3,2},{4,5},{5,4},{6,7},{7,6},{8,9},{9,8},{10,11... | collective-permute-start | bytes 294920 | tf_op jit(solution)/shard_map/ppermute | solution.py:510
  80.2 13.2 %collective-permute-start.13 = (bf16[48,1024]{1,0:T(8,128)(2,1)S(1)}, bf16[48,1024]{1,0:T(8,128)(2,1)S(1)}, u32[]{:S(2)}, u32[]{:S(2)}) collective-permute-start(bf16[48,1024]{1,0:T(8,128)(2,1)S(1)} %get-tuple-element.104), channel_id=1, source_target_pairs={{1,2},{3,4},{5,6},{7,8},{9,10},{11,12},{13,14},{15,16},{17,18},{19... | collective-permute-start | bytes 294920 | tf_op jit(solution)/shard_map/ppermute | solution.py:507
  81.1 8.5 %collective-permute-start.15 = (bf16[2,80,256]{2,1,0:T(8,128)(2,1)S(1)}, bf16[2,80,256]{2,1,0:T(8,128)(2,1)S(1)}, u32[]{:S(2)}, u32[]{:S(2)}) collective-permute-start(bf16[2,80,256]{2,1,0:T(8,128)(2,1)S(1)} %get-tuple-element.106), channel_id=1, source_target_pairs={{0,8},{1,9},{2,10},{3,11},{4,12},{5,13},{6,14},{7,15},{8,0},{9,1},... | collective-permute-start | bytes 245768 | tf_op jit(solution)/shard_map/ppermute | solution.py:510
  85.6 7.8 %collective-permute-start.16 = (bf16[2,80,256]{2,1,0:T(8,128)(2,1)S(1)}, bf16[2,80,256]{2,1,0:T(8,128)(2,1)S(1)}, u32[]{:S(2)}, u32[]{:S(2)}) collective-permute-start(bf16[2,80,256]{2,1,0:T(8,128)(2,1)S(1)} %get-tuple-element.107), channel_id=1, source_target_pairs={{0,24},{1,25},{2,26},{3,27},{4,28},{5,29},{6,30},{7,31},{8,16},{9,... | collective-permute-start | bytes 245768 | tf_op jit(solution)/shard_map/ppermute | solution.py:510
  89.6 6.0 %collective-permute-start.33 = (bf16[2,128,256]{2,1,0:T(8,128)(2,1)S(1)}, bf16[2,128,256]{2,1,0:T(8,128)(2,1)S(1)}, u32[]{:S(2)}, u32[]{:S(2)}) collective-permute-start(bf16[2,128,256]{2,1,0:T(8,128)(2,1)S(1)} %s_join.1.mine_ref), channel_id=1, source_target_pairs={{0,8},{1,9},{2,10},{3,11},{4,12},{5,13},{6,14},{7,15},{8,0},{9,1},... | collective-permute-start | bytes 393224 | tf_op jit(solution)/shard_map/ppermute | solution.py:510
  93.5 5.9 %collective-permute-start.17 = (bf16[2,64,256]{2,1,0:T(8,128)(2,1)S(1)}, bf16[2,64,256]{2,1,0:T(8,128)(2,1)S(1)}, u32[]{:S(2)}, u32[]{:S(2)}) collective-permute-start(bf16[2,64,256]{2,1,0:T(8,128)(2,1)S(1)} %get-tuple-element.108.mine_ref), channel_id=1, source_target_pairs={{0,16},{1,17},{2,18},{3,19},{4,20},{5,21},{6,22},{7,23},{8,24},{9,... | collective-permute-start | bytes 196616 | tf_op jit(solution)/shard_map/ppermute | solution.py:510
  95.6 5.0 %collective-permute-start.34 = (bf16[256,256]{1,0:T(8,128)(2,1)S(1)}, bf16[256,256]{1,0:T(8,128)(2,1)S(1)}, u32[]{:S(2)}, u32[]{:S(2)}) collective-permute-start(bf16[256,256]{1,0:T(8,128)(2,1)S(1)} %get-tuple-element.121.refs_0_), channel_id=1, source_target_pairs={{0,2},{1,3},{2,0},{3,1},{4,6},{5,7},{6,4},{7,5},{8,10},{9,11},{10,... | collective-permute-start | bytes 393224 | tf_op jit(solution)/shard_map/ppermute | solution.py:510
  99.4 5.0 %collective-permute-start.18 = (bf16[2,128,256]{2,1,0:T(8,128)(2,1)S(1)}, bf16[2,128,256]{2,1,0:T(8,128)(2,1)S(1)}, u32[]{:S(2)}, u32[]{:S(2)}) collective-permute-start(bf16[2,128,256]{2,1,0:T(8,128)(2,1)S(1)} %p_join.2.mine_ref), channel_id=1, source_target_pairs={{0,8},{1,9},{2,10},{3,11},{4,12},{5,13},{6,14},{7,15},{8,0},{9,1},... | collective-permute-start | bytes 393224 | tf_op jit(solution)/shard_map/ppermute | solution.py:510
  100.9 9.3 %collective-permute-start.36 = (bf16[512,256]{1,0:T(8,128)(2,1)S(1)}, bf16[512,256]{1,0:T(8,128)(2,1)S(1)}, u32[]{:S(2)}, u32[]{:S(2)}) collective-permute-start(bf16[512,256]{1,0:T(8,128)(2,1)S(1)} %get-tuple-element.123.half_one), channel_id=1, source_target_pairs={{0,4},{1,5},{2,6},{3,7},{4,0},{5,1},{6,2},{7,3},{8,12},{9,13},{10,... | collective-permute-start | bytes 786440 | tf_op jit(solution)/shard_map/ppermute | solution.py:510
  102.6 14.6 %collective-permute-start.37 = (bf16[512,256]{1,0:T(8,128)(2,1)S(1)}, bf16[512,256]{1,0:T(8,128)(2,1)S(1)}, u32[]{:S(2)}, u32[]{:S(2)}) collective-permute-start(bf16[512,256]{1,0:T(8,128)(2,1)S(1)} %get-tuple-element.124.half_two), channel_id=1, source_target_pairs={{0,2},{1,3},{2,0},{3,1},{4,6},{5,7},{6,4},{7,5},{8,10},{9,11},{10,... | collective-permute-start | bytes 786440 | tf_op jit(solution)/shard_map/ppermute | solution.py:510
  104.5 12.9 %collective-permute-start.25 = (bf16[2,256,256]{2,1,0:T(8,128)(2,1)S(1)}, bf16[2,256,256]{2,1,0:T(8,128)(2,1)S(1)}, u32[]{:S(2)}, u32[]{:S(2)}) collective-permute-start(bf16[2,256,256]{2,1,0:T(8,128)(2,1)S(1)} %p_join.3.refs_0_), channel_id=1, source_target_pairs={{0,6},{1,7},{2,4},{3,5},{4,2},{5,3},{6,0},{7,1},{8,14},{9,15},{10,... | collective-permute-start | bytes 786440 | tf_op jit(solution)/shard_map/ppermute | solution.py:510
  105.7 14.7 %collective-permute-start.23 = (bf16[2,256,256]{2,1,0:T(8,128)(2,1)S(1)}, bf16[2,256,256]{2,1,0:T(8,128)(2,1)S(1)}, u32[]{:S(2)}, u32[]{:S(2)}) collective-permute-start(bf16[2,256,256]{2,1,0:T(8,128)(2,1)S(1)} %p_join.3.refs_0_), channel_id=1, source_target_pairs={{0,4},{1,5},{2,6},{3,7},{4,0},{5,1},{6,2},{7,3},{8,12},{9,13},{10,... | collective-permute-start | bytes 786440 | tf_op jit(solution)/shard_map/ppermute | solution.py:510
  106.2 14.2 %collective-permute-start.21 = (bf16[2,256,256]{2,1,0:T(8,128)(2,1)S(1)}, bf16[2,256,256]{2,1,0:T(8,128)(2,1)S(1)}, u32[]{:S(2)}, u32[]{:S(2)}) collective-permute-start(bf16[2,256,256]{2,1,0:T(8,128)(2,1)S(1)} %p_join.3.refs_0_), channel_id=1, source_target_pairs={{0,2},{1,3},{2,0},{3,1},{4,6},{5,7},{6,4},{7,5},{8,10},{9,11},{10,... | collective-permute-start | bytes 786440 | tf_op jit(solution)/shard_map/ppermute | solution.py:510
  110.2 10.7 %collective-permute-start.20 = (bf16[2,256,256]{2,1,0:T(8,128)(2,1)S(1)}, bf16[2,256,256]{2,1,0:T(8,128)(2,1)S(1)}, u32[]{:S(2)}, u32[]{:S(2)}) collective-permute-start(bf16[2,256,256]{2,1,0:T(8,128)(2,1)S(1)} %p_join.3.refs_0_), channel_id=1, source_target_pairs={{0,1},{1,0},{2,3},{3,2},{4,5},{5,4},{6,7},{7,6},{8,9},{9,8},{10,11... | collective-permute-start | bytes 786440 | tf_op jit(solution)/shard_map/ppermute | solution.py:510
  117.3 10.7 %collective-permute-start.38 = (bf16[2,512,256]{2,1,0:T(8,128)(2,1)S(1)}, bf16[2,512,256]{2,1,0:T(8,128)(2,1)S(1)}, u32[]{:S(2)}, u32[]{:S(2)}) collective-permute-start(bf16[2,512,256]{2,1,0:T(8,128)(2,1)S(1)} %get-tuple-element.125.refs_0_), channel_id=1, source_target_pairs={{0,1},{1,0},{2,3},{3,2},{4,5},{5,4},{6,7},{7,6},{8,9},{9,8},{10,11... | collective-permute-start | bytes 1572872 | tf_op jit(solution)/shard_map/ppermute | solution.py:510
  117.4 10.6 %collective-permute-start.39 = (bf16[2,512,256]{2,1,0:T(8,128)(2,1)S(1)}, bf16[2,512,256]{2,1,0:T(8,128)(2,1)S(1)}, u32[]{:S(2)}, u32[]{:S(2)}) collective-permute-start(bf16[2,512,256]{2,1,0:T(8,128)(2,1)S(1)} %get-tuple-element.126.refs_1_), channel_id=1, source_target_pairs={{0,1},{1,0},{2,3},{3,2},{4,5},{5,4},{6,7},{7,6},{8,9},{9,8},{10,11... | collective-permute-start | bytes 1572872 | tf_op jit(solution)/shard_map/ppermute | solution.py:510
  120.4 6.0 %collective-permute-start.26 = (bf16[2,256,256]{2,1,0:T(8,128)(2,1)S(1)}, bf16[2,256,256]{2,1,0:T(8,128)(2,1)S(1)}, u32[]{:S(2)}, u32[]{:S(2)}) collective-permute-start(bf16[2,256,256]{2,1,0:T(8,128)(2,1)S(1)} %collective-permute-done.25.refs_3_), channel_id=1, source_target_pairs={{0,1},{1,0},{2,3},{3,2},{4,5},{5,4},{6,7},{7,6},{8,9},{9,8},{10,11... | collective-permute-start | bytes 786440 | tf_op jit(solution)/shard_map/ppermute | solution.py:510
  120.5 5.9 %collective-permute-start.24 = (bf16[2,256,256]{2,1,0:T(8,128)(2,1)S(1)}, bf16[2,256,256]{2,1,0:T(8,128)(2,1)S(1)}, u32[]{:S(2)}, u32[]{:S(2)}) collective-permute-start(bf16[2,256,256]{2,1,0:T(8,128)(2,1)S(1)} %collective-permute-done.23.refs_2_), channel_id=1, source_target_pairs={{0,1},{1,0},{2,3},{3,2},{4,5},{5,4},{6,7},{7,6},{8,9},{9,8},{10,11... | collective-permute-start | bytes 786440 | tf_op jit(solution)/shard_map/ppermute | solution.py:510
  120.9 5.5 %collective-permute-start.22 = (bf16[2,256,256]{2,1,0:T(8,128)(2,1)S(1)}, bf16[2,256,256]{2,1,0:T(8,128)(2,1)S(1)}, u32[]{:S(2)}, u32[]{:S(2)}) collective-permute-start(bf16[2,256,256]{2,1,0:T(8,128)(2,1)S(1)} %collective-permute-done.21.refs_1_), channel_id=1, source_target_pairs={{0,1},{1,0},{2,3},{3,2},{4,5},{5,4},{6,7},{7,6},{8,9},{9,8},{10,11... | collective-permute-start | bytes 786440 | tf_op jit(solution)/shard_map/ppermute | solution.py:510
  (18 other events, 221.1 us)

commit v5 on v4

--- a/solution.py
+++ b/solution.py
@@ -147,66 +147,63 @@
 ):
     columns, rows = count_ref.shape
     half = (columns - rows) // 2
-    head = pl.program_id(0)
-
-    @pl.when(head == 0)
-    def _():
-        halo_scr[...] = jnp.zeros_like(halo_scr)
-        near_at = jnp.where(is_odd(), 0, half)
-        halo_scr[pl.ds(pl.multiple_of(near_at, 16), near_ref.shape[0]), :] = near_ref[...]
-        halo_scr[pl.ds(pl.multiple_of(half - near_at, 16), far_ref.shape[0]), :] = far_ref[...]
-        flipped_ref[...] = halo_scr[...].T
-
-    ext_ref[0:rows, :] = zq_ref[...]
-    ext_ref[rows:columns, :] = mm(halo_scr[...], proj_ref[...], (1, 0)).astype(BF16)
-    ext = ext_ref[...]
-    width = ext.shape[1]
-    parts = three_parts(src_ref[pl.ds(head, 1), :] * (1.0 / LN2))
-    vectors = jnp.concatenate([jnp.broadcast_to(part, (LANES, width)) for part in parts], axis=0)
-    source = mm(ext, vectors, (1, 1))
-    source_ref[0] = source[:, :LANES] + source[:, LANES : 2 * LANES] + source[:, 2 * LANES :]
-    parts = three_parts(dst_ref[pl.ds(head, 1), :] * (1.0 / LN2))
-    vectors = jnp.concatenate([jnp.broadcast_to(part, (16, width)) for part in parts], axis=0)
-    target = mm(vectors, zq_ref[...], (1, 1))
-    target = target[0:8] + target[16:24] + target[32:40]
-    target_ref[0] = target
-    target = target[0:1]
-
-    def score(index, highest):
-        where = pl.ds(pl.multiple_of(index * CHUNK, CHUNK), CHUNK)
-        value = repeat_lanes(source_ref[0, where, :], rows) + target
-        small = jnp.exp2(-jnp.abs(value))
-        result = jnp.maximum(value, 0.2 * value) + (0.8 / LN2) * jnp.log(1.0 + small) + count_ref[where, :]
-        score_scr[where, :] = result
-        return jnp.maximum(highest, jnp.max(fold_rows(result), axis=0))
-
-    highest = lax.fori_loop(0, columns // CHUNK, score, jnp.full((8, rows), NEG, F32), unroll=2)
-    highest = jnp.max(highest, axis=0, keepdims=True)
-
-    def weigh(index, carry):
-        where = pl.ds(pl.multiple_of(index * CHUNK, CHUNK), CHUNK)
-        weight_ref[0, where, :] = jnp.exp2(score_scr[where, :] - highest).astype(BF16)
-        return carry
-
-    lax.fori_loop(0, columns // CHUNK, weigh, 0, unroll=2)
-    weights = weight_ref[0]
-    wide = jnp.concatenate([ext, jnp.ones((columns, LANES), BF16)], axis=1)
-    summed = mm(weights, wide, (0, 0))
-    scale = 1.0 / summed[:, width:]
-    scale_ref[0] = scale
-    pre = summed[:, :width] * repeat_lanes(scale, width) + skip_ref[...] + bias_ref[...]
-    pre_ref[...] = pre
-    act = jnp.where(pre > 0, pre, jnp.exp(jnp.minimum(pre, 0.0)) - 1.0)
+    heads, width = src_ref.shape
+    halo_scr[...] = jnp.zeros_like(halo_scr)
+    near_at = jnp.where(is_odd(), 0, half)
+    halo_scr[pl.ds(pl.multiple_of(near_at, 16), near_ref.shape[0]), :] = near_ref[...]
+    halo_scr[pl.ds(pl.multiple_of(half - near_at, 16), far_ref.shape[0]), :] = far_ref[...]
+    flipped_ref[...] = halo_scr[...].T
+    stats_ref[...] = jnp.zeros_like(stats_ref)
     nodes, real = real_rows(mask_ref, rows, width)
-    cot = jnp.where(real, pad_rows(cot_ref[...].astype(F32), rows), 0.0)
-    mean = jnp.sum(jnp.where(real, act, 0.0), axis=0, keepdims=True) / nodes
-    centred = jnp.where(real, act - mean, 0.0)
-    stats_ref[...] = jnp.zeros_like(stats_ref)
-    stats_ref[0:1, :] = jnp.broadcast_to(nodes, mean.shape)
-    stats_ref[1:2, :] = mean
-    stats_ref[2:3, :] = jnp.sum(centred * centred, axis=0, keepdims=True)
-    stats_ref[3:4, :] = jnp.sum(cot, axis=0, keepdims=True)
-    stats_ref[4:5, :] = jnp.sum(cot * centred, axis=0, keepdims=True)
+    for head in range(heads):
+        lanes = slice(head * width, (head + 1) * width)
+        own = zq_ref[:, lanes]
+        ext_ref[0:rows, lanes] = own
+        ext_ref[rows:columns, lanes] = mm(halo_scr[...], proj_ref[:, lanes], (1, 0)).astype(BF16)
+        ext = ext_ref[:, lanes]
+        parts = three_parts(src_ref[head : head + 1, :] * (1.0 / LN2))
+        vectors = jnp.concatenate([jnp.broadcast_to(part, (LANES, width)) for part in parts], axis=0)
+        source = mm(ext, vectors, (1, 1))
+        source_ref[head] = source[:, :LANES] + source[:, LANES : 2 * LANES] + source[:, 2 * LANES :]
+        parts = three_parts(dst_ref[head : head + 1, :] * (1.0 / LN2))
+        vectors = jnp.concatenate([jnp.broadcast_to(part, (16, width)) for part in parts], axis=0)
+        target = mm(vectors, own, (1, 1))
+        target = target[0:8] + target[16:24] + target[32:40]
+        target_ref[head] = target
+        target = target[0:1]
+
+        def score(index, highest, head=head, target=target):
+            where = pl.ds(pl.multiple_of(index * CHUNK, CHUNK), CHUNK)
+            value = repeat_lanes(source_ref[head, where, :], rows) + target
+            small = jnp.exp2(-jnp.abs(value))
+            result = jnp.maximum(value, 0.2 * value) + (0.8 / LN2) * jnp.log(1.0 + small) + count_ref[where, :]
+            score_scr[where, :] = result
+            return jnp.maximum(highest, jnp.max(fold_rows(result), axis=0))
+
+        highest = lax.fori_loop(0, columns // CHUNK, score, jnp.full((8, rows), NEG, F32), unroll=2)
+        highest = jnp.max(highest, axis=0, keepdims=True)
+
+        def weigh(index, carry, head=head, highest=highest):
+            where = pl.ds(pl.multiple_of(index * CHUNK, CHUNK), CHUNK)
+            weight_ref[head, where, :] = jnp.exp2(score_scr[where, :] - highest).astype(BF16)
+            return carry
+
+        lax.fori_loop(0, columns // CHUNK, weigh, 0, unroll=2)
+        wide = jnp.concatenate([ext, jnp.ones((columns, LANES), BF16)], axis=1)
+        summed = mm(weight_ref[head], wide, (0, 0))
+        scale = 1.0 / summed[:, width:]
+        scale_ref[head] = scale
+        pre = summed[:, :width] * repeat_lanes(scale, width) + skip_ref[:, lanes] + bias_ref[:, lanes]
+        pre_ref[:, lanes] = pre
+        act = jnp.where(pre > 0, pre, jnp.exp(jnp.minimum(pre, 0.0)) - 1.0)
+        cot = jnp.where(real, pad_rows(cot_ref[:, lanes].astype(F32), rows), 0.0)
+        mean = jnp.sum(jnp.where(real, act, 0.0), axis=0, keepdims=True) / nodes
+        centred = jnp.where(real, act - mean, 0.0)
+        stats_ref[0:1, lanes] = jnp.broadcast_to(nodes, mean.shape)
+        stats_ref[1:2, lanes] = mean
+        stats_ref[2:3, lanes] = jnp.sum(centred * centred, axis=0, keepdims=True)
+        stats_ref[3:4, lanes] = jnp.sum(cot, axis=0, keepdims=True)
+        stats_ref[4:5, lanes] = jnp.sum(cot * centred, axis=0, keepdims=True)
 
 
 def merged(first, second):
@@ -550,18 +547,11 @@
         name="project",
     )(in_hbm(feats), in_hbm(w_proj), in_hbm(w_skip), in_hbm(neighbours.T), in_hbm(edge_mask.T))
 
+    vmem = pl.BlockSpec(memory_space=pltpu.VMEM)
+    anywhere = pl.BlockSpec(memory_space=pl.ANY)
     ext, weight, source, target, scale, pre, stats, halo_flipped = pl.pallas_call(
         attend_kernel,
-        grid=(heads,),
-        in_specs=[
-            by_head(rows), whole(halo_pad, depth), whole(halo_pad, depth), by_head(depth), by_head(rows),
-            whole(columns, rows), whole(heads, width), whole(heads, width), by_head(1), by_head(node_rows),
-            whole(1, node_rows),
-        ],
-        out_specs=[
-            by_head(columns), stacked(columns, rows), stacked(columns, LANES), stacked(8, rows), stacked(rows, LANES),
-            by_head(rows), by_head(8), whole(depth, columns - rows),
-        ],
+        in_specs=[vmem] * 11,
         out_shape=[
             shape_of((columns, concat), BF16),
             shape_of((heads, columns, rows), BF16),
@@ -573,10 +563,10 @@
             shape_of((depth, columns - rows), BF16),
         ],
         scratch_shapes=[pltpu.VMEM((columns - rows, depth), BF16), pltpu.VMEM((columns, rows), F32)],
-        compiler_params=params(),
+        compiler_params=params(8),
         cost_estimate=cost(8),
         name="attend",
-    )(zq, near, far, in_hbm(w_proj), skip, count, attn_src, attn_dst, bias2, in_hbm(cotangent), mask)
+    )(zq, near, far, w_proj, skip, count, attn_src, attn_dst, bias2, cotangent, mask)
 
     for which in range(bits - 1):
         stats = pl.pallas_call(
@@ -588,8 +578,6 @@
         )(stats, swapped(stats, 1 << which))
     other = swapped(stats, 1 << (bits - 1))
 
-    vmem = pl.BlockSpec(memory_space=pltpu.VMEM)
-    anywhere = pl.BlockSpec(memory_space=pl.ANY)
     half_grad = shape_of((2, depth, width), BF16)
     output, dskip, skip_send, skip_keep, small, gain_grad, shift_grad = pl.pallas_call(
         functools.partial(norm_kernel, last_bit=bits - 1),

time: 130 us -> 128 us (0.985)
  Pallas kernels: 40.4 us -> 38.7 us
    pallas_call x1, Pallas kernels: 8.62 us -> 6.52 us  [per_device(): pl.pallas_call(attend_kernel, in_specs=[vmem] * 11, out_shape=[shape_of((...]
  transfers between devices with their start and end apart: 40 -> 40, of which waited for: 17 -> 17; matrix products, arithmetic and copies ran while one was open for 0% -> 0% of each run, Pallas kernels for 19% -> 20%
where the time goes in v5:
time: 128 us
  starting transfers between devices  49.3 us (39%)
  Pallas kernels  38.7 us (30%)
  waiting for transfers between devices  38.7 us (30%)
    ppermute x38, starting transfers between devices, swapped(): lax.ppermute(value, AXES, [(source, source ^ distance) for source in rang...  48 us
    ppermute x38, waiting for transfers between devices, swapped(): lax.ppermute(value, AXES, [(source, source ^ distance) for source in rang...  38.7 us
    pallas_call x2, Pallas kernels, backward(): pl.pallas_call(functools.partial(back_kernel, part=part), in_specs=[vmem]...  8.12 us
    pallas_call x1, Pallas kernels, per_device(): pl.pallas_call(functools.partial(project_kernel, halo=halo), grid=(heads,...  6.71 us
    pallas_call x1, Pallas kernels, per_device(): pl.pallas_call(attend_kernel, in_specs=[vmem] * 11, out_shape=[shape_of((...  6.52 us
    pallas_call x4, Pallas kernels, assemble(): pl.pallas_call(functools.partial(assemble_kernel, first=first, pieces=len...  6.46 us
    pallas_call x1, Pallas kernels, per_device(): pl.pallas_call(functools.partial(norm_kernel, last_bit=bits - 1), in_spec...  3.48 us
  transfers between devices with their start and end apart: 40, of which 17 were waited for; matrix products, arithmetic and copies ran while one was open for 0% of the time, Pallas kernels for 20%

profile of v5, /device:TPU:0, one launch (start us, length us, event | category | flops | bytes accessed | tf_op | source)
XLA Modules:
  0.0 128.1 jit_solution(12463645110727328189)
XLA Ops:
  3.5 6.7 %project.1 = (bf16[384,1024]{1,0:T(8,128)(2,1)S(1)}, f32[384,1024]{1,0:T(8,128)S(1)}, f32[512,384]{1,0:T(8,128)S(1)}, bf16[1024,384]{1,0:T(8,128)(2,1)S(1)}) custom-call(bf16[376,1024]{1,0:T(8,128)(2,1)} %feats_ref.3, bf16[1024,1024]{1,0:T(8,128)(2,1)} %proj_ref.7, bf16[1024,1024]{1,0:T(8,128)(2,1)} %skip_ref.1, s32[16,376]{1,0:T(8,128)} %bitcast.11, ...), custom_call_target="tpu_custom_call" | custom-call | flops 5500000256 | bytes 5000000 | tf_op jit(solution)/shard_map/project/pallas_call | solution.py:531
  10.3 6.5 %attend.1 = (bf16[512,1024]{1,0:T(8,128)(2,1)S(1)}, bf16[4,512,384]{2,1,0:T(8,128)(2,1)S(1)}, f32[4,512,128]{2,1,0:T(8,128)S(1)}, f32[4,8,384]{2,1,0:T(8,128)S(1...) custom-call(bf16[384,1024]{1,0:T(8,128)(2,1)S(1)} %get-tuple-element, ...), custom_call_target="tpu_custom_call" | custom-call | flops 8800000000 | bytes 8000000 | tf_op jit(solution)/shard_map/attend/pallas_call | solution.py:552
  16.9 4.0 %collective-permute-start.2 = (f32[8,1024]{1,0:T(8,128)S(1)}, f32[8,1024]{1,0:T(8,128)S(1)}, u32[]{:S(2)}, u32[]{:S(2)}) collective-permute-start(f32[8,1024]{1,0:T(8,128)S(1)} %get-tuple-element.76.mine_ref), channel_id=1, source_target_pairs={{0,1},{1,0},{2,3},{3,2},{4,5},{5,4},{6,7},{7,6},{8,9},{9,8},{10,11... | collective-permute-start | bytes 98312 | tf_op jit(solution)/shard_map/ppermute | solution.py:507
  23.2 2.5 %collective-permute-done.3.other_ref = f32[8,1024]{1,0:T(8,128)S(1)} collective-permute-done((f32[8,1024]{1,0:T(8,128)S(1)}, f32[8,1024]{1,0:T(8,128)S(1)}, u32[]{:S(2)}, u32[]{:S(2)}) %collective-permute-start.3) | collective-permute-done | bytes 32800 | tf_op jit(solution)/shard_map/ppermute | solution.py:507
  25.8 1.8 %collective-permute-start.4 = (f32[8,1024]{1,0:T(8,128)S(1)}, f32[8,1024]{1,0:T(8,128)S(1)}, u32[]{:S(2)}, u32[]{:S(2)}) collective-permute-start(f32[8,1024]{1,0:T(8,128)S(1)} %merge.5.mine_ref), channel_id=1, source_target_pairs={{0,4},{1,5},{2,6},{3,7},{4,0},{5,1},{6,2},{7,3},{8,12},{9,13},{10,... | collective-permute-start | bytes 98312 | tf_op jit(solution)/shard_map/ppermute | solution.py:507
  27.6 2.1 %collective-permute-done.4.other_ref = f32[8,1024]{1,0:T(8,128)S(1)} collective-permute-done((f32[8,1024]{1,0:T(8,128)S(1)}, f32[8,1024]{1,0:T(8,128)S(1)}, u32[]{:S(2)}, u32[]{:S(2)}) %collective-permute-start.4) | collective-permute-done | bytes 32800 | tf_op jit(solution)/shard_map/ppermute | solution.py:507
  29.8 2.8 %collective-permute-start.5 = (f32[8,1024]{1,0:T(8,128)S(1)}, f32[8,1024]{1,0:T(8,128)S(1)}, u32[]{:S(2)}, u32[]{:S(2)}) collective-permute-start(f32[8,1024]{1,0:T(8,128)S(1)} %merge.6.mine_ref), channel_id=1, source_target_pairs={{0,8},{1,9},{2,10},{3,11},{4,12},{5,13},{6,14},{7,15},{8,0},{9,1},... | collective-permute-start | bytes 98312 | tf_op jit(solution)/shard_map/ppermute | solution.py:507
  32.6 1.9 %collective-permute-done.5.other_ref = f32[8,1024]{1,0:T(8,128)S(1)} collective-permute-done((f32[8,1024]{1,0:T(8,128)S(1)}, f32[8,1024]{1,0:T(8,128)S(1)}, u32[]{:S(2)}, u32[]{:S(2)}) %collective-permute-start.5) | collective-permute-done | bytes 32800 | tf_op jit(solution)/shard_map/ppermute | solution.py:507
  34.5 3.1 %collective-permute-start.6 = (f32[8,1024]{1,0:T(8,128)S(1)}, f32[8,1024]{1,0:T(8,128)S(1)}, u32[]{:S(2)}, u32[]{:S(2)}) collective-permute-start(f32[8,1024]{1,0:T(8,128)S(1)} %merge.7.stats_ref), channel_id=1, source_target_pairs={{0,16},{1,17},{2,18},{3,19},{4,20},{5,21},{6,22},{7,23},{8,24},{9,... | collective-permute-start | bytes 98312 | tf_op jit(solution)/shard_map/ppermute | solution.py:507
  37.6 1.9 %collective-permute-done.6.other_ref = f32[8,1024]{1,0:T(8,128)S(1)} collective-permute-done((f32[8,1024]{1,0:T(8,128)S(1)}, f32[8,1024]{1,0:T(8,128)S(1)}, u32[]{:S(2)}, u32[]{:S(2)}) %collective-permute-start.6) | collective-permute-done | bytes 32800 | tf_op jit(solution)/shard_map/ppermute | solution.py:507
  39.5 3.5 %norm.1 = (bf16[376,1024]{1,0:T(8,128)(2,1)}, bf16[384,1024]{1,0:T(8,128)(2,1)S(1)}, bf16[2,1024,256]{2,1,0:T(8,128)(2,1)S(1)}, bf16[2,1024,256]{2,1,0:T(8,128)(...) custom-call(f32[384,1024]{1,0:T(8,128)S(1)} %get-tuple-element.75.pre_ref, ...), custom_call_target="tpu_custom_call" | custom-call | flops 110000000 | bytes 100000 | tf_op jit(solution)/shard_map/norm/pallas_call | solution.py:582
  43.1 3.9 %back.2 = (bf16[2,1040,256]{2,1,0:T(8,128)(2,1)S(1)}, bf16[384,512]{1,0:T(8,128)(2,1)S(1)}, bf16[48,512]{1,0:T(8,128)(2,1)S(1)}, bf16[48,512]{1,0:T(8,128)(2,1)S(1)}) custom-call(bf16[4,512,384]{2,1,0:T(8,128)(2,1)S(1)} %get-tuple-element.79.weight_ref, f32[4,512,128]{2,1,0:T(8,128)S(1)} %get-tuple-element.80.source_ref, ...), custom_call_target="tpu_custom_call" | custom-call | flops 110000000 | bytes 100000 | tf_op jit(solution)/shard_map/back/pallas_call | solution.py:602
  51.4 4.2 %back.3 = (bf16[2,1040,256]{2,1,0:T(8,128)(2,1)S(1)}, bf16[384,512]{1,0:T(8,128)(2,1)S(1)}, bf16[48,1024]{1,0:T(8,128)(2,1)S(1)}, bf16[48,1024]{1,0:T(8,128)(2,1)S(1)}) custom-call(bf16[4,512,384]{2,1,0:T(8,128)(2,1)S(1)} %get-tuple-element.79.weight_ref, f32[4,512,128]{2,1,0:T(8,128)S(1)} %get-tuple-element.80.source_ref, ...), custom_call_target="tpu_custom_call" | custom-call | flops 110000000 | bytes 100000 | tf_op jit(solution)/shard_map/back/pallas_call | solution.py:602
  59.4 4.8 %collective-permute-done.29.refs_3_ = bf16[2,256,256]{2,1,0:T(8,128)(2,1)S(1)} collective-permute-done((bf16[2,256,256]{2,1,0:T(8,128)(2,1)S(1)}, bf16[2,256,256]{2,1,0:T(8,128)(2,1)S(1)}, u32[]{:S(2)}, u32[]{:S(2)}) %collective-permute-start.29) | collective-permute-done | bytes 262176 | tf_op jit(solution)/shard_map/ppermute | solution.py:507
  64.4 2.0 %collective-permute-start.30 = (bf16[2,128,256]{2,1,0:T(8,128)(2,1)S(1)}, bf16[2,128,256]{2,1,0:T(8,128)(2,1)S(1)}, u32[]{:S(2)}, u32[]{:S(2)}) collective-permute-start(bf16[2,128,256]{2,1,0:T(8,128)(2,1)S(1)} %get-tuple-element.118), channel_id=1, source_target_pairs={{0,8},{1,9},{2,10},{3,11},{4,12},{5,13},{6,14},{7,15},{8,0},{9,1},... | collective-permute-start | bytes 393224 | tf_op jit(solution)/shard_map/ppermute | solution.py:507
  66.3 3.1 %collective-permute-done.30.other_ref = bf16[2,128,256]{2,1,0:T(8,128)(2,1)S(1)} collective-permute-done((bf16[2,128,256]{2,1,0:T(8,128)(2,1)S(1)}, bf16[2,128,256]{2,1,0:T(8,128)(2,1)S(1)}, u32[]{:S(2)}, u32[]{:S(2)}) %collective-permute-start.30) | collective-permute-done | bytes 131104 | tf_op jit(solution)/shard_map/ppermute | solution.py:507
  69.4 3.5 %collective-permute-start.31 = (bf16[2,64,256]{2,1,0:T(8,128)(2,1)S(1)}, bf16[2,64,256]{2,1,0:T(8,128)(2,1)S(1)}, u32[]{:S(2)}, u32[]{:S(2)}) collective-permute-start(bf16[2,64,256]{2,1,0:T(8,128)(2,1)S(1)} %get-tuple-element.120), channel_id=1, source_target_pairs={{0,16},{1,17},{2,18},{3,19},{4,20},{5,21},{6,22},{7,23},{8,24},{9,... | collective-permute-start | bytes 196616 | tf_op jit(solution)/shard_map/ppermute | solution.py:507
  73.0 2.0 %collective-permute-done.11.refs_3_ = bf16[2,272,256]{2,1,0:T(8,128)(2,1)S(1)} collective-permute-done((bf16[2,272,256]{2,1,0:T(8,128)(2,1)S(1)}, bf16[2,272,256]{2,1,0:T(8,128)(2,1)S(1)}, u32[]{:S(2)}, u32[]{:S(2)}) %collective-permute-start.11) | collective-permute-done | bytes 278560 | tf_op jit(solution)/shard_map/ppermute | solution.py:507
  75.1 3.0 %collective-permute-start.14 = (bf16[2,80,256]{2,1,0:T(8,128)(2,1)S(1)}, bf16[2,80,256]{2,1,0:T(8,128)(2,1)S(1)}, u32[]{:S(2)}, u32[]{:S(2)}) collective-permute-start(bf16[2,80,256]{2,1,0:T(8,128)(2,1)S(1)} %get-tuple-element.105), channel_id=1, source_target_pairs={{0,16},{1,17},{2,18},{3,19},{4,20},{5,21},{6,22},{7,23},{8,24},{9,... | collective-permute-start | bytes 245768 | tf_op jit(solution)/shard_map/ppermute | solution.py:507
  79.0 4.4 %collective-permute-start.15 = (bf16[2,80,256]{2,1,0:T(8,128)(2,1)S(1)}, bf16[2,80,256]{2,1,0:T(8,128)(2,1)S(1)}, u32[]{:S(2)}, u32[]{:S(2)}) collective-permute-start(bf16[2,80,256]{2,1,0:T(8,128)(2,1)S(1)} %get-tuple-element.106), channel_id=1, source_target_pairs={{0,8},{1,9},{2,10},{3,11},{4,12},{5,13},{6,14},{7,15},{8,0},{9,1},... | collective-permute-start | bytes 245768 | tf_op jit(solution)/shard_map/ppermute | solution.py:507
  83.8 3.9 %collective-permute-start.16 = (bf16[2,80,256]{2,1,0:T(8,128)(2,1)S(1)}, bf16[2,80,256]{2,1,0:T(8,128)(2,1)S(1)}, u32[]{:S(2)}, u32[]{:S(2)}) collective-permute-start(bf16[2,80,256]{2,1,0:T(8,128)(2,1)S(1)} %get-tuple-element.107), channel_id=1, source_target_pairs={{0,24},{1,25},{2,26},{3,27},{4,28},{5,29},{6,30},{7,31},{8,16},{9,... | collective-permute-start | bytes 245768 | tf_op jit(solution)/shard_map/ppermute | solution.py:507
  87.8 3.7 %collective-permute-done.16.refs_3_ = bf16[2,80,256]{2,1,0:T(8,128)(2,1)S(1)} collective-permute-done((bf16[2,80,256]{2,1,0:T(8,128)(2,1)S(1)}, bf16[2,80,256]{2,1,0:T(8,128)(2,1)S(1)}, u32[]{:S(2)}, u32[]{:S(2)}) %collective-permute-start.16) | collective-permute-done | bytes 81952 | tf_op jit(solution)/shard_map/ppermute | solution.py:507
  91.7 1.7 %collective-permute-done.33.other_ref = bf16[2,128,256]{2,1,0:T(8,128)(2,1)S(1)} collective-permute-done((bf16[2,128,256]{2,1,0:T(8,128)(2,1)S(1)}, bf16[2,128,256]{2,1,0:T(8,128)(2,1)S(1)}, u32[]{:S(2)}, u32[]{:S(2)}) %collective-permute-start.33) | collective-permute-done | bytes 131104 | tf_op jit(solution)/shard_map/ppermute | solution.py:507
  93.9 1.9 %collective-permute-start.35 = (bf16[256,256]{1,0:T(8,128)(2,1)S(1)}, bf16[256,256]{1,0:T(8,128)(2,1)S(1)}, u32[]{:S(2)}, u32[]{:S(2)}) collective-permute-start(bf16[256,256]{1,0:T(8,128)(2,1)S(1)} %get-tuple-element.122.refs_1_), channel_id=1, source_target_pairs={{0,4},{1,5},{2,6},{3,7},{4,0},{5,1},{6,2},{7,3},{8,12},{9,13},{10,... | collective-permute-start | bytes 393224 | tf_op jit(solution)/shard_map/ppermute | solution.py:507
  95.8 1.8 %collective-permute-done.17.other_ref = bf16[2,64,256]{2,1,0:T(8,128)(2,1)S(1)} collective-permute-done((bf16[2,64,256]{2,1,0:T(8,128)(2,1)S(1)}, bf16[2,64,256]{2,1,0:T(8,128)(2,1)S(1)}, u32[]{:S(2)}, u32[]{:S(2)}) %collective-permute-start.17) | collective-permute-done | bytes 65568 | tf_op jit(solution)/shard_map/ppermute | solution.py:507
  98.9 2.0 %collective-permute-start.36 = (bf16[512,256]{1,0:T(8,128)(2,1)S(1)}, bf16[512,256]{1,0:T(8,128)(2,1)S(1)}, u32[]{:S(2)}, u32[]{:S(2)}) collective-permute-start(bf16[512,256]{1,0:T(8,128)(2,1)S(1)} %get-tuple-element.123.half_one), channel_id=1, source_target_pairs={{0,4},{1,5},{2,6},{3,7},{4,0},{5,1},{6,2},{7,3},{8,12},{9,13},{10,... | collective-permute-start | bytes 786440 | tf_op jit(solution)/shard_map/ppermute | solution.py:507
  101.0 1.6 %collective-permute-done.18.other_ref = bf16[2,128,256]{2,1,0:T(8,128)(2,1)S(1)} collective-permute-done((bf16[2,128,256]{2,1,0:T(8,128)(2,1)S(1)}, bf16[2,128,256]{2,1,0:T(8,128)(2,1)S(1)}, u32[]{:S(2)}, u32[]{:S(2)}) %collective-permute-start.18) | collective-permute-done | bytes 131104 | tf_op jit(solution)/shard_map/ppermute | solution.py:507
  104.4 1.7 %collective-permute-start.21 = (bf16[2,256,256]{2,1,0:T(8,128)(2,1)S(1)}, bf16[2,256,256]{2,1,0:T(8,128)(2,1)S(1)}, u32[]{:S(2)}, u32[]{:S(2)}) collective-permute-start(bf16[2,256,256]{2,1,0:T(8,128)(2,1)S(1)} %p_join.3.refs_0_), channel_id=1, source_target_pairs={{0,2},{1,3},{2,0},{3,1},{4,6},{5,7},{6,4},{7,5},{8,10},{9,11},{10,... | collective-permute-start | bytes 786440 | tf_op jit(solution)/shard_map/ppermute | solution.py:507
  106.2 2.0 %collective-permute-done.36.far_one = bf16[512,256]{1,0:T(8,128)(2,1)S(1)} collective-permute-done((bf16[512,256]{1,0:T(8,128)(2,1)S(1)}, bf16[512,256]{1,0:T(8,128)(2,1)S(1)}, u32[]{:S(2)}, u32[]{:S(2)}) %collective-permute-start.36) | collective-permute-done | bytes 262176 | tf_op jit(solution)/shard_map/ppermute | solution.py:507
  108.2 7.3 %collective-permute-done.37.far_two = bf16[512,256]{1,0:T(8,128)(2,1)S(1)} collective-permute-done((bf16[512,256]{1,0:T(8,128)(2,1)S(1)}, bf16[512,256]{1,0:T(8,128)(2,1)S(1)}, u32[]{:S(2)}, u32[]{:S(2)}) %collective-permute-start.37) | collective-permute-done | bytes 262176 | tf_op jit(solution)/shard_map/ppermute | solution.py:507
  116.2 1.8 %features.1.total_ref = f32[384,1024]{1,0:T(8,128)S(1)} custom-call(bf16[384,512]{1,0:T(8,128)(2,1)S(1)} %get-tuple-element.87.own_one, bf16[384,512]{1,0:T(8,128)(2,1)S(1)} %get-tuple-element.94.own_two, bf16[384,1024]{1,0:T(8,128)(2,1)S(1)} %get-tuple-element.84.dskip_ref, bf16[1024,1024]{1,0:T(8,128)(2,1)S(1)} %copy-done, bf16[1024,1024]{1,0:T(8,128)(2,1)S(1)} %copy-done.1), custom_call_target="tpu_custom_call" | custom-call | flops 110000000 | bytes 100000 | tf_op jit(solution)/shard_map/features/pallas_call | solution.py:713
  119.2 2.1 %features_halo.1 = bf16[376,1024]{1,0:T(8,128)(2,1)} custom-call(f32[384,1024]{1,0:T(8,128)S(1)} %features.1.total_ref, bf16[48,1024]{1,0:T(8,128)(2,1)S(1)} %collective-permute-done.12.near_ref.refs_4_, bf16[48,1024]{1,0:T(8,128)(2,1)S(1)} %collective-permute-done.13.far_ref.refs_5_, s32[1,2,47]{2,1,0:T(2,128)S(1)} %copy-done.7, bf16[1024,1024]{1,0:T(8,128)(2,1)S(1)} %copy-done), custom_call_target="tpu_custom_call" | custom-call | flops 110000000 | bytes 100000 | tf_op jit(solution)/shard_map/features_halo/pallas_call | solution.py:740
  (99 shorter events, 27.5 us)
Async XLA Ops:
  2.2 8.0 %collective-permute-start = (bf16[48,1024]{1,0:T(8,128)(2,1)S(1)}, bf16[48,1024]{1,0:T(8,128)(2,1)S(1)}, u32[]{:S(2)}, u32[]{:S(2)}) collective-permute-start(bf16[48,1024]{1,0:T(8,128)(2,1)S(1)} %get-tuple-element.71), channel_id=1, source_target_pairs={{0,1},{1,0},{2,3},{3,2},{4,5},{5,4},{6,7},{7,6},{8,9},{9,8},{10,11... | collective-permute-start | bytes 294920 | tf_op jit(solution)/shard_map/ppermute | solution.py:507
  2.8 7.5 %collective-permute-start.1 = (bf16[48,1024]{1,0:T(8,128)(2,1)S(1)}, bf16[48,1024]{1,0:T(8,128)(2,1)S(1)}, u32[]{:S(2)}, u32[]{:S(2)}) collective-permute-start(bf16[48,1024]{1,0:T(8,128)(2,1)S(1)} %get-tuple-element.72), channel_id=1, source_target_pairs={{1,2},{3,4},{5,6},{7,8},{9,10},{11,12},{13,14},{15,16},{17,18},{19... | collective-permute-start | bytes 294920 | tf_op jit(solution)/shard_map/ppermute | solution.py:504
  47.0 8.5 %collective-permute-start.8 = (bf16[2,1040,256]{2,1,0:T(8,128)(2,1)S(1)}, bf16[2,1040,256]{2,1,0:T(8,128)(2,1)S(1)}, u32[]{:S(2)}, u32[]{:S(2)}) collective-permute-start(bf16[2,1040,256]{2,1,0:T(8,128)(2,1)S(1)} %get-tuple-element.92.outs_0_), channel_id=1, source_target_pairs={{0,1},{1,0},{2,3},{3,2},{4,5},{5,4},{6,7},{7,6},{8,9},{9,8},{10,11... | collective-permute-start | bytes 3194888 | tf_op jit(solution)/shard_map/ppermute | solution.py:507
  47.8 10.3 %collective-permute-start.27 = (bf16[2,256,256]{2,1,0:T(8,128)(2,1)S(1)}, bf16[2,256,256]{2,1,0:T(8,128)(2,1)S(1)}, u32[]{:S(2)}, u32[]{:S(2)}) collective-permute-start(bf16[2,256,256]{2,1,0:T(8,128)(2,1)S(1)} %get-tuple-element.114), channel_id=1, source_target_pairs={{0,2},{1,3},{2,0},{3,1},{4,6},{5,7},{6,4},{7,5},{8,10},{9,11},{10,... | collective-permute-start | bytes 786440 | tf_op jit(solution)/shard_map/ppermute | solution.py:507
  48.5 10.9 %collective-permute-start.28 = (bf16[2,256,256]{2,1,0:T(8,128)(2,1)S(1)}, bf16[2,256,256]{2,1,0:T(8,128)(2,1)S(1)}, u32[]{:S(2)}, u32[]{:S(2)}) collective-permute-start(bf16[2,256,256]{2,1,0:T(8,128)(2,1)S(1)} %get-tuple-element.115), channel_id=1, source_target_pairs={{0,4},{1,5},{2,6},{3,7},{4,0},{5,1},{6,2},{7,3},{8,12},{9,13},{10,... | collective-permute-start | bytes 786440 | tf_op jit(solution)/shard_map/ppermute | solution.py:507
  50.1 14.2 %collective-permute-start.29 = (bf16[2,256,256]{2,1,0:T(8,128)(2,1)S(1)}, bf16[2,256,256]{2,1,0:T(8,128)(2,1)S(1)}, u32[]{:S(2)}, u32[]{:S(2)}) collective-permute-start(bf16[2,256,256]{2,1,0:T(8,128)(2,1)S(1)} %get-tuple-element.116), channel_id=1, source_target_pairs={{0,6},{1,7},{2,4},{3,5},{4,2},{5,3},{6,0},{7,1},{8,14},{9,15},{10,... | collective-permute-start | bytes 786440 | tf_op jit(solution)/shard_map/ppermute | solution.py:507
  55.9 17.1 %collective-permute-start.9 = (bf16[2,272,256]{2,1,0:T(8,128)(2,1)S(1)}, bf16[2,272,256]{2,1,0:T(8,128)(2,1)S(1)}, u32[]{:S(2)}, u32[]{:S(2)}) collective-permute-start(bf16[2,272,256]{2,1,0:T(8,128)(2,1)S(1)} %get-tuple-element.98), channel_id=1, source_target_pairs={{0,2},{1,3},{2,0},{3,1},{4,6},{5,7},{6,4},{7,5},{8,10},{9,11},{10,... | collective-permute-start | bytes 835592 | tf_op jit(solution)/shard_map/ppermute | solution.py:507
  56.6 16.4 %collective-permute-start.10 = (bf16[2,272,256]{2,1,0:T(8,128)(2,1)S(1)}, bf16[2,272,256]{2,1,0:T(8,128)(2,1)S(1)}, u32[]{:S(2)}, u32[]{:S(2)}) collective-permute-start(bf16[2,272,256]{2,1,0:T(8,128)(2,1)S(1)} %get-tuple-element.99), channel_id=1, source_target_pairs={{0,4},{1,5},{2,6},{3,7},{4,0},{5,1},{6,2},{7,3},{8,12},{9,13},{10,... | collective-permute-start | bytes 835592 | tf_op jit(solution)/shard_map/ppermute | solution.py:507
  58.1 16.8 %collective-permute-start.11 = (bf16[2,272,256]{2,1,0:T(8,128)(2,1)S(1)}, bf16[2,272,256]{2,1,0:T(8,128)(2,1)S(1)}, u32[]{:S(2)}, u32[]{:S(2)}) collective-permute-start(bf16[2,272,256]{2,1,0:T(8,128)(2,1)S(1)} %get-tuple-element.100), channel_id=1, source_target_pairs={{0,6},{1,7},{2,4},{3,5},{4,2},{5,3},{6,0},{7,1},{8,14},{9,15},{10,... | collective-permute-start | bytes 835592 | tf_op jit(solution)/shard_map/ppermute | solution.py:507
  64.4 5.0 %collective-permute-start.30 = (bf16[2,128,256]{2,1,0:T(8,128)(2,1)S(1)}, bf16[2,128,256]{2,1,0:T(8,128)(2,1)S(1)}, u32[]{:S(2)}, u32[]{:S(2)}) collective-permute-start(bf16[2,128,256]{2,1,0:T(8,128)(2,1)S(1)} %get-tuple-element.118), channel_id=1, source_target_pairs={{0,8},{1,9},{2,10},{3,11},{4,12},{5,13},{6,14},{7,15},{8,0},{9,1},... | collective-permute-start | bytes 393224 | tf_op jit(solution)/shard_map/ppermute | solution.py:507
  69.4 8.6 %collective-permute-start.31 = (bf16[2,64,256]{2,1,0:T(8,128)(2,1)S(1)}, bf16[2,64,256]{2,1,0:T(8,128)(2,1)S(1)}, u32[]{:S(2)}, u32[]{:S(2)}) collective-permute-start(bf16[2,64,256]{2,1,0:T(8,128)(2,1)S(1)} %get-tuple-element.120), channel_id=1, source_target_pairs={{0,16},{1,17},{2,18},{3,19},{4,20},{5,21},{6,22},{7,23},{8,24},{9,... | collective-permute-start | bytes 196616 | tf_op jit(solution)/shard_map/ppermute | solution.py:507
  75.1 12.6 %collective-permute-start.14 = (bf16[2,80,256]{2,1,0:T(8,128)(2,1)S(1)}, bf16[2,80,256]{2,1,0:T(8,128)(2,1)S(1)}, u32[]{:S(2)}, u32[]{:S(2)}) collective-permute-start(bf16[2,80,256]{2,1,0:T(8,128)(2,1)S(1)} %get-tuple-element.105), channel_id=1, source_target_pairs={{0,16},{1,17},{2,18},{3,19},{4,20},{5,21},{6,22},{7,23},{8,24},{9,... | collective-permute-start | bytes 245768 | tf_op jit(solution)/shard_map/ppermute | solution.py:507
  78.1 5.7 %collective-permute-start.32 = (bf16[2,64,256]{2,1,0:T(8,128)(2,1)S(1)}, bf16[2,64,256]{2,1,0:T(8,128)(2,1)S(1)}, u32[]{:S(2)}, u32[]{:S(2)}) collective-permute-start(bf16[2,64,256]{2,1,0:T(8,128)(2,1)S(1)} %s_line.3.mine_ref), channel_id=1, source_target_pairs={{0,16},{1,17},{2,18},{3,19},{4,20},{5,21},{6,22},{7,23},{8,24},{9,... | collective-permute-start | bytes 196616 | tf_op jit(solution)/shard_map/ppermute | solution.py:507
  78.3 13.2 %collective-permute-start.12 = (bf16[48,1024]{1,0:T(8,128)(2,1)S(1)}, bf16[48,1024]{1,0:T(8,128)(2,1)S(1)}, u32[]{:S(2)}, u32[]{:S(2)}) collective-permute-start(bf16[48,1024]{1,0:T(8,128)(2,1)S(1)} %get-tuple-element.102), channel_id=1, source_target_pairs={{0,1},{1,0},{2,3},{3,2},{4,5},{5,4},{6,7},{7,6},{8,9},{9,8},{10,11... | collective-permute-start | bytes 294920 | tf_op jit(solution)/shard_map/ppermute | solution.py:507
  78.3 13.2 %collective-permute-start.13 = (bf16[48,1024]{1,0:T(8,128)(2,1)S(1)}, bf16[48,1024]{1,0:T(8,128)(2,1)S(1)}, u32[]{:S(2)}, u32[]{:S(2)}) collective-permute-start(bf16[48,1024]{1,0:T(8,128)(2,1)S(1)} %get-tuple-element.104), channel_id=1, source_target_pairs={{1,2},{3,4},{5,6},{7,8},{9,10},{11,12},{13,14},{15,16},{17,18},{19... | collective-permute-start | bytes 294920 | tf_op jit(solution)/shard_map/ppermute | solution.py:504
  79.0 8.8 %collective-permute-start.15 = (bf16[2,80,256]{2,1,0:T(8,128)(2,1)S(1)}, bf16[2,80,256]{2,1,0:T(8,128)(2,1)S(1)}, u32[]{:S(2)}, u32[]{:S(2)}) collective-permute-start(bf16[2,80,256]{2,1,0:T(8,128)(2,1)S(1)} %get-tuple-element.106), channel_id=1, source_target_pairs={{0,8},{1,9},{2,10},{3,11},{4,12},{5,13},{6,14},{7,15},{8,0},{9,1},... | collective-permute-start | bytes 245768 | tf_op jit(solution)/shard_map/ppermute | solution.py:507
  83.8 7.8 %collective-permute-start.16 = (bf16[2,80,256]{2,1,0:T(8,128)(2,1)S(1)}, bf16[2,80,256]{2,1,0:T(8,128)(2,1)S(1)}, u32[]{:S(2)}, u32[]{:S(2)}) collective-permute-start(bf16[2,80,256]{2,1,0:T(8,128)(2,1)S(1)} %get-tuple-element.107), channel_id=1, source_target_pairs={{0,24},{1,25},{2,26},{3,27},{4,28},{5,29},{6,30},{7,31},{8,16},{9,... | collective-permute-start | bytes 245768 | tf_op jit(solution)/shard_map/ppermute | solution.py:507
  87.7 5.7 %collective-permute-start.33 = (bf16[2,128,256]{2,1,0:T(8,128)(2,1)S(1)}, bf16[2,128,256]{2,1,0:T(8,128)(2,1)S(1)}, u32[]{:S(2)}, u32[]{:S(2)}) collective-permute-start(bf16[2,128,256]{2,1,0:T(8,128)(2,1)S(1)} %s_join.1.mine_ref), channel_id=1, source_target_pairs={{0,8},{1,9},{2,10},{3,11},{4,12},{5,13},{6,14},{7,15},{8,0},{9,1},... | collective-permute-start | bytes 393224 | tf_op jit(solution)/shard_map/ppermute | solution.py:507
  91.6 5.9 %collective-permute-start.17 = (bf16[2,64,256]{2,1,0:T(8,128)(2,1)S(1)}, bf16[2,64,256]{2,1,0:T(8,128)(2,1)S(1)}, u32[]{:S(2)}, u32[]{:S(2)}) collective-permute-start(bf16[2,64,256]{2,1,0:T(8,128)(2,1)S(1)} %get-tuple-element.108.mine_ref), channel_id=1, source_target_pairs={{0,16},{1,17},{2,18},{3,19},{4,20},{5,21},{6,22},{7,23},{8,24},{9,... | collective-permute-start | bytes 196616 | tf_op jit(solution)/shard_map/ppermute | solution.py:507
  93.4 5.0 %collective-permute-start.34 = (bf16[256,256]{1,0:T(8,128)(2,1)S(1)}, bf16[256,256]{1,0:T(8,128)(2,1)S(1)}, u32[]{:S(2)}, u32[]{:S(2)}) collective-permute-start(bf16[256,256]{1,0:T(8,128)(2,1)S(1)} %get-tuple-element.121.refs_0_), channel_id=1, source_target_pairs={{0,2},{1,3},{2,0},{3,1},{4,6},{5,7},{6,4},{7,5},{8,10},{9,11},{10,... | collective-permute-start | bytes 393224 | tf_op jit(solution)/shard_map/ppermute | solution.py:507
  97.6 5.0 %collective-permute-start.18 = (bf16[2,128,256]{2,1,0:T(8,128)(2,1)S(1)}, bf16[2,128,256]{2,1,0:T(8,128)(2,1)S(1)}, u32[]{:S(2)}, u32[]{:S(2)}) collective-permute-start(bf16[2,128,256]{2,1,0:T(8,128)(2,1)S(1)} %p_join.2.mine_ref), channel_id=1, source_target_pairs={{0,8},{1,9},{2,10},{3,11},{4,12},{5,13},{6,14},{7,15},{8,0},{9,1},... | collective-permute-start | bytes 393224 | tf_op jit(solution)/shard_map/ppermute | solution.py:507
  98.9 9.3 %collective-permute-start.36 = (bf16[512,256]{1,0:T(8,128)(2,1)S(1)}, bf16[512,256]{1,0:T(8,128)(2,1)S(1)}, u32[]{:S(2)}, u32[]{:S(2)}) collective-permute-start(bf16[512,256]{1,0:T(8,128)(2,1)S(1)} %get-tuple-element.123.half_one), channel_id=1, source_target_pairs={{0,4},{1,5},{2,6},{3,7},{4,0},{5,1},{6,2},{7,3},{8,12},{9,13},{10,... | collective-permute-start | bytes 786440 | tf_op jit(solution)/shard_map/ppermute | solution.py:507
  100.9 14.7 %collective-permute-start.37 = (bf16[512,256]{1,0:T(8,128)(2,1)S(1)}, bf16[512,256]{1,0:T(8,128)(2,1)S(1)}, u32[]{:S(2)}, u32[]{:S(2)}) collective-permute-start(bf16[512,256]{1,0:T(8,128)(2,1)S(1)} %get-tuple-element.124.half_two), channel_id=1, source_target_pairs={{0,2},{1,3},{2,0},{3,1},{4,6},{5,7},{6,4},{7,5},{8,10},{9,11},{10,... | collective-permute-start | bytes 786440 | tf_op jit(solution)/shard_map/ppermute | solution.py:507
  102.6 13.0 %collective-permute-start.25 = (bf16[2,256,256]{2,1,0:T(8,128)(2,1)S(1)}, bf16[2,256,256]{2,1,0:T(8,128)(2,1)S(1)}, u32[]{:S(2)}, u32[]{:S(2)}) collective-permute-start(bf16[2,256,256]{2,1,0:T(8,128)(2,1)S(1)} %p_join.3.refs_0_), channel_id=1, source_target_pairs={{0,6},{1,7},{2,4},{3,5},{4,2},{5,3},{6,0},{7,1},{8,14},{9,15},{10,... | collective-permute-start | bytes 786440 | tf_op jit(solution)/shard_map/ppermute | solution.py:507
  103.8 14.8 %collective-permute-start.23 = (bf16[2,256,256]{2,1,0:T(8,128)(2,1)S(1)}, bf16[2,256,256]{2,1,0:T(8,128)(2,1)S(1)}, u32[]{:S(2)}, u32[]{:S(2)}) collective-permute-start(bf16[2,256,256]{2,1,0:T(8,128)(2,1)S(1)} %p_join.3.refs_0_), channel_id=1, source_target_pairs={{0,4},{1,5},{2,6},{3,7},{4,0},{5,1},{6,2},{7,3},{8,12},{9,13},{10,... | collective-permute-start | bytes 786440 | tf_op jit(solution)/shard_map/ppermute | solution.py:507
  104.4 14.3 %collective-permute-start.21 = (bf16[2,256,256]{2,1,0:T(8,128)(2,1)S(1)}, bf16[2,256,256]{2,1,0:T(8,128)(2,1)S(1)}, u32[]{:S(2)}, u32[]{:S(2)}) collective-permute-start(bf16[2,256,256]{2,1,0:T(8,128)(2,1)S(1)} %p_join.3.refs_0_), channel_id=1, source_target_pairs={{0,2},{1,3},{2,0},{3,1},{4,6},{5,7},{6,4},{7,5},{8,10},{9,11},{10,... | collective-permute-start | bytes 786440 | tf_op jit(solution)/shard_map/ppermute | solution.py:507
  108.2 10.9 %collective-permute-start.20 = (bf16[2,256,256]{2,1,0:T(8,128)(2,1)S(1)}, bf16[2,256,256]{2,1,0:T(8,128)(2,1)S(1)}, u32[]{:S(2)}, u32[]{:S(2)}) collective-permute-start(bf16[2,256,256]{2,1,0:T(8,128)(2,1)S(1)} %p_join.3.refs_0_), channel_id=1, source_target_pairs={{0,1},{1,0},{2,3},{3,2},{4,5},{5,4},{6,7},{7,6},{8,9},{9,8},{10,11... | collective-permute-start | bytes 786440 | tf_op jit(solution)/shard_map/ppermute | solution.py:507
  115.6 10.7 %collective-permute-start.38 = (bf16[2,512,256]{2,1,0:T(8,128)(2,1)S(1)}, bf16[2,512,256]{2,1,0:T(8,128)(2,1)S(1)}, u32[]{:S(2)}, u32[]{:S(2)}) collective-permute-start(bf16[2,512,256]{2,1,0:T(8,128)(2,1)S(1)} %get-tuple-element.125.refs_0_), channel_id=1, source_target_pairs={{0,1},{1,0},{2,3},{3,2},{4,5},{5,4},{6,7},{7,6},{8,9},{9,8},{10,11... | collective-permute-start | bytes 1572872 | tf_op jit(solution)/shard_map/ppermute | solution.py:507
  115.7 10.6 %collective-permute-start.39 = (bf16[2,512,256]{2,1,0:T(8,128)(2,1)S(1)}, bf16[2,512,256]{2,1,0:T(8,128)(2,1)S(1)}, u32[]{:S(2)}, u32[]{:S(2)}) collective-permute-start(bf16[2,512,256]{2,1,0:T(8,128)(2,1)S(1)} %get-tuple-element.126.refs_1_), channel_id=1, source_target_pairs={{0,1},{1,0},{2,3},{3,2},{4,5},{5,4},{6,7},{7,6},{8,9},{9,8},{10,11... | collective-permute-start | bytes 1572872 | tf_op jit(solution)/shard_map/ppermute | solution.py:507
  118.6 6.0 %collective-permute-start.26 = (bf16[2,256,256]{2,1,0:T(8,128)(2,1)S(1)}, bf16[2,256,256]{2,1,0:T(8,128)(2,1)S(1)}, u32[]{:S(2)}, u32[]{:S(2)}) collective-permute-start(bf16[2,256,256]{2,1,0:T(8,128)(2,1)S(1)} %collective-permute-done.25.refs_3_), channel_id=1, source_target_pairs={{0,1},{1,0},{2,3},{3,2},{4,5},{5,4},{6,7},{7,6},{8,9},{9,8},{10,11... | collective-permute-start | bytes 786440 | tf_op jit(solution)/shard_map/ppermute | solution.py:507
  118.7 5.9 %collective-permute-start.24 = (bf16[2,256,256]{2,1,0:T(8,128)(2,1)S(1)}, bf16[2,256,256]{2,1,0:T(8,128)(2,1)S(1)}, u32[]{:S(2)}, u32[]{:S(2)}) collective-permute-start(bf16[2,256,256]{2,1,0:T(8,128)(2,1)S(1)} %collective-permute-done.23.refs_2_), channel_id=1, source_target_pairs={{0,1},{1,0},{2,3},{3,2},{4,5},{5,4},{6,7},{7,6},{8,9},{9,8},{10,11... | collective-permute-start | bytes 786440 | tf_op jit(solution)/shard_map/ppermute | solution.py:507
  119.1 5.5 %collective-permute-start.22 = (bf16[2,256,256]{2,1,0:T(8,128)(2,1)S(1)}, bf16[2,256,256]{2,1,0:T(8,128)(2,1)S(1)}, u32[]{:S(2)}, u32[]{:S(2)}) collective-permute-start(bf16[2,256,256]{2,1,0:T(8,128)(2,1)S(1)} %collective-permute-done.21.refs_1_), channel_id=1, source_target_pairs={{0,1},{1,0},{2,3},{3,2},{4,5},{5,4},{6,7},{7,6},{8,9},{9,8},{10,11... | collective-permute-start | bytes 786440 | tf_op jit(solution)/shard_map/ppermute | solution.py:507
  (18 other events, 162.0 us)

commit v6 on v5

--- a/solution.py
+++ b/solution.py
@@ -17,6 +17,7 @@
 CHUNK = 32
 LANES = 128
 MIB = 1024 * 1024
+COSTS = {"p_plane": 0.1, "p_line": 0.5, "p_join": 0.5}
 
 
 def params(mib=24):
@@ -278,7 +279,7 @@
         small_ref[head] = vectors[head]
 
 
-def vectors_kernel(mine_ref, other_ref, src_ref, dst_ref, bias_ref):
+def vectors_kernel(mine_ref, other_ref, dep_ref, src_ref, dst_ref, bias_ref):
     odd = is_odd()
     width = src_ref.shape[1]
     for head in range(4):
@@ -317,7 +318,8 @@
         out_ref[size:, :] = near[...]
 
 
-def plane_join_kernel(half_one, half_two, far_one, far_two, low_ref, high_ref):
+def plane_join_kernel(half_one, half_two, far_one, far_two, *rest):
+    low_ref, high_ref = rest[-2:]
     size = half_one.shape[0] // 2
     low_ref[0] = half_one[...]
     high_ref[0] = far_one[...]
@@ -440,7 +442,7 @@
         place_blocks(grad_ref.at[step], grads.astype(BF16), own_place())
 
 
-def feats_kernel(own_one, own_two, dskip_ref, proj_ref, skip_ref, total_ref):
+def feats_kernel(own_one, own_two, dskip_ref, proj_ref, skip_ref, dep_ref, total_ref):
     width = own_one.shape[1] // 2
     total = mm(dskip_ref[...], skip_ref[...], (1, 1))
     for step in range(4):
@@ -622,7 +624,7 @@
             in_specs=[vmem] * len(arrays) + [anywhere] * len(deps),
             out_shape=[shape_of(shape, BF16) for shape in shapes],
             compiler_params=params(1),
-            cost_estimate=cost(0.1),
+            cost_estimate=cost(COSTS.get(name, 0.1)),
             name=name,
         )(*arrays, *deps)
 
@@ -639,7 +641,7 @@
             out_shape=shapes,
             scratch_shapes=[pltpu.VMEM((4, 2, 8, width), F32)],
             compiler_params=params(1),
-            cost_estimate=cost(0.1),
+            cost_estimate=cost(COSTS.get(name, 0.1)),
             name=name,
         )(*arrays, *deps)
 
@@ -712,15 +714,16 @@
     p_got = over_plane([p_share] * 3)
     feats_total = pl.pallas_call(
         feats_kernel,
-        in_specs=[vmem] * 5,
+        in_specs=[vmem] * 5 + [anywhere],
         out_specs=vmem,
         out_shape=shape_of((rows, depth), F32),
         compiler_params=params(8),
         cost_estimate=cost(0.1),
         name="features",
-    )(own_send, own_keep, dskip, w_proj, w_skip)
+    )(own_send, own_keep, dskip, w_proj, w_skip, s_far[0])
     grad_src, grad_dst, grad_bias = pl.pallas_call(
         vectors_kernel,
+        in_specs=[vmem] * 2 + [anywhere],
         out_shape=[
             jax.ShapeDtypeStruct((heads, width), F32),
             jax.ShapeDtypeStruct((heads, width), F32),
@@ -729,14 +732,7 @@
         compiler_params=params(1),
         cost_estimate=cost(0.1),
         name="vectors",
-    )(small, small_other)
-    p_got = [p_share, *(after(share, grad_src, back_near, back_far, feats_total) for share in p_got)]
-    p_other = [swapped(share, 1) for share in p_got]
-    s_halves = step_call(plane_join_kernel, "s_half", [(2, depth // 2, width)] * 2, [*s_sent, *s_far])
-    s_other = [swapped(half, 1) for half in s_halves]
-    grad_skip = assemble(s_other, 0, assemble(s_halves, 2))
-    grad_proj = assemble(p_other, 0, assemble(p_got, 2))
-
+    )(small, small_other, s_far[0])
     grad_feats = pl.pallas_call(
         feats_halo_kernel,
         in_specs=[vmem] * 5,
@@ -747,6 +743,14 @@
         cost_estimate=cost(0.1),
         name="features_halo",
     )(feats_total, back_near, back_far, send_index, w_proj)
+    p_got = [p_share, *p_got]
+    p_other = [swapped(share, 1) for share in p_got]
+    s_halves = step_call(
+        plane_join_kernel, "s_half", [(2, depth // 2, width)] * 2, [*s_sent, *s_far], [grad_feats, grad_src]
+    )
+    s_other = [swapped(half, 1) for half in s_halves]
+    grad_skip = assemble(s_other, 0, assemble(s_halves, 2))
+    grad_proj = assemble(p_other, 0, assemble(p_got, 2))
 
     return (
         output,

time: 128 us -> 127 us (level)
  waiting for transfers between devices: 38.7 us -> 36.7 us
    ppermute x38, waiting for transfers between devices: 38.7 us -> 36.7 us  [swapped(): lax.ppermute(value, AXES, [(source, source ^ distance) for source in rang...]
  transfers between devices with their start and end apart: 40 -> 40, of which waited for: 17 -> 20; matrix products, arithmetic and copies ran while one was open for 0% -> 0% of each run, Pallas kernels for 20% -> 20%
where the time goes in v6:
time: 127 us; the launch traced here: 126 us
  starting transfers between devices  48.5 us (38%)
  Pallas kernels  38.7 us (30%)
  waiting for transfers between devices  36.7 us (29%)
    ppermute x38, starting transfers between devices, swapped(): lax.ppermute(value, AXES, [(source, source ^ distance) for source in rang...  47.2 us
    ppermute x38, waiting for transfers between devices, swapped(): lax.ppermute(value, AXES, [(source, source ^ distance) for source in rang...  36.7 us
    pallas_call x2, Pallas kernels, backward(): pl.pallas_call(functools.partial(back_kernel, part=part), in_specs=[vmem]...  8.12 us
    pallas_call x1, Pallas kernels, per_device(): pl.pallas_call(functools.partial(project_kernel, halo=halo), grid=(heads,...  6.71 us
    pallas_call x1, Pallas kernels, per_device(): pl.pallas_call(attend_kernel, in_specs=[vmem] * 11, out_shape=[shape_of((...  6.52 us
    pallas_call x4, Pallas kernels, assemble(): pl.pallas_call(functools.partial(assemble_kernel, first=first, pieces=len...  6.46 us
    pallas_call x1, Pallas kernels, per_device(): pl.pallas_call(functools.partial(norm_kernel, last_bit=bits - 1), in_spec...  3.48 us
  transfers between devices with their start and end apart: 40, of which 20 were waited for; matrix products, arithmetic and copies ran while one was open for 0% of the time, Pallas kernels for 20%

profile of v6, /device:TPU:0, one launch (start us, length us, event | category | flops | bytes accessed | tf_op | source)
XLA Modules:
  0.0 126.4 jit_solution(7750932549846526735)
XLA Ops:
  3.5 6.7 %project.1 = (bf16[384,1024]{1,0:T(8,128)(2,1)S(1)}, f32[384,1024]{1,0:T(8,128)S(1)}, f32[512,384]{1,0:T(8,128)S(1)}, bf16[1024,384]{1,0:T(8,128)(2,1)S(1)}) custom-call(bf16[376,1024]{1,0:T(8,128)(2,1)} %feats_ref.3, bf16[1024,1024]{1,0:T(8,128)(2,1)} %proj_ref.7, bf16[1024,1024]{1,0:T(8,128)(2,1)} %skip_ref.1, s32[16,376]{1,0:T(8,128)} %bitcast.11, ...), custom_call_target="tpu_custom_call" | custom-call | flops 5500000256 | bytes 5000000 | tf_op jit(solution)/shard_map/project/pallas_call | solution.py:533
  10.3 6.5 %attend.1 = (bf16[512,1024]{1,0:T(8,128)(2,1)S(1)}, bf16[4,512,384]{2,1,0:T(8,128)(2,1)S(1)}, f32[4,512,128]{2,1,0:T(8,128)S(1)}, f32[4,8,384]{2,1,0:T(8,128)S(1...) custom-call(bf16[384,1024]{1,0:T(8,128)(2,1)S(1)} %get-tuple-element, ...), custom_call_target="tpu_custom_call" | custom-call | flops 8800000000 | bytes 8000000 | tf_op jit(solution)/shard_map/attend/pallas_call | solution.py:554
  16.9 4.0 %collective-permute-start.2 = (f32[8,1024]{1,0:T(8,128)S(1)}, f32[8,1024]{1,0:T(8,128)S(1)}, u32[]{:S(2)}, u32[]{:S(2)}) collective-permute-start(f32[8,1024]{1,0:T(8,128)S(1)} %get-tuple-element.73.mine_ref), channel_id=1, source_target_pairs={{0,1},{1,0},{2,3},{3,2},{4,5},{5,4},{6,7},{7,6},{8,9},{9,8},{10,11... | collective-permute-start | bytes 98312 | tf_op jit(solution)/shard_map/ppermute | solution.py:509
  23.2 2.5 %collective-permute-done.3.other_ref = f32[8,1024]{1,0:T(8,128)S(1)} collective-permute-done((f32[8,1024]{1,0:T(8,128)S(1)}, f32[8,1024]{1,0:T(8,128)S(1)}, u32[]{:S(2)}, u32[]{:S(2)}) %collective-permute-start.3) | collective-permute-done | bytes 32800 | tf_op jit(solution)/shard_map/ppermute | solution.py:509
  25.8 1.8 %collective-permute-start.4 = (f32[8,1024]{1,0:T(8,128)S(1)}, f32[8,1024]{1,0:T(8,128)S(1)}, u32[]{:S(2)}, u32[]{:S(2)}) collective-permute-start(f32[8,1024]{1,0:T(8,128)S(1)} %merge.5.mine_ref), channel_id=1, source_target_pairs={{0,4},{1,5},{2,6},{3,7},{4,0},{5,1},{6,2},{7,3},{8,12},{9,13},{10,... | collective-permute-start | bytes 98312 | tf_op jit(solution)/shard_map/ppermute | solution.py:509
  27.6 2.1 %collective-permute-done.4.other_ref = f32[8,1024]{1,0:T(8,128)S(1)} collective-permute-done((f32[8,1024]{1,0:T(8,128)S(1)}, f32[8,1024]{1,0:T(8,128)S(1)}, u32[]{:S(2)}, u32[]{:S(2)}) %collective-permute-start.4) | collective-permute-done | bytes 32800 | tf_op jit(solution)/shard_map/ppermute | solution.py:509
  29.8 2.8 %collective-permute-start.5 = (f32[8,1024]{1,0:T(8,128)S(1)}, f32[8,1024]{1,0:T(8,128)S(1)}, u32[]{:S(2)}, u32[]{:S(2)}) collective-permute-start(f32[8,1024]{1,0:T(8,128)S(1)} %merge.6.mine_ref), channel_id=1, source_target_pairs={{0,8},{1,9},{2,10},{3,11},{4,12},{5,13},{6,14},{7,15},{8,0},{9,1},... | collective-permute-start | bytes 98312 | tf_op jit(solution)/shard_map/ppermute | solution.py:509
  32.6 1.9 %collective-permute-done.5.other_ref = f32[8,1024]{1,0:T(8,128)S(1)} collective-permute-done((f32[8,1024]{1,0:T(8,128)S(1)}, f32[8,1024]{1,0:T(8,128)S(1)}, u32[]{:S(2)}, u32[]{:S(2)}) %collective-permute-start.5) | collective-permute-done | bytes 32800 | tf_op jit(solution)/shard_map/ppermute | solution.py:509
  34.5 3.1 %collective-permute-start.6 = (f32[8,1024]{1,0:T(8,128)S(1)}, f32[8,1024]{1,0:T(8,128)S(1)}, u32[]{:S(2)}, u32[]{:S(2)}) collective-permute-start(f32[8,1024]{1,0:T(8,128)S(1)} %merge.7.stats_ref), channel_id=1, source_target_pairs={{0,16},{1,17},{2,18},{3,19},{4,20},{5,21},{6,22},{7,23},{8,24},{9,... | collective-permute-start | bytes 98312 | tf_op jit(solution)/shard_map/ppermute | solution.py:509
  37.6 1.9 %collective-permute-done.6.other_ref = f32[8,1024]{1,0:T(8,128)S(1)} collective-permute-done((f32[8,1024]{1,0:T(8,128)S(1)}, f32[8,1024]{1,0:T(8,128)S(1)}, u32[]{:S(2)}, u32[]{:S(2)}) %collective-permute-start.6) | collective-permute-done | bytes 32800 | tf_op jit(solution)/shard_map/ppermute | solution.py:509
  39.5 3.5 %norm.1 = (bf16[376,1024]{1,0:T(8,128)(2,1)}, bf16[384,1024]{1,0:T(8,128)(2,1)S(1)}, bf16[2,1024,256]{2,1,0:T(8,128)(2,1)S(1)}, bf16[2,1024,256]{2,1,0:T(8,128)(...) custom-call(f32[384,1024]{1,0:T(8,128)S(1)} %get-tuple-element.72.pre_ref, ...), custom_call_target="tpu_custom_call" | custom-call | flops 110000000 | bytes 100000 | tf_op jit(solution)/shard_map/norm/pallas_call | solution.py:584
  43.1 3.9 %back.2 = (bf16[2,1040,256]{2,1,0:T(8,128)(2,1)S(1)}, bf16[384,512]{1,0:T(8,128)(2,1)S(1)}, bf16[48,512]{1,0:T(8,128)(2,1)S(1)}, bf16[48,512]{1,0:T(8,128)(2,1)S(1)}) custom-call(bf16[4,512,384]{2,1,0:T(8,128)(2,1)S(1)} %get-tuple-element.76.weight_ref, f32[4,512,128]{2,1,0:T(8,128)S(1)} %get-tuple-element.77.source_ref, ...), custom_call_target="tpu_custom_call" | custom-call | flops 110000000 | bytes 100000 | tf_op jit(solution)/shard_map/back/pallas_call | solution.py:604
  51.4 4.2 %back.3 = (bf16[2,1040,256]{2,1,0:T(8,128)(2,1)S(1)}, bf16[384,512]{1,0:T(8,128)(2,1)S(1)}, bf16[48,1024]{1,0:T(8,128)(2,1)S(1)}, bf16[48,1024]{1,0:T(8,128)(2,1)S(1)}) custom-call(bf16[4,512,384]{2,1,0:T(8,128)(2,1)S(1)} %get-tuple-element.76.weight_ref, f32[4,512,128]{2,1,0:T(8,128)S(1)} %get-tuple-element.77.source_ref, ...), custom_call_target="tpu_custom_call" | custom-call | flops 110000000 | bytes 100000 | tf_op jit(solution)/shard_map/back/pallas_call | solution.py:604
  59.4 4.8 %collective-permute-done.10.refs_3_ = bf16[2,256,256]{2,1,0:T(8,128)(2,1)S(1)} collective-permute-done((bf16[2,256,256]{2,1,0:T(8,128)(2,1)S(1)}, bf16[2,256,256]{2,1,0:T(8,128)(2,1)S(1)}, u32[]{:S(2)}, u32[]{:S(2)}) %collective-permute-start.10) | collective-permute-done | bytes 262176 | tf_op jit(solution)/shard_map/ppermute | solution.py:509
  64.4 2.0 %collective-permute-start.12 = (bf16[2,128,256]{2,1,0:T(8,128)(2,1)S(1)}, bf16[2,128,256]{2,1,0:T(8,128)(2,1)S(1)}, u32[]{:S(2)}, u32[]{:S(2)}) collective-permute-start(bf16[2,128,256]{2,1,0:T(8,128)(2,1)S(1)} %get-tuple-element.98), channel_id=1, source_target_pairs={{0,8},{1,9},{2,10},{3,11},{4,12},{5,13},{6,14},{7,15},{8,0},{9,1},... | collective-permute-start | bytes 393224 | tf_op jit(solution)/shard_map/ppermute | solution.py:509
  66.3 3.1 %collective-permute-done.12.other_ref = bf16[2,128,256]{2,1,0:T(8,128)(2,1)S(1)} collective-permute-done((bf16[2,128,256]{2,1,0:T(8,128)(2,1)S(1)}, bf16[2,128,256]{2,1,0:T(8,128)(2,1)S(1)}, u32[]{:S(2)}, u32[]{:S(2)}) %collective-permute-start.12) | collective-permute-done | bytes 131104 | tf_op jit(solution)/shard_map/ppermute | solution.py:509
  69.4 3.5 %collective-permute-start.13 = (bf16[2,64,256]{2,1,0:T(8,128)(2,1)S(1)}, bf16[2,64,256]{2,1,0:T(8,128)(2,1)S(1)}, u32[]{:S(2)}, u32[]{:S(2)}) collective-permute-start(bf16[2,64,256]{2,1,0:T(8,128)(2,1)S(1)} %get-tuple-element.100), channel_id=1, source_target_pairs={{0,16},{1,17},{2,18},{3,19},{4,20},{5,21},{6,22},{7,23},{8,24},{9,... | collective-permute-start | bytes 196616 | tf_op jit(solution)/shard_map/ppermute | solution.py:509
  73.0 2.0 %collective-permute-done.16.refs_3_ = bf16[2,272,256]{2,1,0:T(8,128)(2,1)S(1)} collective-permute-done((bf16[2,272,256]{2,1,0:T(8,128)(2,1)S(1)}, bf16[2,272,256]{2,1,0:T(8,128)(2,1)S(1)}, u32[]{:S(2)}, u32[]{:S(2)}) %collective-permute-start.16) | collective-permute-done | bytes 278560 | tf_op jit(solution)/shard_map/ppermute | solution.py:509
  75.2 3.1 %collective-permute-start.17 = (bf16[2,64,256]{2,1,0:T(8,128)(2,1)S(1)}, bf16[2,64,256]{2,1,0:T(8,128)(2,1)S(1)}, u32[]{:S(2)}, u32[]{:S(2)}) collective-permute-start(bf16[2,64,256]{2,1,0:T(8,128)(2,1)S(1)} %s_line.3.mine_ref), channel_id=1, source_target_pairs={{0,16},{1,17},{2,18},{3,19},{4,20},{5,21},{6,22},{7,23},{8,24},{9,... | collective-permute-start | bytes 196616 | tf_op jit(solution)/shard_map/ppermute | solution.py:509
  79.1 5.1 %collective-permute-start.25 = (bf16[2,80,256]{2,1,0:T(8,128)(2,1)S(1)}, bf16[2,80,256]{2,1,0:T(8,128)(2,1)S(1)}, u32[]{:S(2)}, u32[]{:S(2)}) collective-permute-start(bf16[2,80,256]{2,1,0:T(8,128)(2,1)S(1)} %get-tuple-element.113), channel_id=1, source_target_pairs={{0,8},{1,9},{2,10},{3,11},{4,12},{5,13},{6,14},{7,15},{8,0},{9,1},... | collective-permute-start | bytes 245768 | tf_op jit(solution)/shard_map/ppermute | solution.py:509
  84.1 2.7 %collective-permute-start.26 = (bf16[2,80,256]{2,1,0:T(8,128)(2,1)S(1)}, bf16[2,80,256]{2,1,0:T(8,128)(2,1)S(1)}, u32[]{:S(2)}, u32[]{:S(2)}) collective-permute-start(bf16[2,80,256]{2,1,0:T(8,128)(2,1)S(1)} %get-tuple-element.114), channel_id=1, source_target_pairs={{0,24},{1,25},{2,26},{3,27},{4,28},{5,29},{6,30},{7,31},{8,16},{9,... | collective-permute-start | bytes 245768 | tf_op jit(solution)/shard_map/ppermute | solution.py:509
  88.6 3.6 %collective-permute-done.26.refs_3_ = bf16[2,80,256]{2,1,0:T(8,128)(2,1)S(1)} collective-permute-done((bf16[2,80,256]{2,1,0:T(8,128)(2,1)S(1)}, bf16[2,80,256]{2,1,0:T(8,128)(2,1)S(1)}, u32[]{:S(2)}, u32[]{:S(2)}) %collective-permute-start.26) | collective-permute-done | bytes 81952 | tf_op jit(solution)/shard_map/ppermute | solution.py:509
  93.6 2.1 %collective-permute-start.20 = (bf16[256,256]{1,0:T(8,128)(2,1)S(1)}, bf16[256,256]{1,0:T(8,128)(2,1)S(1)}, u32[]{:S(2)}, u32[]{:S(2)}) collective-permute-start(bf16[256,256]{1,0:T(8,128)(2,1)S(1)} %get-tuple-element.106.refs_1_), channel_id=1, source_target_pairs={{0,4},{1,5},{2,6},{3,7},{4,0},{5,1},{6,2},{7,3},{8,12},{9,13},{10,... | collective-permute-start | bytes 393224 | tf_op jit(solution)/shard_map/ppermute | solution.py:509
  95.7 1.8 %collective-permute-done.27.other_ref = bf16[2,64,256]{2,1,0:T(8,128)(2,1)S(1)} collective-permute-done((bf16[2,64,256]{2,1,0:T(8,128)(2,1)S(1)}, bf16[2,64,256]{2,1,0:T(8,128)(2,1)S(1)}, u32[]{:S(2)}, u32[]{:S(2)}) %collective-permute-start.27) | collective-permute-done | bytes 65568 | tf_op jit(solution)/shard_map/ppermute | solution.py:509
  99.2 1.8 %collective-permute-start.21 = (bf16[512,256]{1,0:T(8,128)(2,1)S(1)}, bf16[512,256]{1,0:T(8,128)(2,1)S(1)}, u32[]{:S(2)}, u32[]{:S(2)}) collective-permute-start(bf16[512,256]{1,0:T(8,128)(2,1)S(1)} %get-tuple-element.107.half_one), channel_id=1, source_target_pairs={{0,4},{1,5},{2,6},{3,7},{4,0},{5,1},{6,2},{7,3},{8,12},{9,13},{10,... | collective-permute-start | bytes 786440 | tf_op jit(solution)/shard_map/ppermute | solution.py:509
  106.1 2.4 %collective-permute-done.21.dep_ref.far_one = bf16[512,256]{1,0:T(8,128)(2,1)S(1)} collective-permute-done((bf16[512,256]{1,0:T(8,128)(2,1)S(1)}, bf16[512,256]{1,0:T(8,128)(2,1)S(1)}, u32[]{:S(2)}, u32[]{:S(2)}) %collective-permute-start.21) | collective-permute-done | bytes 262176 | tf_op jit(solution)/shard_map/ppermute | solution.py:509
  109.2 1.8 %features.1.total_ref = f32[384,1024]{1,0:T(8,128)S(1)} custom-call(bf16[384,512]{1,0:T(8,128)(2,1)S(1)} %get-tuple-element.84.own_one, bf16[384,512]{1,0:T(8,128)(2,1)S(1)} %get-tuple-element.91.own_two, bf16[384,1024]{1,0:T(8,128)(2,1)S(1)} %get-tuple-element.81.dskip_ref, bf16[1024,1024]{1,0:T(8,128)(2,1)S(1)} %copy-done, ...), custom_call_target="tpu_custom_call" | custom-call | flops 110000000 | bytes 100000 | tf_op jit(solution)/shard_map/features/pallas_call | solution.py:715
  111.0 2.1 %features_halo.1.rest_0_ = bf16[376,1024]{1,0:T(8,128)(2,1)} custom-call(f32[384,1024]{1,0:T(8,128)S(1)} %features.1.total_ref, bf16[48,1024]{1,0:T(8,128)(2,1)S(1)} %collective-permute-done.22.near_ref.refs_4_, bf16[48,1024]{1,0:T(8,128)(2,1)S(1)} %collective-permute-done.23.far_ref.refs_5_, s32[1,2,47]{2,1,0:T(2,128)S(1)} %copy-done.9, ...), custom_call_target="tpu_custom_call" | custom-call | flops 110000000 | bytes 100000 | tf_op jit(solution)/shard_map/features_halo/pallas_call | solution.py:736
  113.1 2.4 %collective-permute-done.37.far_two = bf16[512,256]{1,0:T(8,128)(2,1)S(1)} collective-permute-done((bf16[512,256]{1,0:T(8,128)(2,1)S(1)}, bf16[512,256]{1,0:T(8,128)(2,1)S(1)}, u32[]{:S(2)}, u32[]{:S(2)}) %collective-permute-start.37) | collective-permute-done | bytes 262176 | tf_op jit(solution)/shard_map/ppermute | solution.py:509
  121.3 1.6 %assemble.6.refs_2_ = f32[1024,1024]{1,0:T(8,128)} custom-call(bf16[2,512,256]{2,1,0:T(8,128)(2,1)S(1)} %get-tuple-element.119.refs_0_, bf16[2,512,256]{2,1,0:T(8,128)(2,1)S(1)} %get-tuple-element.120.refs_1_), custom_call_target="tpu_custom_call" | custom-call | flops 110000000 | bytes 100000 | tf_op jit(solution)/shard_map/assemble/pallas_call | solution.py:668
  122.9 1.6 %assemble.5 = f32[1024,1024]{1,0:T(8,128)} custom-call(bf16[2,256,256]{2,1,0:T(8,128)(2,1)S(1)} %collective-permute-done.30.refs_0_, bf16[2,256,256]{2,1,0:T(8,128)(2,1)S(1)} %collective-permute-done.32.refs_1_, bf16[2,256,256]{2,1,0:T(8,128)(2,1)S(1)} %collective-permute-done.34.refs_2_, ...), custom_call_target="tpu_custom_call", output_to_operand_aliasing={{}: (4, {})} | custom-call | flops 110000000 | bytes 100000 | tf_op jit(solution)/shard_map/assemble/pallas_call | solution.py:668
  124.6 1.6 %assemble.7 = f32[1024,1024]{1,0:T(8,128)} custom-call(bf16[2,512,256]{2,1,0:T(8,128)(2,1)S(1)} %collective-permute-done.38.refs_0_, bf16[2,512,256]{2,1,0:T(8,128)(2,1)S(1)} %collective-permute-done.39.refs_1_, f32[1024,1024]{1,0:T(8,128)} %assemble.6.refs_2_), custom_call_target="tpu_custom_call", output_to_operand_aliasing={{}: (2, {})} | custom-call | flops 110000000 | bytes 100000 | tf_op jit(solution)/shard_map/assemble/pallas_call | solution.py:668
  (103 shorter events, 31.2 us)
Async XLA Ops:
  2.2 8.0 %collective-permute-start = (bf16[48,1024]{1,0:T(8,128)(2,1)S(1)}, bf16[48,1024]{1,0:T(8,128)(2,1)S(1)}, u32[]{:S(2)}, u32[]{:S(2)}) collective-permute-start(bf16[48,1024]{1,0:T(8,128)(2,1)S(1)} %get-tuple-element.68), channel_id=1, source_target_pairs={{0,1},{1,0},{2,3},{3,2},{4,5},{5,4},{6,7},{7,6},{8,9},{9,8},{10,11... | collective-permute-start | bytes 294920 | tf_op jit(solution)/shard_map/ppermute | solution.py:509
  2.8 7.5 %collective-permute-start.1 = (bf16[48,1024]{1,0:T(8,128)(2,1)S(1)}, bf16[48,1024]{1,0:T(8,128)(2,1)S(1)}, u32[]{:S(2)}, u32[]{:S(2)}) collective-permute-start(bf16[48,1024]{1,0:T(8,128)(2,1)S(1)} %get-tuple-element.69), channel_id=1, source_target_pairs={{1,2},{3,4},{5,6},{7,8},{9,10},{11,12},{13,14},{15,16},{17,18},{19... | collective-permute-start | bytes 294920 | tf_op jit(solution)/shard_map/ppermute | solution.py:506
  34.5 5.0 %collective-permute-start.6 = (f32[8,1024]{1,0:T(8,128)S(1)}, f32[8,1024]{1,0:T(8,128)S(1)}, u32[]{:S(2)}, u32[]{:S(2)}) collective-permute-start(f32[8,1024]{1,0:T(8,128)S(1)} %merge.7.stats_ref), channel_id=1, source_target_pairs={{0,16},{1,17},{2,18},{3,19},{4,20},{5,21},{6,22},{7,23},{8,24},{9,... | collective-permute-start | bytes 98312 | tf_op jit(solution)/shard_map/ppermute | solution.py:509
  47.0 8.5 %collective-permute-start.11 = (bf16[2,1040,256]{2,1,0:T(8,128)(2,1)S(1)}, bf16[2,1040,256]{2,1,0:T(8,128)(2,1)S(1)}, u32[]{:S(2)}, u32[]{:S(2)}) collective-permute-start(bf16[2,1040,256]{2,1,0:T(8,128)(2,1)S(1)} %get-tuple-element.89.outs_0_), channel_id=1, source_target_pairs={{0,1},{1,0},{2,3},{3,2},{4,5},{5,4},{6,7},{7,6},{8,9},{9,8},{10,11... | collective-permute-start | bytes 3194888 | tf_op jit(solution)/shard_map/ppermute | solution.py:509
  47.8 10.3 %collective-permute-start.8 = (bf16[2,256,256]{2,1,0:T(8,128)(2,1)S(1)}, bf16[2,256,256]{2,1,0:T(8,128)(2,1)S(1)}, u32[]{:S(2)}, u32[]{:S(2)}) collective-permute-start(bf16[2,256,256]{2,1,0:T(8,128)(2,1)S(1)} %get-tuple-element.92), channel_id=1, source_target_pairs={{0,2},{1,3},{2,0},{3,1},{4,6},{5,7},{6,4},{7,5},{8,10},{9,11},{10,... | collective-permute-start | bytes 786440 | tf_op jit(solution)/shard_map/ppermute | solution.py:509
  48.5 10.9 %collective-permute-start.9 = (bf16[2,256,256]{2,1,0:T(8,128)(2,1)S(1)}, bf16[2,256,256]{2,1,0:T(8,128)(2,1)S(1)}, u32[]{:S(2)}, u32[]{:S(2)}) collective-permute-start(bf16[2,256,256]{2,1,0:T(8,128)(2,1)S(1)} %get-tuple-element.93), channel_id=1, source_target_pairs={{0,4},{1,5},{2,6},{3,7},{4,0},{5,1},{6,2},{7,3},{8,12},{9,13},{10,... | collective-permute-start | bytes 786440 | tf_op jit(solution)/shard_map/ppermute | solution.py:509
  50.1 14.2 %collective-permute-start.10 = (bf16[2,256,256]{2,1,0:T(8,128)(2,1)S(1)}, bf16[2,256,256]{2,1,0:T(8,128)(2,1)S(1)}, u32[]{:S(2)}, u32[]{:S(2)}) collective-permute-start(bf16[2,256,256]{2,1,0:T(8,128)(2,1)S(1)} %get-tuple-element.94), channel_id=1, source_target_pairs={{0,6},{1,7},{2,4},{3,5},{4,2},{5,3},{6,0},{7,1},{8,14},{9,15},{10,... | collective-permute-start | bytes 786440 | tf_op jit(solution)/shard_map/ppermute | solution.py:509
  55.9 17.1 %collective-permute-start.14 = (bf16[2,272,256]{2,1,0:T(8,128)(2,1)S(1)}, bf16[2,272,256]{2,1,0:T(8,128)(2,1)S(1)}, u32[]{:S(2)}, u32[]{:S(2)}) collective-permute-start(bf16[2,272,256]{2,1,0:T(8,128)(2,1)S(1)} %get-tuple-element.101), channel_id=1, source_target_pairs={{0,2},{1,3},{2,0},{3,1},{4,6},{5,7},{6,4},{7,5},{8,10},{9,11},{10,... | collective-permute-start | bytes 835592 | tf_op jit(solution)/shard_map/ppermute | solution.py:509
  56.6 16.4 %collective-permute-start.15 = (bf16[2,272,256]{2,1,0:T(8,128)(2,1)S(1)}, bf16[2,272,256]{2,1,0:T(8,128)(2,1)S(1)}, u32[]{:S(2)}, u32[]{:S(2)}) collective-permute-start(bf16[2,272,256]{2,1,0:T(8,128)(2,1)S(1)} %get-tuple-element.102), channel_id=1, source_target_pairs={{0,4},{1,5},{2,6},{3,7},{4,0},{5,1},{6,2},{7,3},{8,12},{9,13},{10,... | collective-permute-start | bytes 835592 | tf_op jit(solution)/shard_map/ppermute | solution.py:509
  58.1 16.8 %collective-permute-start.16 = (bf16[2,272,256]{2,1,0:T(8,128)(2,1)S(1)}, bf16[2,272,256]{2,1,0:T(8,128)(2,1)S(1)}, u32[]{:S(2)}, u32[]{:S(2)}) collective-permute-start(bf16[2,272,256]{2,1,0:T(8,128)(2,1)S(1)} %get-tuple-element.103), channel_id=1, source_target_pairs={{0,6},{1,7},{2,4},{3,5},{4,2},{5,3},{6,0},{7,1},{8,14},{9,15},{10,... | collective-permute-start | bytes 835592 | tf_op jit(solution)/shard_map/ppermute | solution.py:509
  64.4 5.0 %collective-permute-start.12 = (bf16[2,128,256]{2,1,0:T(8,128)(2,1)S(1)}, bf16[2,128,256]{2,1,0:T(8,128)(2,1)S(1)}, u32[]{:S(2)}, u32[]{:S(2)}) collective-permute-start(bf16[2,128,256]{2,1,0:T(8,128)(2,1)S(1)} %get-tuple-element.98), channel_id=1, source_target_pairs={{0,8},{1,9},{2,10},{3,11},{4,12},{5,13},{6,14},{7,15},{8,0},{9,1},... | collective-permute-start | bytes 393224 | tf_op jit(solution)/shard_map/ppermute | solution.py:509
  69.4 5.8 %collective-permute-start.13 = (bf16[2,64,256]{2,1,0:T(8,128)(2,1)S(1)}, bf16[2,64,256]{2,1,0:T(8,128)(2,1)S(1)}, u32[]{:S(2)}, u32[]{:S(2)}) collective-permute-start(bf16[2,64,256]{2,1,0:T(8,128)(2,1)S(1)} %get-tuple-element.100), channel_id=1, source_target_pairs={{0,16},{1,17},{2,18},{3,19},{4,20},{5,21},{6,22},{7,23},{8,24},{9,... | collective-permute-start | bytes 196616 | tf_op jit(solution)/shard_map/ppermute | solution.py:509
  75.2 8.9 %collective-permute-start.17 = (bf16[2,64,256]{2,1,0:T(8,128)(2,1)S(1)}, bf16[2,64,256]{2,1,0:T(8,128)(2,1)S(1)}, u32[]{:S(2)}, u32[]{:S(2)}) collective-permute-start(bf16[2,64,256]{2,1,0:T(8,128)(2,1)S(1)} %s_line.3.mine_ref), channel_id=1, source_target_pairs={{0,16},{1,17},{2,18},{3,19},{4,20},{5,21},{6,22},{7,23},{8,24},{9,... | collective-permute-start | bytes 196616 | tf_op jit(solution)/shard_map/ppermute | solution.py:509
  78.3 8.5 %collective-permute-start.24 = (bf16[2,80,256]{2,1,0:T(8,128)(2,1)S(1)}, bf16[2,80,256]{2,1,0:T(8,128)(2,1)S(1)}, u32[]{:S(2)}, u32[]{:S(2)}) collective-permute-start(bf16[2,80,256]{2,1,0:T(8,128)(2,1)S(1)} %get-tuple-element.112), channel_id=1, source_target_pairs={{0,16},{1,17},{2,18},{3,19},{4,20},{5,21},{6,22},{7,23},{8,24},{9,... | collective-permute-start | bytes 245768 | tf_op jit(solution)/shard_map/ppermute | solution.py:509
  78.4 13.8 %collective-permute-start.22 = (bf16[48,1024]{1,0:T(8,128)(2,1)S(1)}, bf16[48,1024]{1,0:T(8,128)(2,1)S(1)}, u32[]{:S(2)}, u32[]{:S(2)}) collective-permute-start(bf16[48,1024]{1,0:T(8,128)(2,1)S(1)} %get-tuple-element.109), channel_id=1, source_target_pairs={{0,1},{1,0},{2,3},{3,2},{4,5},{5,4},{6,7},{7,6},{8,9},{9,8},{10,11... | collective-permute-start | bytes 294920 | tf_op jit(solution)/shard_map/ppermute | solution.py:509
  78.4 13.8 %collective-permute-start.23 = (bf16[48,1024]{1,0:T(8,128)(2,1)S(1)}, bf16[48,1024]{1,0:T(8,128)(2,1)S(1)}, u32[]{:S(2)}, u32[]{:S(2)}) collective-permute-start(bf16[48,1024]{1,0:T(8,128)(2,1)S(1)} %get-tuple-element.111), channel_id=1, source_target_pairs={{1,2},{3,4},{5,6},{7,8},{9,10},{11,12},{13,14},{15,16},{17,18},{19... | collective-permute-start | bytes 294920 | tf_op jit(solution)/shard_map/ppermute | solution.py:506
  79.1 9.5 %collective-permute-start.25 = (bf16[2,80,256]{2,1,0:T(8,128)(2,1)S(1)}, bf16[2,80,256]{2,1,0:T(8,128)(2,1)S(1)}, u32[]{:S(2)}, u32[]{:S(2)}) collective-permute-start(bf16[2,80,256]{2,1,0:T(8,128)(2,1)S(1)} %get-tuple-element.113), channel_id=1, source_target_pairs={{0,8},{1,9},{2,10},{3,11},{4,12},{5,13},{6,14},{7,15},{8,0},{9,1},... | collective-permute-start | bytes 245768 | tf_op jit(solution)/shard_map/ppermute | solution.py:509
  84.1 8.1 %collective-permute-start.26 = (bf16[2,80,256]{2,1,0:T(8,128)(2,1)S(1)}, bf16[2,80,256]{2,1,0:T(8,128)(2,1)S(1)}, u32[]{:S(2)}, u32[]{:S(2)}) collective-permute-start(bf16[2,80,256]{2,1,0:T(8,128)(2,1)S(1)} %get-tuple-element.114), channel_id=1, source_target_pairs={{0,24},{1,25},{2,26},{3,27},{4,28},{5,29},{6,30},{7,31},{8,16},{9,... | collective-permute-start | bytes 245768 | tf_op jit(solution)/shard_map/ppermute | solution.py:509
  86.8 6.6 %collective-permute-start.18 = (bf16[2,128,256]{2,1,0:T(8,128)(2,1)S(1)}, bf16[2,128,256]{2,1,0:T(8,128)(2,1)S(1)}, u32[]{:S(2)}, u32[]{:S(2)}) collective-permute-start(bf16[2,128,256]{2,1,0:T(8,128)(2,1)S(1)} %s_join.1.mine_ref), channel_id=1, source_target_pairs={{0,8},{1,9},{2,10},{3,11},{4,12},{5,13},{6,14},{7,15},{8,0},{9,1},... | collective-permute-start | bytes 393224 | tf_op jit(solution)/shard_map/ppermute | solution.py:509
  92.2 5.2 %collective-permute-start.27 = (bf16[2,64,256]{2,1,0:T(8,128)(2,1)S(1)}, bf16[2,64,256]{2,1,0:T(8,128)(2,1)S(1)}, u32[]{:S(2)}, u32[]{:S(2)}) collective-permute-start(bf16[2,64,256]{2,1,0:T(8,128)(2,1)S(1)} %get-tuple-element.115.mine_ref), channel_id=1, source_target_pairs={{0,16},{1,17},{2,18},{3,19},{4,20},{5,21},{6,22},{7,23},{8,24},{9,... | collective-permute-start | bytes 196616 | tf_op jit(solution)/shard_map/ppermute | solution.py:509
  93.5 5.0 %collective-permute-start.19 = (bf16[256,256]{1,0:T(8,128)(2,1)S(1)}, bf16[256,256]{1,0:T(8,128)(2,1)S(1)}, u32[]{:S(2)}, u32[]{:S(2)}) collective-permute-start(bf16[256,256]{1,0:T(8,128)(2,1)S(1)} %get-tuple-element.105.refs_0_), channel_id=1, source_target_pairs={{0,2},{1,3},{2,0},{3,1},{4,6},{5,7},{6,4},{7,5},{8,10},{9,11},{10,... | collective-permute-start | bytes 393224 | tf_op jit(solution)/shard_map/ppermute | solution.py:509
  93.6 5.6 %collective-permute-start.20 = (bf16[256,256]{1,0:T(8,128)(2,1)S(1)}, bf16[256,256]{1,0:T(8,128)(2,1)S(1)}, u32[]{:S(2)}, u32[]{:S(2)}) collective-permute-start(bf16[256,256]{1,0:T(8,128)(2,1)S(1)} %get-tuple-element.106.refs_1_), channel_id=1, source_target_pairs={{0,4},{1,5},{2,6},{3,7},{4,0},{5,1},{6,2},{7,3},{8,12},{9,13},{10,... | collective-permute-start | bytes 393224 | tf_op jit(solution)/shard_map/ppermute | solution.py:509
  97.5 5.0 %collective-permute-start.28 = (bf16[2,128,256]{2,1,0:T(8,128)(2,1)S(1)}, bf16[2,128,256]{2,1,0:T(8,128)(2,1)S(1)}, u32[]{:S(2)}, u32[]{:S(2)}) collective-permute-start(bf16[2,128,256]{2,1,0:T(8,128)(2,1)S(1)} %p_join.2.mine_ref), channel_id=1, source_target_pairs={{0,8},{1,9},{2,10},{3,11},{4,12},{5,13},{6,14},{7,15},{8,0},{9,1},... | collective-permute-start | bytes 393224 | tf_op jit(solution)/shard_map/ppermute | solution.py:509
  99.2 9.3 %collective-permute-start.21 = (bf16[512,256]{1,0:T(8,128)(2,1)S(1)}, bf16[512,256]{1,0:T(8,128)(2,1)S(1)}, u32[]{:S(2)}, u32[]{:S(2)}) collective-permute-start(bf16[512,256]{1,0:T(8,128)(2,1)S(1)} %get-tuple-element.107.half_one), channel_id=1, source_target_pairs={{0,4},{1,5},{2,6},{3,7},{4,0},{5,1},{6,2},{7,3},{8,12},{9,13},{10,... | collective-permute-start | bytes 786440 | tf_op jit(solution)/shard_map/ppermute | solution.py:509
  101.0 14.5 %collective-permute-start.37 = (bf16[512,256]{1,0:T(8,128)(2,1)S(1)}, bf16[512,256]{1,0:T(8,128)(2,1)S(1)}, u32[]{:S(2)}, u32[]{:S(2)}) collective-permute-start(bf16[512,256]{1,0:T(8,128)(2,1)S(1)} %get-tuple-element.117.half_two), channel_id=1, source_target_pairs={{0,2},{1,3},{2,0},{3,1},{4,6},{5,7},{6,4},{7,5},{8,10},{9,11},{10,... | collective-permute-start | bytes 786440 | tf_op jit(solution)/shard_map/ppermute | solution.py:509
  102.6 14.2 %collective-permute-start.35 = (bf16[2,256,256]{2,1,0:T(8,128)(2,1)S(1)}, bf16[2,256,256]{2,1,0:T(8,128)(2,1)S(1)}, u32[]{:S(2)}, u32[]{:S(2)}) collective-permute-start(bf16[2,256,256]{2,1,0:T(8,128)(2,1)S(1)} %p_join.3.refs_0_), channel_id=1, source_target_pairs={{0,6},{1,7},{2,4},{3,5},{4,2},{5,3},{6,0},{7,1},{8,14},{9,15},{10,... | collective-permute-start | bytes 786440 | tf_op jit(solution)/shard_map/ppermute | solution.py:509
  103.3 14.8 %collective-permute-start.33 = (bf16[2,256,256]{2,1,0:T(8,128)(2,1)S(1)}, bf16[2,256,256]{2,1,0:T(8,128)(2,1)S(1)}, u32[]{:S(2)}, u32[]{:S(2)}) collective-permute-start(bf16[2,256,256]{2,1,0:T(8,128)(2,1)S(1)} %p_join.3.refs_0_), channel_id=1, source_target_pairs={{0,4},{1,5},{2,6},{3,7},{4,0},{5,1},{6,2},{7,3},{8,12},{9,13},{10,... | collective-permute-start | bytes 786440 | tf_op jit(solution)/shard_map/ppermute | solution.py:509
  104.6 14.5 %collective-permute-start.31 = (bf16[2,256,256]{2,1,0:T(8,128)(2,1)S(1)}, bf16[2,256,256]{2,1,0:T(8,128)(2,1)S(1)}, u32[]{:S(2)}, u32[]{:S(2)}) collective-permute-start(bf16[2,256,256]{2,1,0:T(8,128)(2,1)S(1)} %p_join.3.refs_0_), channel_id=1, source_target_pairs={{0,2},{1,3},{2,0},{3,1},{4,6},{5,7},{6,4},{7,5},{8,10},{9,11},{10,... | collective-permute-start | bytes 786440 | tf_op jit(solution)/shard_map/ppermute | solution.py:509
  108.5 10.6 %collective-permute-start.30 = (bf16[2,256,256]{2,1,0:T(8,128)(2,1)S(1)}, bf16[2,256,256]{2,1,0:T(8,128)(2,1)S(1)}, u32[]{:S(2)}, u32[]{:S(2)}) collective-permute-start(bf16[2,256,256]{2,1,0:T(8,128)(2,1)S(1)} %p_join.3.refs_0_), channel_id=1, source_target_pairs={{0,1},{1,0},{2,3},{3,2},{4,5},{5,4},{6,7},{7,6},{8,9},{9,8},{10,11... | collective-permute-start | bytes 786440 | tf_op jit(solution)/shard_map/ppermute | solution.py:509
  116.7 7.9 %collective-permute-start.38 = (bf16[2,512,256]{2,1,0:T(8,128)(2,1)S(1)}, bf16[2,512,256]{2,1,0:T(8,128)(2,1)S(1)}, u32[]{:S(2)}, u32[]{:S(2)}) collective-permute-start(bf16[2,512,256]{2,1,0:T(8,128)(2,1)S(1)} %get-tuple-element.119.refs_0_), channel_id=1, source_target_pairs={{0,1},{1,0},{2,3},{3,2},{4,5},{5,4},{6,7},{7,6},{8,9},{9,8},{10,11... | collective-permute-start | bytes 1572872 | tf_op jit(solution)/shard_map/ppermute | solution.py:509
  116.8 7.8 %collective-permute-start.39 = (bf16[2,512,256]{2,1,0:T(8,128)(2,1)S(1)}, bf16[2,512,256]{2,1,0:T(8,128)(2,1)S(1)}, u32[]{:S(2)}, u32[]{:S(2)}) collective-permute-start(bf16[2,512,256]{2,1,0:T(8,128)(2,1)S(1)} %get-tuple-element.120.refs_1_), channel_id=1, source_target_pairs={{0,1},{1,0},{2,3},{3,2},{4,5},{5,4},{6,7},{7,6},{8,9},{9,8},{10,11... | collective-permute-start | bytes 1572872 | tf_op jit(solution)/shard_map/ppermute | solution.py:509
  118.1 4.9 %collective-permute-start.36 = (bf16[2,256,256]{2,1,0:T(8,128)(2,1)S(1)}, bf16[2,256,256]{2,1,0:T(8,128)(2,1)S(1)}, u32[]{:S(2)}, u32[]{:S(2)}) collective-permute-start(bf16[2,256,256]{2,1,0:T(8,128)(2,1)S(1)} %collective-permute-done.35.refs_3_), channel_id=1, source_target_pairs={{0,1},{1,0},{2,3},{3,2},{4,5},{5,4},{6,7},{7,6},{8,9},{9,8},{10,11... | collective-permute-start | bytes 786440 | tf_op jit(solution)/shard_map/ppermute | solution.py:509
  (20 other events, 151.8 us)

commit v7 on v6

--- a/solution.py
+++ b/solution.py
@@ -139,7 +139,7 @@
         count_ref[pl.ds(start, 8), :] = jnp.where(total > 0, jnp.log(jnp.maximum(total, 1.0)) * (1.0 / LN2), NEG)
         return carry
 
-    lax.fori_loop(0, share // 8, chunk, 0, unroll=2)
+    lax.fori_loop(0, share // 8, chunk, 0, unroll=4)
 
 
 def attend_kernel(
@@ -181,7 +181,7 @@
             score_scr[where, :] = result
             return jnp.maximum(highest, jnp.max(fold_rows(result), axis=0))
 
-        highest = lax.fori_loop(0, columns // CHUNK, score, jnp.full((8, rows), NEG, F32), unroll=2)
+        highest = lax.fori_loop(0, columns // CHUNK, score, jnp.full((8, rows), NEG, F32), unroll=4)
         highest = jnp.max(highest, axis=0, keepdims=True)
 
         def weigh(index, carry, head=head, highest=highest):
@@ -189,7 +189,7 @@
             weight_ref[head, where, :] = jnp.exp2(score_scr[where, :] - highest).astype(BF16)
             return carry
 
-        lax.fori_loop(0, columns // CHUNK, weigh, 0, unroll=2)
+        lax.fori_loop(0, columns // CHUNK, weigh, 0, unroll=4)
         wide = jnp.concatenate([ext, jnp.ones((columns, LANES), BF16)], axis=1)
         summed = mm(weight_ref[head], wide, (0, 0))
         scale = 1.0 / summed[:, width:]
@@ -398,7 +398,7 @@
             return total + jnp.sum(fold_rows(weight), axis=0), mean + jnp.sum(fold_rows(weight * dal_scr[where, :]), axis=0)
 
         nothing = jnp.zeros((8, rows), F32)
-        total, mean = lax.fori_loop(0, columns // CHUNK, average, (nothing, nothing), unroll=2)
+        total, mean = lax.fori_loop(0, columns // CHUNK, average, (nothing, nothing), unroll=4)
         scale = 1.0 / jnp.sum(total, axis=0, keepdims=True)
         mean = jnp.sum(mean, axis=0, keepdims=True) * scale
 
@@ -410,7 +410,7 @@
             sum_scr[where, :] = sum(du[:, at : at + LANES] for at in range(0, rows, LANES))
             return by_target + jnp.sum(fold_rows(du), axis=0)
 
-        by_target = lax.fori_loop(0, columns // CHUNK, slopes, nothing, unroll=2)
+        by_target = lax.fori_loop(0, columns // CHUNK, slopes, nothing, unroll=4)
         by_target = jnp.sum(by_target, axis=0, keepdims=True)
         by_source = jnp.sum(sum_scr[...], axis=1, keepdims=True)
         ext = ext_ref[:, lanes]

time: 127 us -> 126 us (level)
  no operation moved by 1% of the time
where the time goes in v7:
time: 126 us
  starting transfers between devices  48.5 us (38%)
  Pallas kernels  37.9 us (30%)
  waiting for transfers between devices  36.8 us (29%)
    ppermute x38, starting transfers between devices, swapped(): lax.ppermute(value, AXES, [(source, source ^ distance) for source in rang...  47.2 us
    ppermute x38, waiting for transfers between devices, swapped(): lax.ppermute(value, AXES, [(source, source ^ distance) for source in rang...  36.8 us
    pallas_call x2, Pallas kernels, backward(): pl.pallas_call(functools.partial(back_kernel, part=part), in_specs=[vmem]...  7.94 us
    pallas_call x4, Pallas kernels, assemble(): pl.pallas_call(functools.partial(assemble_kernel, first=first, pieces=len...  6.46 us
    pallas_call x1, Pallas kernels, per_device(): pl.pallas_call(functools.partial(project_kernel, halo=halo), grid=(heads,...  6.44 us
    pallas_call x1, Pallas kernels, per_device(): pl.pallas_call(attend_kernel, in_specs=[vmem] * 11, out_shape=[shape_of((...  6.2 us
    pallas_call x1, Pallas kernels, per_device(): pl.pallas_call(functools.partial(norm_kernel, last_bit=bits - 1), in_spec...  3.48 us
  transfers between devices with their start and end apart: 40, of which 20 were waited for; matrix products, arithmetic and copies ran while one was open for 0% of the time, Pallas kernels for 20%

profile of v7, /device:TPU:0, one launch (start us, length us, event | category | flops | bytes accessed | tf_op | source)
XLA Modules:
  0.0 125.7 jit_solution(4318718132081320656)
XLA Ops:
  3.5 6.4 %project.1 = (bf16[384,1024]{1,0:T(8,128)(2,1)S(1)}, f32[384,1024]{1,0:T(8,128)S(1)}, f32[512,384]{1,0:T(8,128)S(1)}, bf16[1024,384]{1,0:T(8,128)(2,1)S(1)}) custom-call(bf16[376,1024]{1,0:T(8,128)(2,1)} %feats_ref.3, bf16[1024,1024]{1,0:T(8,128)(2,1)} %proj_ref.7, bf16[1024,1024]{1,0:T(8,128)(2,1)} %skip_ref.1, s32[16,376]{1,0:T(8,128)} %bitcast.11, ...), custom_call_target="tpu_custom_call" | custom-call | flops 5500000256 | bytes 5000000 | tf_op jit(solution)/shard_map/project/pallas_call | solution.py:533
  10.1 6.2 %attend.1 = (bf16[512,1024]{1,0:T(8,128)(2,1)S(1)}, bf16[4,512,384]{2,1,0:T(8,128)(2,1)S(1)}, f32[4,512,128]{2,1,0:T(8,128)S(1)}, f32[4,8,384]{2,1,0:T(8,128)S(1...) custom-call(bf16[384,1024]{1,0:T(8,128)(2,1)S(1)} %get-tuple-element, ...), custom_call_target="tpu_custom_call" | custom-call | flops 8800000000 | bytes 8000000 | tf_op jit(solution)/shard_map/attend/pallas_call | solution.py:554
  16.3 4.0 %collective-permute-start.2 = (f32[8,1024]{1,0:T(8,128)S(1)}, f32[8,1024]{1,0:T(8,128)S(1)}, u32[]{:S(2)}, u32[]{:S(2)}) collective-permute-start(f32[8,1024]{1,0:T(8,128)S(1)} %get-tuple-element.73.mine_ref), channel_id=1, source_target_pairs={{0,1},{1,0},{2,3},{3,2},{4,5},{5,4},{6,7},{7,6},{8,9},{9,8},{10,11... | collective-permute-start | bytes 98312 | tf_op jit(solution)/shard_map/ppermute | solution.py:509
  22.6 2.5 %collective-permute-done.3.other_ref = f32[8,1024]{1,0:T(8,128)S(1)} collective-permute-done((f32[8,1024]{1,0:T(8,128)S(1)}, f32[8,1024]{1,0:T(8,128)S(1)}, u32[]{:S(2)}, u32[]{:S(2)}) %collective-permute-start.3) | collective-permute-done | bytes 32800 | tf_op jit(solution)/shard_map/ppermute | solution.py:509
  25.2 1.8 %collective-permute-start.4 = (f32[8,1024]{1,0:T(8,128)S(1)}, f32[8,1024]{1,0:T(8,128)S(1)}, u32[]{:S(2)}, u32[]{:S(2)}) collective-permute-start(f32[8,1024]{1,0:T(8,128)S(1)} %merge.5.mine_ref), channel_id=1, source_target_pairs={{0,4},{1,5},{2,6},{3,7},{4,0},{5,1},{6,2},{7,3},{8,12},{9,13},{10,... | collective-permute-start | bytes 98312 | tf_op jit(solution)/shard_map/ppermute | solution.py:509
  27.0 2.1 %collective-permute-done.4.other_ref = f32[8,1024]{1,0:T(8,128)S(1)} collective-permute-done((f32[8,1024]{1,0:T(8,128)S(1)}, f32[8,1024]{1,0:T(8,128)S(1)}, u32[]{:S(2)}, u32[]{:S(2)}) %collective-permute-start.4) | collective-permute-done | bytes 32800 | tf_op jit(solution)/shard_map/ppermute | solution.py:509
  29.2 2.8 %collective-permute-start.5 = (f32[8,1024]{1,0:T(8,128)S(1)}, f32[8,1024]{1,0:T(8,128)S(1)}, u32[]{:S(2)}, u32[]{:S(2)}) collective-permute-start(f32[8,1024]{1,0:T(8,128)S(1)} %merge.6.mine_ref), channel_id=1, source_target_pairs={{0,8},{1,9},{2,10},{3,11},{4,12},{5,13},{6,14},{7,15},{8,0},{9,1},... | collective-permute-start | bytes 98312 | tf_op jit(solution)/shard_map/ppermute | solution.py:509
  32.0 1.9 %collective-permute-done.5.other_ref = f32[8,1024]{1,0:T(8,128)S(1)} collective-permute-done((f32[8,1024]{1,0:T(8,128)S(1)}, f32[8,1024]{1,0:T(8,128)S(1)}, u32[]{:S(2)}, u32[]{:S(2)}) %collective-permute-start.5) | collective-permute-done | bytes 32800 | tf_op jit(solution)/shard_map/ppermute | solution.py:509
  33.9 3.1 %collective-permute-start.6 = (f32[8,1024]{1,0:T(8,128)S(1)}, f32[8,1024]{1,0:T(8,128)S(1)}, u32[]{:S(2)}, u32[]{:S(2)}) collective-permute-start(f32[8,1024]{1,0:T(8,128)S(1)} %merge.7.stats_ref), channel_id=1, source_target_pairs={{0,16},{1,17},{2,18},{3,19},{4,20},{5,21},{6,22},{7,23},{8,24},{9,... | collective-permute-start | bytes 98312 | tf_op jit(solution)/shard_map/ppermute | solution.py:509
  37.0 1.9 %collective-permute-done.6.other_ref = f32[8,1024]{1,0:T(8,128)S(1)} collective-permute-done((f32[8,1024]{1,0:T(8,128)S(1)}, f32[8,1024]{1,0:T(8,128)S(1)}, u32[]{:S(2)}, u32[]{:S(2)}) %collective-permute-start.6) | collective-permute-done | bytes 32800 | tf_op jit(solution)/shard_map/ppermute | solution.py:509
  38.9 3.5 %norm.1 = (bf16[376,1024]{1,0:T(8,128)(2,1)}, bf16[384,1024]{1,0:T(8,128)(2,1)S(1)}, bf16[2,1024,256]{2,1,0:T(8,128)(2,1)S(1)}, bf16[2,1024,256]{2,1,0:T(8,128)(...) custom-call(f32[384,1024]{1,0:T(8,128)S(1)} %get-tuple-element.72.pre_ref, ...), custom_call_target="tpu_custom_call" | custom-call | flops 110000000 | bytes 100000 | tf_op jit(solution)/shard_map/norm/pallas_call | solution.py:584
  42.5 3.9 %back.2 = (bf16[2,1040,256]{2,1,0:T(8,128)(2,1)S(1)}, bf16[384,512]{1,0:T(8,128)(2,1)S(1)}, bf16[48,512]{1,0:T(8,128)(2,1)S(1)}, bf16[48,512]{1,0:T(8,128)(2,1)S(1)}) custom-call(bf16[4,512,384]{2,1,0:T(8,128)(2,1)S(1)} %get-tuple-element.76.weight_ref, f32[4,512,128]{2,1,0:T(8,128)S(1)} %get-tuple-element.77.source_ref, ...), custom_call_target="tpu_custom_call" | custom-call | flops 110000000 | bytes 100000 | tf_op jit(solution)/shard_map/back/pallas_call | solution.py:604
  50.7 4.1 %back.3 = (bf16[2,1040,256]{2,1,0:T(8,128)(2,1)S(1)}, bf16[384,512]{1,0:T(8,128)(2,1)S(1)}, bf16[48,1024]{1,0:T(8,128)(2,1)S(1)}, bf16[48,1024]{1,0:T(8,128)(2,1)S(1)}) custom-call(bf16[4,512,384]{2,1,0:T(8,128)(2,1)S(1)} %get-tuple-element.76.weight_ref, f32[4,512,128]{2,1,0:T(8,128)S(1)} %get-tuple-element.77.source_ref, ...), custom_call_target="tpu_custom_call" | custom-call | flops 110000000 | bytes 100000 | tf_op jit(solution)/shard_map/back/pallas_call | solution.py:604
  58.6 4.9 %collective-permute-done.10.refs_3_ = bf16[2,256,256]{2,1,0:T(8,128)(2,1)S(1)} collective-permute-done((bf16[2,256,256]{2,1,0:T(8,128)(2,1)S(1)}, bf16[2,256,256]{2,1,0:T(8,128)(2,1)S(1)}, u32[]{:S(2)}, u32[]{:S(2)}) %collective-permute-start.10) | collective-permute-done | bytes 262176 | tf_op jit(solution)/shard_map/ppermute | solution.py:509
  63.7 2.0 %collective-permute-start.12 = (bf16[2,128,256]{2,1,0:T(8,128)(2,1)S(1)}, bf16[2,128,256]{2,1,0:T(8,128)(2,1)S(1)}, u32[]{:S(2)}, u32[]{:S(2)}) collective-permute-start(bf16[2,128,256]{2,1,0:T(8,128)(2,1)S(1)} %get-tuple-element.98), channel_id=1, source_target_pairs={{0,8},{1,9},{2,10},{3,11},{4,12},{5,13},{6,14},{7,15},{8,0},{9,1},... | collective-permute-start | bytes 393224 | tf_op jit(solution)/shard_map/ppermute | solution.py:509
  65.7 3.1 %collective-permute-done.12.other_ref = bf16[2,128,256]{2,1,0:T(8,128)(2,1)S(1)} collective-permute-done((bf16[2,128,256]{2,1,0:T(8,128)(2,1)S(1)}, bf16[2,128,256]{2,1,0:T(8,128)(2,1)S(1)}, u32[]{:S(2)}, u32[]{:S(2)}) %collective-permute-start.12) | collective-permute-done | bytes 131104 | tf_op jit(solution)/shard_map/ppermute | solution.py:509
  68.8 3.5 %collective-permute-start.13 = (bf16[2,64,256]{2,1,0:T(8,128)(2,1)S(1)}, bf16[2,64,256]{2,1,0:T(8,128)(2,1)S(1)}, u32[]{:S(2)}, u32[]{:S(2)}) collective-permute-start(bf16[2,64,256]{2,1,0:T(8,128)(2,1)S(1)} %get-tuple-element.100), channel_id=1, source_target_pairs={{0,16},{1,17},{2,18},{3,19},{4,20},{5,21},{6,22},{7,23},{8,24},{9,... | collective-permute-start | bytes 196616 | tf_op jit(solution)/shard_map/ppermute | solution.py:509
  72.3 2.0 %collective-permute-done.16.refs_3_ = bf16[2,272,256]{2,1,0:T(8,128)(2,1)S(1)} collective-permute-done((bf16[2,272,256]{2,1,0:T(8,128)(2,1)S(1)}, bf16[2,272,256]{2,1,0:T(8,128)(2,1)S(1)}, u32[]{:S(2)}, u32[]{:S(2)}) %collective-permute-start.16) | collective-permute-done | bytes 278560 | tf_op jit(solution)/shard_map/ppermute | solution.py:509
  74.5 3.1 %collective-permute-start.17 = (bf16[2,64,256]{2,1,0:T(8,128)(2,1)S(1)}, bf16[2,64,256]{2,1,0:T(8,128)(2,1)S(1)}, u32[]{:S(2)}, u32[]{:S(2)}) collective-permute-start(bf16[2,64,256]{2,1,0:T(8,128)(2,1)S(1)} %s_line.3.mine_ref), channel_id=1, source_target_pairs={{0,16},{1,17},{2,18},{3,19},{4,20},{5,21},{6,22},{7,23},{8,24},{9,... | collective-permute-start | bytes 196616 | tf_op jit(solution)/shard_map/ppermute | solution.py:509
  78.3 5.1 %collective-permute-start.25 = (bf16[2,80,256]{2,1,0:T(8,128)(2,1)S(1)}, bf16[2,80,256]{2,1,0:T(8,128)(2,1)S(1)}, u32[]{:S(2)}, u32[]{:S(2)}) collective-permute-start(bf16[2,80,256]{2,1,0:T(8,128)(2,1)S(1)} %get-tuple-element.113), channel_id=1, source_target_pairs={{0,8},{1,9},{2,10},{3,11},{4,12},{5,13},{6,14},{7,15},{8,0},{9,1},... | collective-permute-start | bytes 245768 | tf_op jit(solution)/shard_map/ppermute | solution.py:509
  83.4 2.7 %collective-permute-start.26 = (bf16[2,80,256]{2,1,0:T(8,128)(2,1)S(1)}, bf16[2,80,256]{2,1,0:T(8,128)(2,1)S(1)}, u32[]{:S(2)}, u32[]{:S(2)}) collective-permute-start(bf16[2,80,256]{2,1,0:T(8,128)(2,1)S(1)} %get-tuple-element.114), channel_id=1, source_target_pairs={{0,24},{1,25},{2,26},{3,27},{4,28},{5,29},{6,30},{7,31},{8,16},{9,... | collective-permute-start | bytes 245768 | tf_op jit(solution)/shard_map/ppermute | solution.py:509
  86.3 1.7 %collective-permute-done.25.refs_2_ = bf16[2,80,256]{2,1,0:T(8,128)(2,1)S(1)} collective-permute-done((bf16[2,80,256]{2,1,0:T(8,128)(2,1)S(1)}, bf16[2,80,256]{2,1,0:T(8,128)(2,1)S(1)}, u32[]{:S(2)}, u32[]{:S(2)}) %collective-permute-start.25) | collective-permute-done | bytes 81952 | tf_op jit(solution)/shard_map/ppermute | solution.py:509
  88.0 3.5 %collective-permute-done.26.refs_3_ = bf16[2,80,256]{2,1,0:T(8,128)(2,1)S(1)} collective-permute-done((bf16[2,80,256]{2,1,0:T(8,128)(2,1)S(1)}, bf16[2,80,256]{2,1,0:T(8,128)(2,1)S(1)}, u32[]{:S(2)}, u32[]{:S(2)}) %collective-permute-start.26) | collective-permute-done | bytes 81952 | tf_op jit(solution)/shard_map/ppermute | solution.py:509
  92.9 2.1 %collective-permute-start.20 = (bf16[256,256]{1,0:T(8,128)(2,1)S(1)}, bf16[256,256]{1,0:T(8,128)(2,1)S(1)}, u32[]{:S(2)}, u32[]{:S(2)}) collective-permute-start(bf16[256,256]{1,0:T(8,128)(2,1)S(1)} %get-tuple-element.106.refs_1_), channel_id=1, source_target_pairs={{0,4},{1,5},{2,6},{3,7},{4,0},{5,1},{6,2},{7,3},{8,12},{9,13},{10,... | collective-permute-start | bytes 393224 | tf_op jit(solution)/shard_map/ppermute | solution.py:509
  95.0 1.7 %collective-permute-done.27.other_ref = bf16[2,64,256]{2,1,0:T(8,128)(2,1)S(1)} collective-permute-done((bf16[2,64,256]{2,1,0:T(8,128)(2,1)S(1)}, bf16[2,64,256]{2,1,0:T(8,128)(2,1)S(1)}, u32[]{:S(2)}, u32[]{:S(2)}) %collective-permute-start.27) | collective-permute-done | bytes 65568 | tf_op jit(solution)/shard_map/ppermute | solution.py:509
  98.6 1.8 %collective-permute-start.21 = (bf16[512,256]{1,0:T(8,128)(2,1)S(1)}, bf16[512,256]{1,0:T(8,128)(2,1)S(1)}, u32[]{:S(2)}, u32[]{:S(2)}) collective-permute-start(bf16[512,256]{1,0:T(8,128)(2,1)S(1)} %get-tuple-element.107.half_one), channel_id=1, source_target_pairs={{0,4},{1,5},{2,6},{3,7},{4,0},{5,1},{6,2},{7,3},{8,12},{9,13},{10,... | collective-permute-start | bytes 786440 | tf_op jit(solution)/shard_map/ppermute | solution.py:509
  105.4 2.5 %collective-permute-done.21.dep_ref.far_one = bf16[512,256]{1,0:T(8,128)(2,1)S(1)} collective-permute-done((bf16[512,256]{1,0:T(8,128)(2,1)S(1)}, bf16[512,256]{1,0:T(8,128)(2,1)S(1)}, u32[]{:S(2)}, u32[]{:S(2)}) %collective-permute-start.21) | collective-permute-done | bytes 262176 | tf_op jit(solution)/shard_map/ppermute | solution.py:509
  108.5 1.8 %features.1.total_ref = f32[384,1024]{1,0:T(8,128)S(1)} custom-call(bf16[384,512]{1,0:T(8,128)(2,1)S(1)} %get-tuple-element.84.own_one, bf16[384,512]{1,0:T(8,128)(2,1)S(1)} %get-tuple-element.91.own_two, bf16[384,1024]{1,0:T(8,128)(2,1)S(1)} %get-tuple-element.81.dskip_ref, bf16[1024,1024]{1,0:T(8,128)(2,1)S(1)} %copy-done, ...), custom_call_target="tpu_custom_call" | custom-call | flops 110000000 | bytes 100000 | tf_op jit(solution)/shard_map/features/pallas_call | solution.py:715
  110.3 2.1 %features_halo.1.rest_0_ = bf16[376,1024]{1,0:T(8,128)(2,1)} custom-call(f32[384,1024]{1,0:T(8,128)S(1)} %features.1.total_ref, bf16[48,1024]{1,0:T(8,128)(2,1)S(1)} %collective-permute-done.22.near_ref.refs_4_, bf16[48,1024]{1,0:T(8,128)(2,1)S(1)} %collective-permute-done.23.far_ref.refs_5_, s32[1,2,47]{2,1,0:T(2,128)S(1)} %copy-done.9, ...), custom_call_target="tpu_custom_call" | custom-call | flops 110000000 | bytes 100000 | tf_op jit(solution)/shard_map/features_halo/pallas_call | solution.py:736
  112.5 2.4 %collective-permute-done.37.far_two = bf16[512,256]{1,0:T(8,128)(2,1)S(1)} collective-permute-done((bf16[512,256]{1,0:T(8,128)(2,1)S(1)}, bf16[512,256]{1,0:T(8,128)(2,1)S(1)}, u32[]{:S(2)}, u32[]{:S(2)}) %collective-permute-start.37) | collective-permute-done | bytes 262176 | tf_op jit(solution)/shard_map/ppermute | solution.py:509
  122.3 1.6 %assemble.5 = f32[1024,1024]{1,0:T(8,128)} custom-call(bf16[2,256,256]{2,1,0:T(8,128)(2,1)S(1)} %collective-permute-done.30.refs_0_, bf16[2,256,256]{2,1,0:T(8,128)(2,1)S(1)} %collective-permute-done.32.refs_1_, bf16[2,256,256]{2,1,0:T(8,128)(2,1)S(1)} %collective-permute-done.34.refs_2_, ...), custom_call_target="tpu_custom_call", output_to_operand_aliasing={{}: (4, {})} | custom-call | flops 110000000 | bytes 100000 | tf_op jit(solution)/shard_map/assemble/pallas_call | solution.py:668
  123.9 1.6 %assemble.7 = f32[1024,1024]{1,0:T(8,128)} custom-call(bf16[2,512,256]{2,1,0:T(8,128)(2,1)S(1)} %collective-permute-done.38.refs_0_, bf16[2,512,256]{2,1,0:T(8,128)(2,1)S(1)} %collective-permute-done.39.refs_1_, f32[1024,1024]{1,0:T(8,128)} %assemble.6.refs_2_), custom_call_target="tpu_custom_call", output_to_operand_aliasing={{}: (2, {})} | custom-call | flops 110000000 | bytes 100000 | tf_op jit(solution)/shard_map/assemble/pallas_call | solution.py:668
  (103 shorter events, 31.2 us)
Async XLA Ops:
  2.2 7.7 %collective-permute-start = (bf16[48,1024]{1,0:T(8,128)(2,1)S(1)}, bf16[48,1024]{1,0:T(8,128)(2,1)S(1)}, u32[]{:S(2)}, u32[]{:S(2)}) collective-permute-start(bf16[48,1024]{1,0:T(8,128)(2,1)S(1)} %get-tuple-element.68), channel_id=1, source_target_pairs={{0,1},{1,0},{2,3},{3,2},{4,5},{5,4},{6,7},{7,6},{8,9},{9,8},{10,11... | collective-permute-start | bytes 294920 | tf_op jit(solution)/shard_map/ppermute | solution.py:509
  2.8 7.2 %collective-permute-start.1 = (bf16[48,1024]{1,0:T(8,128)(2,1)S(1)}, bf16[48,1024]{1,0:T(8,128)(2,1)S(1)}, u32[]{:S(2)}, u32[]{:S(2)}) collective-permute-start(bf16[48,1024]{1,0:T(8,128)(2,1)S(1)} %get-tuple-element.69), channel_id=1, source_target_pairs={{1,2},{3,4},{5,6},{7,8},{9,10},{11,12},{13,14},{15,16},{17,18},{19... | collective-permute-start | bytes 294920 | tf_op jit(solution)/shard_map/ppermute | solution.py:506
  33.9 5.0 %collective-permute-start.6 = (f32[8,1024]{1,0:T(8,128)S(1)}, f32[8,1024]{1,0:T(8,128)S(1)}, u32[]{:S(2)}, u32[]{:S(2)}) collective-permute-start(f32[8,1024]{1,0:T(8,128)S(1)} %merge.7.stats_ref), channel_id=1, source_target_pairs={{0,16},{1,17},{2,18},{3,19},{4,20},{5,21},{6,22},{7,23},{8,24},{9,... | collective-permute-start | bytes 98312 | tf_op jit(solution)/shard_map/ppermute | solution.py:509
  46.4 8.4 %collective-permute-start.11 = (bf16[2,1040,256]{2,1,0:T(8,128)(2,1)S(1)}, bf16[2,1040,256]{2,1,0:T(8,128)(2,1)S(1)}, u32[]{:S(2)}, u32[]{:S(2)}) collective-permute-start(bf16[2,1040,256]{2,1,0:T(8,128)(2,1)S(1)} %get-tuple-element.89.outs_0_), channel_id=1, source_target_pairs={{0,1},{1,0},{2,3},{3,2},{4,5},{5,4},{6,7},{7,6},{8,9},{9,8},{10,11... | collective-permute-start | bytes 3194888 | tf_op jit(solution)/shard_map/ppermute | solution.py:509
  47.2 10.1 %collective-permute-start.8 = (bf16[2,256,256]{2,1,0:T(8,128)(2,1)S(1)}, bf16[2,256,256]{2,1,0:T(8,128)(2,1)S(1)}, u32[]{:S(2)}, u32[]{:S(2)}) collective-permute-start(bf16[2,256,256]{2,1,0:T(8,128)(2,1)S(1)} %get-tuple-element.92), channel_id=1, source_target_pairs={{0,2},{1,3},{2,0},{3,1},{4,6},{5,7},{6,4},{7,5},{8,10},{9,11},{10,... | collective-permute-start | bytes 786440 | tf_op jit(solution)/shard_map/ppermute | solution.py:509
  47.8 10.8 %collective-permute-start.9 = (bf16[2,256,256]{2,1,0:T(8,128)(2,1)S(1)}, bf16[2,256,256]{2,1,0:T(8,128)(2,1)S(1)}, u32[]{:S(2)}, u32[]{:S(2)}) collective-permute-start(bf16[2,256,256]{2,1,0:T(8,128)(2,1)S(1)} %get-tuple-element.93), channel_id=1, source_target_pairs={{0,4},{1,5},{2,6},{3,7},{4,0},{5,1},{6,2},{7,3},{8,12},{9,13},{10,... | collective-permute-start | bytes 786440 | tf_op jit(solution)/shard_map/ppermute | solution.py:509
  49.4 14.2 %collective-permute-start.10 = (bf16[2,256,256]{2,1,0:T(8,128)(2,1)S(1)}, bf16[2,256,256]{2,1,0:T(8,128)(2,1)S(1)}, u32[]{:S(2)}, u32[]{:S(2)}) collective-permute-start(bf16[2,256,256]{2,1,0:T(8,128)(2,1)S(1)} %get-tuple-element.94), channel_id=1, source_target_pairs={{0,6},{1,7},{2,4},{3,5},{4,2},{5,3},{6,0},{7,1},{8,14},{9,15},{10,... | collective-permute-start | bytes 786440 | tf_op jit(solution)/shard_map/ppermute | solution.py:509
  55.1 17.2 %collective-permute-start.14 = (bf16[2,272,256]{2,1,0:T(8,128)(2,1)S(1)}, bf16[2,272,256]{2,1,0:T(8,128)(2,1)S(1)}, u32[]{:S(2)}, u32[]{:S(2)}) collective-permute-start(bf16[2,272,256]{2,1,0:T(8,128)(2,1)S(1)} %get-tuple-element.101), channel_id=1, source_target_pairs={{0,2},{1,3},{2,0},{3,1},{4,6},{5,7},{6,4},{7,5},{8,10},{9,11},{10,... | collective-permute-start | bytes 835592 | tf_op jit(solution)/shard_map/ppermute | solution.py:509
  55.8 16.5 %collective-permute-start.15 = (bf16[2,272,256]{2,1,0:T(8,128)(2,1)S(1)}, bf16[2,272,256]{2,1,0:T(8,128)(2,1)S(1)}, u32[]{:S(2)}, u32[]{:S(2)}) collective-permute-start(bf16[2,272,256]{2,1,0:T(8,128)(2,1)S(1)} %get-tuple-element.102), channel_id=1, source_target_pairs={{0,4},{1,5},{2,6},{3,7},{4,0},{5,1},{6,2},{7,3},{8,12},{9,13},{10,... | collective-permute-start | bytes 835592 | tf_op jit(solution)/shard_map/ppermute | solution.py:509
  57.3 17.0 %collective-permute-start.16 = (bf16[2,272,256]{2,1,0:T(8,128)(2,1)S(1)}, bf16[2,272,256]{2,1,0:T(8,128)(2,1)S(1)}, u32[]{:S(2)}, u32[]{:S(2)}) collective-permute-start(bf16[2,272,256]{2,1,0:T(8,128)(2,1)S(1)} %get-tuple-element.103), channel_id=1, source_target_pairs={{0,6},{1,7},{2,4},{3,5},{4,2},{5,3},{6,0},{7,1},{8,14},{9,15},{10,... | collective-permute-start | bytes 835592 | tf_op jit(solution)/shard_map/ppermute | solution.py:509
  63.7 5.0 %collective-permute-start.12 = (bf16[2,128,256]{2,1,0:T(8,128)(2,1)S(1)}, bf16[2,128,256]{2,1,0:T(8,128)(2,1)S(1)}, u32[]{:S(2)}, u32[]{:S(2)}) collective-permute-start(bf16[2,128,256]{2,1,0:T(8,128)(2,1)S(1)} %get-tuple-element.98), channel_id=1, source_target_pairs={{0,8},{1,9},{2,10},{3,11},{4,12},{5,13},{6,14},{7,15},{8,0},{9,1},... | collective-permute-start | bytes 393224 | tf_op jit(solution)/shard_map/ppermute | solution.py:509
  68.8 5.7 %collective-permute-start.13 = (bf16[2,64,256]{2,1,0:T(8,128)(2,1)S(1)}, bf16[2,64,256]{2,1,0:T(8,128)(2,1)S(1)}, u32[]{:S(2)}, u32[]{:S(2)}) collective-permute-start(bf16[2,64,256]{2,1,0:T(8,128)(2,1)S(1)} %get-tuple-element.100), channel_id=1, source_target_pairs={{0,16},{1,17},{2,18},{3,19},{4,20},{5,21},{6,22},{7,23},{8,24},{9,... | collective-permute-start | bytes 196616 | tf_op jit(solution)/shard_map/ppermute | solution.py:509
  74.5 8.9 %collective-permute-start.17 = (bf16[2,64,256]{2,1,0:T(8,128)(2,1)S(1)}, bf16[2,64,256]{2,1,0:T(8,128)(2,1)S(1)}, u32[]{:S(2)}, u32[]{:S(2)}) collective-permute-start(bf16[2,64,256]{2,1,0:T(8,128)(2,1)S(1)} %s_line.3.mine_ref), channel_id=1, source_target_pairs={{0,16},{1,17},{2,18},{3,19},{4,20},{5,21},{6,22},{7,23},{8,24},{9,... | collective-permute-start | bytes 196616 | tf_op jit(solution)/shard_map/ppermute | solution.py:509
  77.6 8.5 %collective-permute-start.24 = (bf16[2,80,256]{2,1,0:T(8,128)(2,1)S(1)}, bf16[2,80,256]{2,1,0:T(8,128)(2,1)S(1)}, u32[]{:S(2)}, u32[]{:S(2)}) collective-permute-start(bf16[2,80,256]{2,1,0:T(8,128)(2,1)S(1)} %get-tuple-element.112), channel_id=1, source_target_pairs={{0,16},{1,17},{2,18},{3,19},{4,20},{5,21},{6,22},{7,23},{8,24},{9,... | collective-permute-start | bytes 245768 | tf_op jit(solution)/shard_map/ppermute | solution.py:509
  77.7 13.8 %collective-permute-start.22 = (bf16[48,1024]{1,0:T(8,128)(2,1)S(1)}, bf16[48,1024]{1,0:T(8,128)(2,1)S(1)}, u32[]{:S(2)}, u32[]{:S(2)}) collective-permute-start(bf16[48,1024]{1,0:T(8,128)(2,1)S(1)} %get-tuple-element.109), channel_id=1, source_target_pairs={{0,1},{1,0},{2,3},{3,2},{4,5},{5,4},{6,7},{7,6},{8,9},{9,8},{10,11... | collective-permute-start | bytes 294920 | tf_op jit(solution)/shard_map/ppermute | solution.py:509
  77.7 13.8 %collective-permute-start.23 = (bf16[48,1024]{1,0:T(8,128)(2,1)S(1)}, bf16[48,1024]{1,0:T(8,128)(2,1)S(1)}, u32[]{:S(2)}, u32[]{:S(2)}) collective-permute-start(bf16[48,1024]{1,0:T(8,128)(2,1)S(1)} %get-tuple-element.111), channel_id=1, source_target_pairs={{1,2},{3,4},{5,6},{7,8},{9,10},{11,12},{13,14},{15,16},{17,18},{19... | collective-permute-start | bytes 294920 | tf_op jit(solution)/shard_map/ppermute | solution.py:506
  78.3 9.6 %collective-permute-start.25 = (bf16[2,80,256]{2,1,0:T(8,128)(2,1)S(1)}, bf16[2,80,256]{2,1,0:T(8,128)(2,1)S(1)}, u32[]{:S(2)}, u32[]{:S(2)}) collective-permute-start(bf16[2,80,256]{2,1,0:T(8,128)(2,1)S(1)} %get-tuple-element.113), channel_id=1, source_target_pairs={{0,8},{1,9},{2,10},{3,11},{4,12},{5,13},{6,14},{7,15},{8,0},{9,1},... | collective-permute-start | bytes 245768 | tf_op jit(solution)/shard_map/ppermute | solution.py:509
  83.4 8.0 %collective-permute-start.26 = (bf16[2,80,256]{2,1,0:T(8,128)(2,1)S(1)}, bf16[2,80,256]{2,1,0:T(8,128)(2,1)S(1)}, u32[]{:S(2)}, u32[]{:S(2)}) collective-permute-start(bf16[2,80,256]{2,1,0:T(8,128)(2,1)S(1)} %get-tuple-element.114), channel_id=1, source_target_pairs={{0,24},{1,25},{2,26},{3,27},{4,28},{5,29},{6,30},{7,31},{8,16},{9,... | collective-permute-start | bytes 245768 | tf_op jit(solution)/shard_map/ppermute | solution.py:509
  86.1 6.6 %collective-permute-start.18 = (bf16[2,128,256]{2,1,0:T(8,128)(2,1)S(1)}, bf16[2,128,256]{2,1,0:T(8,128)(2,1)S(1)}, u32[]{:S(2)}, u32[]{:S(2)}) collective-permute-start(bf16[2,128,256]{2,1,0:T(8,128)(2,1)S(1)} %s_join.1.mine_ref), channel_id=1, source_target_pairs={{0,8},{1,9},{2,10},{3,11},{4,12},{5,13},{6,14},{7,15},{8,0},{9,1},... | collective-permute-start | bytes 393224 | tf_op jit(solution)/shard_map/ppermute | solution.py:509
  91.5 5.2 %collective-permute-start.27 = (bf16[2,64,256]{2,1,0:T(8,128)(2,1)S(1)}, bf16[2,64,256]{2,1,0:T(8,128)(2,1)S(1)}, u32[]{:S(2)}, u32[]{:S(2)}) collective-permute-start(bf16[2,64,256]{2,1,0:T(8,128)(2,1)S(1)} %get-tuple-element.115.mine_ref), channel_id=1, source_target_pairs={{0,16},{1,17},{2,18},{3,19},{4,20},{5,21},{6,22},{7,23},{8,24},{9,... | collective-permute-start | bytes 196616 | tf_op jit(solution)/shard_map/ppermute | solution.py:509
  92.8 5.0 %collective-permute-start.19 = (bf16[256,256]{1,0:T(8,128)(2,1)S(1)}, bf16[256,256]{1,0:T(8,128)(2,1)S(1)}, u32[]{:S(2)}, u32[]{:S(2)}) collective-permute-start(bf16[256,256]{1,0:T(8,128)(2,1)S(1)} %get-tuple-element.105.refs_0_), channel_id=1, source_target_pairs={{0,2},{1,3},{2,0},{3,1},{4,6},{5,7},{6,4},{7,5},{8,10},{9,11},{10,... | collective-permute-start | bytes 393224 | tf_op jit(solution)/shard_map/ppermute | solution.py:509
  92.9 5.6 %collective-permute-start.20 = (bf16[256,256]{1,0:T(8,128)(2,1)S(1)}, bf16[256,256]{1,0:T(8,128)(2,1)S(1)}, u32[]{:S(2)}, u32[]{:S(2)}) collective-permute-start(bf16[256,256]{1,0:T(8,128)(2,1)S(1)} %get-tuple-element.106.refs_1_), channel_id=1, source_target_pairs={{0,4},{1,5},{2,6},{3,7},{4,0},{5,1},{6,2},{7,3},{8,12},{9,13},{10,... | collective-permute-start | bytes 393224 | tf_op jit(solution)/shard_map/ppermute | solution.py:509
  96.8 5.0 %collective-permute-start.28 = (bf16[2,128,256]{2,1,0:T(8,128)(2,1)S(1)}, bf16[2,128,256]{2,1,0:T(8,128)(2,1)S(1)}, u32[]{:S(2)}, u32[]{:S(2)}) collective-permute-start(bf16[2,128,256]{2,1,0:T(8,128)(2,1)S(1)} %p_join.2.mine_ref), channel_id=1, source_target_pairs={{0,8},{1,9},{2,10},{3,11},{4,12},{5,13},{6,14},{7,15},{8,0},{9,1},... | collective-permute-start | bytes 393224 | tf_op jit(solution)/shard_map/ppermute | solution.py:509
  98.6 9.3 %collective-permute-start.21 = (bf16[512,256]{1,0:T(8,128)(2,1)S(1)}, bf16[512,256]{1,0:T(8,128)(2,1)S(1)}, u32[]{:S(2)}, u32[]{:S(2)}) collective-permute-start(bf16[512,256]{1,0:T(8,128)(2,1)S(1)} %get-tuple-element.107.half_one), channel_id=1, source_target_pairs={{0,4},{1,5},{2,6},{3,7},{4,0},{5,1},{6,2},{7,3},{8,12},{9,13},{10,... | collective-permute-start | bytes 786440 | tf_op jit(solution)/shard_map/ppermute | solution.py:509
  100.4 14.5 %collective-permute-start.37 = (bf16[512,256]{1,0:T(8,128)(2,1)S(1)}, bf16[512,256]{1,0:T(8,128)(2,1)S(1)}, u32[]{:S(2)}, u32[]{:S(2)}) collective-permute-start(bf16[512,256]{1,0:T(8,128)(2,1)S(1)} %get-tuple-element.117.half_two), channel_id=1, source_target_pairs={{0,2},{1,3},{2,0},{3,1},{4,6},{5,7},{6,4},{7,5},{8,10},{9,11},{10,... | collective-permute-start | bytes 786440 | tf_op jit(solution)/shard_map/ppermute | solution.py:509
  101.8 14.3 %collective-permute-start.35 = (bf16[2,256,256]{2,1,0:T(8,128)(2,1)S(1)}, bf16[2,256,256]{2,1,0:T(8,128)(2,1)S(1)}, u32[]{:S(2)}, u32[]{:S(2)}) collective-permute-start(bf16[2,256,256]{2,1,0:T(8,128)(2,1)S(1)} %p_join.3.refs_0_), channel_id=1, source_target_pairs={{0,6},{1,7},{2,4},{3,5},{4,2},{5,3},{6,0},{7,1},{8,14},{9,15},{10,... | collective-permute-start | bytes 786440 | tf_op jit(solution)/shard_map/ppermute | solution.py:509
  102.6 14.7 %collective-permute-start.33 = (bf16[2,256,256]{2,1,0:T(8,128)(2,1)S(1)}, bf16[2,256,256]{2,1,0:T(8,128)(2,1)S(1)}, u32[]{:S(2)}, u32[]{:S(2)}) collective-permute-start(bf16[2,256,256]{2,1,0:T(8,128)(2,1)S(1)} %p_join.3.refs_0_), channel_id=1, source_target_pairs={{0,4},{1,5},{2,6},{3,7},{4,0},{5,1},{6,2},{7,3},{8,12},{9,13},{10,... | collective-permute-start | bytes 786440 | tf_op jit(solution)/shard_map/ppermute | solution.py:509
  103.9 14.5 %collective-permute-start.31 = (bf16[2,256,256]{2,1,0:T(8,128)(2,1)S(1)}, bf16[2,256,256]{2,1,0:T(8,128)(2,1)S(1)}, u32[]{:S(2)}, u32[]{:S(2)}) collective-permute-start(bf16[2,256,256]{2,1,0:T(8,128)(2,1)S(1)} %p_join.3.refs_0_), channel_id=1, source_target_pairs={{0,2},{1,3},{2,0},{3,1},{4,6},{5,7},{6,4},{7,5},{8,10},{9,11},{10,... | collective-permute-start | bytes 786440 | tf_op jit(solution)/shard_map/ppermute | solution.py:509
  107.9 10.6 %collective-permute-start.30 = (bf16[2,256,256]{2,1,0:T(8,128)(2,1)S(1)}, bf16[2,256,256]{2,1,0:T(8,128)(2,1)S(1)}, u32[]{:S(2)}, u32[]{:S(2)}) collective-permute-start(bf16[2,256,256]{2,1,0:T(8,128)(2,1)S(1)} %p_join.3.refs_0_), channel_id=1, source_target_pairs={{0,1},{1,0},{2,3},{3,2},{4,5},{5,4},{6,7},{7,6},{8,9},{9,8},{10,11... | collective-permute-start | bytes 786440 | tf_op jit(solution)/shard_map/ppermute | solution.py:509
  116.1 7.8 %collective-permute-start.38 = (bf16[2,512,256]{2,1,0:T(8,128)(2,1)S(1)}, bf16[2,512,256]{2,1,0:T(8,128)(2,1)S(1)}, u32[]{:S(2)}, u32[]{:S(2)}) collective-permute-start(bf16[2,512,256]{2,1,0:T(8,128)(2,1)S(1)} %get-tuple-element.119.refs_0_), channel_id=1, source_target_pairs={{0,1},{1,0},{2,3},{3,2},{4,5},{5,4},{6,7},{7,6},{8,9},{9,8},{10,11... | collective-permute-start | bytes 1572872 | tf_op jit(solution)/shard_map/ppermute | solution.py:509
  116.1 7.8 %collective-permute-start.39 = (bf16[2,512,256]{2,1,0:T(8,128)(2,1)S(1)}, bf16[2,512,256]{2,1,0:T(8,128)(2,1)S(1)}, u32[]{:S(2)}, u32[]{:S(2)}) collective-permute-start(bf16[2,512,256]{2,1,0:T(8,128)(2,1)S(1)} %get-tuple-element.120.refs_1_), channel_id=1, source_target_pairs={{0,1},{1,0},{2,3},{3,2},{4,5},{5,4},{6,7},{7,6},{8,9},{9,8},{10,11... | collective-permute-start | bytes 1572872 | tf_op jit(solution)/shard_map/ppermute | solution.py:509
  117.4 4.9 %collective-permute-start.36 = (bf16[2,256,256]{2,1,0:T(8,128)(2,1)S(1)}, bf16[2,256,256]{2,1,0:T(8,128)(2,1)S(1)}, u32[]{:S(2)}, u32[]{:S(2)}) collective-permute-start(bf16[2,256,256]{2,1,0:T(8,128)(2,1)S(1)} %collective-permute-done.35.refs_3_), channel_id=1, source_target_pairs={{0,1},{1,0},{2,3},{3,2},{4,5},{5,4},{6,7},{7,6},{8,9},{9,8},{10,11... | collective-permute-start | bytes 786440 | tf_op jit(solution)/shard_map/ppermute | solution.py:509
  (20 other events, 149.6 us)

commit v8 on v7

--- a/solution.py
+++ b/solution.py
@@ -738,7 +738,7 @@
         in_specs=[vmem] * 5,
         out_specs=vmem,
         scratch_shapes=[pltpu.VMEM((8, 2 * LANES), jnp.int32)],
-        out_shape=jax.ShapeDtypeStruct((node_rows, depth), BF16),
+        out_shape=pltpu.HBM((node_rows, depth), BF16),
         compiler_params=params(8),
         cost_estimate=cost(0.1),
         name="features_halo",

time: 126 us -> 126 us (level)
  no operation moved by 1% of the time
where the time goes in v8:
time: 126 us
  starting transfers between devices  48.5 us (38%)
  Pallas kernels  37.9 us (30%)
  waiting for transfers between devices  36.8 us (29%)
    ppermute x38, starting transfers between devices, swapped(): lax.ppermute(value, AXES, [(source, source ^ distance) for source in rang...  47.2 us
    ppermute x38, waiting for transfers between devices, swapped(): lax.ppermute(value, AXES, [(source, source ^ distance) for source in rang...  36.8 us
    pallas_call x2, Pallas kernels, backward(): pl.pallas_call(functools.partial(back_kernel, part=part), in_specs=[vmem]...  7.94 us
    pallas_call x4, Pallas kernels, assemble(): pl.pallas_call(functools.partial(assemble_kernel, first=first, pieces=len...  6.46 us
    pallas_call x1, Pallas kernels, per_device(): pl.pallas_call(functools.partial(project_kernel, halo=halo), grid=(heads,...  6.44 us
    pallas_call x1, Pallas kernels, per_device(): pl.pallas_call(attend_kernel, in_specs=[vmem] * 11, out_shape=[shape_of((...  6.2 us
    pallas_call x1, Pallas kernels, per_device(): pl.pallas_call(functools.partial(norm_kernel, last_bit=bits - 1), in_spec...  3.48 us
  transfers between devices with their start and end apart: 40, of which 20 were waited for; matrix products, arithmetic and copies ran while one was open for 0% of the time, Pallas kernels for 20%

profile of v8, /device:TPU:0, one launch (start us, length us, event | category | flops | bytes accessed | tf_op | source)
XLA Modules:
  0.0 125.7 jit_solution(4318718132081320656)
XLA Ops:
  3.5 6.4 %project.1 = (bf16[384,1024]{1,0:T(8,128)(2,1)S(1)}, f32[384,1024]{1,0:T(8,128)S(1)}, f32[512,384]{1,0:T(8,128)S(1)}, bf16[1024,384]{1,0:T(8,128)(2,1)S(1)}) custom-call(bf16[376,1024]{1,0:T(8,128)(2,1)} %feats_ref.3, bf16[1024,1024]{1,0:T(8,128)(2,1)} %proj_ref.7, bf16[1024,1024]{1,0:T(8,128)(2,1)} %skip_ref.1, s32[16,376]{1,0:T(8,128)} %bitcast.11, ...), custom_call_target="tpu_custom_call" | custom-call | flops 5500000256 | bytes 5000000 | tf_op jit(solution)/shard_map/project/pallas_call | solution.py:533
  10.1 6.2 %attend.1 = (bf16[512,1024]{1,0:T(8,128)(2,1)S(1)}, bf16[4,512,384]{2,1,0:T(8,128)(2,1)S(1)}, f32[4,512,128]{2,1,0:T(8,128)S(1)}, f32[4,8,384]{2,1,0:T(8,128)S(1...) custom-call(bf16[384,1024]{1,0:T(8,128)(2,1)S(1)} %get-tuple-element, ...), custom_call_target="tpu_custom_call" | custom-call | flops 8800000000 | bytes 8000000 | tf_op jit(solution)/shard_map/attend/pallas_call | solution.py:554
  16.3 4.0 %collective-permute-start.2 = (f32[8,1024]{1,0:T(8,128)S(1)}, f32[8,1024]{1,0:T(8,128)S(1)}, u32[]{:S(2)}, u32[]{:S(2)}) collective-permute-start(f32[8,1024]{1,0:T(8,128)S(1)} %get-tuple-element.73.mine_ref), channel_id=1, source_target_pairs={{0,1},{1,0},{2,3},{3,2},{4,5},{5,4},{6,7},{7,6},{8,9},{9,8},{10,11... | collective-permute-start | bytes 98312 | tf_op jit(solution)/shard_map/ppermute | solution.py:509
  22.6 2.5 %collective-permute-done.3.other_ref = f32[8,1024]{1,0:T(8,128)S(1)} collective-permute-done((f32[8,1024]{1,0:T(8,128)S(1)}, f32[8,1024]{1,0:T(8,128)S(1)}, u32[]{:S(2)}, u32[]{:S(2)}) %collective-permute-start.3) | collective-permute-done | bytes 32800 | tf_op jit(solution)/shard_map/ppermute | solution.py:509
  25.2 1.8 %collective-permute-start.4 = (f32[8,1024]{1,0:T(8,128)S(1)}, f32[8,1024]{1,0:T(8,128)S(1)}, u32[]{:S(2)}, u32[]{:S(2)}) collective-permute-start(f32[8,1024]{1,0:T(8,128)S(1)} %merge.5.mine_ref), channel_id=1, source_target_pairs={{0,4},{1,5},{2,6},{3,7},{4,0},{5,1},{6,2},{7,3},{8,12},{9,13},{10,... | collective-permute-start | bytes 98312 | tf_op jit(solution)/shard_map/ppermute | solution.py:509
  27.0 2.1 %collective-permute-done.4.other_ref = f32[8,1024]{1,0:T(8,128)S(1)} collective-permute-done((f32[8,1024]{1,0:T(8,128)S(1)}, f32[8,1024]{1,0:T(8,128)S(1)}, u32[]{:S(2)}, u32[]{:S(2)}) %collective-permute-start.4) | collective-permute-done | bytes 32800 | tf_op jit(solution)/shard_map/ppermute | solution.py:509
  29.2 2.8 %collective-permute-start.5 = (f32[8,1024]{1,0:T(8,128)S(1)}, f32[8,1024]{1,0:T(8,128)S(1)}, u32[]{:S(2)}, u32[]{:S(2)}) collective-permute-start(f32[8,1024]{1,0:T(8,128)S(1)} %merge.6.mine_ref), channel_id=1, source_target_pairs={{0,8},{1,9},{2,10},{3,11},{4,12},{5,13},{6,14},{7,15},{8,0},{9,1},... | collective-permute-start | bytes 98312 | tf_op jit(solution)/shard_map/ppermute | solution.py:509
  32.0 1.9 %collective-permute-done.5.other_ref = f32[8,1024]{1,0:T(8,128)S(1)} collective-permute-done((f32[8,1024]{1,0:T(8,128)S(1)}, f32[8,1024]{1,0:T(8,128)S(1)}, u32[]{:S(2)}, u32[]{:S(2)}) %collective-permute-start.5) | collective-permute-done | bytes 32800 | tf_op jit(solution)/shard_map/ppermute | solution.py:509
  33.9 3.1 %collective-permute-start.6 = (f32[8,1024]{1,0:T(8,128)S(1)}, f32[8,1024]{1,0:T(8,128)S(1)}, u32[]{:S(2)}, u32[]{:S(2)}) collective-permute-start(f32[8,1024]{1,0:T(8,128)S(1)} %merge.7.stats_ref), channel_id=1, source_target_pairs={{0,16},{1,17},{2,18},{3,19},{4,20},{5,21},{6,22},{7,23},{8,24},{9,... | collective-permute-start | bytes 98312 | tf_op jit(solution)/shard_map/ppermute | solution.py:509
  37.0 1.9 %collective-permute-done.6.other_ref = f32[8,1024]{1,0:T(8,128)S(1)} collective-permute-done((f32[8,1024]{1,0:T(8,128)S(1)}, f32[8,1024]{1,0:T(8,128)S(1)}, u32[]{:S(2)}, u32[]{:S(2)}) %collective-permute-start.6) | collective-permute-done | bytes 32800 | tf_op jit(solution)/shard_map/ppermute | solution.py:509
  38.9 3.5 %norm.1 = (bf16[376,1024]{1,0:T(8,128)(2,1)}, bf16[384,1024]{1,0:T(8,128)(2,1)S(1)}, bf16[2,1024,256]{2,1,0:T(8,128)(2,1)S(1)}, bf16[2,1024,256]{2,1,0:T(8,128)(...) custom-call(f32[384,1024]{1,0:T(8,128)S(1)} %get-tuple-element.72.pre_ref, ...), custom_call_target="tpu_custom_call" | custom-call | flops 110000000 | bytes 100000 | tf_op jit(solution)/shard_map/norm/pallas_call | solution.py:584
  42.5 3.9 %back.2 = (bf16[2,1040,256]{2,1,0:T(8,128)(2,1)S(1)}, bf16[384,512]{1,0:T(8,128)(2,1)S(1)}, bf16[48,512]{1,0:T(8,128)(2,1)S(1)}, bf16[48,512]{1,0:T(8,128)(2,1)S(1)}) custom-call(bf16[4,512,384]{2,1,0:T(8,128)(2,1)S(1)} %get-tuple-element.76.weight_ref, f32[4,512,128]{2,1,0:T(8,128)S(1)} %get-tuple-element.77.source_ref, ...), custom_call_target="tpu_custom_call" | custom-call | flops 110000000 | bytes 100000 | tf_op jit(solution)/shard_map/back/pallas_call | solution.py:604
  50.7 4.1 %back.3 = (bf16[2,1040,256]{2,1,0:T(8,128)(2,1)S(1)}, bf16[384,512]{1,0:T(8,128)(2,1)S(1)}, bf16[48,1024]{1,0:T(8,128)(2,1)S(1)}, bf16[48,1024]{1,0:T(8,128)(2,1)S(1)}) custom-call(bf16[4,512,384]{2,1,0:T(8,128)(2,1)S(1)} %get-tuple-element.76.weight_ref, f32[4,512,128]{2,1,0:T(8,128)S(1)} %get-tuple-element.77.source_ref, ...), custom_call_target="tpu_custom_call" | custom-call | flops 110000000 | bytes 100000 | tf_op jit(solution)/shard_map/back/pallas_call | solution.py:604
  58.6 4.9 %collective-permute-done.10.refs_3_ = bf16[2,256,256]{2,1,0:T(8,128)(2,1)S(1)} collective-permute-done((bf16[2,256,256]{2,1,0:T(8,128)(2,1)S(1)}, bf16[2,256,256]{2,1,0:T(8,128)(2,1)S(1)}, u32[]{:S(2)}, u32[]{:S(2)}) %collective-permute-start.10) | collective-permute-done | bytes 262176 | tf_op jit(solution)/shard_map/ppermute | solution.py:509
  63.7 2.0 %collective-permute-start.12 = (bf16[2,128,256]{2,1,0:T(8,128)(2,1)S(1)}, bf16[2,128,256]{2,1,0:T(8,128)(2,1)S(1)}, u32[]{:S(2)}, u32[]{:S(2)}) collective-permute-start(bf16[2,128,256]{2,1,0:T(8,128)(2,1)S(1)} %get-tuple-element.98), channel_id=1, source_target_pairs={{0,8},{1,9},{2,10},{3,11},{4,12},{5,13},{6,14},{7,15},{8,0},{9,1},... | collective-permute-start | bytes 393224 | tf_op jit(solution)/shard_map/ppermute | solution.py:509
  65.7 3.1 %collective-permute-done.12.other_ref = bf16[2,128,256]{2,1,0:T(8,128)(2,1)S(1)} collective-permute-done((bf16[2,128,256]{2,1,0:T(8,128)(2,1)S(1)}, bf16[2,128,256]{2,1,0:T(8,128)(2,1)S(1)}, u32[]{:S(2)}, u32[]{:S(2)}) %collective-permute-start.12) | collective-permute-done | bytes 131104 | tf_op jit(solution)/shard_map/ppermute | solution.py:509
  68.8 3.5 %collective-permute-start.13 = (bf16[2,64,256]{2,1,0:T(8,128)(2,1)S(1)}, bf16[2,64,256]{2,1,0:T(8,128)(2,1)S(1)}, u32[]{:S(2)}, u32[]{:S(2)}) collective-permute-start(bf16[2,64,256]{2,1,0:T(8,128)(2,1)S(1)} %get-tuple-element.100), channel_id=1, source_target_pairs={{0,16},{1,17},{2,18},{3,19},{4,20},{5,21},{6,22},{7,23},{8,24},{9,... | collective-permute-start | bytes 196616 | tf_op jit(solution)/shard_map/ppermute | solution.py:509
  72.3 2.0 %collective-permute-done.16.refs_3_ = bf16[2,272,256]{2,1,0:T(8,128)(2,1)S(1)} collective-permute-done((bf16[2,272,256]{2,1,0:T(8,128)(2,1)S(1)}, bf16[2,272,256]{2,1,0:T(8,128)(2,1)S(1)}, u32[]{:S(2)}, u32[]{:S(2)}) %collective-permute-start.16) | collective-permute-done | bytes 278560 | tf_op jit(solution)/shard_map/ppermute | solution.py:509
  74.5 3.1 %collective-permute-start.17 = (bf16[2,64,256]{2,1,0:T(8,128)(2,1)S(1)}, bf16[2,64,256]{2,1,0:T(8,128)(2,1)S(1)}, u32[]{:S(2)}, u32[]{:S(2)}) collective-permute-start(bf16[2,64,256]{2,1,0:T(8,128)(2,1)S(1)} %s_line.3.mine_ref), channel_id=1, source_target_pairs={{0,16},{1,17},{2,18},{3,19},{4,20},{5,21},{6,22},{7,23},{8,24},{9,... | collective-permute-start | bytes 196616 | tf_op jit(solution)/shard_map/ppermute | solution.py:509
  78.3 5.1 %collective-permute-start.25 = (bf16[2,80,256]{2,1,0:T(8,128)(2,1)S(1)}, bf16[2,80,256]{2,1,0:T(8,128)(2,1)S(1)}, u32[]{:S(2)}, u32[]{:S(2)}) collective-permute-start(bf16[2,80,256]{2,1,0:T(8,128)(2,1)S(1)} %get-tuple-element.113), channel_id=1, source_target_pairs={{0,8},{1,9},{2,10},{3,11},{4,12},{5,13},{6,14},{7,15},{8,0},{9,1},... | collective-permute-start | bytes 245768 | tf_op jit(solution)/shard_map/ppermute | solution.py:509
  83.4 2.7 %collective-permute-start.26 = (bf16[2,80,256]{2,1,0:T(8,128)(2,1)S(1)}, bf16[2,80,256]{2,1,0:T(8,128)(2,1)S(1)}, u32[]{:S(2)}, u32[]{:S(2)}) collective-permute-start(bf16[2,80,256]{2,1,0:T(8,128)(2,1)S(1)} %get-tuple-element.114), channel_id=1, source_target_pairs={{0,24},{1,25},{2,26},{3,27},{4,28},{5,29},{6,30},{7,31},{8,16},{9,... | collective-permute-start | bytes 245768 | tf_op jit(solution)/shard_map/ppermute | solution.py:509
  86.3 1.7 %collective-permute-done.25.refs_2_ = bf16[2,80,256]{2,1,0:T(8,128)(2,1)S(1)} collective-permute-done((bf16[2,80,256]{2,1,0:T(8,128)(2,1)S(1)}, bf16[2,80,256]{2,1,0:T(8,128)(2,1)S(1)}, u32[]{:S(2)}, u32[]{:S(2)}) %collective-permute-start.25) | collective-permute-done | bytes 81952 | tf_op jit(solution)/shard_map/ppermute | solution.py:509
  88.0 3.5 %collective-permute-done.26.refs_3_ = bf16[2,80,256]{2,1,0:T(8,128)(2,1)S(1)} collective-permute-done((bf16[2,80,256]{2,1,0:T(8,128)(2,1)S(1)}, bf16[2,80,256]{2,1,0:T(8,128)(2,1)S(1)}, u32[]{:S(2)}, u32[]{:S(2)}) %collective-permute-start.26) | collective-permute-done | bytes 81952 | tf_op jit(solution)/shard_map/ppermute | solution.py:509
  92.9 2.1 %collective-permute-start.20 = (bf16[256,256]{1,0:T(8,128)(2,1)S(1)}, bf16[256,256]{1,0:T(8,128)(2,1)S(1)}, u32[]{:S(2)}, u32[]{:S(2)}) collective-permute-start(bf16[256,256]{1,0:T(8,128)(2,1)S(1)} %get-tuple-element.106.refs_1_), channel_id=1, source_target_pairs={{0,4},{1,5},{2,6},{3,7},{4,0},{5,1},{6,2},{7,3},{8,12},{9,13},{10,... | collective-permute-start | bytes 393224 | tf_op jit(solution)/shard_map/ppermute | solution.py:509
  95.0 1.7 %collective-permute-done.27.other_ref = bf16[2,64,256]{2,1,0:T(8,128)(2,1)S(1)} collective-permute-done((bf16[2,64,256]{2,1,0:T(8,128)(2,1)S(1)}, bf16[2,64,256]{2,1,0:T(8,128)(2,1)S(1)}, u32[]{:S(2)}, u32[]{:S(2)}) %collective-permute-start.27) | collective-permute-done | bytes 65568 | tf_op jit(solution)/shard_map/ppermute | solution.py:509
  98.6 1.8 %collective-permute-start.21 = (bf16[512,256]{1,0:T(8,128)(2,1)S(1)}, bf16[512,256]{1,0:T(8,128)(2,1)S(1)}, u32[]{:S(2)}, u32[]{:S(2)}) collective-permute-start(bf16[512,256]{1,0:T(8,128)(2,1)S(1)} %get-tuple-element.107.half_one), channel_id=1, source_target_pairs={{0,4},{1,5},{2,6},{3,7},{4,0},{5,1},{6,2},{7,3},{8,12},{9,13},{10,... | collective-permute-start | bytes 786440 | tf_op jit(solution)/shard_map/ppermute | solution.py:509
  105.4 2.5 %collective-permute-done.21.dep_ref.far_one = bf16[512,256]{1,0:T(8,128)(2,1)S(1)} collective-permute-done((bf16[512,256]{1,0:T(8,128)(2,1)S(1)}, bf16[512,256]{1,0:T(8,128)(2,1)S(1)}, u32[]{:S(2)}, u32[]{:S(2)}) %collective-permute-start.21) | collective-permute-done | bytes 262176 | tf_op jit(solution)/shard_map/ppermute | solution.py:509
  108.5 1.8 %features.1.total_ref = f32[384,1024]{1,0:T(8,128)S(1)} custom-call(bf16[384,512]{1,0:T(8,128)(2,1)S(1)} %get-tuple-element.84.own_one, bf16[384,512]{1,0:T(8,128)(2,1)S(1)} %get-tuple-element.91.own_two, bf16[384,1024]{1,0:T(8,128)(2,1)S(1)} %get-tuple-element.81.dskip_ref, bf16[1024,1024]{1,0:T(8,128)(2,1)S(1)} %copy-done, ...), custom_call_target="tpu_custom_call" | custom-call | flops 110000000 | bytes 100000 | tf_op jit(solution)/shard_map/features/pallas_call | solution.py:715
  110.3 2.1 %features_halo.1.rest_0_ = bf16[376,1024]{1,0:T(8,128)(2,1)} custom-call(f32[384,1024]{1,0:T(8,128)S(1)} %features.1.total_ref, bf16[48,1024]{1,0:T(8,128)(2,1)S(1)} %collective-permute-done.22.near_ref.refs_4_, bf16[48,1024]{1,0:T(8,128)(2,1)S(1)} %collective-permute-done.23.far_ref.refs_5_, s32[1,2,47]{2,1,0:T(2,128)S(1)} %copy-done.9, ...), custom_call_target="tpu_custom_call" | custom-call | flops 110000000 | bytes 100000 | tf_op jit(solution)/shard_map/features_halo/pallas_call | solution.py:736
  112.5 2.4 %collective-permute-done.37.far_two = bf16[512,256]{1,0:T(8,128)(2,1)S(1)} collective-permute-done((bf16[512,256]{1,0:T(8,128)(2,1)S(1)}, bf16[512,256]{1,0:T(8,128)(2,1)S(1)}, u32[]{:S(2)}, u32[]{:S(2)}) %collective-permute-start.37) | collective-permute-done | bytes 262176 | tf_op jit(solution)/shard_map/ppermute | solution.py:509
  122.3 1.6 %assemble.5 = f32[1024,1024]{1,0:T(8,128)} custom-call(bf16[2,256,256]{2,1,0:T(8,128)(2,1)S(1)} %collective-permute-done.30.refs_0_, bf16[2,256,256]{2,1,0:T(8,128)(2,1)S(1)} %collective-permute-done.32.refs_1_, bf16[2,256,256]{2,1,0:T(8,128)(2,1)S(1)} %collective-permute-done.34.refs_2_, ...), custom_call_target="tpu_custom_call", output_to_operand_aliasing={{}: (4, {})} | custom-call | flops 110000000 | bytes 100000 | tf_op jit(solution)/shard_map/assemble/pallas_call | solution.py:668
  123.9 1.6 %assemble.7 = f32[1024,1024]{1,0:T(8,128)} custom-call(bf16[2,512,256]{2,1,0:T(8,128)(2,1)S(1)} %collective-permute-done.38.refs_0_, bf16[2,512,256]{2,1,0:T(8,128)(2,1)S(1)} %collective-permute-done.39.refs_1_, f32[1024,1024]{1,0:T(8,128)} %assemble.6.refs_2_), custom_call_target="tpu_custom_call", output_to_operand_aliasing={{}: (2, {})} | custom-call | flops 110000000 | bytes 100000 | tf_op jit(solution)/shard_map/assemble/pallas_call | solution.py:668
  (103 shorter events, 31.2 us)
Async XLA Ops:
  2.2 7.7 %collective-permute-start = (bf16[48,1024]{1,0:T(8,128)(2,1)S(1)}, bf16[48,1024]{1,0:T(8,128)(2,1)S(1)}, u32[]{:S(2)}, u32[]{:S(2)}) collective-permute-start(bf16[48,1024]{1,0:T(8,128)(2,1)S(1)} %get-tuple-element.68), channel_id=1, source_target_pairs={{0,1},{1,0},{2,3},{3,2},{4,5},{5,4},{6,7},{7,6},{8,9},{9,8},{10,11... | collective-permute-start | bytes 294920 | tf_op jit(solution)/shard_map/ppermute | solution.py:509
  2.8 7.2 %collective-permute-start.1 = (bf16[48,1024]{1,0:T(8,128)(2,1)S(1)}, bf16[48,1024]{1,0:T(8,128)(2,1)S(1)}, u32[]{:S(2)}, u32[]{:S(2)}) collective-permute-start(bf16[48,1024]{1,0:T(8,128)(2,1)S(1)} %get-tuple-element.69), channel_id=1, source_target_pairs={{1,2},{3,4},{5,6},{7,8},{9,10},{11,12},{13,14},{15,16},{17,18},{19... | collective-permute-start | bytes 294920 | tf_op jit(solution)/shard_map/ppermute | solution.py:506
  33.9 5.0 %collective-permute-start.6 = (f32[8,1024]{1,0:T(8,128)S(1)}, f32[8,1024]{1,0:T(8,128)S(1)}, u32[]{:S(2)}, u32[]{:S(2)}) collective-permute-start(f32[8,1024]{1,0:T(8,128)S(1)} %merge.7.stats_ref), channel_id=1, source_target_pairs={{0,16},{1,17},{2,18},{3,19},{4,20},{5,21},{6,22},{7,23},{8,24},{9,... | collective-permute-start | bytes 98312 | tf_op jit(solution)/shard_map/ppermute | solution.py:509
  46.4 8.4 %collective-permute-start.11 = (bf16[2,1040,256]{2,1,0:T(8,128)(2,1)S(1)}, bf16[2,1040,256]{2,1,0:T(8,128)(2,1)S(1)}, u32[]{:S(2)}, u32[]{:S(2)}) collective-permute-start(bf16[2,1040,256]{2,1,0:T(8,128)(2,1)S(1)} %get-tuple-element.89.outs_0_), channel_id=1, source_target_pairs={{0,1},{1,0},{2,3},{3,2},{4,5},{5,4},{6,7},{7,6},{8,9},{9,8},{10,11... | collective-permute-start | bytes 3194888 | tf_op jit(solution)/shard_map/ppermute | solution.py:509
  47.2 10.1 %collective-permute-start.8 = (bf16[2,256,256]{2,1,0:T(8,128)(2,1)S(1)}, bf16[2,256,256]{2,1,0:T(8,128)(2,1)S(1)}, u32[]{:S(2)}, u32[]{:S(2)}) collective-permute-start(bf16[2,256,256]{2,1,0:T(8,128)(2,1)S(1)} %get-tuple-element.92), channel_id=1, source_target_pairs={{0,2},{1,3},{2,0},{3,1},{4,6},{5,7},{6,4},{7,5},{8,10},{9,11},{10,... | collective-permute-start | bytes 786440 | tf_op jit(solution)/shard_map/ppermute | solution.py:509
  47.8 10.8 %collective-permute-start.9 = (bf16[2,256,256]{2,1,0:T(8,128)(2,1)S(1)}, bf16[2,256,256]{2,1,0:T(8,128)(2,1)S(1)}, u32[]{:S(2)}, u32[]{:S(2)}) collective-permute-start(bf16[2,256,256]{2,1,0:T(8,128)(2,1)S(1)} %get-tuple-element.93), channel_id=1, source_target_pairs={{0,4},{1,5},{2,6},{3,7},{4,0},{5,1},{6,2},{7,3},{8,12},{9,13},{10,... | collective-permute-start | bytes 786440 | tf_op jit(solution)/shard_map/ppermute | solution.py:509
  49.4 14.2 %collective-permute-start.10 = (bf16[2,256,256]{2,1,0:T(8,128)(2,1)S(1)}, bf16[2,256,256]{2,1,0:T(8,128)(2,1)S(1)}, u32[]{:S(2)}, u32[]{:S(2)}) collective-permute-start(bf16[2,256,256]{2,1,0:T(8,128)(2,1)S(1)} %get-tuple-element.94), channel_id=1, source_target_pairs={{0,6},{1,7},{2,4},{3,5},{4,2},{5,3},{6,0},{7,1},{8,14},{9,15},{10,... | collective-permute-start | bytes 786440 | tf_op jit(solution)/shard_map/ppermute | solution.py:509
  55.1 17.2 %collective-permute-start.14 = (bf16[2,272,256]{2,1,0:T(8,128)(2,1)S(1)}, bf16[2,272,256]{2,1,0:T(8,128)(2,1)S(1)}, u32[]{:S(2)}, u32[]{:S(2)}) collective-permute-start(bf16[2,272,256]{2,1,0:T(8,128)(2,1)S(1)} %get-tuple-element.101), channel_id=1, source_target_pairs={{0,2},{1,3},{2,0},{3,1},{4,6},{5,7},{6,4},{7,5},{8,10},{9,11},{10,... | collective-permute-start | bytes 835592 | tf_op jit(solution)/shard_map/ppermute | solution.py:509
  55.8 16.5 %collective-permute-start.15 = (bf16[2,272,256]{2,1,0:T(8,128)(2,1)S(1)}, bf16[2,272,256]{2,1,0:T(8,128)(2,1)S(1)}, u32[]{:S(2)}, u32[]{:S(2)}) collective-permute-start(bf16[2,272,256]{2,1,0:T(8,128)(2,1)S(1)} %get-tuple-element.102), channel_id=1, source_target_pairs={{0,4},{1,5},{2,6},{3,7},{4,0},{5,1},{6,2},{7,3},{8,12},{9,13},{10,... | collective-permute-start | bytes 835592 | tf_op jit(solution)/shard_map/ppermute | solution.py:509
  57.3 17.0 %collective-permute-start.16 = (bf16[2,272,256]{2,1,0:T(8,128)(2,1)S(1)}, bf16[2,272,256]{2,1,0:T(8,128)(2,1)S(1)}, u32[]{:S(2)}, u32[]{:S(2)}) collective-permute-start(bf16[2,272,256]{2,1,0:T(8,128)(2,1)S(1)} %get-tuple-element.103), channel_id=1, source_target_pairs={{0,6},{1,7},{2,4},{3,5},{4,2},{5,3},{6,0},{7,1},{8,14},{9,15},{10,... | collective-permute-start | bytes 835592 | tf_op jit(solution)/shard_map/ppermute | solution.py:509
  63.7 5.0 %collective-permute-start.12 = (bf16[2,128,256]{2,1,0:T(8,128)(2,1)S(1)}, bf16[2,128,256]{2,1,0:T(8,128)(2,1)S(1)}, u32[]{:S(2)}, u32[]{:S(2)}) collective-permute-start(bf16[2,128,256]{2,1,0:T(8,128)(2,1)S(1)} %get-tuple-element.98), channel_id=1, source_target_pairs={{0,8},{1,9},{2,10},{3,11},{4,12},{5,13},{6,14},{7,15},{8,0},{9,1},... | collective-permute-start | bytes 393224 | tf_op jit(solution)/shard_map/ppermute | solution.py:509
  68.8 5.7 %collective-permute-start.13 = (bf16[2,64,256]{2,1,0:T(8,128)(2,1)S(1)}, bf16[2,64,256]{2,1,0:T(8,128)(2,1)S(1)}, u32[]{:S(2)}, u32[]{:S(2)}) collective-permute-start(bf16[2,64,256]{2,1,0:T(8,128)(2,1)S(1)} %get-tuple-element.100), channel_id=1, source_target_pairs={{0,16},{1,17},{2,18},{3,19},{4,20},{5,21},{6,22},{7,23},{8,24},{9,... | collective-permute-start | bytes 196616 | tf_op jit(solution)/shard_map/ppermute | solution.py:509
  74.5 8.9 %collective-permute-start.17 = (bf16[2,64,256]{2,1,0:T(8,128)(2,1)S(1)}, bf16[2,64,256]{2,1,0:T(8,128)(2,1)S(1)}, u32[]{:S(2)}, u32[]{:S(2)}) collective-permute-start(bf16[2,64,256]{2,1,0:T(8,128)(2,1)S(1)} %s_line.3.mine_ref), channel_id=1, source_target_pairs={{0,16},{1,17},{2,18},{3,19},{4,20},{5,21},{6,22},{7,23},{8,24},{9,... | collective-permute-start | bytes 196616 | tf_op jit(solution)/shard_map/ppermute | solution.py:509
  77.6 8.5 %collective-permute-start.24 = (bf16[2,80,256]{2,1,0:T(8,128)(2,1)S(1)}, bf16[2,80,256]{2,1,0:T(8,128)(2,1)S(1)}, u32[]{:S(2)}, u32[]{:S(2)}) collective-permute-start(bf16[2,80,256]{2,1,0:T(8,128)(2,1)S(1)} %get-tuple-element.112), channel_id=1, source_target_pairs={{0,16},{1,17},{2,18},{3,19},{4,20},{5,21},{6,22},{7,23},{8,24},{9,... | collective-permute-start | bytes 245768 | tf_op jit(solution)/shard_map/ppermute | solution.py:509
  77.7 13.8 %collective-permute-start.22 = (bf16[48,1024]{1,0:T(8,128)(2,1)S(1)}, bf16[48,1024]{1,0:T(8,128)(2,1)S(1)}, u32[]{:S(2)}, u32[]{:S(2)}) collective-permute-start(bf16[48,1024]{1,0:T(8,128)(2,1)S(1)} %get-tuple-element.109), channel_id=1, source_target_pairs={{0,1},{1,0},{2,3},{3,2},{4,5},{5,4},{6,7},{7,6},{8,9},{9,8},{10,11... | collective-permute-start | bytes 294920 | tf_op jit(solution)/shard_map/ppermute | solution.py:509
  77.7 13.8 %collective-permute-start.23 = (bf16[48,1024]{1,0:T(8,128)(2,1)S(1)}, bf16[48,1024]{1,0:T(8,128)(2,1)S(1)}, u32[]{:S(2)}, u32[]{:S(2)}) collective-permute-start(bf16[48,1024]{1,0:T(8,128)(2,1)S(1)} %get-tuple-element.111), channel_id=1, source_target_pairs={{1,2},{3,4},{5,6},{7,8},{9,10},{11,12},{13,14},{15,16},{17,18},{19... | collective-permute-start | bytes 294920 | tf_op jit(solution)/shard_map/ppermute | solution.py:506
  78.3 9.6 %collective-permute-start.25 = (bf16[2,80,256]{2,1,0:T(8,128)(2,1)S(1)}, bf16[2,80,256]{2,1,0:T(8,128)(2,1)S(1)}, u32[]{:S(2)}, u32[]{:S(2)}) collective-permute-start(bf16[2,80,256]{2,1,0:T(8,128)(2,1)S(1)} %get-tuple-element.113), channel_id=1, source_target_pairs={{0,8},{1,9},{2,10},{3,11},{4,12},{5,13},{6,14},{7,15},{8,0},{9,1},... | collective-permute-start | bytes 245768 | tf_op jit(solution)/shard_map/ppermute | solution.py:509
  83.4 8.0 %collective-permute-start.26 = (bf16[2,80,256]{2,1,0:T(8,128)(2,1)S(1)}, bf16[2,80,256]{2,1,0:T(8,128)(2,1)S(1)}, u32[]{:S(2)}, u32[]{:S(2)}) collective-permute-start(bf16[2,80,256]{2,1,0:T(8,128)(2,1)S(1)} %get-tuple-element.114), channel_id=1, source_target_pairs={{0,24},{1,25},{2,26},{3,27},{4,28},{5,29},{6,30},{7,31},{8,16},{9,... | collective-permute-start | bytes 245768 | tf_op jit(solution)/shard_map/ppermute | solution.py:509
  86.1 6.6 %collective-permute-start.18 = (bf16[2,128,256]{2,1,0:T(8,128)(2,1)S(1)}, bf16[2,128,256]{2,1,0:T(8,128)(2,1)S(1)}, u32[]{:S(2)}, u32[]{:S(2)}) collective-permute-start(bf16[2,128,256]{2,1,0:T(8,128)(2,1)S(1)} %s_join.1.mine_ref), channel_id=1, source_target_pairs={{0,8},{1,9},{2,10},{3,11},{4,12},{5,13},{6,14},{7,15},{8,0},{9,1},... | collective-permute-start | bytes 393224 | tf_op jit(solution)/shard_map/ppermute | solution.py:509
  91.5 5.2 %collective-permute-start.27 = (bf16[2,64,256]{2,1,0:T(8,128)(2,1)S(1)}, bf16[2,64,256]{2,1,0:T(8,128)(2,1)S(1)}, u32[]{:S(2)}, u32[]{:S(2)}) collective-permute-start(bf16[2,64,256]{2,1,0:T(8,128)(2,1)S(1)} %get-tuple-element.115.mine_ref), channel_id=1, source_target_pairs={{0,16},{1,17},{2,18},{3,19},{4,20},{5,21},{6,22},{7,23},{8,24},{9,... | collective-permute-start | bytes 196616 | tf_op jit(solution)/shard_map/ppermute | solution.py:509
  92.8 5.0 %collective-permute-start.19 = (bf16[256,256]{1,0:T(8,128)(2,1)S(1)}, bf16[256,256]{1,0:T(8,128)(2,1)S(1)}, u32[]{:S(2)}, u32[]{:S(2)}) collective-permute-start(bf16[256,256]{1,0:T(8,128)(2,1)S(1)} %get-tuple-element.105.refs_0_), channel_id=1, source_target_pairs={{0,2},{1,3},{2,0},{3,1},{4,6},{5,7},{6,4},{7,5},{8,10},{9,11},{10,... | collective-permute-start | bytes 393224 | tf_op jit(solution)/shard_map/ppermute | solution.py:509
  92.9 5.6 %collective-permute-start.20 = (bf16[256,256]{1,0:T(8,128)(2,1)S(1)}, bf16[256,256]{1,0:T(8,128)(2,1)S(1)}, u32[]{:S(2)}, u32[]{:S(2)}) collective-permute-start(bf16[256,256]{1,0:T(8,128)(2,1)S(1)} %get-tuple-element.106.refs_1_), channel_id=1, source_target_pairs={{0,4},{1,5},{2,6},{3,7},{4,0},{5,1},{6,2},{7,3},{8,12},{9,13},{10,... | collective-permute-start | bytes 393224 | tf_op jit(solution)/shard_map/ppermute | solution.py:509
  96.8 5.0 %collective-permute-start.28 = (bf16[2,128,256]{2,1,0:T(8,128)(2,1)S(1)}, bf16[2,128,256]{2,1,0:T(8,128)(2,1)S(1)}, u32[]{:S(2)}, u32[]{:S(2)}) collective-permute-start(bf16[2,128,256]{2,1,0:T(8,128)(2,1)S(1)} %p_join.2.mine_ref), channel_id=1, source_target_pairs={{0,8},{1,9},{2,10},{3,11},{4,12},{5,13},{6,14},{7,15},{8,0},{9,1},... | collective-permute-start | bytes 393224 | tf_op jit(solution)/shard_map/ppermute | solution.py:509
  98.6 9.3 %collective-permute-start.21 = (bf16[512,256]{1,0:T(8,128)(2,1)S(1)}, bf16[512,256]{1,0:T(8,128)(2,1)S(1)}, u32[]{:S(2)}, u32[]{:S(2)}) collective-permute-start(bf16[512,256]{1,0:T(8,128)(2,1)S(1)} %get-tuple-element.107.half_one), channel_id=1, source_target_pairs={{0,4},{1,5},{2,6},{3,7},{4,0},{5,1},{6,2},{7,3},{8,12},{9,13},{10,... | collective-permute-start | bytes 786440 | tf_op jit(solution)/shard_map/ppermute | solution.py:509
  100.4 14.5 %collective-permute-start.37 = (bf16[512,256]{1,0:T(8,128)(2,1)S(1)}, bf16[512,256]{1,0:T(8,128)(2,1)S(1)}, u32[]{:S(2)}, u32[]{:S(2)}) collective-permute-start(bf16[512,256]{1,0:T(8,128)(2,1)S(1)} %get-tuple-element.117.half_two), channel_id=1, source_target_pairs={{0,2},{1,3},{2,0},{3,1},{4,6},{5,7},{6,4},{7,5},{8,10},{9,11},{10,... | collective-permute-start | bytes 786440 | tf_op jit(solution)/shard_map/ppermute | solution.py:509
  101.8 14.3 %collective-permute-start.35 = (bf16[2,256,256]{2,1,0:T(8,128)(2,1)S(1)}, bf16[2,256,256]{2,1,0:T(8,128)(2,1)S(1)}, u32[]{:S(2)}, u32[]{:S(2)}) collective-permute-start(bf16[2,256,256]{2,1,0:T(8,128)(2,1)S(1)} %p_join.3.refs_0_), channel_id=1, source_target_pairs={{0,6},{1,7},{2,4},{3,5},{4,2},{5,3},{6,0},{7,1},{8,14},{9,15},{10,... | collective-permute-start | bytes 786440 | tf_op jit(solution)/shard_map/ppermute | solution.py:509
  102.6 14.7 %collective-permute-start.33 = (bf16[2,256,256]{2,1,0:T(8,128)(2,1)S(1)}, bf16[2,256,256]{2,1,0:T(8,128)(2,1)S(1)}, u32[]{:S(2)}, u32[]{:S(2)}) collective-permute-start(bf16[2,256,256]{2,1,0:T(8,128)(2,1)S(1)} %p_join.3.refs_0_), channel_id=1, source_target_pairs={{0,4},{1,5},{2,6},{3,7},{4,0},{5,1},{6,2},{7,3},{8,12},{9,13},{10,... | collective-permute-start | bytes 786440 | tf_op jit(solution)/shard_map/ppermute | solution.py:509
  103.9 14.5 %collective-permute-start.31 = (bf16[2,256,256]{2,1,0:T(8,128)(2,1)S(1)}, bf16[2,256,256]{2,1,0:T(8,128)(2,1)S(1)}, u32[]{:S(2)}, u32[]{:S(2)}) collective-permute-start(bf16[2,256,256]{2,1,0:T(8,128)(2,1)S(1)} %p_join.3.refs_0_), channel_id=1, source_target_pairs={{0,2},{1,3},{2,0},{3,1},{4,6},{5,7},{6,4},{7,5},{8,10},{9,11},{10,... | collective-permute-start | bytes 786440 | tf_op jit(solution)/shard_map/ppermute | solution.py:509
  107.9 10.6 %collective-permute-start.30 = (bf16[2,256,256]{2,1,0:T(8,128)(2,1)S(1)}, bf16[2,256,256]{2,1,0:T(8,128)(2,1)S(1)}, u32[]{:S(2)}, u32[]{:S(2)}) collective-permute-start(bf16[2,256,256]{2,1,0:T(8,128)(2,1)S(1)} %p_join.3.refs_0_), channel_id=1, source_target_pairs={{0,1},{1,0},{2,3},{3,2},{4,5},{5,4},{6,7},{7,6},{8,9},{9,8},{10,11... | collective-permute-start | bytes 786440 | tf_op jit(solution)/shard_map/ppermute | solution.py:509
  116.1 7.8 %collective-permute-start.38 = (bf16[2,512,256]{2,1,0:T(8,128)(2,1)S(1)}, bf16[2,512,256]{2,1,0:T(8,128)(2,1)S(1)}, u32[]{:S(2)}, u32[]{:S(2)}) collective-permute-start(bf16[2,512,256]{2,1,0:T(8,128)(2,1)S(1)} %get-tuple-element.119.refs_0_), channel_id=1, source_target_pairs={{0,1},{1,0},{2,3},{3,2},{4,5},{5,4},{6,7},{7,6},{8,9},{9,8},{10,11... | collective-permute-start | bytes 1572872 | tf_op jit(solution)/shard_map/ppermute | solution.py:509
  116.1 7.8 %collective-permute-start.39 = (bf16[2,512,256]{2,1,0:T(8,128)(2,1)S(1)}, bf16[2,512,256]{2,1,0:T(8,128)(2,1)S(1)}, u32[]{:S(2)}, u32[]{:S(2)}) collective-permute-start(bf16[2,512,256]{2,1,0:T(8,128)(2,1)S(1)} %get-tuple-element.120.refs_1_), channel_id=1, source_target_pairs={{0,1},{1,0},{2,3},{3,2},{4,5},{5,4},{6,7},{7,6},{8,9},{9,8},{10,11... | collective-permute-start | bytes 1572872 | tf_op jit(solution)/shard_map/ppermute | solution.py:509
  117.4 4.9 %collective-permute-start.36 = (bf16[2,256,256]{2,1,0:T(8,128)(2,1)S(1)}, bf16[2,256,256]{2,1,0:T(8,128)(2,1)S(1)}, u32[]{:S(2)}, u32[]{:S(2)}) collective-permute-start(bf16[2,256,256]{2,1,0:T(8,128)(2,1)S(1)} %collective-permute-done.35.refs_3_), channel_id=1, source_target_pairs={{0,1},{1,0},{2,3},{3,2},{4,5},{5,4},{6,7},{7,6},{8,9},{9,8},{10,11... | collective-permute-start | bytes 786440 | tf_op jit(solution)/shard_map/ppermute | solution.py:509
  (20 other events, 149.6 us)
